TPU v7x, 32 devices: a whole 2x2x4 slice. The times are simulated.
32 devices in a mesh: ex: 8 (over y, x, core), mp: 4 (over z).
Axes of the slice: x: 2, y: 2, z: 4, core: 2. Of those that a mesh axis runs over, the one named last changes fastest.
Arguments:
- acts: bfloat16 [4, 1024, 4096], P('mp', 'ex'), may hold values from -6 to 6
- grads: bfloat16 [4, 1024, 1024], P('mp', 'ex'), may hold values from -12 to 12
- down_factor: bfloat16 [4, 16, 4096], P('mp'), may hold values from -0.09375 to 0.09375
- up_factor_transposed: bfloat16 [4, 16, 1024], P('mp'), may hold values from -0.1875 to 0.1875
- input_projection: bfloat16 [4, 64, 4096], P('mp'), may hold values from -0.09375 to 0.09375
- gradient_projection: bfloat16 [4, 64, 1024], P('mp'), may hold values from -0.1875 to 0.1875
- order: int32 [4, 8, 16], P('mp', 'ex'), may hold values from 0 to 15, each once within a row
- damping: float32 [1], replicated, may hold values from 0.5 to 2
Outputs:
- features: float32 [128, 1024], P(('ex', 'mp'))
- factor_r: float32 [16, 64, 64], P('mp')
Inputs may be any that keep to these rules, and one draw needn't show every extreme that they name: order[b, m] lists each of the 16 examples of shard m once: stored example e of block b is example order[b, m, e] of that shard.
All inputs are finite; a program needn't handle non-finite values.
Results may differ from a plain program's by a relative error of at most 0.0003.
Values sent between devices are 32-bit elements; how exact they have to be, the bound alone decides.
No kernel may reach another device: no remote copies, remote signals or barrier semaphores. Data moves between devices by JAX's collectives and lax.ppermute only.
A program may use at most 64 MiB of HBM per device.

v0:
```python
import math

import jax
import jax.numpy as jnp
from jax import lax
from jax.sharding import PartitionSpec as P

EXAMPLE_LENGTH = 8


def project_features(rows, weight):
    return lax.dot_general(
        rows, weight, (((1,), (1,)), ((), ())), preferred_element_type=jnp.float32
    )


def channel_gram(rows, adapter_rank, sketch_columns):
    grouped = rows.reshape(rows.shape[0], adapter_rank, sketch_columns)
    return jnp.einsum("eck,ecl->ckl", grouped, grouped, precision=lax.Precision.HIGHEST)


def local(
    acts,
    grads,
    down_factor,
    up_factor_transposed,
    input_projection,
    gradient_projection,
    order,
    damping,
):
    input_rows = acts[0]
    output_gradients = grads[0]
    local_example_rows = input_rows.shape[0] // EXAMPLE_LENGTH
    adapter_rank = down_factor.shape[1]
    sketch_columns = input_projection.shape[1]
    feature_width = adapter_rank * sketch_columns
    scaling = 1.0 / math.sqrt(2.0 * EXAMPLE_LENGTH * lax.axis_size("mp"))
    reduced_gradient = project_features(output_gradients, up_factor_transposed[0]).reshape(
        local_example_rows, EXAMPLE_LENGTH, adapter_rank
    )
    reduced_input = project_features(input_rows, down_factor[0]).reshape(
        local_example_rows, EXAMPLE_LENGTH, adapter_rank
    )
    sketch_in = project_features(input_rows, input_projection[0]).reshape(
        local_example_rows, EXAMPLE_LENGTH, sketch_columns
    )
    sketch_out = project_features(output_gradients, gradient_projection[0]).reshape(
        local_example_rows, EXAMPLE_LENGTH, sketch_columns
    )
    first = jnp.einsum("etc,etk->eck", reduced_gradient, sketch_in, precision=lax.Precision.HIGHEST)
    second = jnp.einsum("etc,etk->eck", reduced_input, sketch_out, precision=lax.Precision.HIGHEST)
    partial_value = (first + second).reshape(local_example_rows, feature_width) * scaling
    stored = order[0, 0]
    per_device = local_example_rows // lax.axis_size("mp")
    row_ids = jnp.arange(per_device * lax.axis_size("mp"), dtype=jnp.int32)
    selector = (row_ids[:, None] == stored[None, :]).astype(jnp.float32)
    own_rows = lax.psum_scatter(
        jnp.dot(selector, partial_value, precision=lax.Precision.HIGHEST),
        "mp",
        scatter_dimension=0,
        tiled=True,
    )
    all_examples = local_example_rows * lax.axis_size("ex")
    part_channels = adapter_rank // lax.axis_size("mp")
    channel_rows = lax.all_to_all(own_rows, "mp", split_axis=1, concat_axis=0, tiled=True)
    local_gram = channel_gram(channel_rows, part_channels, sketch_columns)
    own_blocks = lax.psum(local_gram, "ex")
    system = (
        own_blocks / all_examples
        + damping[0] * jnp.eye(sketch_columns, dtype=jnp.float32)[None, :, :]
    )
    r_block = jnp.swapaxes(jnp.linalg.cholesky(system), 1, 2)
    return (own_rows, r_block)


def solution(mesh):
    in_specs = (
        P("mp", "ex", None),
        P("mp", "ex", None),
        P("mp", None, None),
        P("mp", None, None),
        P("mp", None, None),
        P("mp", None, None),
        P("mp", "ex", None),
        P(),
    )
    out_specs = (P(("ex", "mp"), None), P("mp", None, None))
    return jax.shard_map(local, mesh=mesh, in_specs=in_specs, out_specs=out_specs, check_vma=False)
```

profile of v0, /device:TPU:0, one launch (start us, length us, event | category | flops | bytes accessed | tf_op | source)
XLA Modules:
  0.0 148.2 jit_solution(15425274883595457367)
XLA Ops:
  7.2 0.0 copy-start
  7.2 0.0 copy-start.3
  7.2 0.0 all-reduce.6.cloned.1.call-start
  7.2 1.2 copy-done
  8.4 1.5 fusion.3
  9.9 0.0 copy-done.3
  9.9 0.0 copy-start.1
  9.9 0.0 copy-start.5
  9.9 0.4 fusion.1
  10.3 0.5 copy-done.1
  10.8 0.0 copy-done.5
  10.8 0.0 copy-start.4
  10.8 0.2 fusion.8
  11.0 0.7 copy-done.4
  11.7 0.2 fusion.6
  12.0 0.4 fusion.18
  12.4 0.4 fusion
  12.8 0.1 mul.19
  12.9 0.0 copy-start.6
  12.9 0.6 copy-done.6
  13.6 0.8 fusion.16
  14.4 0.0 all-reduce.6.cloned.1.call-update
  15.0 0.0 copy-start.7
  15.1 0.6 copy-done.7
  15.7 0.6 dynamic-slice
  17.0 34.3 %all-reduce.6.cloned.1.call-done = f32[16,1024]{1,0:T(8,128)} async-done(((f32[16,1024]{1,0:T(8,128)}), f32[16,1024]{1,0:T(8,128)}) %all-reduce.6.cloned.1.call-update) | async-done | bytes 65552
  51.2 1.4 constant_dynamic-slice_fusion
  52.6 3.4 %all-to-all-start = ((f32[4,4,256]{2,0,1:T(4,128)}), f32[4,4,256]{2,0,1:T(4,128)S(1)}, u32[]{:S(2)}, u32[]{:S(2)}) async-start(f32[4,4,256]{2,0,1:T(4,128)} %bitcast.11), calls=%async_computation | async-start | bytes 32768 | tf_op jit(solution)/shard_map/all_to_all | solution.py:66
  56.0 0.0 all-reduce.4.cloned.1.call-start
  56.0 5.6 %all-to-all-done = f32[4,4,256]{2,0,1:T(4,128)S(1)} async-done(((f32[4,4,256]{2,0,1:T(4,128)}), f32[4,4,256]{2,0,1:T(4,128)S(1)}, u32[]{:S(2)}, u32[]{:S(2)}) %all-to-all-start) | async-done | bytes 16416 | tf_op jit(solution)/shard_map/all_to_all | solution.py:66
  61.6 0.1 reshape.41
  61.7 1.1 fusion.14
  62.7 0.0 all-reduce.4.cloned.1.call-update
  62.8 0.1 copy.28
  62.9 52.2 %all-reduce.4.cloned.1.call-done = f32[4,64,64]{1,2,0:T(8,128)} async-done(((f32[4,64,64]{1,2,0:T(8,128)}), f32[4,64,64]{1,2,0:T(8,128)}) %all-reduce.4.cloned.1.call-update) | async-done | bytes 65552 | tf_op jit(solution)/shard_map/psum | solution.py:68
  115.1 0.9 multiply_add_fusion
  116.0 0.0 copy-start.2
  116.0 0.1 copy.33
  116.1 0.8 copy-done.2
  116.9 23.5 %custom-call.4 = f32[4,64,64]{2,1,0:T(8,128)S(1)} custom-call(f32[4,64,64]{2,1,0:T(8,128)S(1)} %fusion.10), custom_call_target="Cholesky" | custom-call | tf_op jit(solution)/shard_map/jit(cholesky)/cholesky | solution.py:73
  140.4 0.1 compare_reduce_fusion
  140.6 0.1 select_bitcast_fusion
  140.7 0.8 copy.34
  (5 shorter events, 0.1 us)
Async XLA Ops:
  7.2 1.2 copy-start
  7.2 2.7 %copy-start.3 = (bf16[1,16,4096]{2,1,0:T(8,128)(2,1)S(1)}, bf16[1,16,4096]{2,1,0:T(8,128)(2,1)}, u32[]{:S(2)}) copy-start(bf16[1,16,4096]{2,1,0:T(8,128)(2,1)} %param.10) | copy-start | bytes 393220
  7.2 44.0 %all-reduce.6.cloned.1.call-start = ((), (), s32[]{:S(2)}) async-start(), calls=%async_computation.2 | async-start | bytes 131072
  9.9 1.0 copy-start.1
  9.9 0.9 copy-start.5
  10.8 0.9 copy-start.4
  12.9 0.7 copy-start.6
  15.0 0.7 copy-start.7
  52.6 9.0 %all-to-all-start = ((f32[4,4,256]{2,0,1:T(4,128)}), f32[4,4,256]{2,0,1:T(4,128)S(1)}, u32[]{:S(2)}, u32[]{:S(2)}) async-start(f32[4,4,256]{2,0,1:T(4,128)} %bitcast.11), calls=%async_computation | async-start | bytes 32768 | tf_op jit(solution)/shard_map/all_to_all | solution.py:66
  56.0 59.1 %all-reduce.4.cloned.1.call-start = ((), (), s32[]{:S(2)}) async-start(), calls=%async_computation.1 | async-start | bytes 262144 | tf_op jit(solution)/shard_map/psum | solution.py:68
  116.0 0.9 copy-start.2
Sparse Core Ops, SparseCore 0:
  14.5 36.6 all-reduce.5
  62.9 52.1 all-reduce.3
where the time goes:
time: 149 us; the launch traced here: 148 us
  waiting for transfers between devices  92.1 us (62%)
  other arithmetic  24.7 us (17%)
  between operations  15.5 us (10%)
  local copies, waits for them, and re-layouts  7.56 us (5%)
  matrix products  4.99 us (3%)
  starting transfers between devices  3.43 us (2%)
    psum x1, waiting for transfers between devices, local(): own_blocks = lax.psum(local_gram, 'ex')  52.2 us
    unnamed x3, waiting for transfers between devices  34.3 us
    another operation x4, other arithmetic, local(): r_block = jnp.swapaxes(jnp.linalg.cholesky(system), 1, 2)  23.6 us
    unnamed x19, local copies, waits for them, and re-layouts  7.19 us
    all_to_all x1, waiting for transfers between devices, local(): lax.all_to_all(own_rows, 'mp', split_axis=1, concat_axis=0, tiled=True)  5.6 us
    all_to_all x1, starting transfers between devices, local(): lax.all_to_all(own_rows, 'mp', split_axis=1, concat_axis=0, tiled=True)  3.39 us
  transfers between devices with their start and end apart: 3, of which 3 were waited for; matrix products, arithmetic and copies ran while one was open for 0% of the time, Pallas kernels for 0%

commit v1 on v0

v1 whole, which is shorter than its diff:
```python
import functools
import math

import jax
import jax.numpy as jnp
from jax import lax
from jax.experimental import pallas as pl
from jax.experimental.pallas import tpu as pltpu
from jax.sharding import PartitionSpec as P

EXAMPLE_LENGTH = 8
LANES = 128
SLOT = 32
GROUP = LANES // SLOT
PANEL = 8


def dot_nt(a, b):
    return lax.dot_general(
        a, b, (((1,), (1,)), ((), ())), preferred_element_type=jnp.float32
    )


def dot_tn(a, b):
    return lax.dot_general(
        a, b, (((0,), (0,)), ((), ())), preferred_element_type=jnp.float32
    )


def split(x):
    high = x.astype(jnp.bfloat16)
    return high, (x - high.astype(jnp.float32)).astype(jnp.bfloat16)


def partial_kernel(
    parts, scaling, acts, grads, down, up, proj_in, proj_out, order, send, low, out
):
    tokens = acts.shape[1]
    rank = down.shape[1]
    sketch = proj_in.shape[1]
    examples = tokens // EXAMPLE_LENGTH
    per = rank // parts
    halves = sketch // SLOT
    from_acts = dot_nt(jnp.concatenate([proj_in[0], down[0]], axis=0), acts[0])
    from_grads = dot_nt(jnp.concatenate([proj_out[0], up[0]], axis=0), grads[0])
    sketches = jnp.concatenate([from_acts[:sketch], from_grads[:sketch]], axis=1)
    low[0] = from_grads[sketch:] * scaling
    low[1] = from_acts[sketch:] * scaling

    rows = examples * parts
    lane = lax.broadcasted_iota(jnp.int32, (rows, 2 * tokens), 1)
    source = (lane % tokens) // EXAMPLE_LENGTH
    target = jnp.zeros((8, 2 * tokens), jnp.int32)
    for s in range(examples):
        target = jnp.where(source[:8] == s, order[0, 0, s], target)
    target = jnp.concatenate([target] * (rows // 8), axis=0)
    place = lax.broadcasted_iota(jnp.int32, (rows, 2 * tokens), 0) // parts
    mine = target == place
    highs, lows = [], []
    for c in range(per):
        chosen = jnp.concatenate(
            [low[i, pl.ds(c, parts, stride=per), :] for i in range(2)], axis=1
        )
        chosen = jnp.concatenate([chosen] * examples, axis=0)
        high, rest = split(jnp.where(mine, chosen, 0.0))
        highs.append(high)
        lows.append(rest)
    left_high = jnp.concatenate(highs, axis=0)
    left_low = jnp.concatenate(lows, axis=0)
    right = jnp.concatenate(
        [sketches[h * SLOT : (h + 1) * SLOT] for h in range(halves) for _ in range(per)],
        axis=0,
    )
    right_high, right_low = split(right)
    spread = (
        dot_nt(left_high, right_low) + dot_nt(left_low, right_high)
    ) + dot_nt(left_high, right_high)
    column = lax.broadcasted_iota(jnp.int32, (rows, per * sketch), 1)
    channel = (column // SLOT) % per
    total = spread[:rows]
    for c in range(1, per):
        total = jnp.where(channel == c, spread[c * rows : (c + 1) * rows], total)
    for start in range(0, per * sketch, LANES):
        stop = min(start + LANES, per * sketch)
        out[:, : stop - start] = total[:, start:stop]
        for g in range(parts):
            send[g, :examples, start:stop] = out[
                g * examples : (g + 1) * examples, : stop - start
            ]
            send[g, examples:, start:stop] = out[pl.ds(g, examples, stride=parts), :][
                :, : stop - start
            ]


def column_kernel(recv, columns):
    examples = columns.shape[1]
    total = jnp.sum(recv[:, examples:, :], axis=0)
    width = total.shape[1]
    for m in range(columns.shape[0]):
        columns[m, :, :width] = total
        if columns.shape[2] > width:
            columns[m, :, width:] = jnp.zeros(
                (examples, columns.shape[2] - width), jnp.float32
            )


def feature_kernel(parts, per, recv, features):
    rows_here, width = features.shape
    examples = rows_here * parts
    total = jnp.sum(recv[:, :examples, :], axis=0)
    span = width // parts
    halves = span // (per * SLOT)
    natural = jnp.concatenate(
        [
            total[:, (h * per + c) * SLOT : (h * per + c + 1) * SLOT]
            for c in range(per)
            for h in range(halves)
        ],
        axis=1,
    )
    for r in range(rows_here):
        features[r : r + 1, :] = jnp.concatenate(
            [natural[r * parts + g : r * parts + g + 1, :] for g in range(parts)], axis=1
        )


def pick_lanes(x, index):
    return jnp.take_along_axis(x, index, axis=1)


def reciprocal(x):
    guess = pl.reciprocal(x, approx=True)
    guess = guess * (2.0 - x * guess)
    return guess * (2.0 - x * guess)


def factor_kernel(rows, damping, factors):
    channels, sketch, _ = factors.shape
    halves = sketch // SLOT
    panels = sketch // PANEL
    per_half = SLOT // PANEL
    stacked = jnp.concatenate([rows[m] for m in range(rows.shape[0])], axis=0)
    examples = stacked.shape[0]
    high, rest = split(stacked)
    gram = (dot_tn(high, rest) + dot_tn(rest, high)) + dot_tn(high, high)
    lane = lax.broadcasted_iota(jnp.int32, (PANEL, LANES), 1)
    sub = lax.broadcasted_iota(jnp.int32, (PANEL, LANES), 0)
    slot = lane // SLOT
    within = lane % SLOT
    ridge = damping[0]
    tile = []
    for q in range(panels):
        hr, at = divmod(q, per_half)
        line = []
        for h in range(halves):
            value = None
            for c in range(GROUP):
                start = hr * LANES + c * SLOT + at * PANEL
                block = gram[start : start + PANEL, h * LANES : (h + 1) * LANES]
                value = block if c == 0 else jnp.where(slot == c, block, value)
            value = value * (1.0 / examples)
            if h == hr:
                value = value + jnp.where(within == at * PANEL + sub, ridge, 0.0)
            line.append(value)
        tile.append(line)

    zero = jnp.zeros((PANEL, LANES), jnp.float32)
    finished = []
    for q in range(panels):
        hq, at = divmod(q, per_half)
        column = [
            {
                j: pick_lanes(tile[j][hq], slot * SLOT + at * PANEL + r)
                for j in range(q, panels)
            }
            for r in range(PANEL)
        ]
        block = [
            [
                jnp.broadcast_to(column[r][q][s : s + 1, :], (PANEL, LANES))
                if s >= r
                else None
                for s in range(PANEL)
            ]
            for r in range(PANEL)
        ]
        line = [
            [
                jnp.broadcast_to(tile[q][h][r : r + 1, :], (PANEL, LANES))
                if h >= hq
                else None
                for h in range(halves)
            ]
            for r in range(PANEL)
        ]
        inverse = []
        for r in range(PANEL):
            inv = reciprocal(block[r][r])
            inverse.append(inv)
            for s in range(r + 1, PANEL):
                ratio = block[r][s] * inv
                for t in range(s, PANEL):
                    block[s][t] = block[s][t] - ratio * block[r][t]
                for j in range(q + 1, panels):
                    column[s][j] = column[s][j] - ratio * column[r][j]
                for h in range(hq, halves):
                    line[s][h] = line[s][h] - ratio * line[r][h]
        result = []
        for h in range(halves):
            if h < hq:
                result.append(zero)
                continue
            value = zero
            for r in range(PANEL):
                value = jnp.where(sub == r, line[r][h] * lax.rsqrt(block[r][r]), value)
            if h == hq:
                value = jnp.where(within >= at * PANEL + sub, value, 0.0)
            result.append(value)
        finished.append(result)
        for j in range(q + 1, panels):
            weights = [column[r][j] * inverse[r] for r in range(PANEL)]
            for h in range((q + 1) // per_half, halves):
                value = tile[j][h]
                for r in range(PANEL):
                    value = value - weights[r] * line[r][h]
                tile[j][h] = value

    for q in range(panels):
        for c in range(channels):
            factors[c, q * PANEL : (q + 1) * PANEL, :] = jnp.concatenate(
                [finished[q][h][:, c * SLOT : (c + 1) * SLOT] for h in range(halves)],
                axis=1,
            )


def vmem():
    return pl.BlockSpec(memory_space=pltpu.VMEM)


def smem():
    return pl.BlockSpec(memory_space=pltpu.SMEM)


def local(
    acts,
    grads,
    down_factor,
    up_factor_transposed,
    input_projection,
    gradient_projection,
    order,
    damping,
):
    parts = lax.axis_size("mp")
    shards = lax.axis_size("ex")
    tokens = acts.shape[1]
    rank = down_factor.shape[1]
    sketch = input_projection.shape[1]
    examples = tokens // EXAMPLE_LENGTH
    per = rank // parts
    span = per * sketch
    scaling = 1.0 / math.sqrt(2.0 * EXAMPLE_LENGTH * parts)
    send = pl.pallas_call(
        functools.partial(partial_kernel, parts, scaling),
        out_shape=jax.ShapeDtypeStruct((parts, 2 * examples, span), jnp.float32),
        in_specs=[vmem()] * 6 + [smem()],
        out_specs=vmem(),
        scratch_shapes=[
            pltpu.VMEM((2, rank, tokens), jnp.float32),
            pltpu.VMEM((examples * parts, LANES), jnp.float32),
        ],
        compiler_params=pltpu.CompilerParams(vmem_limit_bytes=32 * 2**20),
        name="partials",
    )(
        acts,
        grads,
        down_factor,
        up_factor_transposed,
        input_projection,
        gradient_projection,
        order,
    )
    recv = lax.all_to_all(send, "mp", split_axis=0, concat_axis=0, tiled=True)
    padded = max(span, GROUP * sketch)
    columns = pl.pallas_call(
        column_kernel,
        out_shape=jax.ShapeDtypeStruct((shards, examples, padded), jnp.float32),
        in_specs=[vmem()],
        out_specs=vmem(),
        name="columns",
    )(recv)
    rows = lax.all_to_all(columns, "ex", split_axis=0, concat_axis=0, tiled=True)
    features = pl.pallas_call(
        functools.partial(feature_kernel, parts, per),
        out_shape=jax.ShapeDtypeStruct((examples // parts, rank * sketch), jnp.float32),
        in_specs=[vmem()],
        out_specs=vmem(),
        name="features",
    )(recv)
    factors = pl.pallas_call(
        factor_kernel,
        out_shape=jax.ShapeDtypeStruct((per, sketch, sketch), jnp.float32),
        in_specs=[vmem(), smem()],
        out_specs=vmem(),
        compiler_params=pltpu.CompilerParams(vmem_limit_bytes=32 * 2**20),
        name="factors",
    )(rows, damping)
    return features, factors


def solution(mesh):
    in_specs = (
        P("mp", "ex", None),
        P("mp", "ex", None),
        P("mp", None, None),
        P("mp", None, None),
        P("mp", None, None),
        P("mp", None, None),
        P("mp", "ex", None),
        P(),
    )
    out_specs = (P(("ex", "mp"), None), P("mp", None, None))
    return jax.shard_map(
        local, mesh=mesh, in_specs=in_specs, out_specs=out_specs, check_vma=False
    )
```

time: 149 us -> 35.5 us (0.24)
  waiting for transfers between devices: 92.1 us -> 3.28 us
  other arithmetic: 24.7 us -> 0 us
  between operations: 15.5 us -> 1.3 us
  blocking collectives: 0 us -> 12.3 us
  Pallas kernels: 0 us -> 7.97 us
  matrix products: 4.99 us -> 0 us
    psum x1 -> x0, waiting for transfers between devices: 52.2 us -> none  [local(): own_blocks = lax.psum(local_gram, 'ex')]
    unnamed x3 -> x0, waiting for transfers between devices: 34.3 us -> none
    another operation x4 -> x0, other arithmetic: 23.6 us -> none  [local(): r_block = jnp.swapaxes(jnp.linalg.cholesky(system), 1, 2)]
    all_to_all x0 -> x1, blocking collectives: none -> 12.3 us  [local(): recv = lax.all_to_all(send, 'mp', split_axis=0, concat_axis=0, tiled=True)]
    pallas_call x0 -> x4, Pallas kernels: none -> 7.97 us  [the longest x1 3.27 us: local(): pl.pallas_call(factor_kernel, out_shape=jax.ShapeDtypeStruct((per, sketch...]
    dot_general x8 -> x0, matrix products: 4.99 us -> none  [the longest x4 2.29 us: project_features(): lax.dot_general(rows, weight, (((1,), (1,)), ((), ())), preferred_element...]
    all_to_all x1, waiting for transfers between devices: 5.6 us -> 3.28 us  [local(): lax.all_to_all(columns, 'ex', split_axis=0, concat_axis=0, tiled=True)]
    unnamed x19 -> x14, local copies, waits for them, and re-layouts: 7.19 us -> 6.43 us
  transfers between devices with their start and end apart: 3 -> 1, of which waited for: 3 -> 1; matrix products, arithmetic and copies ran while one was open for 0% -> 0% of each run, Pallas kernels for 0% -> 5%
where the time goes in v1:
time: 35.5 us; the launch traced here: 35 us
  blocking collectives  12.3 us (35%)
  Pallas kernels  7.97 us (22%)
  local copies, waits for them, and re-layouts  6.43 us (18%)
  starting transfers between devices  3.72 us (10%)
  waiting for transfers between devices  3.28 us (9%)
  between operations  1.3 us (4%)
    all_to_all x1, blocking collectives, local(): recv = lax.all_to_all(send, 'mp', split_axis=0, concat_axis=0, tiled=True)  12.3 us
    unnamed x14, local copies, waits for them, and re-layouts  6.43 us
    all_to_all x1, starting transfers between devices, local(): lax.all_to_all(columns, 'ex', split_axis=0, concat_axis=0, tiled=True)  3.72 us
    all_to_all x1, waiting for transfers between devices, local(): lax.all_to_all(columns, 'ex', split_axis=0, concat_axis=0, tiled=True)  3.28 us
    pallas_call x1, Pallas kernels, local(): pl.pallas_call(factor_kernel, out_shape=jax.ShapeDtypeStruct((per, sketch...  3.27 us
    pallas_call x1, Pallas kernels, local(): pl.pallas_call(functools.partial(feature_kernel, parts, per), out_shape=j...  1.6 us
    pallas_call x1, Pallas kernels, local(): pl.pallas_call(column_kernel, out_shape=jax.ShapeDtypeStruct((shards, exa...  1.57 us
    pallas_call x1, Pallas kernels, local(): pl.pallas_call(functools.partial(partial_kernel, parts, scaling), out_sha...  1.54 us
  transfers between devices with their start and end apart: 1, of which 1 were waited for; matrix products, arithmetic and copies ran while one was open for 0% of the time, Pallas kernels for 5%

profile of v1, /device:TPU:0, one launch (start us, length us, event | category | flops | bytes accessed | tf_op | source)
XLA Modules:
  0.0 35.0 jit_solution(12228445721588382102)
XLA Ops:
  0.6 0.0 copy-start
  0.6 1.2 %copy-done = bf16[1,128,4096]{2,1,0:T(8,128)(2,1)S(1)} copy-done((bf16[1,128,4096]{2,1,0:T(8,128)(2,1)S(1)}, bf16[1,128,4096]{2,1,0:T(8,128)(2,1)}, u32[]{:S(2)}) %copy-start) | copy-done | bytes 1048600
  1.9 0.0 copy-start.1
  1.9 1.0 %copy-done.1 = bf16[1,64,4096]{2,1,0:T(8,128)(2,1)S(1)} copy-done((bf16[1,64,4096]{2,1,0:T(8,128)(2,1)S(1)}, bf16[1,64,4096]{2,1,0:T(8,128)(2,1)}, u32[]{:S(2)}) %copy-start.1) | copy-done | bytes 524312
  2.9 0.0 copy-start.2
  2.9 0.9 %copy-done.2 = bf16[1,128,1024]{2,1,0:T(8,128)(2,1)S(1)} copy-done((bf16[1,128,1024]{2,1,0:T(8,128)(2,1)S(1)}, bf16[1,128,1024]{2,1,0:T(8,128)(2,1)}, u32[]{:S(2)}) %copy-start.2) | copy-done | bytes 262168
  3.9 0.0 copy-start.3
  3.9 0.9 %copy-done.3 = bf16[1,16,4096]{2,1,0:T(8,128)(2,1)S(1)} copy-done((bf16[1,16,4096]{2,1,0:T(8,128)(2,1)S(1)}, bf16[1,16,4096]{2,1,0:T(8,128)(2,1)}, u32[]{:S(2)}) %copy-start.3) | copy-done | bytes 131096
  4.8 0.0 copy-start.4
  4.8 0.9 %copy-done.4 = bf16[1,64,1024]{2,1,0:T(8,128)(2,1)S(1)} copy-done((bf16[1,64,1024]{2,1,0:T(8,128)(2,1)S(1)}, bf16[1,64,1024]{2,1,0:T(8,128)(2,1)}, u32[]{:S(2)}) %copy-start.4) | copy-done | bytes 131096
  5.7 0.0 copy-start.5
  5.7 0.8 %copy-done.5 = bf16[1,16,1024]{2,1,0:T(8,128)(2,1)S(1)} copy-done((bf16[1,16,1024]{2,1,0:T(8,128)(2,1)S(1)}, bf16[1,16,1024]{2,1,0:T(8,128)(2,1)}, u32[]{:S(2)}) %copy-start.5) | copy-done | bytes 32792
  6.4 0.0 copy-start.6
  6.4 0.7 %copy-done.6 = s32[1,1,16]{2,1,0:T(1,128)S(1)} copy-done((s32[1,1,16]{2,1,0:T(1,128)S(1)}, s32[1,1,16]{2,1,0:T(1,128)}, u32[]{:S(2)}) %copy-start.6) | copy-done | bytes 88
  7.1 1.5 %partials.1 = f32[4,32,256]{2,1,0:T(8,128)S(1)} custom-call(bf16[1,128,4096]{2,1,0:T(8,128)(2,1)S(1)} %copy-done, bf16[1,128,1024]{2,1,0:T(8,128)(2,1)S(1)} %copy-done.2, bf16[1,16,4096]{2,1,0:T(8,128)(2,1)S(1)} %copy-done.3, bf16[1,16,1024]{2,1,0:T(8,128)(2,1)S(1)} %copy-done.5, bf16[1,64,4096]{2,1,0:T(8,128)(2,1)S(1)} %copy-done.1, ...), custom_call_target="tpu_custom_call" | custom-call | tf_op jit(solution)/shard_map/partials/pallas_call | solution.py:263
  8.6 12.3 %all_to_all.10.recv = f32[4,32,256]{2,1,0:T(8,128)} all-to-all(f32[4,32,256]{2,1,0:T(8,128)S(1)} %partials.1), channel_id=1, replica_groups=mesh['ex'=8,'mp'=4] {'mp'}, dimensions={0} | all-to-all | bytes 262144 | tf_op jit(solution)/shard_map/all_to_all | solution.py:283
  20.9 1.6 %columns.1 = f32[8,16,256]{2,1,0:T(8,128)} custom-call(f32[4,32,256]{2,1,0:T(8,128)} %all_to_all.10.recv), custom_call_target="tpu_custom_call" | custom-call | tf_op jit(solution)/shard_map/columns/pallas_call | solution.py:285
  22.5 3.7 %all-to-all-start.1 = ((f32[8,16,256]{2,1,0:T(8,128)}), f32[8,16,256]{2,1,0:T(8,128)S(1)}, u32[]{:S(2)}, u32[]{:S(2)}) async-start(f32[8,16,256]{2,1,0:T(8,128)} %columns.1), calls=%async_computation.1 | async-start | bytes 262144 | tf_op jit(solution)/shard_map/all_to_all | solution.py:292
  26.9 1.6 %features.1 = f32[4,1024]{1,0:T(4,128)} custom-call(f32[4,32,256]{2,1,0:T(8,128)} %all_to_all.10.recv), custom_call_target="tpu_custom_call" | custom-call | tf_op jit(solution)/shard_map/features/pallas_call | solution.py:293
  28.5 3.3 %all-to-all-done.1.rows = f32[8,16,256]{2,1,0:T(8,128)S(1)} async-done(((f32[8,16,256]{2,1,0:T(8,128)}), f32[8,16,256]{2,1,0:T(8,128)S(1)}, u32[]{:S(2)}, u32[]{:S(2)}) %all-to-all-start.1) | async-done | bytes 131104 | tf_op jit(solution)/shard_map/all_to_all | solution.py:292
  31.7 3.3 %factors.1 = f32[4,64,64]{2,1,0:T(8,128)} custom-call(f32[8,16,256]{2,1,0:T(8,128)S(1)} %all-to-all-done.1.rows, f32[1]{0:T(128)S(6)} %copy.10.damping), custom_call_target="tpu_custom_call" | custom-call | tf_op jit(solution)/shard_map/factors/pallas_call | solution.py:300
Async XLA Ops:
  0.6 1.2 %copy-start = (bf16[1,128,4096]{2,1,0:T(8,128)(2,1)S(1)}, bf16[1,128,4096]{2,1,0:T(8,128)(2,1)}, u32[]{:S(2)}) copy-start(bf16[1,128,4096]{2,1,0:T(8,128)(2,1)} %acts.1) | copy-start | bytes 3145732
  1.9 1.0 %copy-start.1 = (bf16[1,64,4096]{2,1,0:T(8,128)(2,1)S(1)}, bf16[1,64,4096]{2,1,0:T(8,128)(2,1)}, u32[]{:S(2)}) copy-start(bf16[1,64,4096]{2,1,0:T(8,128)(2,1)} %proj_in.1) | copy-start | bytes 1572868
  2.9 0.9 %copy-start.2 = (bf16[1,128,1024]{2,1,0:T(8,128)(2,1)S(1)}, bf16[1,128,1024]{2,1,0:T(8,128)(2,1)}, u32[]{:S(2)}) copy-start(bf16[1,128,1024]{2,1,0:T(8,128)(2,1)} %grads.1) | copy-start | bytes 786436
  3.9 0.9 %copy-start.3 = (bf16[1,16,4096]{2,1,0:T(8,128)(2,1)S(1)}, bf16[1,16,4096]{2,1,0:T(8,128)(2,1)}, u32[]{:S(2)}) copy-start(bf16[1,16,4096]{2,1,0:T(8,128)(2,1)} %down.1) | copy-start | bytes 393220
  4.8 0.9 %copy-start.4 = (bf16[1,64,1024]{2,1,0:T(8,128)(2,1)S(1)}, bf16[1,64,1024]{2,1,0:T(8,128)(2,1)}, u32[]{:S(2)}) copy-start(bf16[1,64,1024]{2,1,0:T(8,128)(2,1)} %proj_out.1) | copy-start | bytes 393220
  5.7 0.8 %copy-start.5 = (bf16[1,16,1024]{2,1,0:T(8,128)(2,1)S(1)}, bf16[1,16,1024]{2,1,0:T(8,128)(2,1)}, u32[]{:S(2)}) copy-start(bf16[1,16,1024]{2,1,0:T(8,128)(2,1)} %up.1) | copy-start | bytes 98308
  6.4 0.7 %copy-start.6 = (s32[1,1,16]{2,1,0:T(1,128)S(1)}, s32[1,1,16]{2,1,0:T(1,128)}, u32[]{:S(2)}) copy-start(s32[1,1,16]{2,1,0:T(1,128)} %order.1) | copy-start | bytes 196
  22.5 9.3 %all-to-all-start.1 = ((f32[8,16,256]{2,1,0:T(8,128)}), f32[8,16,256]{2,1,0:T(8,128)S(1)}, u32[]{:S(2)}, u32[]{:S(2)}) async-start(f32[8,16,256]{2,1,0:T(8,128)} %columns.1), calls=%async_computation.1 | async-start | bytes 262144 | tf_op jit(solution)/shard_map/all_to_all | solution.py:292

commit v2 on v1

--- a/solution.py
+++ b/solution.py
@@ -13,6 +13,7 @@
 SLOT = 32
 GROUP = LANES // SLOT
 PANEL = 8
+CHUNK = 1024
 
 
 def dot_nt(a, b):
@@ -33,16 +34,83 @@
 
 
 def partial_kernel(
-    parts, scaling, acts, grads, down, up, proj_in, proj_out, order, send, low, out
+    parts,
+    scaling,
+    acts_hbm,
+    grads_hbm,
+    down_hbm,
+    up_hbm,
+    proj_in_hbm,
+    proj_out_hbm,
+    order_hbm,
+    send,
+    acts,
+    grads,
+    weights_in,
+    weights_out,
+    order,
+    low,
+    out,
+    sems,
+    order_sem,
 ):
-    tokens = acts.shape[1]
-    rank = down.shape[1]
-    sketch = proj_in.shape[1]
+    tokens, width = acts.shape
+    rank = down_hbm.shape[1]
+    sketch = proj_in_hbm.shape[1]
     examples = tokens // EXAMPLE_LENGTH
     per = rank // parts
     halves = sketch // SLOT
-    from_acts = dot_nt(jnp.concatenate([proj_in[0], down[0]], axis=0), acts[0])
-    from_grads = dot_nt(jnp.concatenate([proj_out[0], up[0]], axis=0), grads[0])
+
+    def copies(source, target, sem, start, size):
+        return pltpu.make_async_copy(
+            source.at[0, :, pl.ds(start, size)],
+            target.at[:, pl.ds(start, size)],
+            sem,
+        )
+
+    order_copy = pltpu.make_async_copy(order_hbm.at[0], order, order_sem)
+    stages = []
+    for start in range(0, width, CHUNK):
+        stages.append(
+            [
+                (acts_hbm, acts, start),
+                (proj_in_hbm, weights_in.at[pl.ds(0, sketch)], start),
+                (down_hbm, weights_in.at[pl.ds(sketch, rank)], start),
+            ]
+        )
+    for start in range(0, grads.shape[1], CHUNK):
+        stages.append(
+            [
+                (grads_hbm, grads, start),
+                (proj_out_hbm, weights_out.at[pl.ds(0, sketch)], start),
+                (up_hbm, weights_out.at[pl.ds(sketch, rank)], start),
+            ]
+        )
+    pending = [
+        [
+            copies(source, target, sems.at[n, i], start, CHUNK)
+            for i, (source, target, start) in enumerate(stage)
+        ]
+        for n, stage in enumerate(stages)
+    ]
+    for stage in pending:
+        for copy in stage:
+            copy.start()
+    order_copy.start()
+
+    def product(first, rows, weights):
+        total = None
+        for n in range(rows.shape[1] // CHUNK):
+            for copy in pending[first + n]:
+                copy.wait()
+            here = pl.ds(n * CHUNK, CHUNK)
+            term = dot_nt(weights[:, here], rows[:, here])
+            total = term if total is None else total + term
+        return total
+
+    from_acts = product(0, acts, weights_in)
+    from_grads = product(width // CHUNK, grads, weights_out)
+    order_copy.wait()
     sketches = jnp.concatenate([from_acts[:sketch], from_grads[:sketch]], axis=1)
     low[0] = from_grads[sketch:] * scaling
     low[1] = from_acts[sketch:] * scaling
@@ -52,7 +120,7 @@
     source = (lane % tokens) // EXAMPLE_LENGTH
     target = jnp.zeros((8, 2 * tokens), jnp.int32)
     for s in range(examples):
-        target = jnp.where(source[:8] == s, order[0, 0, s], target)
+        target = jnp.where(source[:8] == s, order[0, s], target)
     target = jnp.concatenate([target] * (rows // 8), axis=0)
     place = lax.broadcasted_iota(jnp.int32, (rows, 2 * tokens), 0) // parts
     mine = target == place
@@ -237,6 +305,10 @@
     return pl.BlockSpec(memory_space=pltpu.VMEM)
 
 
+def hbm():
+    return pl.BlockSpec(memory_space=pltpu.HBM)
+
+
 def smem():
     return pl.BlockSpec(memory_space=pltpu.SMEM)
 
@@ -253,7 +325,8 @@
 ):
     parts = lax.axis_size("mp")
     shards = lax.axis_size("ex")
-    tokens = acts.shape[1]
+    tokens, width = acts.shape[1:]
+    key_width = grads.shape[2]
     rank = down_factor.shape[1]
     sketch = input_projection.shape[1]
     examples = tokens // EXAMPLE_LENGTH
@@ -263,13 +336,20 @@
     send = pl.pallas_call(
         functools.partial(partial_kernel, parts, scaling),
         out_shape=jax.ShapeDtypeStruct((parts, 2 * examples, span), jnp.float32),
-        in_specs=[vmem()] * 6 + [smem()],
+        in_specs=[hbm()] * 7,
         out_specs=vmem(),
         scratch_shapes=[
+            pltpu.VMEM((tokens, width), acts.dtype),
+            pltpu.VMEM((tokens, key_width), grads.dtype),
+            pltpu.VMEM((sketch + rank, width), acts.dtype),
+            pltpu.VMEM((sketch + rank, key_width), grads.dtype),
+            pltpu.SMEM(order.shape[1:], order.dtype),
             pltpu.VMEM((2, rank, tokens), jnp.float32),
             pltpu.VMEM((examples * parts, LANES), jnp.float32),
+            pltpu.SemaphoreType.DMA(((width + key_width) // CHUNK, 3)),
+            pltpu.SemaphoreType.DMA,
         ],
-        compiler_params=pltpu.CompilerParams(vmem_limit_bytes=32 * 2**20),
+        compiler_params=pltpu.CompilerParams(vmem_limit_bytes=62000000),
         name="partials",
     )(
         acts,

time: 35.5 us -> 30.9 us (0.87)
  local copies, waits for them, and re-layouts: 6.43 us -> 0 us
  Pallas kernels: 7.97 us -> 9.75 us
    unnamed x14 -> x0, local copies, waits for them, and re-layouts: 6.43 us -> none
    pallas_call x1, Pallas kernels: 1.54 us -> 3.31 us  [local(): pl.pallas_call(functools.partial(partial_kernel, parts, scaling), out_sha...]
where the time goes in v2:
time: 30.9 us; the launch traced here: 30.6 us
  blocking collectives  12.5 us (40%)
  Pallas kernels  9.75 us (32%)
  starting transfers between devices  3.72 us (12%)
  waiting for transfers between devices  3.28 us (11%)
  between operations  1.29 us (4%)
    all_to_all x1, blocking collectives, local(): recv = lax.all_to_all(send, 'mp', split_axis=0, concat_axis=0, tiled=True)  12.5 us
    all_to_all x1, starting transfers between devices, local(): lax.all_to_all(columns, 'ex', split_axis=0, concat_axis=0, tiled=True)  3.72 us
    pallas_call x1, Pallas kernels, local(): pl.pallas_call(functools.partial(partial_kernel, parts, scaling), out_sha...  3.31 us
    all_to_all x1, waiting for transfers between devices, local(): lax.all_to_all(columns, 'ex', split_axis=0, concat_axis=0, tiled=True)  3.28 us
    pallas_call x1, Pallas kernels, local(): pl.pallas_call(factor_kernel, out_shape=jax.ShapeDtypeStruct((per, sketch...  3.27 us
    pallas_call x1, Pallas kernels, local(): pl.pallas_call(functools.partial(feature_kernel, parts, per), out_shape=j...  1.6 us
    pallas_call x1, Pallas kernels, local(): pl.pallas_call(column_kernel, out_shape=jax.ShapeDtypeStruct((shards, exa...  1.57 us
  transfers between devices with their start and end apart: 1, of which 1 were waited for; matrix products, arithmetic and copies ran while one was open for 0% of the time, Pallas kernels for 5%

profile of v2, /device:TPU:0, one launch (start us, length us, event | category | flops | bytes accessed | tf_op | source)
XLA Modules:
  0.0 30.6 jit_solution(11890904824362768048)
XLA Ops:
  0.6 3.3 %partials.1 = f32[4,32,256]{2,1,0:T(8,128)} custom-call(bf16[1,128,4096]{2,1,0:T(8,128)(2,1)} %acts_hbm.1, bf16[1,128,1024]{2,1,0:T(8,128)(2,1)} %grads_hbm.1, bf16[1,16,4096]{2,1,0:T(8,128)(2,1)} %down_hbm.1, bf16[1,16,1024]{2,1,0:T(8,128)(2,1)} %up_hbm.1, bf16[1,64,4096]{2,1,0:T(8,128)(2,1)} %proj_in_hbm.1, bf16[1,64,1024]{2,1,0:T(8,128)(2,1)} %proj_out_hbm.1, ...), custom_call_target="tpu_custom_call" | custom-call | tf_op jit(solution)/shard_map/partials/pallas_call | solution.py:336
  3.9 12.5 %all_to_all.10.recv = f32[4,32,256]{2,1,0:T(8,128)} all-to-all(f32[4,32,256]{2,1,0:T(8,128)} %partials.1), channel_id=1, replica_groups=mesh['ex'=8,'mp'=4] {'mp'}, dimensions={0} | all-to-all | bytes 262144 | tf_op jit(solution)/shard_map/all_to_all | solution.py:363
  16.5 1.6 %columns.1 = f32[8,16,256]{2,1,0:T(8,128)} custom-call(f32[4,32,256]{2,1,0:T(8,128)} %all_to_all.10.recv), custom_call_target="tpu_custom_call" | custom-call | tf_op jit(solution)/shard_map/columns/pallas_call | solution.py:365
  18.0 3.7 %all-to-all-start.1 = ((f32[8,16,256]{2,1,0:T(8,128)}), f32[8,16,256]{2,1,0:T(8,128)S(1)}, u32[]{:S(2)}, u32[]{:S(2)}) async-start(f32[8,16,256]{2,1,0:T(8,128)} %columns.1), calls=%async_computation.1 | async-start | bytes 262144 | tf_op jit(solution)/shard_map/all_to_all | solution.py:372
  22.4 1.6 %features.1 = f32[4,1024]{1,0:T(4,128)} custom-call(f32[4,32,256]{2,1,0:T(8,128)} %all_to_all.10.recv), custom_call_target="tpu_custom_call" | custom-call | tf_op jit(solution)/shard_map/features/pallas_call | solution.py:373
  24.0 3.3 %all-to-all-done.1.rows = f32[8,16,256]{2,1,0:T(8,128)S(1)} async-done(((f32[8,16,256]{2,1,0:T(8,128)}), f32[8,16,256]{2,1,0:T(8,128)S(1)}, u32[]{:S(2)}, u32[]{:S(2)}) %all-to-all-start.1) | async-done | bytes 131104 | tf_op jit(solution)/shard_map/all_to_all | solution.py:372
  27.3 3.3 %factors.1 = f32[4,64,64]{2,1,0:T(8,128)} custom-call(f32[8,16,256]{2,1,0:T(8,128)S(1)} %all-to-all-done.1.rows, f32[1]{0:T(128)S(6)} %copy.10.damping), custom_call_target="tpu_custom_call" | custom-call | tf_op jit(solution)/shard_map/factors/pallas_call | solution.py:380
Async XLA Ops:
  18.0 9.3 %all-to-all-start.1 = ((f32[8,16,256]{2,1,0:T(8,128)}), f32[8,16,256]{2,1,0:T(8,128)S(1)}, u32[]{:S(2)}, u32[]{:S(2)}) async-start(f32[8,16,256]{2,1,0:T(8,128)} %columns.1), calls=%async_computation.1 | async-start | bytes 262144 | tf_op jit(solution)/shard_map/all_to_all | solution.py:372

commit v3 on v2

--- a/solution.py
+++ b/solution.py
@@ -43,17 +43,10 @@
     proj_in_hbm,
     proj_out_hbm,
     order_hbm,
-    send,
-    acts,
-    grads,
-    weights_in,
-    weights_out,
-    order,
-    low,
-    out,
-    sems,
-    order_sem,
+    *refs,
 ):
+    sends, refs = refs[:parts], refs[parts:]
+    acts, grads, weights_in, weights_out, order, low, out, sems, order_sem = refs
     tokens, width = acts.shape
     rank = down_hbm.shape[1]
     sketch = proj_in_hbm.shape[1]
@@ -148,34 +141,40 @@
     total = spread[:rows]
     for c in range(1, per):
         total = jnp.where(channel == c, spread[c * rows : (c + 1) * rows], total)
+    me = lax.axis_index("mp")
     for start in range(0, per * sketch, LANES):
         stop = min(start + LANES, per * sketch)
         out[:, : stop - start] = total[:, start:stop]
-        for g in range(parts):
-            send[g, :examples, start:stop] = out[
-                g * examples : (g + 1) * examples, : stop - start
-            ]
-            send[g, examples:, start:stop] = out[pl.ds(g, examples, stride=parts), :][
+        for d in range(parts):
+            g = lax.rem(me + d, parts)
+            sends[d][:examples, start:stop] = out[
+                pl.ds(pl.multiple_of(g * examples, examples), examples), : stop - start
+            ]
+            sends[d][examples:, start:stop] = out[pl.ds(g, examples, stride=parts), :][
                 :, : stop - start
             ]
 
 
-def column_kernel(recv, columns):
-    examples = columns.shape[1]
-    total = jnp.sum(recv[:, examples:, :], axis=0)
+def column_kernel(*refs):
+    chunks, columns = refs[:-1], refs[-1]
+    examples, padded = columns.shape
+    total = chunks[0][examples:, :]
+    for chunk in chunks[1:]:
+        total = total + chunk[examples:, :]
     width = total.shape[1]
-    for m in range(columns.shape[0]):
-        columns[m, :, :width] = total
-        if columns.shape[2] > width:
-            columns[m, :, width:] = jnp.zeros(
-                (examples, columns.shape[2] - width), jnp.float32
-            )
-
-
-def feature_kernel(parts, per, recv, features):
+    columns[:, :width] = total
+    if padded > width:
+        columns[:, width:] = jnp.zeros((examples, padded - width), jnp.float32)
+
+
+def feature_kernel(per, *refs):
+    chunks, features = refs[:-1], refs[-1]
+    parts = len(chunks)
     rows_here, width = features.shape
     examples = rows_here * parts
-    total = jnp.sum(recv[:, :examples, :], axis=0)
+    total = chunks[0][:examples, :]
+    for chunk in chunks[1:]:
+        total = total + chunk[:examples, :]
     span = width // parts
     halves = span // (per * SLOT)
     natural = jnp.concatenate(
@@ -202,12 +201,13 @@
     return guess * (2.0 - x * guess)
 
 
-def factor_kernel(rows, damping, factors):
+def factor_kernel(damping, *refs):
+    rows, factors = refs[:-1], refs[-1]
     channels, sketch, _ = factors.shape
     halves = sketch // SLOT
     panels = sketch // PANEL
     per_half = SLOT // PANEL
-    stacked = jnp.concatenate([rows[m] for m in range(rows.shape[0])], axis=0)
+    stacked = jnp.concatenate([part[...] for part in rows], axis=0)
     examples = stacked.shape[0]
     high, rest = split(stacked)
     gram = (dot_tn(high, rest) + dot_tn(rest, high)) + dot_tn(high, high)
@@ -301,6 +301,11 @@
             )
 
 
+def shift(x, axis, distance):
+    size = lax.axis_size(axis)
+    return lax.ppermute(x, axis, [(i, (i + distance) % size) for i in range(size)])
+
+
 def vmem():
     return pl.BlockSpec(memory_space=pltpu.VMEM)
 
@@ -333,11 +338,11 @@
     per = rank // parts
     span = per * sketch
     scaling = 1.0 / math.sqrt(2.0 * EXAMPLE_LENGTH * parts)
-    send = pl.pallas_call(
+    sends = pl.pallas_call(
         functools.partial(partial_kernel, parts, scaling),
-        out_shape=jax.ShapeDtypeStruct((parts, 2 * examples, span), jnp.float32),
+        out_shape=[jax.ShapeDtypeStruct((2 * examples, span), jnp.float32)] * parts,
         in_specs=[hbm()] * 7,
-        out_specs=vmem(),
+        out_specs=[vmem()] * parts,
         scratch_shapes=[
             pltpu.VMEM((tokens, width), acts.dtype),
             pltpu.VMEM((tokens, key_width), grads.dtype),
@@ -360,31 +365,30 @@
         gradient_projection,
         order,
     )
-    recv = lax.all_to_all(send, "mp", split_axis=0, concat_axis=0, tiled=True)
-    padded = max(span, GROUP * sketch)
+    chunks = [sends[0]] + [shift(sends[d], "mp", d) for d in range(1, parts)]
     columns = pl.pallas_call(
         column_kernel,
-        out_shape=jax.ShapeDtypeStruct((shards, examples, padded), jnp.float32),
-        in_specs=[vmem()],
+        out_shape=jax.ShapeDtypeStruct((examples, max(span, GROUP * sketch)), jnp.float32),
+        in_specs=[vmem()] * parts,
         out_specs=vmem(),
         name="columns",
-    )(recv)
-    rows = lax.all_to_all(columns, "ex", split_axis=0, concat_axis=0, tiled=True)
+    )(*chunks)
+    rows = [columns] + [shift(columns, "ex", d) for d in range(1, shards)]
     features = pl.pallas_call(
-        functools.partial(feature_kernel, parts, per),
+        functools.partial(feature_kernel, per),
         out_shape=jax.ShapeDtypeStruct((examples // parts, rank * sketch), jnp.float32),
-        in_specs=[vmem()],
+        in_specs=[vmem()] * parts,
         out_specs=vmem(),
         name="features",
-    )(recv)
+    )(*chunks)
     factors = pl.pallas_call(
         factor_kernel,
         out_shape=jax.ShapeDtypeStruct((per, sketch, sketch), jnp.float32),
-        in_specs=[vmem(), smem()],
+        in_specs=[smem()] + [vmem()] * shards,
         out_specs=vmem(),
         compiler_params=pltpu.CompilerParams(vmem_limit_bytes=32 * 2**20),
         name="factors",
-    )(rows, damping)
+    )(damping, *rows)
     return features, factors
 
 

time: 30.9 us -> 29.5 us (0.955)
  blocking collectives: 12.5 us -> 0 us
  starting transfers between devices: 3.72 us -> 12.9 us
  waiting for transfers between devices: 3.28 us -> 4.87 us
  local copies, waits for them, and re-layouts: 0 us -> 0.61 us
    ppermute x0 -> x10, starting transfers between devices: none -> 12.9 us  [shift(): lax.ppermute(x, axis, [(i, (i + distance) % size) for i in range(size)])]
    all_to_all x1 -> x0, blocking collectives: 12.5 us -> none  [local(): recv = lax.all_to_all(send, 'mp', split_axis=0, concat_axis=0, tiled=True)]
    ppermute x0 -> x10, waiting for transfers between devices: none -> 4.87 us  [shift(): lax.ppermute(x, axis, [(i, (i + distance) % size) for i in range(size)])]
    all_to_all x1 -> x0, starting transfers between devices: 3.72 us -> none  [local(): lax.all_to_all(columns, 'ex', split_axis=0, concat_axis=0, tiled=True)]
    all_to_all x1 -> x0, waiting for transfers between devices: 3.28 us -> none  [local(): lax.all_to_all(columns, 'ex', split_axis=0, concat_axis=0, tiled=True)]
    unnamed x0 -> x8, local copies, waits for them, and re-layouts: none -> 0.61 us
  transfers between devices with their start and end apart: 1 -> 10, of which waited for: 1 -> 5; matrix products, arithmetic and copies ran while one was open for 0% -> 0% of each run, Pallas kernels for 5% -> 5%
where the time goes in v3:
time: 29.5 us; the launch traced here: 29.2 us
  starting transfers between devices  12.9 us (44%)
  Pallas kernels  9.49 us (32%)
  waiting for transfers between devices  4.87 us (17%)
  between operations  1.32 us (4%)
  local copies, waits for them, and re-layouts  0.61 us (2%)
    ppermute x10, starting transfers between devices, shift(): lax.ppermute(x, axis, [(i, (i + distance) % size) for i in range(size)])  12.9 us
    ppermute x10, waiting for transfers between devices, shift(): lax.ppermute(x, axis, [(i, (i + distance) % size) for i in range(size)])  4.87 us
    pallas_call x1, Pallas kernels, local(): pl.pallas_call(functools.partial(partial_kernel, parts, scaling), out_sha...  3.3 us
    pallas_call x1, Pallas kernels, local(): pl.pallas_call(factor_kernel, out_shape=jax.ShapeDtypeStruct((per, sketch...  3.26 us
    pallas_call x1, Pallas kernels, local(): pl.pallas_call(functools.partial(feature_kernel, per), out_shape=jax.Shap...  1.51 us
    pallas_call x1, Pallas kernels, local(): pl.pallas_call(column_kernel, out_shape=jax.ShapeDtypeStruct((examples, m...  1.41 us
    unnamed x8, local copies, waits for them, and re-layouts  0.61 us
  transfers between devices with their start and end apart: 10, of which 5 were waited for; matrix products, arithmetic and copies ran while one was open for 0% of the time, Pallas kernels for 5%

profile of v3, /device:TPU:0, one launch (start us, length us, event | category | flops | bytes accessed | tf_op | source)
XLA Modules:
  0.0 29.2 jit_solution(12894455075178217700)
XLA Ops:
  0.6 3.3 %partials.1 = (f32[32,256]{1,0:T(8,128)}, f32[32,256]{1,0:T(8,128)}, f32[32,256]{1,0:T(8,128)}, f32[32,256]{1,0:T(8,128)}) custom-call(bf16[1,128,4096]{2,1,0:T(8,128)(2,1)} %acts_hbm.1, bf16[1,128,1024]{2,1,0:T(8,128)(2,1)} %grads_hbm.1, bf16[1,16,4096]{2,1,0:T(8,128)(2,1)} %down_hbm.1, bf16[1,16,1024]{2,1,0:T(8,128)(2,1)} %up_hbm.1, ...), custom_call_target="tpu_custom_call" | custom-call | tf_op jit(solution)/shard_map/partials/pallas_call | solution.py:341
  3.9 3.1 %collective-permute-start = (f32[32,256]{1,0:T(8,128)}, f32[32,256]{1,0:T(8,128)S(1)}, u32[]{:S(2)}, u32[]{:S(2)}) collective-permute-start(f32[32,256]{1,0:T(8,128)} %get-tuple-element.7), channel_id=1, source_target_pairs={{0,1},{1,2},{2,3},{3,0},{4,5},{5,6},{6,7},{7,4},{8,9},{9,10},{10,1... | collective-permute-start | bytes 98312 | tf_op jit(solution)/shard_map/ppermute | solution.py:306
  7.0 2.6 %collective-permute-start.1 = (f32[32,256]{1,0:T(8,128)}, f32[32,256]{1,0:T(8,128)S(1)}, u32[]{:S(2)}, u32[]{:S(2)}) collective-permute-start(f32[32,256]{1,0:T(8,128)} %get-tuple-element.8), channel_id=1, source_target_pairs={{0,2},{1,3},{2,0},{3,1},{4,6},{5,7},{6,4},{7,5},{8,10},{9,11},{10,... | collective-permute-start | bytes 98312 | tf_op jit(solution)/shard_map/ppermute | solution.py:306
  9.6 1.3 %collective-permute-start.2 = (f32[32,256]{1,0:T(8,128)}, f32[32,256]{1,0:T(8,128)S(1)}, u32[]{:S(2)}, u32[]{:S(2)}) collective-permute-start(f32[32,256]{1,0:T(8,128)} %get-tuple-element.9), channel_id=1, source_target_pairs={{0,3},{1,0},{2,1},{3,2},{4,7},{5,4},{6,5},{7,6},{8,11},{9,8},{10,9... | collective-permute-start | bytes 98312 | tf_op jit(solution)/shard_map/ppermute | solution.py:306
  11.0 0.2 collective-permute-done.refs_1_
  11.1 0.0 copy-start.1
  11.2 1.2 %collective-permute-done.1.refs_2_ = f32[32,256]{1,0:T(8,128)S(1)} collective-permute-done((f32[32,256]{1,0:T(8,128)}, f32[32,256]{1,0:T(8,128)S(1)}, u32[]{:S(2)}, u32[]{:S(2)}) %collective-permute-start.1) | collective-permute-done | bytes 32800 | tf_op jit(solution)/shard_map/ppermute | solution.py:306
  12.4 0.0 copy-start.2
  12.4 1.3 %collective-permute-done.2.refs_3_ = f32[32,256]{1,0:T(8,128)S(1)} collective-permute-done((f32[32,256]{1,0:T(8,128)}, f32[32,256]{1,0:T(8,128)S(1)}, u32[]{:S(2)}, u32[]{:S(2)}) %collective-permute-start.2) | collective-permute-done | bytes 32800 | tf_op jit(solution)/shard_map/ppermute | solution.py:306
  13.7 0.0 copy-start.3
  13.7 0.0 copy-done.1
  13.7 0.0 copy-done.2
  13.7 0.6 %copy-done.3 = f32[32,256]{1,0:T(8,128)} copy-done((f32[32,256]{1,0:T(8,128)}, f32[32,256]{1,0:T(8,128)S(1)}, u32[]{:S(2)}) %copy-start.3) | copy-done | bytes 32792
  14.3 1.4 %columns.1.refs_0_ = f32[16,256]{1,0:T(8,128)} custom-call(f32[32,256]{1,0:T(8,128)} %get-tuple-element.6.refs_0_, f32[32,256]{1,0:T(8,128)} %copy-done.1, f32[32,256]{1,0:T(8,128)} %copy-done.2, f32[32,256]{1,0:T(8,128)} %copy-done.3), custom_call_target="tpu_custom_call" | custom-call | tf_op jit(solution)/shard_map/columns/pallas_call | solution.py:369
  15.7 0.8 %collective-permute-start.9 = (f32[16,256]{1,0:T(8,128)}, f32[16,256]{1,0:T(8,128)S(1)}, u32[]{:S(2)}, u32[]{:S(2)}) collective-permute-start(f32[16,256]{1,0:T(8,128)} %columns.1.refs_0_), channel_id=1, source_target_pairs={{0,28},{4,0},{8,4},{12,8},{16,12},{20,16},{24,20},{28,24},{1,29},{... | collective-permute-start | bytes 49160 | tf_op jit(solution)/shard_map/ppermute | solution.py:306
  16.5 1.7 %collective-permute-start.8 = (f32[16,256]{1,0:T(8,128)}, f32[16,256]{1,0:T(8,128)S(1)}, u32[]{:S(2)}, u32[]{:S(2)}) collective-permute-start(f32[16,256]{1,0:T(8,128)} %columns.1.refs_0_), channel_id=1, source_target_pairs={{0,24},{4,28},{8,0},{12,4},{16,8},{20,12},{24,16},{28,20},{1,25},{... | collective-permute-start | bytes 49160 | tf_op jit(solution)/shard_map/ppermute | solution.py:306
  18.2 0.3 %collective-permute-start.7 = (f32[16,256]{1,0:T(8,128)}, f32[16,256]{1,0:T(8,128)S(1)}, u32[]{:S(2)}, u32[]{:S(2)}) collective-permute-start(f32[16,256]{1,0:T(8,128)} %columns.1.refs_0_), channel_id=1, source_target_pairs={{0,20},{4,24},{8,28},{12,0},{16,4},{20,8},{24,12},{28,16},{1,21},{... | collective-permute-start | bytes 49160 | tf_op jit(solution)/shard_map/ppermute | solution.py:306
  18.5 1.5 %collective-permute-start.6 = (f32[16,256]{1,0:T(8,128)}, f32[16,256]{1,0:T(8,128)S(1)}, u32[]{:S(2)}, u32[]{:S(2)}) collective-permute-start(f32[16,256]{1,0:T(8,128)} %columns.1.refs_0_), channel_id=1, source_target_pairs={{0,16},{4,20},{8,24},{12,28},{16,0},{20,4},{24,8},{28,12},{1,17},{... | collective-permute-start | bytes 49160 | tf_op jit(solution)/shard_map/ppermute | solution.py:306
  20.1 0.1 collective-permute-start.5
  20.2 0.0 collective-permute-done.9.refs_7_
  20.2 1.5 %collective-permute-start.4 = (f32[16,256]{1,0:T(8,128)}, f32[16,256]{1,0:T(8,128)S(1)}, u32[]{:S(2)}, u32[]{:S(2)}) collective-permute-start(f32[16,256]{1,0:T(8,128)} %columns.1.refs_0_), channel_id=1, source_target_pairs={{0,8},{4,12},{8,16},{12,20},{16,24},{20,28},{24,0},{28,4},{1,9},{5... | collective-permute-start | bytes 49160 | tf_op jit(solution)/shard_map/ppermute | solution.py:306
  21.7 0.0 collective-permute-done.8.refs_6_
  21.7 0.0 collective-permute-start.3
  22.3 0.0 copy-start
  22.3 1.5 %features.1 = f32[4,1024]{1,0:T(4,128)} custom-call(f32[32,256]{1,0:T(8,128)} %get-tuple-element.6.refs_0_, f32[32,256]{1,0:T(8,128)} %copy-done.1, f32[32,256]{1,0:T(8,128)} %copy-done.2, f32[32,256]{1,0:T(8,128)} %copy-done.3), custom_call_target="tpu_custom_call" | custom-call | tf_op jit(solution)/shard_map/features/pallas_call | solution.py:377
  23.8 0.0 collective-permute-done.7.refs_5_
  23.9 0.0 collective-permute-done.6.refs_4_
  23.9 0.0 collective-permute-done.5.refs_3_
  23.9 1.2 %collective-permute-done.4.refs_2_ = f32[16,256]{1,0:T(8,128)S(1)} collective-permute-done((f32[16,256]{1,0:T(8,128)}, f32[16,256]{1,0:T(8,128)S(1)}, u32[]{:S(2)}, u32[]{:S(2)}) %collective-permute-start.4) | collective-permute-done | bytes 16416 | tf_op jit(solution)/shard_map/ppermute | solution.py:306
  25.0 0.9 %collective-permute-done.3.refs_1_ = f32[16,256]{1,0:T(8,128)S(1)} collective-permute-done((f32[16,256]{1,0:T(8,128)}, f32[16,256]{1,0:T(8,128)S(1)}, u32[]{:S(2)}, u32[]{:S(2)}) %collective-permute-start.3) | collective-permute-done | bytes 16416 | tf_op jit(solution)/shard_map/ppermute | solution.py:306
  25.9 0.0 copy-done
  25.9 3.3 %factors.1 = f32[4,64,64]{2,1,0:T(8,128)} custom-call(f32[1]{0:T(128)S(6)} %copy.10.damping, f32[16,256]{1,0:T(8,128)S(1)} %copy-done, f32[16,256]{1,0:T(8,128)S(1)} %collective-permute-done.3.refs_1_, f32[16,256]{1,0:T(8,128)S(1)} %collective-permute-done.4.refs_2_, f32[16,256]{1,0:T(8,128)S(1)} %collective-permute-done.5.refs_3_, ...), custom_call_target="tpu_custom_call" | custom-call | tf_op jit(solution)/shard_map/factors/pallas_call | solution.py:384
Async XLA Ops:
  3.9 7.2 %collective-permute-start = (f32[32,256]{1,0:T(8,128)}, f32[32,256]{1,0:T(8,128)S(1)}, u32[]{:S(2)}, u32[]{:S(2)}) collective-permute-start(f32[32,256]{1,0:T(8,128)} %get-tuple-element.7), channel_id=1, source_target_pairs={{0,1},{1,2},{2,3},{3,0},{4,5},{5,6},{6,7},{7,4},{8,9},{9,10},{10,1... | collective-permute-start | bytes 98312 | tf_op jit(solution)/shard_map/ppermute | solution.py:306
  7.0 5.4 %collective-permute-start.1 = (f32[32,256]{1,0:T(8,128)}, f32[32,256]{1,0:T(8,128)S(1)}, u32[]{:S(2)}, u32[]{:S(2)}) collective-permute-start(f32[32,256]{1,0:T(8,128)} %get-tuple-element.8), channel_id=1, source_target_pairs={{0,2},{1,3},{2,0},{3,1},{4,6},{5,7},{6,4},{7,5},{8,10},{9,11},{10,... | collective-permute-start | bytes 98312 | tf_op jit(solution)/shard_map/ppermute | solution.py:306
  9.6 4.1 %collective-permute-start.2 = (f32[32,256]{1,0:T(8,128)}, f32[32,256]{1,0:T(8,128)S(1)}, u32[]{:S(2)}, u32[]{:S(2)}) collective-permute-start(f32[32,256]{1,0:T(8,128)} %get-tuple-element.9), channel_id=1, source_target_pairs={{0,3},{1,0},{2,1},{3,2},{4,7},{5,4},{6,5},{7,6},{8,11},{9,8},{10,9... | collective-permute-start | bytes 98312 | tf_op jit(solution)/shard_map/ppermute | solution.py:306
  11.1 2.6 %copy-start.1 = (f32[32,256]{1,0:T(8,128)}, f32[32,256]{1,0:T(8,128)S(1)}, u32[]{:S(2)}) copy-start(f32[32,256]{1,0:T(8,128)S(1)} %collective-permute-done.refs_1_) | copy-start | bytes 98308
  12.4 1.3 %copy-start.2 = (f32[32,256]{1,0:T(8,128)}, f32[32,256]{1,0:T(8,128)S(1)}, u32[]{:S(2)}) copy-start(f32[32,256]{1,0:T(8,128)S(1)} %collective-permute-done.1.refs_2_) | copy-start | bytes 98308
  13.7 0.6 %copy-start.3 = (f32[32,256]{1,0:T(8,128)}, f32[32,256]{1,0:T(8,128)S(1)}, u32[]{:S(2)}) copy-start(f32[32,256]{1,0:T(8,128)S(1)} %collective-permute-done.2.refs_3_) | copy-start | bytes 98308
  15.7 4.4 %collective-permute-start.9 = (f32[16,256]{1,0:T(8,128)}, f32[16,256]{1,0:T(8,128)S(1)}, u32[]{:S(2)}, u32[]{:S(2)}) collective-permute-start(f32[16,256]{1,0:T(8,128)} %columns.1.refs_0_), channel_id=1, source_target_pairs={{0,28},{4,0},{8,4},{12,8},{16,12},{20,16},{24,20},{28,24},{1,29},{... | collective-permute-start | bytes 49160 | tf_op jit(solution)/shard_map/ppermute | solution.py:306
  16.5 5.1 %collective-permute-start.8 = (f32[16,256]{1,0:T(8,128)}, f32[16,256]{1,0:T(8,128)S(1)}, u32[]{:S(2)}, u32[]{:S(2)}) collective-permute-start(f32[16,256]{1,0:T(8,128)} %columns.1.refs_0_), channel_id=1, source_target_pairs={{0,24},{4,28},{8,0},{12,4},{16,8},{20,12},{24,16},{28,20},{1,25},{... | collective-permute-start | bytes 49160 | tf_op jit(solution)/shard_map/ppermute | solution.py:306
  18.2 5.6 %collective-permute-start.7 = (f32[16,256]{1,0:T(8,128)}, f32[16,256]{1,0:T(8,128)S(1)}, u32[]{:S(2)}, u32[]{:S(2)}) collective-permute-start(f32[16,256]{1,0:T(8,128)} %columns.1.refs_0_), channel_id=1, source_target_pairs={{0,20},{4,24},{8,28},{12,0},{16,4},{20,8},{24,12},{28,16},{1,21},{... | collective-permute-start | bytes 49160 | tf_op jit(solution)/shard_map/ppermute | solution.py:306
  18.5 5.3 %collective-permute-start.6 = (f32[16,256]{1,0:T(8,128)}, f32[16,256]{1,0:T(8,128)S(1)}, u32[]{:S(2)}, u32[]{:S(2)}) collective-permute-start(f32[16,256]{1,0:T(8,128)} %columns.1.refs_0_), channel_id=1, source_target_pairs={{0,16},{4,20},{8,24},{12,28},{16,0},{20,4},{24,8},{28,12},{1,17},{... | collective-permute-start | bytes 49160 | tf_op jit(solution)/shard_map/ppermute | solution.py:306
  20.1 3.8 %collective-permute-start.5 = (f32[16,256]{1,0:T(8,128)}, f32[16,256]{1,0:T(8,128)S(1)}, u32[]{:S(2)}, u32[]{:S(2)}) collective-permute-start(f32[16,256]{1,0:T(8,128)} %columns.1.refs_0_), channel_id=1, source_target_pairs={{0,12},{4,16},{8,20},{12,24},{16,28},{20,0},{24,4},{28,8},{1,13},{... | collective-permute-start | bytes 49160 | tf_op jit(solution)/shard_map/ppermute | solution.py:306
  20.2 4.8 %collective-permute-start.4 = (f32[16,256]{1,0:T(8,128)}, f32[16,256]{1,0:T(8,128)S(1)}, u32[]{:S(2)}, u32[]{:S(2)}) collective-permute-start(f32[16,256]{1,0:T(8,128)} %columns.1.refs_0_), channel_id=1, source_target_pairs={{0,8},{4,12},{8,16},{12,20},{16,24},{20,28},{24,0},{28,4},{1,9},{5... | collective-permute-start | bytes 49160 | tf_op jit(solution)/shard_map/ppermute | solution.py:306
  21.7 4.3 %collective-permute-start.3 = (f32[16,256]{1,0:T(8,128)}, f32[16,256]{1,0:T(8,128)S(1)}, u32[]{:S(2)}, u32[]{:S(2)}) collective-permute-start(f32[16,256]{1,0:T(8,128)} %columns.1.refs_0_), channel_id=1, source_target_pairs={{0,4},{4,8},{8,12},{12,16},{16,20},{20,24},{24,28},{28,0},{1,5},{5... | collective-permute-start | bytes 49160 | tf_op jit(solution)/shard_map/ppermute | solution.py:306
  22.3 3.6 %copy-start = (f32[16,256]{1,0:T(8,128)S(1)}, f32[16,256]{1,0:T(8,128)}, u32[]{:S(2)}) copy-start(f32[16,256]{1,0:T(8,128)} %columns.1.refs_0_) | copy-start | bytes 49156

commit v4 on v3

--- a/solution.py
+++ b/solution.py
@@ -167,8 +167,7 @@
         columns[:, width:] = jnp.zeros((examples, padded - width), jnp.float32)
 
 
-def feature_kernel(per, *refs):
-    chunks, features = refs[:-1], refs[-1]
+def write_features(chunks, per, features):
     parts = len(chunks)
     rows_here, width = features.shape
     examples = rows_here * parts
@@ -201,9 +200,11 @@
     return guess * (2.0 - x * guess)
 
 
-def factor_kernel(damping, *refs):
-    rows, factors = refs[:-1], refs[-1]
+def factor_kernel(parts, shards, damping, *refs):
+    chunks, rows = refs[:parts], refs[parts : parts + shards]
+    features, factors = refs[parts + shards :]
     channels, sketch, _ = factors.shape
+    write_features(chunks, channels, features)
     halves = sketch // SLOT
     panels = sketch // PANEL
     per_half = SLOT // PANEL
@@ -314,6 +315,14 @@
     return pl.BlockSpec(memory_space=pltpu.HBM)
 
 
+def in_hbm(*arrays):
+    return [pltpu.with_memory_space_constraint(x, pltpu.HBM) for x in arrays]
+
+
+def in_vmem(*arrays):
+    return [pltpu.with_memory_space_constraint(x, pltpu.VMEM) for x in arrays]
+
+
 def smem():
     return pl.BlockSpec(memory_space=pltpu.SMEM)
 
@@ -340,7 +349,7 @@
     scaling = 1.0 / math.sqrt(2.0 * EXAMPLE_LENGTH * parts)
     sends = pl.pallas_call(
         functools.partial(partial_kernel, parts, scaling),
-        out_shape=[jax.ShapeDtypeStruct((2 * examples, span), jnp.float32)] * parts,
+        out_shape=[pltpu.VMEM((2 * examples, span), jnp.float32)] * parts,
         in_specs=[hbm()] * 7,
         out_specs=[vmem()] * parts,
         scratch_shapes=[
@@ -354,42 +363,40 @@
             pltpu.SemaphoreType.DMA(((width + key_width) // CHUNK, 3)),
             pltpu.SemaphoreType.DMA,
         ],
-        compiler_params=pltpu.CompilerParams(vmem_limit_bytes=62000000),
+        compiler_params=pltpu.CompilerParams(vmem_limit_bytes=8 * 2**20),
         name="partials",
     )(
-        acts,
-        grads,
-        down_factor,
-        up_factor_transposed,
-        input_projection,
-        gradient_projection,
-        order,
+        *in_hbm(
+            acts,
+            grads,
+            down_factor,
+            up_factor_transposed,
+            input_projection,
+            gradient_projection,
+            order,
+        )
     )
     chunks = [sends[0]] + [shift(sends[d], "mp", d) for d in range(1, parts)]
     columns = pl.pallas_call(
         column_kernel,
-        out_shape=jax.ShapeDtypeStruct((examples, max(span, GROUP * sketch)), jnp.float32),
+        out_shape=pltpu.VMEM((examples, max(span, GROUP * sketch)), jnp.float32),
         in_specs=[vmem()] * parts,
         out_specs=vmem(),
+        compiler_params=pltpu.CompilerParams(vmem_limit_bytes=2 * 2**20),
         name="columns",
-    )(*chunks)
+    )(*in_vmem(*chunks))
     rows = [columns] + [shift(columns, "ex", d) for d in range(1, shards)]
-    features = pl.pallas_call(
-        functools.partial(feature_kernel, per),
-        out_shape=jax.ShapeDtypeStruct((examples // parts, rank * sketch), jnp.float32),
-        in_specs=[vmem()] * parts,
-        out_specs=vmem(),
-        name="features",
-    )(*chunks)
-    factors = pl.pallas_call(
-        factor_kernel,
-        out_shape=jax.ShapeDtypeStruct((per, sketch, sketch), jnp.float32),
-        in_specs=[smem()] + [vmem()] * shards,
-        out_specs=vmem(),
-        compiler_params=pltpu.CompilerParams(vmem_limit_bytes=32 * 2**20),
+    return pl.pallas_call(
+        functools.partial(factor_kernel, parts, shards),
+        out_shape=[
+            jax.ShapeDtypeStruct((examples // parts, rank * sketch), jnp.float32),
+            jax.ShapeDtypeStruct((per, sketch, sketch), jnp.float32),
+        ],
+        in_specs=[smem()] + [vmem()] * (parts + shards),
+        out_specs=[vmem()] * 2,
+        compiler_params=pltpu.CompilerParams(vmem_limit_bytes=8 * 2**20),
         name="factors",
-    )(damping, *rows)
-    return features, factors
+    )(damping, *in_vmem(*chunks, *rows))
 
 
 def solution(mesh):

time: 29.5 us -> 26.4 us (0.89)
  Pallas kernels: 9.49 us -> 5.95 us
  waiting for transfers between devices: 4.87 us -> 5.96 us
  local copies, waits for them, and re-layouts: 0.61 us -> 0 us
    pallas_call x3 -> x2, Pallas kernels: 6.18 us -> 3.28 us  [the longest x1 3.27 us: local(): pl.pallas_call(functools.partial(factor_kernel, parts, shards), out_shape...]
    ppermute x10, waiting for transfers between devices: 4.87 us -> 5.96 us  [shift(): lax.ppermute(x, axis, [(i, (i + distance) % size) for i in range(size)])]
    pallas_call x1, Pallas kernels: 3.3 us -> 2.67 us  [local(): pl.pallas_call(functools.partial(partial_kernel, parts, scaling), out_sha...]
    unnamed x8 -> x0, local copies, waits for them, and re-layouts: 0.61 us -> none
  transfers between devices with their start and end apart: 10 -> 10, of which waited for: 5 -> 5; matrix products, arithmetic and copies ran while one was open for 0% -> 0% of each run, Pallas kernels for 5% -> 0%
where the time goes in v4:
time: 26.4 us; the launch traced here: 26.2 us
  starting transfers between devices  13 us (49%)
  waiting for transfers between devices  5.96 us (23%)
  Pallas kernels  5.95 us (23%)
  between operations  1.32 us (5%)
    ppermute x10, starting transfers between devices, shift(): lax.ppermute(x, axis, [(i, (i + distance) % size) for i in range(size)])  13 us
    ppermute x10, waiting for transfers between devices, shift(): lax.ppermute(x, axis, [(i, (i + distance) % size) for i in range(size)])  5.96 us
    pallas_call x1, Pallas kernels, local(): pl.pallas_call(functools.partial(factor_kernel, parts, shards), out_shape...  3.27 us
    pallas_call x1, Pallas kernels, local(): pl.pallas_call(functools.partial(partial_kernel, parts, scaling), out_sha...  2.67 us
  transfers between devices with their start and end apart: 10, of which 5 were waited for; matrix products, arithmetic and copies ran while one was open for 0% of the time, Pallas kernels for 0%

profile of v4, /device:TPU:0, one launch (start us, length us, event | category | flops | bytes accessed | tf_op | source)
XLA Modules:
  0.0 26.2 jit_solution(7531806458199233447)
XLA Ops:
  0.6 2.7 %partials.1 = (f32[32,256]{1,0:T(8,128)S(1)}, f32[32,256]{1,0:T(8,128)S(1)}, f32[32,256]{1,0:T(8,128)S(1)}, f32[32,256]{1,0:T(8,128)S(1)}) custom-call(bf16[1,128,4096]{2,1,0:T(8,128)(2,1)} %acts_hbm.1, bf16[1,128,1024]{2,1,0:T(8,128)(2,1)} %grads_hbm.1, bf16[1,16,4096]{2,1,0:T(8,128)(2,1)} %down_hbm.1, bf16[1,16,1024]{2,1,0:T(8,128)(2,1)} %up_hbm.1, ...), custom_call_target="tpu_custom_call" | custom-call | tf_op jit(solution)/shard_map/partials/pallas_call | solution.py:350
  3.3 3.1 %collective-permute-start = (f32[32,256]{1,0:T(8,128)S(1)}, f32[32,256]{1,0:T(8,128)S(1)}, u32[]{:S(2)}, u32[]{:S(2)}) collective-permute-start(f32[32,256]{1,0:T(8,128)S(1)} %get-tuple-element.7), channel_id=1, source_target_pairs={{0,1},{1,2},{2,3},{3,0},{4,5},{5,6},{6,7},{7,4},{8,9},{9,10},{10,1... | collective-permute-start | bytes 98312 | tf_op jit(solution)/shard_map/ppermute | solution.py:307
  6.4 2.6 %collective-permute-start.1 = (f32[32,256]{1,0:T(8,128)S(1)}, f32[32,256]{1,0:T(8,128)S(1)}, u32[]{:S(2)}, u32[]{:S(2)}) collective-permute-start(f32[32,256]{1,0:T(8,128)S(1)} %get-tuple-element.8), channel_id=1, source_target_pairs={{0,2},{1,3},{2,0},{3,1},{4,6},{5,7},{6,4},{7,5},{8,10},{9,11},{10,... | collective-permute-start | bytes 98312 | tf_op jit(solution)/shard_map/ppermute | solution.py:307
  9.0 1.3 %collective-permute-start.2 = (f32[32,256]{1,0:T(8,128)S(1)}, f32[32,256]{1,0:T(8,128)S(1)}, u32[]{:S(2)}, u32[]{:S(2)}) collective-permute-start(f32[32,256]{1,0:T(8,128)S(1)} %get-tuple-element.9), channel_id=1, source_target_pairs={{0,3},{1,0},{2,1},{3,2},{4,7},{5,4},{6,5},{7,6},{8,11},{9,8},{10,9... | collective-permute-start | bytes 98312 | tf_op jit(solution)/shard_map/ppermute | solution.py:307
  10.3 0.0 collective-permute-done.refs_1_
  10.3 1.2 %collective-permute-done.1.refs_2_ = f32[32,256]{1,0:T(8,128)S(1)} collective-permute-done((f32[32,256]{1,0:T(8,128)S(1)}, f32[32,256]{1,0:T(8,128)S(1)}, u32[]{:S(2)}, u32[]{:S(2)}) %collective-permute-start.1) | collective-permute-done | bytes 32800 | tf_op jit(solution)/shard_map/ppermute | solution.py:307
  11.5 1.3 %collective-permute-done.2.refs_3_ = f32[32,256]{1,0:T(8,128)S(1)} collective-permute-done((f32[32,256]{1,0:T(8,128)S(1)}, f32[32,256]{1,0:T(8,128)S(1)}, u32[]{:S(2)}, u32[]{:S(2)}) %collective-permute-start.2) | collective-permute-done | bytes 32800 | tf_op jit(solution)/shard_map/ppermute | solution.py:307
  12.9 0.8 %collective-permute-start.9 = (f32[16,256]{1,0:T(8,128)S(1)}, f32[16,256]{1,0:T(8,128)S(1)}, u32[]{:S(2)}, u32[]{:S(2)}) collective-permute-start(f32[16,256]{1,0:T(8,128)S(1)} %columns.1.refs_4_), channel_id=1, source_target_pairs={{0,28},{4,0},{8,4},{12,8},{16,12},{20,16},{24,20},{28,24},{1,29},{... | collective-permute-start | bytes 49160 | tf_op jit(solution)/shard_map/ppermute | solution.py:307
  13.7 1.7 %collective-permute-start.8 = (f32[16,256]{1,0:T(8,128)S(1)}, f32[16,256]{1,0:T(8,128)S(1)}, u32[]{:S(2)}, u32[]{:S(2)}) collective-permute-start(f32[16,256]{1,0:T(8,128)S(1)} %columns.1.refs_4_), channel_id=1, source_target_pairs={{0,24},{4,28},{8,0},{12,4},{16,8},{20,12},{24,16},{28,20},{1,25},{... | collective-permute-start | bytes 49160 | tf_op jit(solution)/shard_map/ppermute | solution.py:307
  15.4 0.3 %collective-permute-start.7 = (f32[16,256]{1,0:T(8,128)S(1)}, f32[16,256]{1,0:T(8,128)S(1)}, u32[]{:S(2)}, u32[]{:S(2)}) collective-permute-start(f32[16,256]{1,0:T(8,128)S(1)} %columns.1.refs_4_), channel_id=1, source_target_pairs={{0,20},{4,24},{8,28},{12,0},{16,4},{20,8},{24,12},{28,16},{1,21},{... | collective-permute-start | bytes 49160 | tf_op jit(solution)/shard_map/ppermute | solution.py:307
  15.7 1.5 %collective-permute-start.6 = (f32[16,256]{1,0:T(8,128)S(1)}, f32[16,256]{1,0:T(8,128)S(1)}, u32[]{:S(2)}, u32[]{:S(2)}) collective-permute-start(f32[16,256]{1,0:T(8,128)S(1)} %columns.1.refs_4_), channel_id=1, source_target_pairs={{0,16},{4,20},{8,24},{12,28},{16,0},{20,4},{24,8},{28,12},{1,17},{... | collective-permute-start | bytes 49160 | tf_op jit(solution)/shard_map/ppermute | solution.py:307
  17.2 0.2 collective-permute-start.5
  17.4 0.0 collective-permute-done.9.refs_11_
  17.4 1.5 %collective-permute-start.4 = (f32[16,256]{1,0:T(8,128)S(1)}, f32[16,256]{1,0:T(8,128)S(1)}, u32[]{:S(2)}, u32[]{:S(2)}) collective-permute-start(f32[16,256]{1,0:T(8,128)S(1)} %columns.1.refs_4_), channel_id=1, source_target_pairs={{0,8},{4,12},{8,16},{12,20},{16,24},{20,28},{24,0},{28,4},{1,9},{5... | collective-permute-start | bytes 49160 | tf_op jit(solution)/shard_map/ppermute | solution.py:307
  18.9 0.0 collective-permute-done.8.refs_10_
  18.9 0.0 collective-permute-start.3
  19.5 0.0 collective-permute-done.7.refs_9_
  19.5 0.0 collective-permute-done.6.refs_8_
  19.6 0.8 %collective-permute-done.5.refs_7_ = f32[16,256]{1,0:T(8,128)S(1)} collective-permute-done((f32[16,256]{1,0:T(8,128)S(1)}, f32[16,256]{1,0:T(8,128)S(1)}, u32[]{:S(2)}, u32[]{:S(2)}) %collective-permute-start.5) | collective-permute-done | bytes 16416 | tf_op jit(solution)/shard_map/ppermute | solution.py:307
  20.4 1.7 %collective-permute-done.4.refs_6_ = f32[16,256]{1,0:T(8,128)S(1)} collective-permute-done((f32[16,256]{1,0:T(8,128)S(1)}, f32[16,256]{1,0:T(8,128)S(1)}, u32[]{:S(2)}, u32[]{:S(2)}) %collective-permute-start.4) | collective-permute-done | bytes 16416 | tf_op jit(solution)/shard_map/ppermute | solution.py:307
  22.0 0.9 %collective-permute-done.3.refs_5_ = f32[16,256]{1,0:T(8,128)S(1)} collective-permute-done((f32[16,256]{1,0:T(8,128)S(1)}, f32[16,256]{1,0:T(8,128)S(1)}, u32[]{:S(2)}, u32[]{:S(2)}) %collective-permute-start.3) | collective-permute-done | bytes 16416 | tf_op jit(solution)/shard_map/ppermute | solution.py:307
  22.9 3.3 %factors.1 = (f32[4,1024]{1,0:T(4,128)}, f32[4,64,64]{2,1,0:T(8,128)}) custom-call(f32[1]{0:T(128)S(6)} %copy.10.damping, f32[32,256]{1,0:T(8,128)S(1)} %get-tuple-element.6.refs_0_, f32[32,256]{1,0:T(8,128)S(1)} %collective-permute-done.refs_1_, f32[32,256]{1,0:T(8,128)S(1)} %collective-permute-done.1.refs_2_, ...), custom_call_target="tpu_custom_call" | custom-call | tf_op jit(solution)/shard_map/factors/pallas_call | solution.py:389
  (1 shorter events, 0.0 us)
Async XLA Ops:
  3.3 7.0 %collective-permute-start = (f32[32,256]{1,0:T(8,128)S(1)}, f32[32,256]{1,0:T(8,128)S(1)}, u32[]{:S(2)}, u32[]{:S(2)}) collective-permute-start(f32[32,256]{1,0:T(8,128)S(1)} %get-tuple-element.7), channel_id=1, source_target_pairs={{0,1},{1,2},{2,3},{3,0},{4,5},{5,6},{6,7},{7,4},{8,9},{9,10},{10,1... | collective-permute-start | bytes 98312 | tf_op jit(solution)/shard_map/ppermute | solution.py:307
  6.4 5.2 %collective-permute-start.1 = (f32[32,256]{1,0:T(8,128)S(1)}, f32[32,256]{1,0:T(8,128)S(1)}, u32[]{:S(2)}, u32[]{:S(2)}) collective-permute-start(f32[32,256]{1,0:T(8,128)S(1)} %get-tuple-element.8), channel_id=1, source_target_pairs={{0,2},{1,3},{2,0},{3,1},{4,6},{5,7},{6,4},{7,5},{8,10},{9,11},{10,... | collective-permute-start | bytes 98312 | tf_op jit(solution)/shard_map/ppermute | solution.py:307
  9.0 3.9 %collective-permute-start.2 = (f32[32,256]{1,0:T(8,128)S(1)}, f32[32,256]{1,0:T(8,128)S(1)}, u32[]{:S(2)}, u32[]{:S(2)}) collective-permute-start(f32[32,256]{1,0:T(8,128)S(1)} %get-tuple-element.9), channel_id=1, source_target_pairs={{0,3},{1,0},{2,1},{3,2},{4,7},{5,4},{6,5},{7,6},{8,11},{9,8},{10,9... | collective-permute-start | bytes 98312 | tf_op jit(solution)/shard_map/ppermute | solution.py:307
  12.9 4.5 %collective-permute-start.9 = (f32[16,256]{1,0:T(8,128)S(1)}, f32[16,256]{1,0:T(8,128)S(1)}, u32[]{:S(2)}, u32[]{:S(2)}) collective-permute-start(f32[16,256]{1,0:T(8,128)S(1)} %columns.1.refs_4_), channel_id=1, source_target_pairs={{0,28},{4,0},{8,4},{12,8},{16,12},{20,16},{24,20},{28,24},{1,29},{... | collective-permute-start | bytes 49160 | tf_op jit(solution)/shard_map/ppermute | solution.py:307
  13.7 5.2 %collective-permute-start.8 = (f32[16,256]{1,0:T(8,128)S(1)}, f32[16,256]{1,0:T(8,128)S(1)}, u32[]{:S(2)}, u32[]{:S(2)}) collective-permute-start(f32[16,256]{1,0:T(8,128)S(1)} %columns.1.refs_4_), channel_id=1, source_target_pairs={{0,24},{4,28},{8,0},{12,4},{16,8},{20,12},{24,16},{28,20},{1,25},{... | collective-permute-start | bytes 49160 | tf_op jit(solution)/shard_map/ppermute | solution.py:307
  15.4 4.1 %collective-permute-start.7 = (f32[16,256]{1,0:T(8,128)S(1)}, f32[16,256]{1,0:T(8,128)S(1)}, u32[]{:S(2)}, u32[]{:S(2)}) collective-permute-start(f32[16,256]{1,0:T(8,128)S(1)} %columns.1.refs_4_), channel_id=1, source_target_pairs={{0,20},{4,24},{8,28},{12,0},{16,4},{20,8},{24,12},{28,16},{1,21},{... | collective-permute-start | bytes 49160 | tf_op jit(solution)/shard_map/ppermute | solution.py:307
  15.7 3.9 %collective-permute-start.6 = (f32[16,256]{1,0:T(8,128)S(1)}, f32[16,256]{1,0:T(8,128)S(1)}, u32[]{:S(2)}, u32[]{:S(2)}) collective-permute-start(f32[16,256]{1,0:T(8,128)S(1)} %columns.1.refs_4_), channel_id=1, source_target_pairs={{0,16},{4,20},{8,24},{12,28},{16,0},{20,4},{24,8},{28,12},{1,17},{... | collective-permute-start | bytes 49160 | tf_op jit(solution)/shard_map/ppermute | solution.py:307
  17.2 3.2 %collective-permute-start.5 = (f32[16,256]{1,0:T(8,128)S(1)}, f32[16,256]{1,0:T(8,128)S(1)}, u32[]{:S(2)}, u32[]{:S(2)}) collective-permute-start(f32[16,256]{1,0:T(8,128)S(1)} %columns.1.refs_4_), channel_id=1, source_target_pairs={{0,12},{4,16},{8,20},{12,24},{16,28},{20,0},{24,4},{28,8},{1,13},{... | collective-permute-start | bytes 49160 | tf_op jit(solution)/shard_map/ppermute | solution.py:307
  17.4 4.6 %collective-permute-start.4 = (f32[16,256]{1,0:T(8,128)S(1)}, f32[16,256]{1,0:T(8,128)S(1)}, u32[]{:S(2)}, u32[]{:S(2)}) collective-permute-start(f32[16,256]{1,0:T(8,128)S(1)} %columns.1.refs_4_), channel_id=1, source_target_pairs={{0,8},{4,12},{8,16},{12,20},{16,24},{20,28},{24,0},{28,4},{1,9},{5... | collective-permute-start | bytes 49160 | tf_op jit(solution)/shard_map/ppermute | solution.py:307
  18.9 4.1 %collective-permute-start.3 = (f32[16,256]{1,0:T(8,128)S(1)}, f32[16,256]{1,0:T(8,128)S(1)}, u32[]{:S(2)}, u32[]{:S(2)}) collective-permute-start(f32[16,256]{1,0:T(8,128)S(1)} %columns.1.refs_4_), channel_id=1, source_target_pairs={{0,4},{4,8},{8,12},{12,16},{16,20},{20,24},{24,28},{28,0},{1,5},{5... | collective-permute-start | bytes 49160 | tf_op jit(solution)/shard_map/ppermute | solution.py:307

commit v5 on v4

--- a/solution.py
+++ b/solution.py
@@ -146,7 +146,7 @@
         stop = min(start + LANES, per * sketch)
         out[:, : stop - start] = total[:, start:stop]
         for d in range(parts):
-            g = lax.rem(me + d, parts)
+            g = me ^ d
             sends[d][:examples, start:stop] = out[
                 pl.ds(pl.multiple_of(g * examples, examples), examples), : stop - start
             ]
@@ -165,6 +165,12 @@
     columns[:, :width] = total
     if padded > width:
         columns[:, width:] = jnp.zeros((examples, padded - width), jnp.float32)
+
+
+def stack_kernel(*refs):
+    rows = refs[0].shape[0]
+    for n, part in enumerate(refs[:-1]):
+        refs[-1][n * rows : (n + 1) * rows, :] = part[...]
 
 
 def write_features(chunks, per, features):
@@ -200,9 +206,8 @@
     return guess * (2.0 - x * guess)
 
 
-def factor_kernel(parts, shards, damping, *refs):
-    chunks, rows = refs[:parts], refs[parts : parts + shards]
-    features, factors = refs[parts + shards :]
+def factor_kernel(parts, damping, *refs):
+    chunks, rows, (features, factors) = refs[:parts], refs[parts:-2], refs[-2:]
     channels, sketch, _ = factors.shape
     write_features(chunks, channels, features)
     halves = sketch // SLOT
@@ -302,9 +307,9 @@
             )
 
 
-def shift(x, axis, distance):
+def exchange(x, axis, distance):
     size = lax.axis_size(axis)
-    return lax.ppermute(x, axis, [(i, (i + distance) % size) for i in range(size)])
+    return lax.ppermute(x, axis, [(i, i ^ distance) for i in range(size)])
 
 
 def vmem():
@@ -376,7 +381,7 @@
             order,
         )
     )
-    chunks = [sends[0]] + [shift(sends[d], "mp", d) for d in range(1, parts)]
+    chunks = [sends[0]] + [exchange(sends[d], "mp", d) for d in range(1, parts)]
     columns = pl.pallas_call(
         column_kernel,
         out_shape=pltpu.VMEM((examples, max(span, GROUP * sketch)), jnp.float32),
@@ -385,14 +390,23 @@
         compiler_params=pltpu.CompilerParams(vmem_limit_bytes=2 * 2**20),
         name="columns",
     )(*in_vmem(*chunks))
-    rows = [columns] + [shift(columns, "ex", d) for d in range(1, shards)]
+    near = [columns] + [exchange(columns, "ex", d) for d in range(2, shards, 2)]
+    gathered = pl.pallas_call(
+        stack_kernel,
+        out_shape=pltpu.VMEM((len(near) * examples, columns.shape[1]), jnp.float32),
+        in_specs=[vmem()] * len(near),
+        out_specs=vmem(),
+        compiler_params=pltpu.CompilerParams(vmem_limit_bytes=2 * 2**20),
+        name="stack",
+    )(*in_vmem(*near))
+    rows = [gathered, exchange(gathered, "ex", 1)]
     return pl.pallas_call(
-        functools.partial(factor_kernel, parts, shards),
+        functools.partial(factor_kernel, parts),
         out_shape=[
             jax.ShapeDtypeStruct((examples // parts, rank * sketch), jnp.float32),
             jax.ShapeDtypeStruct((per, sketch, sketch), jnp.float32),
         ],
-        in_specs=[smem()] + [vmem()] * (parts + shards),
+        in_specs=[smem()] + [vmem()] * (parts + len(rows)),
         out_specs=[vmem()] * 2,
         compiler_params=pltpu.CompilerParams(vmem_limit_bytes=8 * 2**20),
         name="factors",

time: 26.4 us -> 26.1 us (0.989)
  starting transfers between devices: 13 us -> 9.17 us
  waiting for transfers between devices: 5.96 us -> 9.51 us
    ppermute x10 -> x7, starting transfers between devices: 13 us -> 9.17 us  [exchange(): return lax.ppermute(x, axis, [(i, i ^ distance) for i in range(size)])]
    ppermute x10 -> x7, waiting for transfers between devices: 5.96 us -> 9.51 us  [exchange(): return lax.ppermute(x, axis, [(i, i ^ distance) for i in range(size)])]
    pallas_call x1 -> x2, Pallas kernels: 3.27 us -> 3.27 us  [the longest x1 3.27 us: local(): pl.pallas_call(functools.partial(factor_kernel, parts), out_shape=[jax.Sh...]
  transfers between devices with their start and end apart: 10 -> 7, of which waited for: 5 -> 6; matrix products, arithmetic and copies ran while one was open for 0% -> 0% of each run, Pallas kernels for 0% -> 0%
where the time goes in v5:
time: 26.1 us; the launch traced here: 25.9 us
  waiting for transfers between devices  9.51 us (36%)
  starting transfers between devices  9.17 us (35%)
  Pallas kernels  5.95 us (23%)
  between operations  1.3 us (5%)
    ppermute x7, waiting for transfers between devices, exchange(): return lax.ppermute(x, axis, [(i, i ^ distance) for i in range(size)])  9.51 us
    ppermute x7, starting transfers between devices, exchange(): return lax.ppermute(x, axis, [(i, i ^ distance) for i in range(size)])  9.17 us
    pallas_call x1, Pallas kernels, local(): pl.pallas_call(functools.partial(factor_kernel, parts), out_shape=[jax.Sh...  3.27 us
    pallas_call x1, Pallas kernels, local(): pl.pallas_call(functools.partial(partial_kernel, parts, scaling), out_sha...  2.67 us
  transfers between devices with their start and end apart: 7, of which 6 were waited for; matrix products, arithmetic and copies ran while one was open for 0% of the time, Pallas kernels for 0%

profile of v5, /device:TPU:0, one launch (start us, length us, event | category | flops | bytes accessed | tf_op | source)
XLA Modules:
  0.0 25.9 jit_solution(16503834820148871172)
XLA Ops:
  0.6 2.7 %partials.1 = (f32[32,256]{1,0:T(8,128)S(1)}, f32[32,256]{1,0:T(8,128)S(1)}, f32[32,256]{1,0:T(8,128)S(1)}, f32[32,256]{1,0:T(8,128)S(1)}) custom-call(bf16[1,128,4096]{2,1,0:T(8,128)(2,1)} %acts_hbm.1, bf16[1,128,1024]{2,1,0:T(8,128)(2,1)} %grads_hbm.1, bf16[1,16,4096]{2,1,0:T(8,128)(2,1)} %down_hbm.1, bf16[1,16,1024]{2,1,0:T(8,128)(2,1)} %up_hbm.1, ...), custom_call_target="tpu_custom_call" | custom-call | tf_op jit(solution)/shard_map/partials/pallas_call | solution.py:355
  3.3 3.1 %collective-permute-start = (f32[32,256]{1,0:T(8,128)S(1)}, f32[32,256]{1,0:T(8,128)S(1)}, u32[]{:S(2)}, u32[]{:S(2)}) collective-permute-start(f32[32,256]{1,0:T(8,128)S(1)} %get-tuple-element.7), channel_id=1, source_target_pairs={{0,1},{1,0},{2,3},{3,2},{4,5},{5,4},{6,7},{7,6},{8,9},{9,8},{10,11... | collective-permute-start | bytes 98312 | tf_op jit(solution)/shard_map/ppermute | solution.py:312
  6.4 2.6 %collective-permute-start.1 = (f32[32,256]{1,0:T(8,128)S(1)}, f32[32,256]{1,0:T(8,128)S(1)}, u32[]{:S(2)}, u32[]{:S(2)}) collective-permute-start(f32[32,256]{1,0:T(8,128)S(1)} %get-tuple-element.8), channel_id=1, source_target_pairs={{0,2},{1,3},{2,0},{3,1},{4,6},{5,7},{6,4},{7,5},{8,10},{9,11},{10,... | collective-permute-start | bytes 98312 | tf_op jit(solution)/shard_map/ppermute | solution.py:312
  9.0 0.0 collective-permute-start.2
  9.0 0.0 collective-permute-done.refs_1_
  9.0 2.8 %collective-permute-done.1.refs_2_ = f32[32,256]{1,0:T(8,128)S(1)} collective-permute-done((f32[32,256]{1,0:T(8,128)S(1)}, f32[32,256]{1,0:T(8,128)S(1)}, u32[]{:S(2)}, u32[]{:S(2)}) %collective-permute-start.1) | collective-permute-done | bytes 32800 | tf_op jit(solution)/shard_map/ppermute | solution.py:312
  11.8 2.9 %collective-permute-done.2.refs_3_ = f32[32,256]{1,0:T(8,128)S(1)} collective-permute-done((f32[32,256]{1,0:T(8,128)S(1)}, f32[32,256]{1,0:T(8,128)S(1)}, u32[]{:S(2)}, u32[]{:S(2)}) %collective-permute-start.2) | collective-permute-done | bytes 32800 | tf_op jit(solution)/shard_map/ppermute | solution.py:312
  14.7 2.4 %collective-permute-start.5 = (f32[16,256]{1,0:T(8,128)S(1)}, f32[16,256]{1,0:T(8,128)S(1)}, u32[]{:S(2)}, u32[]{:S(2)}) collective-permute-start(f32[16,256]{1,0:T(8,128)S(1)} %columns.1.refs_0_), channel_id=1, source_target_pairs={{0,24},{4,28},{8,16},{12,20},{16,8},{20,12},{24,0},{28,4},{1,25},{... | collective-permute-start | bytes 49160 | tf_op jit(solution)/shard_map/ppermute | solution.py:312
  17.1 0.5 %collective-permute-start.4 = (f32[16,256]{1,0:T(8,128)S(1)}, f32[16,256]{1,0:T(8,128)S(1)}, u32[]{:S(2)}, u32[]{:S(2)}) collective-permute-start(f32[16,256]{1,0:T(8,128)S(1)} %columns.1.refs_0_), channel_id=1, source_target_pairs={{0,16},{4,20},{8,24},{12,28},{16,0},{20,4},{24,8},{28,12},{1,17},{... | collective-permute-start | bytes 49160 | tf_op jit(solution)/shard_map/ppermute | solution.py:312
  17.7 0.5 %collective-permute-start.3 = (f32[16,256]{1,0:T(8,128)S(1)}, f32[16,256]{1,0:T(8,128)S(1)}, u32[]{:S(2)}, u32[]{:S(2)}) collective-permute-start(f32[16,256]{1,0:T(8,128)S(1)} %columns.1.refs_0_), channel_id=1, source_target_pairs={{0,8},{4,12},{8,0},{12,4},{16,24},{20,28},{24,16},{28,20},{1,9},{5... | collective-permute-start | bytes 49160 | tf_op jit(solution)/shard_map/ppermute | solution.py:312
  18.2 1.1 %collective-permute-done.5.refs_3_ = f32[16,256]{1,0:T(8,128)S(1)} collective-permute-done((f32[16,256]{1,0:T(8,128)S(1)}, f32[16,256]{1,0:T(8,128)S(1)}, u32[]{:S(2)}, u32[]{:S(2)}) %collective-permute-start.5) | collective-permute-done | bytes 16416 | tf_op jit(solution)/shard_map/ppermute | solution.py:312
  19.3 1.5 %collective-permute-done.4.refs_2_ = f32[16,256]{1,0:T(8,128)S(1)} collective-permute-done((f32[16,256]{1,0:T(8,128)S(1)}, f32[16,256]{1,0:T(8,128)S(1)}, u32[]{:S(2)}, u32[]{:S(2)}) %collective-permute-start.4) | collective-permute-done | bytes 16416 | tf_op jit(solution)/shard_map/ppermute | solution.py:312
  20.9 0.5 %collective-permute-done.3.refs_1_ = f32[16,256]{1,0:T(8,128)S(1)} collective-permute-done((f32[16,256]{1,0:T(8,128)S(1)}, f32[16,256]{1,0:T(8,128)S(1)}, u32[]{:S(2)}, u32[]{:S(2)}) %collective-permute-start.3) | collective-permute-done | bytes 16416 | tf_op jit(solution)/shard_map/ppermute | solution.py:312
  21.4 0.0 collective-permute-start.6
  22.1 0.6 %collective-permute-done.6.refs_5_ = f32[64,256]{1,0:T(8,128)S(1)} collective-permute-done((f32[64,256]{1,0:T(8,128)S(1)}, f32[64,256]{1,0:T(8,128)S(1)}, u32[]{:S(2)}, u32[]{:S(2)}) %collective-permute-start.6) | collective-permute-done | bytes 65568 | tf_op jit(solution)/shard_map/ppermute | solution.py:312
  22.7 3.3 %factors.1 = (f32[4,1024]{1,0:T(4,128)}, f32[4,64,64]{2,1,0:T(8,128)}) custom-call(f32[1]{0:T(128)S(6)} %copy.10.damping, f32[32,256]{1,0:T(8,128)S(1)} %get-tuple-element.6.refs_0_, f32[32,256]{1,0:T(8,128)S(1)} %collective-permute-done.refs_1_, f32[32,256]{1,0:T(8,128)S(1)} %collective-permute-done.1.refs_2_, ...), custom_call_target="tpu_custom_call" | custom-call | tf_op jit(solution)/shard_map/factors/pallas_call | solution.py:403
  (2 shorter events, 0.0 us)
Async XLA Ops:
  3.3 5.7 %collective-permute-start = (f32[32,256]{1,0:T(8,128)S(1)}, f32[32,256]{1,0:T(8,128)S(1)}, u32[]{:S(2)}, u32[]{:S(2)}) collective-permute-start(f32[32,256]{1,0:T(8,128)S(1)} %get-tuple-element.7), channel_id=1, source_target_pairs={{0,1},{1,0},{2,3},{3,2},{4,5},{5,4},{6,7},{7,6},{8,9},{9,8},{10,11... | collective-permute-start | bytes 98312 | tf_op jit(solution)/shard_map/ppermute | solution.py:312
  6.4 5.4 %collective-permute-start.1 = (f32[32,256]{1,0:T(8,128)S(1)}, f32[32,256]{1,0:T(8,128)S(1)}, u32[]{:S(2)}, u32[]{:S(2)}) collective-permute-start(f32[32,256]{1,0:T(8,128)S(1)} %get-tuple-element.8), channel_id=1, source_target_pairs={{0,2},{1,3},{2,0},{3,1},{4,6},{5,7},{6,4},{7,5},{8,10},{9,11},{10,... | collective-permute-start | bytes 98312 | tf_op jit(solution)/shard_map/ppermute | solution.py:312
  9.0 5.7 %collective-permute-start.2 = (f32[32,256]{1,0:T(8,128)S(1)}, f32[32,256]{1,0:T(8,128)S(1)}, u32[]{:S(2)}, u32[]{:S(2)}) collective-permute-start(f32[32,256]{1,0:T(8,128)S(1)} %get-tuple-element.9), channel_id=1, source_target_pairs={{0,3},{1,2},{2,1},{3,0},{4,7},{5,6},{6,5},{7,4},{8,11},{9,10},{10,... | collective-permute-start | bytes 98312 | tf_op jit(solution)/shard_map/ppermute | solution.py:312
  14.7 4.6 %collective-permute-start.5 = (f32[16,256]{1,0:T(8,128)S(1)}, f32[16,256]{1,0:T(8,128)S(1)}, u32[]{:S(2)}, u32[]{:S(2)}) collective-permute-start(f32[16,256]{1,0:T(8,128)S(1)} %columns.1.refs_0_), channel_id=1, source_target_pairs={{0,24},{4,28},{8,16},{12,20},{16,8},{20,12},{24,0},{28,4},{1,25},{... | collective-permute-start | bytes 49160 | tf_op jit(solution)/shard_map/ppermute | solution.py:312
  17.1 3.7 %collective-permute-start.4 = (f32[16,256]{1,0:T(8,128)S(1)}, f32[16,256]{1,0:T(8,128)S(1)}, u32[]{:S(2)}, u32[]{:S(2)}) collective-permute-start(f32[16,256]{1,0:T(8,128)S(1)} %columns.1.refs_0_), channel_id=1, source_target_pairs={{0,16},{4,20},{8,24},{12,28},{16,0},{20,4},{24,8},{28,12},{1,17},{... | collective-permute-start | bytes 49160 | tf_op jit(solution)/shard_map/ppermute | solution.py:312
  17.7 3.7 %collective-permute-start.3 = (f32[16,256]{1,0:T(8,128)S(1)}, f32[16,256]{1,0:T(8,128)S(1)}, u32[]{:S(2)}, u32[]{:S(2)}) collective-permute-start(f32[16,256]{1,0:T(8,128)S(1)} %columns.1.refs_0_), channel_id=1, source_target_pairs={{0,8},{4,12},{8,0},{12,4},{16,24},{20,28},{24,16},{28,20},{1,9},{5... | collective-permute-start | bytes 49160 | tf_op jit(solution)/shard_map/ppermute | solution.py:312
  21.4 1.3 %collective-permute-start.6 = (f32[64,256]{1,0:T(8,128)S(1)}, f32[64,256]{1,0:T(8,128)S(1)}, u32[]{:S(2)}, u32[]{:S(2)}) collective-permute-start(f32[64,256]{1,0:T(8,128)S(1)} %stack.1.refs_4_), channel_id=1, source_target_pairs={{0,4},{4,0},{8,12},{12,8},{16,20},{20,16},{24,28},{28,24},{1,5},{5... | collective-permute-start | bytes 196616 | tf_op jit(solution)/shard_map/ppermute | solution.py:312

commit v6 on v5

--- a/solution.py
+++ b/solution.py
@@ -45,8 +45,7 @@
     order_hbm,
     *refs,
 ):
-    sends, refs = refs[:parts], refs[parts:]
-    acts, grads, weights_in, weights_out, order, low, out, sems, order_sem = refs
+    keep, give, acts, grads, weights_in, weights_out, order, low, out, sems, order_sem = refs
     tokens, width = acts.shape
     rank = down_hbm.shape[1]
     sketch = proj_in_hbm.shape[1]
@@ -142,29 +141,39 @@
     for c in range(1, per):
         total = jnp.where(channel == c, spread[c * rows : (c + 1) * rows], total)
     me = lax.axis_index("mp")
+    odd = lax.axis_index("ex") % 2 == 1
     for start in range(0, per * sketch, LANES):
         stop = min(start + LANES, per * sketch)
         out[:, : stop - start] = total[:, start:stop]
         for d in range(parts):
             g = me ^ d
-            sends[d][:examples, start:stop] = out[
-                pl.ds(pl.multiple_of(g * examples, examples), examples), : stop - start
-            ]
-            sends[d][examples:, start:stop] = out[pl.ds(g, examples, stride=parts), :][
-                :, : stop - start
-            ]
-
-
-def column_kernel(*refs):
-    chunks, columns = refs[:-1], refs[-1]
-    examples, padded = columns.shape
-    total = chunks[0][examples:, :]
+            by_row = out[pl.ds(pl.multiple_of(g * examples, examples), examples), :]
+            by_column = out[pl.ds(g, examples, stride=parts), :]
+            here = pl.ds(d * examples, examples)
+            keep[here, start:stop] = jnp.where(odd, by_column, by_row)[:, : stop - start]
+            give[here, start:stop] = jnp.where(odd, by_row, by_column)[:, : stop - start]
+
+
+def pair_kernel(keep, got, *sends):
+    rows = sends[0].shape[0] // 2
+    for d, send in enumerate(sends):
+        send[:rows, :] = keep[d * rows : (d + 1) * rows, :]
+        send[rows:, :] = got[d * rows : (d + 1) * rows, :]
+
+
+def sum_kernel(*refs):
+    chunks, (columns, own_rows, other_rows) = refs[:-3], refs[-3:]
+    total = chunks[0][...]
     for chunk in chunks[1:]:
-        total = total + chunk[examples:, :]
+        total = total + chunk[...]
     width = total.shape[1]
     columns[:, :width] = total
-    if padded > width:
-        columns[:, width:] = jnp.zeros((examples, padded - width), jnp.float32)
+    if columns.shape[1] > width:
+        columns[:, width:] = jnp.zeros(
+            (total.shape[0], columns.shape[1] - width), jnp.float32
+        )
+    own_rows[...] = total[: own_rows.shape[0]]
+    other_rows[...] = total[own_rows.shape[0] :]
 
 
 def stack_kernel(*refs):
@@ -173,13 +182,8 @@
         refs[-1][n * rows : (n + 1) * rows, :] = part[...]
 
 
-def write_features(chunks, per, features):
-    parts = len(chunks)
+def write_features(total, parts, per, features):
     rows_here, width = features.shape
-    examples = rows_here * parts
-    total = chunks[0][:examples, :]
-    for chunk in chunks[1:]:
-        total = total + chunk[:examples, :]
     span = width // parts
     halves = span // (per * SLOT)
     natural = jnp.concatenate(
@@ -206,14 +210,18 @@
     return guess * (2.0 - x * guess)
 
 
-def factor_kernel(parts, damping, *refs):
-    chunks, rows, (features, factors) = refs[:parts], refs[parts:-2], refs[-2:]
+def factor_kernel(
+    parts, damping, own_rows, sent_rows, own_columns, sent_columns, features, factors
+):
     channels, sketch, _ = factors.shape
-    write_features(chunks, channels, features)
+    odd = lax.axis_index("ex") % 2 == 1
+    write_features(
+        jnp.where(odd, sent_rows[...], own_rows[...]), parts, channels, features
+    )
     halves = sketch // SLOT
     panels = sketch // PANEL
     per_half = SLOT // PANEL
-    stacked = jnp.concatenate([part[...] for part in rows], axis=0)
+    stacked = jnp.where(odd, own_columns[...], sent_columns[...])
     examples = stacked.shape[0]
     high, rest = split(stacked)
     gram = (dot_tn(high, rest) + dot_tn(rest, high)) + dot_tn(high, high)
@@ -307,9 +315,20 @@
             )
 
 
-def exchange(x, axis, distance):
-    size = lax.axis_size(axis)
-    return lax.ppermute(x, axis, [(i, i ^ distance) for i in range(size)])
+def exchange(x, axis, distance, part=None):
+    sources = range(lax.axis_size(axis)) if part is None else range(part, lax.axis_size(axis), 2)
+    return lax.ppermute(x, axis, [(i, i ^ distance) for i in sources])
+
+
+def small_call(kernel, name, outs, *args):
+    return pl.pallas_call(
+        kernel,
+        out_shape=[pltpu.VMEM(shape, jnp.float32) for shape in outs],
+        in_specs=[vmem()] * len(args),
+        out_specs=[vmem()] * len(outs),
+        compiler_params=pltpu.CompilerParams(vmem_limit_bytes=2 * 2**20),
+        name=name,
+    )(*in_vmem(*args))
 
 
 def vmem():
@@ -352,11 +371,11 @@
     per = rank // parts
     span = per * sketch
     scaling = 1.0 / math.sqrt(2.0 * EXAMPLE_LENGTH * parts)
-    sends = pl.pallas_call(
+    keep, give = pl.pallas_call(
         functools.partial(partial_kernel, parts, scaling),
-        out_shape=[pltpu.VMEM((2 * examples, span), jnp.float32)] * parts,
+        out_shape=[pltpu.VMEM((parts * examples, span), jnp.float32)] * 2,
         in_specs=[hbm()] * 7,
-        out_specs=[vmem()] * parts,
+        out_specs=[vmem()] * 2,
         scratch_shapes=[
             pltpu.VMEM((tokens, width), acts.dtype),
             pltpu.VMEM((tokens, key_width), grads.dtype),
@@ -381,36 +400,35 @@
             order,
         )
     )
-    chunks = [sends[0]] + [exchange(sends[d], "mp", d) for d in range(1, parts)]
-    columns = pl.pallas_call(
-        column_kernel,
-        out_shape=pltpu.VMEM((examples, max(span, GROUP * sketch)), jnp.float32),
-        in_specs=[vmem()] * parts,
-        out_specs=vmem(),
-        compiler_params=pltpu.CompilerParams(vmem_limit_bytes=2 * 2**20),
-        name="columns",
-    )(*in_vmem(*chunks))
-    near = [columns] + [exchange(columns, "ex", d) for d in range(2, shards, 2)]
-    gathered = pl.pallas_call(
-        stack_kernel,
-        out_shape=pltpu.VMEM((len(near) * examples, columns.shape[1]), jnp.float32),
-        in_specs=[vmem()] * len(near),
-        out_specs=vmem(),
-        compiler_params=pltpu.CompilerParams(vmem_limit_bytes=2 * 2**20),
-        name="stack",
-    )(*in_vmem(*near))
-    rows = [gathered, exchange(gathered, "ex", 1)]
+    got = exchange(give, "ex", 1)
+    sends = small_call(
+        pair_kernel, "pair", [(2 * examples, span)] * parts, keep, got
+    )
+    chunks = [sends[0]] + [exchange(sends[d], "mp", d) for d in range(parts - 1, 0, -1)]
+    padded = max(span, GROUP * sketch)
+    columns, own_rows, other_rows = small_call(
+        sum_kernel,
+        "sums",
+        [(2 * examples, padded), (examples, span), (examples, span)],
+        *chunks,
+    )
+    sent_rows = exchange(other_rows, "ex", 1, 0)
+    near = [columns] + [exchange(columns, "ex", d, 1) for d in range(2, shards, 2)]
+    (own_columns,) = small_call(
+        stack_kernel, "stack", [(shards * examples, padded)], *near
+    )
+    sent_columns = exchange(own_columns, "ex", 1, 1)
     return pl.pallas_call(
         functools.partial(factor_kernel, parts),
         out_shape=[
             jax.ShapeDtypeStruct((examples // parts, rank * sketch), jnp.float32),
             jax.ShapeDtypeStruct((per, sketch, sketch), jnp.float32),
         ],
-        in_specs=[smem()] + [vmem()] * (parts + len(rows)),
+        in_specs=[smem()] + [vmem()] * 4,
         out_specs=[vmem()] * 2,
         compiler_params=pltpu.CompilerParams(vmem_limit_bytes=8 * 2**20),
         name="factors",
-    )(damping, *in_vmem(*chunks, *rows))
+    )(damping, *in_vmem(own_rows, sent_rows, own_columns, sent_columns))
 
 
 def solution(mesh):

time: 26.1 us -> 32.1 us (1.23)
  starting transfers between devices: 9.17 us -> 19.3 us
  waiting for transfers between devices: 9.51 us -> 5.26 us
    ppermute x7 -> x9, starting transfers between devices: 9.17 us -> 19.3 us  [exchange(): return lax.ppermute(x, axis, [(i, i ^ distance) for i in sources])]
    ppermute x7 -> x9, waiting for transfers between devices: 9.51 us -> 5.26 us  [exchange(): return lax.ppermute(x, axis, [(i, i ^ distance) for i in sources])]
  transfers between devices with their start and end apart: 7 -> 9, of which waited for: 6 -> 4; matrix products, arithmetic and copies ran while one was open for 0% -> 0% of each run, Pallas kernels for 0% -> 0%
where the time goes in v6:
time: 32.1 us; the launch traced here: 31.9 us
  starting transfers between devices  19.3 us (60%)
  Pallas kernels  5.98 us (19%)
  waiting for transfers between devices  5.26 us (16%)
  between operations  1.37 us (4%)
    ppermute x9, starting transfers between devices, exchange(): return lax.ppermute(x, axis, [(i, i ^ distance) for i in sources])  19.3 us
    ppermute x9, waiting for transfers between devices, exchange(): return lax.ppermute(x, axis, [(i, i ^ distance) for i in sources])  5.26 us
    pallas_call x1, Pallas kernels, local(): pl.pallas_call(functools.partial(factor_kernel, parts), out_shape=[jax.Sh...  3.28 us
    pallas_call x1, Pallas kernels, local(): pl.pallas_call(functools.partial(partial_kernel, parts, scaling), out_sha...  2.67 us
  transfers between devices with their start and end apart: 9, of which 4 were waited for; matrix products, arithmetic and copies ran while one was open for 0% of the time, Pallas kernels for 0%

profile of v6, /device:TPU:0, one launch (start us, length us, event | category | flops | bytes accessed | tf_op | source)
XLA Modules:
  0.0 31.9 jit_solution(15965921547529228986)
XLA Ops:
  0.6 2.7 %partials.1 = (f32[64,256]{1,0:T(8,128)S(1)}, f32[64,256]{1,0:T(8,128)S(1)}) custom-call(bf16[1,128,4096]{2,1,0:T(8,128)(2,1)} %acts_hbm.1, bf16[1,128,1024]{2,1,0:T(8,128)(2,1)} %grads_hbm.1, bf16[1,16,4096]{2,1,0:T(8,128)(2,1)} %down_hbm.1, bf16[1,16,1024]{2,1,0:T(8,128)(2,1)} %up_hbm.1, bf16[1,64,4096]{2,1,0:T(8,128)(2,1)} %proj_in_hbm.1, ...), custom_call_target="tpu_custom_call" | custom-call | tf_op jit(solution)/shard_map/partials/pallas_call | solution.py:374
  3.3 0.5 %collective-permute-start = (f32[64,256]{1,0:T(8,128)S(1)}, f32[64,256]{1,0:T(8,128)S(1)}, u32[]{:S(2)}, u32[]{:S(2)}) collective-permute-start(f32[64,256]{1,0:T(8,128)S(1)} %get-tuple-element.12), channel_id=1, source_target_pairs={{0,4},{4,0},{8,12},{12,8},{16,20},{20,16},{24,28},{28,24},{1,5},{5... | collective-permute-start | bytes 196616 | tf_op jit(solution)/shard_map/ppermute | solution.py:320
  3.8 0.9 %collective-permute-done.got = f32[64,256]{1,0:T(8,128)S(1)} collective-permute-done((f32[64,256]{1,0:T(8,128)S(1)}, f32[64,256]{1,0:T(8,128)S(1)}, u32[]{:S(2)}, u32[]{:S(2)}) %collective-permute-start) | collective-permute-done | bytes 65568 | tf_op jit(solution)/shard_map/ppermute | solution.py:320
  4.7 5.0 %collective-permute-start.1 = (f32[32,256]{1,0:T(8,128)S(1)}, f32[32,256]{1,0:T(8,128)S(1)}, u32[]{:S(2)}, u32[]{:S(2)}) collective-permute-start(f32[32,256]{1,0:T(8,128)S(1)} %get-tuple-element.14), channel_id=1, source_target_pairs={{0,3},{1,2},{2,1},{3,0},{4,7},{5,6},{6,5},{7,4},{8,11},{9,10},{10,... | collective-permute-start | bytes 98312 | tf_op jit(solution)/shard_map/ppermute | solution.py:320
  9.8 0.0 collective-permute-start.2
  9.8 0.6 %collective-permute-start.3 = (f32[32,256]{1,0:T(8,128)S(1)}, f32[32,256]{1,0:T(8,128)S(1)}, u32[]{:S(2)}, u32[]{:S(2)}) collective-permute-start(f32[32,256]{1,0:T(8,128)S(1)} %get-tuple-element.16), channel_id=1, source_target_pairs={{0,1},{1,0},{2,3},{3,2},{4,5},{5,4},{6,7},{7,6},{8,9},{9,8},{10,11... | collective-permute-start | bytes 98312 | tf_op jit(solution)/shard_map/ppermute | solution.py:320
  10.4 1.3 %collective-permute-done.1.refs_1_ = f32[32,256]{1,0:T(8,128)S(1)} collective-permute-done((f32[32,256]{1,0:T(8,128)S(1)}, f32[32,256]{1,0:T(8,128)S(1)}, u32[]{:S(2)}, u32[]{:S(2)}) %collective-permute-start.1) | collective-permute-done | bytes 32800 | tf_op jit(solution)/shard_map/ppermute | solution.py:320
  11.7 2.9 %collective-permute-done.2.refs_2_ = f32[32,256]{1,0:T(8,128)S(1)} collective-permute-done((f32[32,256]{1,0:T(8,128)S(1)}, f32[32,256]{1,0:T(8,128)S(1)}, u32[]{:S(2)}, u32[]{:S(2)}) %collective-permute-start.2) | collective-permute-done | bytes 32800 | tf_op jit(solution)/shard_map/ppermute | solution.py:320
  14.6 0.0 collective-permute-done.3.refs_3_
  14.6 0.7 %collective-permute-start.7 = (f32[32,256]{1,0:T(8,128)S(1)}, f32[32,256]{1,0:T(8,128)S(1)}, u32[]{:S(2)}, u32[]{:S(2)}) collective-permute-start(f32[32,256]{1,0:T(8,128)S(1)} %get-tuple-element.19.refs_0_), channel_id=1, source_target_pairs={{4,28},{12,20},{20,12},{28,4},{5,29},{13,21},{21,13},{29,5},{6,30}... | collective-permute-start | bytes 98312 | tf_op jit(solution)/shard_map/ppermute | solution.py:320
  15.3 0.7 %collective-permute-start.6 = (f32[32,256]{1,0:T(8,128)S(1)}, f32[32,256]{1,0:T(8,128)S(1)}, u32[]{:S(2)}, u32[]{:S(2)}) collective-permute-start(f32[32,256]{1,0:T(8,128)S(1)} %get-tuple-element.19.refs_0_), channel_id=1, source_target_pairs={{4,20},{12,28},{20,4},{28,12},{5,21},{13,29},{21,5},{29,13},{6,22}... | collective-permute-start | bytes 98312 | tf_op jit(solution)/shard_map/ppermute | solution.py:320
  15.9 0.7 %collective-permute-start.5 = (f32[32,256]{1,0:T(8,128)S(1)}, f32[32,256]{1,0:T(8,128)S(1)}, u32[]{:S(2)}, u32[]{:S(2)}) collective-permute-start(f32[32,256]{1,0:T(8,128)S(1)} %get-tuple-element.19.refs_0_), channel_id=1, source_target_pairs={{4,12},{12,4},{20,28},{28,20},{5,13},{13,5},{21,29},{29,21},{6,14}... | collective-permute-start | bytes 98312 | tf_op jit(solution)/shard_map/ppermute | solution.py:320
  16.6 0.0 collective-permute-done.7.refs_3_
  16.6 0.0 collective-permute-done.6.refs_2_
  16.6 0.0 collective-permute-done.5.refs_1_
  16.6 1.3 %collective-permute-start.8 = (f32[128,256]{1,0:T(8,128)S(1)}, f32[128,256]{1,0:T(8,128)S(1)}, u32[]{:S(2)}, u32[]{:S(2)}) collective-permute-start(f32[128,256]{1,0:T(8,128)S(1)} %stack.1.own_columns), channel_id=1, source_target_pairs={{4,0},{12,8},{20,16},{28,24},{5,1},{13,9},{21,17},{29,25},{6,2},{1... | collective-permute-start | bytes 393224 | tf_op jit(solution)/shard_map/ppermute | solution.py:320
  17.9 9.8 %collective-permute-start.4 = (f32[16,256]{1,0:T(8,128)S(1)}, f32[16,256]{1,0:T(8,128)S(1)}, u32[]{:S(2)}, u32[]{:S(2)}) collective-permute-start(f32[16,256]{1,0:T(8,128)S(1)} %get-tuple-element.18), channel_id=1, source_target_pairs={{0,4},{8,12},{16,20},{24,28},{1,5},{9,13},{17,21},{25,29},{2,6},{1... | collective-permute-start | bytes 49160 | tf_op jit(solution)/shard_map/ppermute | solution.py:320
  28.4 0.2 collective-permute-done.4.sent_rows
  28.6 0.0 collective-permute-done.8.sent_columns
  28.6 3.3 %factors.1 = (f32[4,1024]{1,0:T(4,128)}, f32[4,64,64]{2,1,0:T(8,128)}) custom-call(f32[1]{0:T(128)S(6)} %copy.10.damping, f32[16,256]{1,0:T(8,128)S(1)} %get-tuple-element.17.own_rows, f32[16,256]{1,0:T(8,128)S(1)} %collective-permute-done.4.sent_rows, f32[128,256]{1,0:T(8,128)S(1)} %stack.1.own_columns, f32[128,256]{1,0:T(8,128)S(1)} %collective-permute-done.8.sent_columns), custom_call_target="tpu_custom_call" | custom-call | tf_op jit(solution)/shard_map/factors/pallas_call | solution.py:421
  (3 shorter events, 0.0 us)
Async XLA Ops:
  3.3 1.4 %collective-permute-start = (f32[64,256]{1,0:T(8,128)S(1)}, f32[64,256]{1,0:T(8,128)S(1)}, u32[]{:S(2)}, u32[]{:S(2)}) collective-permute-start(f32[64,256]{1,0:T(8,128)S(1)} %get-tuple-element.12), channel_id=1, source_target_pairs={{0,4},{4,0},{8,12},{12,8},{16,20},{20,16},{24,28},{28,24},{1,5},{5... | collective-permute-start | bytes 196616 | tf_op jit(solution)/shard_map/ppermute | solution.py:320
  4.7 6.9 %collective-permute-start.1 = (f32[32,256]{1,0:T(8,128)S(1)}, f32[32,256]{1,0:T(8,128)S(1)}, u32[]{:S(2)}, u32[]{:S(2)}) collective-permute-start(f32[32,256]{1,0:T(8,128)S(1)} %get-tuple-element.14), channel_id=1, source_target_pairs={{0,3},{1,2},{2,1},{3,0},{4,7},{5,6},{6,5},{7,4},{8,11},{9,10},{10,... | collective-permute-start | bytes 98312 | tf_op jit(solution)/shard_map/ppermute | solution.py:320
  9.8 4.8 %collective-permute-start.2 = (f32[32,256]{1,0:T(8,128)S(1)}, f32[32,256]{1,0:T(8,128)S(1)}, u32[]{:S(2)}, u32[]{:S(2)}) collective-permute-start(f32[32,256]{1,0:T(8,128)S(1)} %get-tuple-element.15), channel_id=1, source_target_pairs={{0,2},{1,3},{2,0},{3,1},{4,6},{5,7},{6,4},{7,5},{8,10},{9,11},{10,... | collective-permute-start | bytes 98312 | tf_op jit(solution)/shard_map/ppermute | solution.py:320
  9.8 4.8 %collective-permute-start.3 = (f32[32,256]{1,0:T(8,128)S(1)}, f32[32,256]{1,0:T(8,128)S(1)}, u32[]{:S(2)}, u32[]{:S(2)}) collective-permute-start(f32[32,256]{1,0:T(8,128)S(1)} %get-tuple-element.16), channel_id=1, source_target_pairs={{0,1},{1,0},{2,3},{3,2},{4,5},{5,4},{6,7},{7,6},{8,9},{9,8},{10,11... | collective-permute-start | bytes 98312 | tf_op jit(solution)/shard_map/ppermute | solution.py:320
  14.6 2.0 %collective-permute-start.7 = (f32[32,256]{1,0:T(8,128)S(1)}, f32[32,256]{1,0:T(8,128)S(1)}, u32[]{:S(2)}, u32[]{:S(2)}) collective-permute-start(f32[32,256]{1,0:T(8,128)S(1)} %get-tuple-element.19.refs_0_), channel_id=1, source_target_pairs={{4,28},{12,20},{20,12},{28,4},{5,29},{13,21},{21,13},{29,5},{6,30}... | collective-permute-start | bytes 98312 | tf_op jit(solution)/shard_map/ppermute | solution.py:320
  15.3 1.4 %collective-permute-start.6 = (f32[32,256]{1,0:T(8,128)S(1)}, f32[32,256]{1,0:T(8,128)S(1)}, u32[]{:S(2)}, u32[]{:S(2)}) collective-permute-start(f32[32,256]{1,0:T(8,128)S(1)} %get-tuple-element.19.refs_0_), channel_id=1, source_target_pairs={{4,20},{12,28},{20,4},{28,12},{5,21},{13,29},{21,5},{29,13},{6,22}... | collective-permute-start | bytes 98312 | tf_op jit(solution)/shard_map/ppermute | solution.py:320
  15.9 0.7 %collective-permute-start.5 = (f32[32,256]{1,0:T(8,128)S(1)}, f32[32,256]{1,0:T(8,128)S(1)}, u32[]{:S(2)}, u32[]{:S(2)}) collective-permute-start(f32[32,256]{1,0:T(8,128)S(1)} %get-tuple-element.19.refs_0_), channel_id=1, source_target_pairs={{4,12},{12,4},{20,28},{28,20},{5,13},{13,5},{21,29},{29,21},{6,14}... | collective-permute-start | bytes 98312 | tf_op jit(solution)/shard_map/ppermute | solution.py:320
  16.6 12.0 %collective-permute-start.8 = (f32[128,256]{1,0:T(8,128)S(1)}, f32[128,256]{1,0:T(8,128)S(1)}, u32[]{:S(2)}, u32[]{:S(2)}) collective-permute-start(f32[128,256]{1,0:T(8,128)S(1)} %stack.1.own_columns), channel_id=1, source_target_pairs={{4,0},{12,8},{20,16},{28,24},{5,1},{13,9},{21,17},{29,25},{6,2},{1... | collective-permute-start | bytes 393224 | tf_op jit(solution)/shard_map/ppermute | solution.py:320
  17.9 10.7 %collective-permute-start.4 = (f32[16,256]{1,0:T(8,128)S(1)}, f32[16,256]{1,0:T(8,128)S(1)}, u32[]{:S(2)}, u32[]{:S(2)}) collective-permute-start(f32[16,256]{1,0:T(8,128)S(1)} %get-tuple-element.18), channel_id=1, source_target_pairs={{0,4},{8,12},{16,20},{24,28},{1,5},{9,13},{17,21},{25,29},{2,6},{1... | collective-permute-start | bytes 49160 | tf_op jit(solution)/shard_map/ppermute | solution.py:320

commit v7 on v6

--- a/solution.py
+++ b/solution.py
@@ -162,7 +162,7 @@
 
 
 def sum_kernel(*refs):
-    chunks, (columns, own_rows, other_rows) = refs[:-3], refs[-3:]
+    chunks, columns = refs[:-1], refs[-1]
     total = chunks[0][...]
     for chunk in chunks[1:]:
         total = total + chunk[...]
@@ -172,8 +172,6 @@
         columns[:, width:] = jnp.zeros(
             (total.shape[0], columns.shape[1] - width), jnp.float32
         )
-    own_rows[...] = total[: own_rows.shape[0]]
-    other_rows[...] = total[own_rows.shape[0] :]
 
 
 def stack_kernel(*refs):
@@ -211,17 +209,17 @@
 
 
 def factor_kernel(
-    parts, damping, own_rows, sent_rows, own_columns, sent_columns, features, factors
+    parts, damping, own, sent, features, factors
 ):
     channels, sketch, _ = factors.shape
     odd = lax.axis_index("ex") % 2 == 1
-    write_features(
-        jnp.where(odd, sent_rows[...], own_rows[...]), parts, channels, features
-    )
+    rows, width = features.shape[0] * parts, features.shape[1] // parts
+    own_rows = jnp.where(odd, sent[rows : 2 * rows, :width], own[:rows, :width])
+    write_features(own_rows, parts, channels, features)
     halves = sketch // SLOT
     panels = sketch // PANEL
     per_half = SLOT // PANEL
-    stacked = jnp.where(odd, own_columns[...], sent_columns[...])
+    stacked = jnp.where(odd, own[...], sent[...])
     examples = stacked.shape[0]
     high, rest = split(stacked)
     gram = (dot_tn(high, rest) + dot_tn(rest, high)) + dot_tn(high, high)
@@ -316,8 +314,14 @@
 
 
 def exchange(x, axis, distance, part=None):
-    sources = range(lax.axis_size(axis)) if part is None else range(part, lax.axis_size(axis), 2)
-    return lax.ppermute(x, axis, [(i, i ^ distance) for i in sources])
+    return lax.ppermute(
+        x,
+        axis,
+        [
+            (i, i if part is not None and i % 2 != part else i ^ distance)
+            for i in range(lax.axis_size(axis))
+        ],
+    )
 
 
 def small_call(kernel, name, outs, *args):
@@ -406,29 +410,21 @@
     )
     chunks = [sends[0]] + [exchange(sends[d], "mp", d) for d in range(parts - 1, 0, -1)]
     padded = max(span, GROUP * sketch)
-    columns, own_rows, other_rows = small_call(
-        sum_kernel,
-        "sums",
-        [(2 * examples, padded), (examples, span), (examples, span)],
-        *chunks,
-    )
-    sent_rows = exchange(other_rows, "ex", 1, 0)
+    (columns,) = small_call(sum_kernel, "sums", [(2 * examples, padded)], *chunks)
     near = [columns] + [exchange(columns, "ex", d, 1) for d in range(2, shards, 2)]
-    (own_columns,) = small_call(
-        stack_kernel, "stack", [(shards * examples, padded)], *near
-    )
-    sent_columns = exchange(own_columns, "ex", 1, 1)
+    (own,) = small_call(stack_kernel, "stack", [(shards * examples, padded)], *near)
+    sent = exchange(own, "ex", 1)
     return pl.pallas_call(
         functools.partial(factor_kernel, parts),
         out_shape=[
             jax.ShapeDtypeStruct((examples // parts, rank * sketch), jnp.float32),
             jax.ShapeDtypeStruct((per, sketch, sketch), jnp.float32),
         ],
-        in_specs=[smem()] + [vmem()] * 4,
+        in_specs=[smem()] + [vmem()] * 2,
         out_specs=[vmem()] * 2,
         compiler_params=pltpu.CompilerParams(vmem_limit_bytes=8 * 2**20),
         name="factors",
-    )(damping, *in_vmem(own_rows, sent_rows, own_columns, sent_columns))
+    )(damping, *in_vmem(own, sent))
 
 
 def solution(mesh):

time: 32.1 us -> 29.1 us (0.907)
  starting transfers between devices: 19.3 us -> 16.2 us
    ppermute x9 -> x8, starting transfers between devices: 19.3 us -> 16.2 us  [exchange(): lax.ppermute(x, axis, [(i, i if part is not None and i % 2 != part else i...]
    ppermute x9 -> x8, waiting for transfers between devices: 5.26 us -> 5.42 us  [exchange(): lax.ppermute(x, axis, [(i, i if part is not None and i % 2 != part else i...]
  transfers between devices with their start and end apart: 9 -> 8, of which waited for: 4 -> 4; matrix products, arithmetic and copies ran while one was open for 0% -> 0% of each run, Pallas kernels for 0% -> 0%
where the time goes in v7:
time: 29.1 us; the launch traced here: 28.9 us
  starting transfers between devices  16.2 us (56%)
  Pallas kernels  5.97 us (21%)
  waiting for transfers between devices  5.42 us (19%)
  between operations  1.36 us (5%)
    ppermute x8, starting transfers between devices, exchange(): lax.ppermute(x, axis, [(i, i if part is not None and i % 2 != part else i...  16.2 us
    ppermute x8, waiting for transfers between devices, exchange(): lax.ppermute(x, axis, [(i, i if part is not None and i % 2 != part else i...  5.42 us
    pallas_call x1, Pallas kernels, local(): pl.pallas_call(functools.partial(factor_kernel, parts), out_shape=[jax.Sh...  3.28 us
    pallas_call x1, Pallas kernels, local(): pl.pallas_call(functools.partial(partial_kernel, parts, scaling), out_sha...  2.67 us
  transfers between devices with their start and end apart: 8, of which 4 were waited for; matrix products, arithmetic and copies ran while one was open for 0% of the time, Pallas kernels for 0%

profile of v7, /device:TPU:0, one launch (start us, length us, event | category | flops | bytes accessed | tf_op | source)
XLA Modules:
  0.0 28.9 jit_solution(12304809483377005098)
XLA Ops:
  0.6 2.7 %partials.1 = (f32[64,256]{1,0:T(8,128)S(1)}, f32[64,256]{1,0:T(8,128)S(1)}) custom-call(bf16[1,128,4096]{2,1,0:T(8,128)(2,1)} %acts_hbm.1, bf16[1,128,1024]{2,1,0:T(8,128)(2,1)} %grads_hbm.1, bf16[1,16,4096]{2,1,0:T(8,128)(2,1)} %down_hbm.1, bf16[1,16,1024]{2,1,0:T(8,128)(2,1)} %up_hbm.1, bf16[1,64,4096]{2,1,0:T(8,128)(2,1)} %proj_in_hbm.1, ...), custom_call_target="tpu_custom_call" | custom-call | tf_op jit(solution)/shard_map/partials/pallas_call | solution.py:378
  3.3 0.5 %collective-permute-start = (f32[64,256]{1,0:T(8,128)S(1)}, f32[64,256]{1,0:T(8,128)S(1)}, u32[]{:S(2)}, u32[]{:S(2)}) collective-permute-start(f32[64,256]{1,0:T(8,128)S(1)} %get-tuple-element.9), channel_id=1, source_target_pairs={{0,4},{4,0},{8,12},{12,8},{16,20},{20,16},{24,28},{28,24},{1,5},{5... | collective-permute-start | bytes 196616 | tf_op jit(solution)/shard_map/ppermute | solution.py:317
  3.8 0.9 %collective-permute-done.got = f32[64,256]{1,0:T(8,128)S(1)} collective-permute-done((f32[64,256]{1,0:T(8,128)S(1)}, f32[64,256]{1,0:T(8,128)S(1)}, u32[]{:S(2)}, u32[]{:S(2)}) %collective-permute-start) | collective-permute-done | bytes 65568 | tf_op jit(solution)/shard_map/ppermute | solution.py:317
  4.7 5.0 %collective-permute-start.1 = (f32[32,256]{1,0:T(8,128)S(1)}, f32[32,256]{1,0:T(8,128)S(1)}, u32[]{:S(2)}, u32[]{:S(2)}) collective-permute-start(f32[32,256]{1,0:T(8,128)S(1)} %get-tuple-element.11), channel_id=1, source_target_pairs={{0,3},{1,2},{2,1},{3,0},{4,7},{5,6},{6,5},{7,4},{8,11},{9,10},{10,... | collective-permute-start | bytes 98312 | tf_op jit(solution)/shard_map/ppermute | solution.py:317
  9.8 0.0 collective-permute-start.2
  9.8 0.6 %collective-permute-start.3 = (f32[32,256]{1,0:T(8,128)S(1)}, f32[32,256]{1,0:T(8,128)S(1)}, u32[]{:S(2)}, u32[]{:S(2)}) collective-permute-start(f32[32,256]{1,0:T(8,128)S(1)} %get-tuple-element.13), channel_id=1, source_target_pairs={{0,1},{1,0},{2,3},{3,2},{4,5},{5,4},{6,7},{7,6},{8,9},{9,8},{10,11... | collective-permute-start | bytes 98312 | tf_op jit(solution)/shard_map/ppermute | solution.py:317
  10.4 1.3 %collective-permute-done.1.refs_1_ = f32[32,256]{1,0:T(8,128)S(1)} collective-permute-done((f32[32,256]{1,0:T(8,128)S(1)}, f32[32,256]{1,0:T(8,128)S(1)}, u32[]{:S(2)}, u32[]{:S(2)}) %collective-permute-start.1) | collective-permute-done | bytes 32800 | tf_op jit(solution)/shard_map/ppermute | solution.py:317
  11.7 2.9 %collective-permute-done.2.refs_2_ = f32[32,256]{1,0:T(8,128)S(1)} collective-permute-done((f32[32,256]{1,0:T(8,128)S(1)}, f32[32,256]{1,0:T(8,128)S(1)}, u32[]{:S(2)}, u32[]{:S(2)}) %collective-permute-start.2) | collective-permute-done | bytes 32800 | tf_op jit(solution)/shard_map/ppermute | solution.py:317
  14.6 0.0 collective-permute-done.3.refs_3_
  14.6 0.7 %collective-permute-start.6 = (f32[32,256]{1,0:T(8,128)S(1)}, f32[32,256]{1,0:T(8,128)S(1)}, u32[]{:S(2)}, u32[]{:S(2)}) collective-permute-start(f32[32,256]{1,0:T(8,128)S(1)} %sums.1.refs_0_), channel_id=1, source_target_pairs={{0,0},{4,28},{8,8},{12,20},{16,16},{20,12},{24,24},{28,4},{1,1},{5... | collective-permute-start | bytes 98312 | tf_op jit(solution)/shard_map/ppermute | solution.py:317
  15.3 0.7 %collective-permute-start.5 = (f32[32,256]{1,0:T(8,128)S(1)}, f32[32,256]{1,0:T(8,128)S(1)}, u32[]{:S(2)}, u32[]{:S(2)}) collective-permute-start(f32[32,256]{1,0:T(8,128)S(1)} %sums.1.refs_0_), channel_id=1, source_target_pairs={{0,0},{4,20},{8,8},{12,28},{16,16},{20,4},{24,24},{28,12},{1,1},{5... | collective-permute-start | bytes 98312 | tf_op jit(solution)/shard_map/ppermute | solution.py:317
  15.9 0.7 %collective-permute-start.4 = (f32[32,256]{1,0:T(8,128)S(1)}, f32[32,256]{1,0:T(8,128)S(1)}, u32[]{:S(2)}, u32[]{:S(2)}) collective-permute-start(f32[32,256]{1,0:T(8,128)S(1)} %sums.1.refs_0_), channel_id=1, source_target_pairs={{0,0},{4,12},{8,8},{12,4},{16,16},{20,28},{24,24},{28,20},{1,1},{5... | collective-permute-start | bytes 98312 | tf_op jit(solution)/shard_map/ppermute | solution.py:317
  16.6 0.0 collective-permute-done.6.refs_3_
  16.6 0.0 collective-permute-done.5.refs_2_
  16.6 0.0 collective-permute-done.4.refs_1_
  16.6 8.0 %collective-permute-start.7 = (f32[128,256]{1,0:T(8,128)S(1)}, f32[128,256]{1,0:T(8,128)S(1)}, u32[]{:S(2)}, u32[]{:S(2)}) collective-permute-start(f32[128,256]{1,0:T(8,128)S(1)} %stack.1.own), channel_id=1, source_target_pairs={{0,4},{4,0},{8,12},{12,8},{16,20},{20,16},{24,28},{28,24},{1,5},{5... | collective-permute-start | bytes 393224 | tf_op jit(solution)/shard_map/ppermute | solution.py:317
  25.3 0.3 %collective-permute-done.7.sent = f32[128,256]{1,0:T(8,128)S(1)} collective-permute-done((f32[128,256]{1,0:T(8,128)S(1)}, f32[128,256]{1,0:T(8,128)S(1)}, u32[]{:S(2)}, u32[]{:S(2)}) %collective-permute-start.7) | collective-permute-done | bytes 131104 | tf_op jit(solution)/shard_map/ppermute | solution.py:317
  25.6 3.3 %factors.1 = (f32[4,1024]{1,0:T(4,128)}, f32[4,64,64]{2,1,0:T(8,128)}) custom-call(f32[1]{0:T(128)S(6)} %copy.10.damping, f32[128,256]{1,0:T(8,128)S(1)} %stack.1.own, f32[128,256]{1,0:T(8,128)S(1)} %collective-permute-done.7.sent), custom_call_target="tpu_custom_call" | custom-call | tf_op jit(solution)/shard_map/factors/pallas_call | solution.py:417
  (3 shorter events, 0.0 us)
Async XLA Ops:
  3.3 1.4 %collective-permute-start = (f32[64,256]{1,0:T(8,128)S(1)}, f32[64,256]{1,0:T(8,128)S(1)}, u32[]{:S(2)}, u32[]{:S(2)}) collective-permute-start(f32[64,256]{1,0:T(8,128)S(1)} %get-tuple-element.9), channel_id=1, source_target_pairs={{0,4},{4,0},{8,12},{12,8},{16,20},{20,16},{24,28},{28,24},{1,5},{5... | collective-permute-start | bytes 196616 | tf_op jit(solution)/shard_map/ppermute | solution.py:317
  4.7 6.9 %collective-permute-start.1 = (f32[32,256]{1,0:T(8,128)S(1)}, f32[32,256]{1,0:T(8,128)S(1)}, u32[]{:S(2)}, u32[]{:S(2)}) collective-permute-start(f32[32,256]{1,0:T(8,128)S(1)} %get-tuple-element.11), channel_id=1, source_target_pairs={{0,3},{1,2},{2,1},{3,0},{4,7},{5,6},{6,5},{7,4},{8,11},{9,10},{10,... | collective-permute-start | bytes 98312 | tf_op jit(solution)/shard_map/ppermute | solution.py:317
  9.8 4.8 %collective-permute-start.2 = (f32[32,256]{1,0:T(8,128)S(1)}, f32[32,256]{1,0:T(8,128)S(1)}, u32[]{:S(2)}, u32[]{:S(2)}) collective-permute-start(f32[32,256]{1,0:T(8,128)S(1)} %get-tuple-element.12), channel_id=1, source_target_pairs={{0,2},{1,3},{2,0},{3,1},{4,6},{5,7},{6,4},{7,5},{8,10},{9,11},{10,... | collective-permute-start | bytes 98312 | tf_op jit(solution)/shard_map/ppermute | solution.py:317
  9.8 4.8 %collective-permute-start.3 = (f32[32,256]{1,0:T(8,128)S(1)}, f32[32,256]{1,0:T(8,128)S(1)}, u32[]{:S(2)}, u32[]{:S(2)}) collective-permute-start(f32[32,256]{1,0:T(8,128)S(1)} %get-tuple-element.13), channel_id=1, source_target_pairs={{0,1},{1,0},{2,3},{3,2},{4,5},{5,4},{6,7},{7,6},{8,9},{9,8},{10,11... | collective-permute-start | bytes 98312 | tf_op jit(solution)/shard_map/ppermute | solution.py:317
  14.6 2.0 %collective-permute-start.6 = (f32[32,256]{1,0:T(8,128)S(1)}, f32[32,256]{1,0:T(8,128)S(1)}, u32[]{:S(2)}, u32[]{:S(2)}) collective-permute-start(f32[32,256]{1,0:T(8,128)S(1)} %sums.1.refs_0_), channel_id=1, source_target_pairs={{0,0},{4,28},{8,8},{12,20},{16,16},{20,12},{24,24},{28,4},{1,1},{5... | collective-permute-start | bytes 98312 | tf_op jit(solution)/shard_map/ppermute | solution.py:317
  15.3 1.4 %collective-permute-start.5 = (f32[32,256]{1,0:T(8,128)S(1)}, f32[32,256]{1,0:T(8,128)S(1)}, u32[]{:S(2)}, u32[]{:S(2)}) collective-permute-start(f32[32,256]{1,0:T(8,128)S(1)} %sums.1.refs_0_), channel_id=1, source_target_pairs={{0,0},{4,20},{8,8},{12,28},{16,16},{20,4},{24,24},{28,12},{1,1},{5... | collective-permute-start | bytes 98312 | tf_op jit(solution)/shard_map/ppermute | solution.py:317
  15.9 0.7 %collective-permute-start.4 = (f32[32,256]{1,0:T(8,128)S(1)}, f32[32,256]{1,0:T(8,128)S(1)}, u32[]{:S(2)}, u32[]{:S(2)}) collective-permute-start(f32[32,256]{1,0:T(8,128)S(1)} %sums.1.refs_0_), channel_id=1, source_target_pairs={{0,0},{4,12},{8,8},{12,4},{16,16},{20,28},{24,24},{28,20},{1,1},{5... | collective-permute-start | bytes 98312 | tf_op jit(solution)/shard_map/ppermute | solution.py:317
  16.6 9.0 %collective-permute-start.7 = (f32[128,256]{1,0:T(8,128)S(1)}, f32[128,256]{1,0:T(8,128)S(1)}, u32[]{:S(2)}, u32[]{:S(2)}) collective-permute-start(f32[128,256]{1,0:T(8,128)S(1)} %stack.1.own), channel_id=1, source_target_pairs={{0,4},{4,0},{8,12},{12,8},{16,20},{20,16},{24,28},{28,24},{1,5},{5... | collective-permute-start | bytes 393224 | tf_op jit(solution)/shard_map/ppermute | solution.py:317

commit v8 on v5

--- a/solution.py
+++ b/solution.py
@@ -46,7 +46,7 @@
     *refs,
 ):
     sends, refs = refs[:parts], refs[parts:]
-    acts, grads, weights_in, weights_out, order, low, out, sems, order_sem = refs
+    acts, grads, weights_in, weights_out, order, low, mask, out, sems, order_sem = refs
     tokens, width = acts.shape
     rank = down_hbm.shape[1]
     sketch = proj_in_hbm.shape[1]
@@ -62,52 +62,26 @@
         )
 
     order_copy = pltpu.make_async_copy(order_hbm.at[0], order, order_sem)
-    stages = []
-    for start in range(0, width, CHUNK):
-        stages.append(
-            [
-                (acts_hbm, acts, start),
-                (proj_in_hbm, weights_in.at[pl.ds(0, sketch)], start),
-                (down_hbm, weights_in.at[pl.ds(sketch, rank)], start),
-            ]
-        )
-    for start in range(0, grads.shape[1], CHUNK):
-        stages.append(
-            [
-                (grads_hbm, grads, start),
-                (proj_out_hbm, weights_out.at[pl.ds(0, sketch)], start),
-                (up_hbm, weights_out.at[pl.ds(sketch, rank)], start),
-            ]
-        )
-    pending = [
-        [
-            copies(source, target, sems.at[n, i], start, CHUNK)
-            for i, (source, target, start) in enumerate(stage)
-        ]
-        for n, stage in enumerate(stages)
+    order_copy.start()
+    sources = [
+        (grads_hbm, grads, proj_out_hbm, up_hbm, weights_out),
+        (acts_hbm, acts, proj_in_hbm, down_hbm, weights_in),
     ]
-    for stage in pending:
-        for copy in stage:
-            copy.start()
-    order_copy.start()
-
-    def product(first, rows, weights):
-        total = None
-        for n in range(rows.shape[1] // CHUNK):
-            for copy in pending[first + n]:
-                copy.wait()
-            here = pl.ds(n * CHUNK, CHUNK)
-            term = dot_nt(weights[:, here], rows[:, here])
-            total = term if total is None else total + term
-        return total
-
-    from_acts = product(0, acts, weights_in)
-    from_grads = product(width // CHUNK, grads, weights_out)
+    pending = []
+    for data_hbm, data, first_hbm, second_hbm, weights in sources:
+        for start in range(0, data.shape[1], CHUNK):
+            n = len(pending)
+            pending.append(
+                [
+                    copies(first_hbm, weights.at[pl.ds(0, sketch)], sems.at[n, 0], start, CHUNK),
+                    copies(second_hbm, weights.at[pl.ds(sketch, rank)], sems.at[n, 1], start, CHUNK),
+                    copies(data_hbm, data, sems.at[n, 2], start, CHUNK),
+                ]
+            )
+            for copy in pending[-1]:
+                copy.start()
+
     order_copy.wait()
-    sketches = jnp.concatenate([from_acts[:sketch], from_grads[:sketch]], axis=1)
-    low[0] = from_grads[sketch:] * scaling
-    low[1] = from_acts[sketch:] * scaling
-
     rows = examples * parts
     lane = lax.broadcasted_iota(jnp.int32, (rows, 2 * tokens), 1)
     source = (lane % tokens) // EXAMPLE_LENGTH
@@ -116,14 +90,31 @@
         target = jnp.where(source[:8] == s, order[0, s], target)
     target = jnp.concatenate([target] * (rows // 8), axis=0)
     place = lax.broadcasted_iota(jnp.int32, (rows, 2 * tokens), 0) // parts
-    mine = target == place
+    mask[...] = jnp.where(target == place, scaling, 0.0)
+
+    def product(first, data, weights):
+        total = None
+        for n in range(data.shape[1] // CHUNK):
+            for copy in pending[first + n]:
+                copy.wait()
+            here = pl.ds(n * CHUNK, CHUNK)
+            term = dot_nt(weights[:, here], data[:, here])
+            total = term if total is None else total + term
+        return total
+
+    from_grads = product(0, grads, weights_out)
+    from_acts = product(grads.shape[1] // CHUNK, acts, weights_in)
+    sketches = jnp.concatenate([from_acts[:sketch], from_grads[:sketch]], axis=1)
+    low[0] = from_grads[sketch:]
+    low[1] = from_acts[sketch:]
+
     highs, lows = [], []
     for c in range(per):
         chosen = jnp.concatenate(
             [low[i, pl.ds(c, parts, stride=per), :] for i in range(2)], axis=1
         )
         chosen = jnp.concatenate([chosen] * examples, axis=0)
-        high, rest = split(jnp.where(mine, chosen, 0.0))
+        high, rest = split(chosen * mask[...])
         highs.append(high)
         lows.append(rest)
     left_high = jnp.concatenate(highs, axis=0)
@@ -364,6 +355,7 @@
             pltpu.VMEM((sketch + rank, key_width), grads.dtype),
             pltpu.SMEM(order.shape[1:], order.dtype),
             pltpu.VMEM((2, rank, tokens), jnp.float32),
+            pltpu.VMEM((examples * parts, 2 * tokens), jnp.float32),
             pltpu.VMEM((examples * parts, LANES), jnp.float32),
             pltpu.SemaphoreType.DMA(((width + key_width) // CHUNK, 3)),
             pltpu.SemaphoreType.DMA,
@@ -381,7 +373,7 @@
             order,
         )
     )
-    chunks = [sends[0]] + [exchange(sends[d], "mp", d) for d in range(1, parts)]
+    chunks = [sends[0]] + [exchange(sends[d], "mp", d) for d in range(parts - 1, 0, -1)]
     columns = pl.pallas_call(
         column_kernel,
         out_shape=pltpu.VMEM((examples, max(span, GROUP * sketch)), jnp.float32),

time: 26.1 us -> 24.6 us (0.943)
  waiting for transfers between devices: 9.51 us -> 7.97 us
    ppermute x7, waiting for transfers between devices: 9.51 us -> 7.97 us  [exchange(): return lax.ppermute(x, axis, [(i, i ^ distance) for i in range(size)])]
where the time goes in v8:
time: 24.6 us; the launch traced here: 24.4 us
  starting transfers between devices  9.31 us (38%)
  waiting for transfers between devices  7.97 us (32%)
  Pallas kernels  5.85 us (24%)
  between operations  1.3 us (5%)
    ppermute x7, starting transfers between devices, exchange(): return lax.ppermute(x, axis, [(i, i ^ distance) for i in range(size)])  9.31 us
    ppermute x7, waiting for transfers between devices, exchange(): return lax.ppermute(x, axis, [(i, i ^ distance) for i in range(size)])  7.97 us
    pallas_call x1, Pallas kernels, local(): pl.pallas_call(functools.partial(factor_kernel, parts), out_shape=[jax.Sh...  3.27 us
    pallas_call x1, Pallas kernels, local(): pl.pallas_call(functools.partial(partial_kernel, parts, scaling), out_sha...  2.57 us
  transfers between devices with their start and end apart: 7, of which 6 were waited for; matrix products, arithmetic and copies ran while one was open for 0% of the time, Pallas kernels for 0%

profile of v8, /device:TPU:0, one launch (start us, length us, event | category | flops | bytes accessed | tf_op | source)
XLA Modules:
  0.0 24.4 jit_solution(11458785482344312167)
XLA Ops:
  0.6 2.6 %partials.1 = (f32[32,256]{1,0:T(8,128)S(1)}, f32[32,256]{1,0:T(8,128)S(1)}, f32[32,256]{1,0:T(8,128)S(1)}, f32[32,256]{1,0:T(8,128)S(1)}) custom-call(bf16[1,128,4096]{2,1,0:T(8,128)(2,1)} %acts_hbm.1, bf16[1,128,1024]{2,1,0:T(8,128)(2,1)} %grads_hbm.1, bf16[1,16,4096]{2,1,0:T(8,128)(2,1)} %down_hbm.1, bf16[1,16,1024]{2,1,0:T(8,128)(2,1)} %up_hbm.1, ...), custom_call_target="tpu_custom_call" | custom-call | tf_op jit(solution)/shard_map/partials/pallas_call | solution.py:346
  3.2 5.1 %collective-permute-start = (f32[32,256]{1,0:T(8,128)S(1)}, f32[32,256]{1,0:T(8,128)S(1)}, u32[]{:S(2)}, u32[]{:S(2)}) collective-permute-start(f32[32,256]{1,0:T(8,128)S(1)} %get-tuple-element.7), channel_id=1, source_target_pairs={{0,3},{1,2},{2,1},{3,0},{4,7},{5,6},{6,5},{7,4},{8,11},{9,10},{10,... | collective-permute-start | bytes 98312 | tf_op jit(solution)/shard_map/ppermute | solution.py:303
  8.3 0.0 collective-permute-start.1
  8.3 0.6 %collective-permute-start.2 = (f32[32,256]{1,0:T(8,128)S(1)}, f32[32,256]{1,0:T(8,128)S(1)}, u32[]{:S(2)}, u32[]{:S(2)}) collective-permute-start(f32[32,256]{1,0:T(8,128)S(1)} %get-tuple-element.9), channel_id=1, source_target_pairs={{0,1},{1,0},{2,3},{3,2},{4,5},{5,4},{6,7},{7,6},{8,9},{9,8},{10,11... | collective-permute-start | bytes 98312 | tf_op jit(solution)/shard_map/ppermute | solution.py:303
  9.0 1.3 %collective-permute-done.refs_1_ = f32[32,256]{1,0:T(8,128)S(1)} collective-permute-done((f32[32,256]{1,0:T(8,128)S(1)}, f32[32,256]{1,0:T(8,128)S(1)}, u32[]{:S(2)}, u32[]{:S(2)}) %collective-permute-start) | collective-permute-done | bytes 32800 | tf_op jit(solution)/shard_map/ppermute | solution.py:303
  10.2 2.9 %collective-permute-done.1.refs_2_ = f32[32,256]{1,0:T(8,128)S(1)} collective-permute-done((f32[32,256]{1,0:T(8,128)S(1)}, f32[32,256]{1,0:T(8,128)S(1)}, u32[]{:S(2)}, u32[]{:S(2)}) %collective-permute-start.1) | collective-permute-done | bytes 32800 | tf_op jit(solution)/shard_map/ppermute | solution.py:303
  13.1 0.0 collective-permute-done.2.refs_3_
  13.1 2.5 %collective-permute-start.5 = (f32[16,256]{1,0:T(8,128)S(1)}, f32[16,256]{1,0:T(8,128)S(1)}, u32[]{:S(2)}, u32[]{:S(2)}) collective-permute-start(f32[16,256]{1,0:T(8,128)S(1)} %columns.1.refs_0_), channel_id=1, source_target_pairs={{0,24},{4,28},{8,16},{12,20},{16,8},{20,12},{24,0},{28,4},{1,25},{... | collective-permute-start | bytes 49160 | tf_op jit(solution)/shard_map/ppermute | solution.py:303
  15.7 0.5 %collective-permute-start.4 = (f32[16,256]{1,0:T(8,128)S(1)}, f32[16,256]{1,0:T(8,128)S(1)}, u32[]{:S(2)}, u32[]{:S(2)}) collective-permute-start(f32[16,256]{1,0:T(8,128)S(1)} %columns.1.refs_0_), channel_id=1, source_target_pairs={{0,16},{4,20},{8,24},{12,28},{16,0},{20,4},{24,8},{28,12},{1,17},{... | collective-permute-start | bytes 49160 | tf_op jit(solution)/shard_map/ppermute | solution.py:303
  16.2 0.5 %collective-permute-start.3 = (f32[16,256]{1,0:T(8,128)S(1)}, f32[16,256]{1,0:T(8,128)S(1)}, u32[]{:S(2)}, u32[]{:S(2)}) collective-permute-start(f32[16,256]{1,0:T(8,128)S(1)} %columns.1.refs_0_), channel_id=1, source_target_pairs={{0,8},{4,12},{8,0},{12,4},{16,24},{20,28},{24,16},{28,20},{1,9},{5... | collective-permute-start | bytes 49160 | tf_op jit(solution)/shard_map/ppermute | solution.py:303
  16.7 1.2 %collective-permute-done.5.refs_3_ = f32[16,256]{1,0:T(8,128)S(1)} collective-permute-done((f32[16,256]{1,0:T(8,128)S(1)}, f32[16,256]{1,0:T(8,128)S(1)}, u32[]{:S(2)}, u32[]{:S(2)}) %collective-permute-start.5) | collective-permute-done | bytes 16416 | tf_op jit(solution)/shard_map/ppermute | solution.py:303
  17.9 1.5 %collective-permute-done.4.refs_2_ = f32[16,256]{1,0:T(8,128)S(1)} collective-permute-done((f32[16,256]{1,0:T(8,128)S(1)}, f32[16,256]{1,0:T(8,128)S(1)}, u32[]{:S(2)}, u32[]{:S(2)}) %collective-permute-start.4) | collective-permute-done | bytes 16416 | tf_op jit(solution)/shard_map/ppermute | solution.py:303
  19.4 0.5 %collective-permute-done.3.refs_1_ = f32[16,256]{1,0:T(8,128)S(1)} collective-permute-done((f32[16,256]{1,0:T(8,128)S(1)}, f32[16,256]{1,0:T(8,128)S(1)}, u32[]{:S(2)}, u32[]{:S(2)}) %collective-permute-start.3) | collective-permute-done | bytes 16416 | tf_op jit(solution)/shard_map/ppermute | solution.py:303
  19.9 0.0 collective-permute-start.6
  20.6 0.6 %collective-permute-done.6.refs_5_ = f32[64,256]{1,0:T(8,128)S(1)} collective-permute-done((f32[64,256]{1,0:T(8,128)S(1)}, f32[64,256]{1,0:T(8,128)S(1)}, u32[]{:S(2)}, u32[]{:S(2)}) %collective-permute-start.6) | collective-permute-done | bytes 65568 | tf_op jit(solution)/shard_map/ppermute | solution.py:303
  21.2 3.3 %factors.1 = (f32[4,1024]{1,0:T(4,128)}, f32[4,64,64]{2,1,0:T(8,128)}) custom-call(f32[1]{0:T(128)S(6)} %copy.10.damping, f32[32,256]{1,0:T(8,128)S(1)} %get-tuple-element.6.refs_0_, f32[32,256]{1,0:T(8,128)S(1)} %collective-permute-done.refs_1_, f32[32,256]{1,0:T(8,128)S(1)} %collective-permute-done.1.refs_2_, ...), custom_call_target="tpu_custom_call" | custom-call | tf_op jit(solution)/shard_map/factors/pallas_call | solution.py:395
  (2 shorter events, 0.0 us)
Async XLA Ops:
  3.2 7.0 %collective-permute-start = (f32[32,256]{1,0:T(8,128)S(1)}, f32[32,256]{1,0:T(8,128)S(1)}, u32[]{:S(2)}, u32[]{:S(2)}) collective-permute-start(f32[32,256]{1,0:T(8,128)S(1)} %get-tuple-element.7), channel_id=1, source_target_pairs={{0,3},{1,2},{2,1},{3,0},{4,7},{5,6},{6,5},{7,4},{8,11},{9,10},{10,... | collective-permute-start | bytes 98312 | tf_op jit(solution)/shard_map/ppermute | solution.py:303
  8.3 4.8 %collective-permute-start.1 = (f32[32,256]{1,0:T(8,128)S(1)}, f32[32,256]{1,0:T(8,128)S(1)}, u32[]{:S(2)}, u32[]{:S(2)}) collective-permute-start(f32[32,256]{1,0:T(8,128)S(1)} %get-tuple-element.8), channel_id=1, source_target_pairs={{0,2},{1,3},{2,0},{3,1},{4,6},{5,7},{6,4},{7,5},{8,10},{9,11},{10,... | collective-permute-start | bytes 98312 | tf_op jit(solution)/shard_map/ppermute | solution.py:303
  8.3 4.8 %collective-permute-start.2 = (f32[32,256]{1,0:T(8,128)S(1)}, f32[32,256]{1,0:T(8,128)S(1)}, u32[]{:S(2)}, u32[]{:S(2)}) collective-permute-start(f32[32,256]{1,0:T(8,128)S(1)} %get-tuple-element.9), channel_id=1, source_target_pairs={{0,1},{1,0},{2,3},{3,2},{4,5},{5,4},{6,7},{7,6},{8,9},{9,8},{10,11... | collective-permute-start | bytes 98312 | tf_op jit(solution)/shard_map/ppermute | solution.py:303
  13.1 4.8 %collective-permute-start.5 = (f32[16,256]{1,0:T(8,128)S(1)}, f32[16,256]{1,0:T(8,128)S(1)}, u32[]{:S(2)}, u32[]{:S(2)}) collective-permute-start(f32[16,256]{1,0:T(8,128)S(1)} %columns.1.refs_0_), channel_id=1, source_target_pairs={{0,24},{4,28},{8,16},{12,20},{16,8},{20,12},{24,0},{28,4},{1,25},{... | collective-permute-start | bytes 49160 | tf_op jit(solution)/shard_map/ppermute | solution.py:303
  15.7 3.7 %collective-permute-start.4 = (f32[16,256]{1,0:T(8,128)S(1)}, f32[16,256]{1,0:T(8,128)S(1)}, u32[]{:S(2)}, u32[]{:S(2)}) collective-permute-start(f32[16,256]{1,0:T(8,128)S(1)} %columns.1.refs_0_), channel_id=1, source_target_pairs={{0,16},{4,20},{8,24},{12,28},{16,0},{20,4},{24,8},{28,12},{1,17},{... | collective-permute-start | bytes 49160 | tf_op jit(solution)/shard_map/ppermute | solution.py:303
  16.2 3.7 %collective-permute-start.3 = (f32[16,256]{1,0:T(8,128)S(1)}, f32[16,256]{1,0:T(8,128)S(1)}, u32[]{:S(2)}, u32[]{:S(2)}) collective-permute-start(f32[16,256]{1,0:T(8,128)S(1)} %columns.1.refs_0_), channel_id=1, source_target_pairs={{0,8},{4,12},{8,0},{12,4},{16,24},{20,28},{24,16},{28,20},{1,9},{5... | collective-permute-start | bytes 49160 | tf_op jit(solution)/shard_map/ppermute | solution.py:303
  19.9 1.3 %collective-permute-start.6 = (f32[64,256]{1,0:T(8,128)S(1)}, f32[64,256]{1,0:T(8,128)S(1)}, u32[]{:S(2)}, u32[]{:S(2)}) collective-permute-start(f32[64,256]{1,0:T(8,128)S(1)} %stack.1.refs_4_), channel_id=1, source_target_pairs={{0,4},{4,0},{8,12},{12,8},{16,20},{20,16},{24,28},{28,24},{1,5},{5... | collective-permute-start | bytes 196616 | tf_op jit(solution)/shard_map/ppermute | solution.py:303

commit v9 on v8

--- a/solution.py
+++ b/solution.py
@@ -193,7 +193,6 @@
 
 def reciprocal(x):
     guess = pl.reciprocal(x, approx=True)
-    guess = guess * (2.0 - x * guess)
     return guess * (2.0 - x * guess)
 
 
@@ -259,17 +258,25 @@
             for r in range(PANEL)
         ]
         inverse = []
-        for r in range(PANEL):
-            inv = reciprocal(block[r][r])
-            inverse.append(inv)
-            for s in range(r + 1, PANEL):
-                ratio = block[r][s] * inv
-                for t in range(s, PANEL):
-                    block[s][t] = block[s][t] - ratio * block[r][t]
-                for j in range(q + 1, panels):
-                    column[s][j] = column[s][j] - ratio * column[r][j]
-                for h in range(hq, halves):
-                    line[s][h] = line[s][h] - ratio * line[r][h]
+
+        def eliminate(r, s, inv):
+            ratio = block[r][s] * inv
+            for t in range(s, PANEL):
+                block[s][t] = block[s][t] - ratio * block[r][t]
+            for j in range(q + 1, panels):
+                column[s][j] = column[s][j] - ratio * column[r][j]
+            for h in range(hq, halves):
+                line[s][h] = line[s][h] - ratio * line[r][h]
+
+        for r in range(0, PANEL, 2):
+            pivot = block[r][r]
+            minor = pivot * block[r + 1][r + 1] - block[r][r + 1] * block[r][r + 1]
+            inverse.append(reciprocal(pivot))
+            inverse.append(pivot * reciprocal(minor))
+            eliminate(r, r + 1, inverse[r])
+            for s in range(r + 2, PANEL):
+                eliminate(r, s, inverse[r])
+                eliminate(r + 1, s, inverse[r + 1])
         result = []
         for h in range(halves):
             if h < hq:
@@ -382,7 +389,7 @@
         compiler_params=pltpu.CompilerParams(vmem_limit_bytes=2 * 2**20),
         name="columns",
     )(*in_vmem(*chunks))
-    near = [columns] + [exchange(columns, "ex", d) for d in range(2, shards, 2)]
+    near = [columns] + [exchange(columns, "ex", d) for d in range(3, shards, 2)]
     gathered = pl.pallas_call(
         stack_kernel,
         out_shape=pltpu.VMEM((len(near) * examples, columns.shape[1]), jnp.float32),

time: 24.6 us -> 22.9 us (0.931)
  Pallas kernels: 5.85 us -> 4.9 us
  starting transfers between devices: 9.31 us -> 8.78 us
    pallas_call x1, Pallas kernels: 3.27 us -> 2.32 us  [local(): pl.pallas_call(functools.partial(factor_kernel, parts), out_shape=[jax.Sh...]
    ppermute x7, starting transfers between devices: 9.31 us -> 8.78 us  [exchange(): return lax.ppermute(x, axis, [(i, i ^ distance) for i in range(size)])]
where the time goes in v9:
time: 22.9 us; the launch traced here: 22.7 us
  starting transfers between devices  8.78 us (38%)
  waiting for transfers between devices  7.75 us (34%)
  Pallas kernels  4.9 us (21%)
  between operations  1.3 us (6%)
    ppermute x7, starting transfers between devices, exchange(): return lax.ppermute(x, axis, [(i, i ^ distance) for i in range(size)])  8.78 us
    ppermute x7, waiting for transfers between devices, exchange(): return lax.ppermute(x, axis, [(i, i ^ distance) for i in range(size)])  7.75 us
    pallas_call x1, Pallas kernels, local(): pl.pallas_call(functools.partial(partial_kernel, parts, scaling), out_sha...  2.57 us
    pallas_call x1, Pallas kernels, local(): pl.pallas_call(functools.partial(factor_kernel, parts), out_shape=[jax.Sh...  2.32 us
  transfers between devices with their start and end apart: 7, of which 6 were waited for; matrix products, arithmetic and copies ran while one was open for 0% of the time, Pallas kernels for 0%

profile of v9, /device:TPU:0, one launch (start us, length us, event | category | flops | bytes accessed | tf_op | source)
XLA Modules:
  0.0 22.7 jit_solution(388829835638903810)
XLA Ops:
  0.6 2.6 %partials.1 = (f32[32,256]{1,0:T(8,128)S(1)}, f32[32,256]{1,0:T(8,128)S(1)}, f32[32,256]{1,0:T(8,128)S(1)}, f32[32,256]{1,0:T(8,128)S(1)}) custom-call(bf16[1,128,4096]{2,1,0:T(8,128)(2,1)} %acts_hbm.1, bf16[1,128,1024]{2,1,0:T(8,128)(2,1)} %grads_hbm.1, bf16[1,16,4096]{2,1,0:T(8,128)(2,1)} %down_hbm.1, bf16[1,16,1024]{2,1,0:T(8,128)(2,1)} %up_hbm.1, ...), custom_call_target="tpu_custom_call" | custom-call | tf_op jit(solution)/shard_map/partials/pallas_call | solution.py:353
  3.2 5.1 %collective-permute-start = (f32[32,256]{1,0:T(8,128)S(1)}, f32[32,256]{1,0:T(8,128)S(1)}, u32[]{:S(2)}, u32[]{:S(2)}) collective-permute-start(f32[32,256]{1,0:T(8,128)S(1)} %get-tuple-element.7), channel_id=1, source_target_pairs={{0,3},{1,2},{2,1},{3,0},{4,7},{5,6},{6,5},{7,4},{8,11},{9,10},{10,... | collective-permute-start | bytes 98312 | tf_op jit(solution)/shard_map/ppermute | solution.py:310
  8.3 0.0 collective-permute-start.1
  8.3 0.6 %collective-permute-start.2 = (f32[32,256]{1,0:T(8,128)S(1)}, f32[32,256]{1,0:T(8,128)S(1)}, u32[]{:S(2)}, u32[]{:S(2)}) collective-permute-start(f32[32,256]{1,0:T(8,128)S(1)} %get-tuple-element.9), channel_id=1, source_target_pairs={{0,1},{1,0},{2,3},{3,2},{4,5},{5,4},{6,7},{7,6},{8,9},{9,8},{10,11... | collective-permute-start | bytes 98312 | tf_op jit(solution)/shard_map/ppermute | solution.py:310
  9.0 1.3 %collective-permute-done.refs_1_ = f32[32,256]{1,0:T(8,128)S(1)} collective-permute-done((f32[32,256]{1,0:T(8,128)S(1)}, f32[32,256]{1,0:T(8,128)S(1)}, u32[]{:S(2)}, u32[]{:S(2)}) %collective-permute-start) | collective-permute-done | bytes 32800 | tf_op jit(solution)/shard_map/ppermute | solution.py:310
  10.2 2.9 %collective-permute-done.1.refs_2_ = f32[32,256]{1,0:T(8,128)S(1)} collective-permute-done((f32[32,256]{1,0:T(8,128)S(1)}, f32[32,256]{1,0:T(8,128)S(1)}, u32[]{:S(2)}, u32[]{:S(2)}) %collective-permute-start.1) | collective-permute-done | bytes 32800 | tf_op jit(solution)/shard_map/ppermute | solution.py:310
  13.1 0.0 collective-permute-done.2.refs_3_
  13.1 0.5 %collective-permute-start.5 = (f32[16,256]{1,0:T(8,128)S(1)}, f32[16,256]{1,0:T(8,128)S(1)}, u32[]{:S(2)}, u32[]{:S(2)}) collective-permute-start(f32[16,256]{1,0:T(8,128)S(1)} %columns.1.refs_0_), channel_id=1, source_target_pairs={{0,28},{4,24},{8,20},{12,16},{16,12},{20,8},{24,4},{28,0},{1,29},{... | collective-permute-start | bytes 49160 | tf_op jit(solution)/shard_map/ppermute | solution.py:310
  13.7 2.2 %collective-permute-start.4 = (f32[16,256]{1,0:T(8,128)S(1)}, f32[16,256]{1,0:T(8,128)S(1)}, u32[]{:S(2)}, u32[]{:S(2)}) collective-permute-start(f32[16,256]{1,0:T(8,128)S(1)} %columns.1.refs_0_), channel_id=1, source_target_pairs={{0,20},{4,16},{8,28},{12,24},{16,4},{20,0},{24,12},{28,8},{1,21},{... | collective-permute-start | bytes 49160 | tf_op jit(solution)/shard_map/ppermute | solution.py:310
  15.9 0.1 collective-permute-start.3
  16.0 1.3 %collective-permute-done.5.refs_3_ = f32[16,256]{1,0:T(8,128)S(1)} collective-permute-done((f32[16,256]{1,0:T(8,128)S(1)}, f32[16,256]{1,0:T(8,128)S(1)}, u32[]{:S(2)}, u32[]{:S(2)}) %collective-permute-start.5) | collective-permute-done | bytes 16416 | tf_op jit(solution)/shard_map/ppermute | solution.py:310
  17.4 0.3 %collective-permute-done.4.refs_2_ = f32[16,256]{1,0:T(8,128)S(1)} collective-permute-done((f32[16,256]{1,0:T(8,128)S(1)}, f32[16,256]{1,0:T(8,128)S(1)}, u32[]{:S(2)}, u32[]{:S(2)}) %collective-permute-start.4) | collective-permute-done | bytes 16416 | tf_op jit(solution)/shard_map/ppermute | solution.py:310
  17.6 1.5 %collective-permute-done.3.refs_1_ = f32[16,256]{1,0:T(8,128)S(1)} collective-permute-done((f32[16,256]{1,0:T(8,128)S(1)}, f32[16,256]{1,0:T(8,128)S(1)}, u32[]{:S(2)}, u32[]{:S(2)}) %collective-permute-start.3) | collective-permute-done | bytes 16416 | tf_op jit(solution)/shard_map/ppermute | solution.py:310
  19.2 0.2 collective-permute-start.6
  20.0 0.4 %collective-permute-done.6.refs_5_ = f32[64,256]{1,0:T(8,128)S(1)} collective-permute-done((f32[64,256]{1,0:T(8,128)S(1)}, f32[64,256]{1,0:T(8,128)S(1)}, u32[]{:S(2)}, u32[]{:S(2)}) %collective-permute-start.6) | collective-permute-done | bytes 65568 | tf_op jit(solution)/shard_map/ppermute | solution.py:310
  20.4 2.3 %factors.1 = (f32[4,1024]{1,0:T(4,128)}, f32[4,64,64]{2,1,0:T(8,128)}) custom-call(f32[1]{0:T(128)S(6)} %copy.10.damping, f32[32,256]{1,0:T(8,128)S(1)} %get-tuple-element.6.refs_0_, f32[32,256]{1,0:T(8,128)S(1)} %collective-permute-done.refs_1_, f32[32,256]{1,0:T(8,128)S(1)} %collective-permute-done.1.refs_2_, ...), custom_call_target="tpu_custom_call" | custom-call | tf_op jit(solution)/shard_map/factors/pallas_call | solution.py:402
  (2 shorter events, 0.0 us)
Async XLA Ops:
  3.2 7.0 %collective-permute-start = (f32[32,256]{1,0:T(8,128)S(1)}, f32[32,256]{1,0:T(8,128)S(1)}, u32[]{:S(2)}, u32[]{:S(2)}) collective-permute-start(f32[32,256]{1,0:T(8,128)S(1)} %get-tuple-element.7), channel_id=1, source_target_pairs={{0,3},{1,2},{2,1},{3,0},{4,7},{5,6},{6,5},{7,4},{8,11},{9,10},{10,... | collective-permute-start | bytes 98312 | tf_op jit(solution)/shard_map/ppermute | solution.py:310
  8.3 4.8 %collective-permute-start.1 = (f32[32,256]{1,0:T(8,128)S(1)}, f32[32,256]{1,0:T(8,128)S(1)}, u32[]{:S(2)}, u32[]{:S(2)}) collective-permute-start(f32[32,256]{1,0:T(8,128)S(1)} %get-tuple-element.8), channel_id=1, source_target_pairs={{0,2},{1,3},{2,0},{3,1},{4,6},{5,7},{6,4},{7,5},{8,10},{9,11},{10,... | collective-permute-start | bytes 98312 | tf_op jit(solution)/shard_map/ppermute | solution.py:310
  8.3 4.8 %collective-permute-start.2 = (f32[32,256]{1,0:T(8,128)S(1)}, f32[32,256]{1,0:T(8,128)S(1)}, u32[]{:S(2)}, u32[]{:S(2)}) collective-permute-start(f32[32,256]{1,0:T(8,128)S(1)} %get-tuple-element.9), channel_id=1, source_target_pairs={{0,1},{1,0},{2,3},{3,2},{4,5},{5,4},{6,7},{7,6},{8,9},{9,8},{10,11... | collective-permute-start | bytes 98312 | tf_op jit(solution)/shard_map/ppermute | solution.py:310
  13.1 4.2 %collective-permute-start.5 = (f32[16,256]{1,0:T(8,128)S(1)}, f32[16,256]{1,0:T(8,128)S(1)}, u32[]{:S(2)}, u32[]{:S(2)}) collective-permute-start(f32[16,256]{1,0:T(8,128)S(1)} %columns.1.refs_0_), channel_id=1, source_target_pairs={{0,28},{4,24},{8,20},{12,16},{16,12},{20,8},{24,4},{28,0},{1,29},{... | collective-permute-start | bytes 49160 | tf_op jit(solution)/shard_map/ppermute | solution.py:310
  13.7 4.0 %collective-permute-start.4 = (f32[16,256]{1,0:T(8,128)S(1)}, f32[16,256]{1,0:T(8,128)S(1)}, u32[]{:S(2)}, u32[]{:S(2)}) collective-permute-start(f32[16,256]{1,0:T(8,128)S(1)} %columns.1.refs_0_), channel_id=1, source_target_pairs={{0,20},{4,16},{8,28},{12,24},{16,4},{20,0},{24,12},{28,8},{1,21},{... | collective-permute-start | bytes 49160 | tf_op jit(solution)/shard_map/ppermute | solution.py:310
  15.9 3.3 %collective-permute-start.3 = (f32[16,256]{1,0:T(8,128)S(1)}, f32[16,256]{1,0:T(8,128)S(1)}, u32[]{:S(2)}, u32[]{:S(2)}) collective-permute-start(f32[16,256]{1,0:T(8,128)S(1)} %columns.1.refs_0_), channel_id=1, source_target_pairs={{0,12},{4,8},{8,4},{12,0},{16,28},{20,24},{24,20},{28,16},{1,13},{... | collective-permute-start | bytes 49160 | tf_op jit(solution)/shard_map/ppermute | solution.py:310
  19.2 1.3 %collective-permute-start.6 = (f32[64,256]{1,0:T(8,128)S(1)}, f32[64,256]{1,0:T(8,128)S(1)}, u32[]{:S(2)}, u32[]{:S(2)}) collective-permute-start(f32[64,256]{1,0:T(8,128)S(1)} %stack.1.refs_4_), channel_id=1, source_target_pairs={{0,4},{4,0},{8,12},{12,8},{16,20},{20,16},{24,28},{28,24},{1,5},{5... | collective-permute-start | bytes 196616 | tf_op jit(solution)/shard_map/ppermute | solution.py:310

commit v10 on v9

--- a/solution.py
+++ b/solution.py
@@ -146,16 +146,17 @@
             ]
 
 
-def column_kernel(*refs):
-    chunks, columns = refs[:-1], refs[-1]
+def sum_kernel(*refs):
+    chunks, (columns, feature_rows) = refs[:-2], refs[-2:]
     examples, padded = columns.shape
-    total = chunks[0][examples:, :]
+    total = chunks[0][...]
     for chunk in chunks[1:]:
-        total = total + chunk[examples:, :]
+        total = total + chunk[...]
     width = total.shape[1]
-    columns[:, :width] = total
-    if padded > width:
-        columns[:, width:] = jnp.zeros((examples, padded - width), jnp.float32)
+    for ref, value in ((feature_rows, total[:examples]), (columns, total[examples:])):
+        ref[:, :width] = value
+        if padded > width:
+            ref[:, width:] = jnp.zeros((examples, padded - width), jnp.float32)
 
 
 def stack_kernel(*refs):
@@ -164,13 +165,8 @@
         refs[-1][n * rows : (n + 1) * rows, :] = part[...]
 
 
-def write_features(chunks, per, features):
-    parts = len(chunks)
+def write_features(total, parts, per, features):
     rows_here, width = features.shape
-    examples = rows_here * parts
-    total = chunks[0][:examples, :]
-    for chunk in chunks[1:]:
-        total = total + chunk[:examples, :]
     span = width // parts
     halves = span // (per * SLOT)
     natural = jnp.concatenate(
@@ -196,15 +192,16 @@
     return guess * (2.0 - x * guess)
 
 
-def factor_kernel(parts, damping, *refs):
-    chunks, rows, (features, factors) = refs[:parts], refs[parts:-2], refs[-2:]
+def factor_kernel(parts, damping, held, sent, features, factors):
     channels, sketch, _ = factors.shape
-    write_features(chunks, channels, features)
+    examples = features.shape[0] * parts
+    gathered = held.shape[0] - examples
+    span = features.shape[1] // parts
+    write_features(sent[gathered:, :span], parts, channels, features)
     halves = sketch // SLOT
     panels = sketch // PANEL
     per_half = SLOT // PANEL
-    stacked = jnp.concatenate([part[...] for part in rows], axis=0)
-    examples = stacked.shape[0]
+    stacked = jnp.concatenate([held[:gathered, :], sent[:gathered, :]], axis=0)
     high, rest = split(stacked)
     gram = (dot_tn(high, rest) + dot_tn(rest, high)) + dot_tn(high, high)
     lane = lax.broadcasted_iota(jnp.int32, (PANEL, LANES), 1)
@@ -222,7 +219,7 @@
                 start = hr * LANES + c * SLOT + at * PANEL
                 block = gram[start : start + PANEL, h * LANES : (h + 1) * LANES]
                 value = block if c == 0 else jnp.where(slot == c, block, value)
-            value = value * (1.0 / examples)
+            value = value * (1.0 / stacked.shape[0])
             if h == hr:
                 value = value + jnp.where(within == at * PANEL + sub, ridge, 0.0)
             line.append(value)
@@ -305,9 +302,17 @@
             )
 
 
-def exchange(x, axis, distance):
-    size = lax.axis_size(axis)
-    return lax.ppermute(x, axis, [(i, i ^ distance) for i in range(size)])
+def exchange(x, ex_distance, mp_distance=0):
+    shards, parts = lax.axis_size("ex"), lax.axis_size("mp")
+    return lax.ppermute(
+        x,
+        ("ex", "mp"),
+        [
+            (m * parts + b, (m ^ ex_distance) * parts + (b ^ mp_distance))
+            for m in range(shards)
+            for b in range(parts)
+        ],
+    )
 
 
 def vmem():
@@ -380,36 +385,37 @@
             order,
         )
     )
-    chunks = [sends[0]] + [exchange(sends[d], "mp", d) for d in range(parts - 1, 0, -1)]
-    columns = pl.pallas_call(
-        column_kernel,
-        out_shape=pltpu.VMEM((examples, max(span, GROUP * sketch)), jnp.float32),
+    chunks = [exchange(sends[d], 1, d) for d in range(parts - 1, -1, -1)]
+    padded = max(span, GROUP * sketch)
+    columns, feature_rows = pl.pallas_call(
+        sum_kernel,
+        out_shape=[pltpu.VMEM((examples, padded), jnp.float32)] * 2,
         in_specs=[vmem()] * parts,
-        out_specs=vmem(),
+        out_specs=[vmem()] * 2,
         compiler_params=pltpu.CompilerParams(vmem_limit_bytes=2 * 2**20),
-        name="columns",
+        name="sums",
     )(*in_vmem(*chunks))
-    near = [columns] + [exchange(columns, "ex", d) for d in range(3, shards, 2)]
-    gathered = pl.pallas_call(
+    near = [columns] + [exchange(columns, d) for d in range(3, shards, 2)] + [feature_rows]
+    held = pl.pallas_call(
         stack_kernel,
-        out_shape=pltpu.VMEM((len(near) * examples, columns.shape[1]), jnp.float32),
+        out_shape=pltpu.VMEM((len(near) * examples, padded), jnp.float32),
         in_specs=[vmem()] * len(near),
         out_specs=vmem(),
         compiler_params=pltpu.CompilerParams(vmem_limit_bytes=2 * 2**20),
         name="stack",
     )(*in_vmem(*near))
-    rows = [gathered, exchange(gathered, "ex", 1)]
+    sent = exchange(held, 1)
     return pl.pallas_call(
         functools.partial(factor_kernel, parts),
         out_shape=[
             jax.ShapeDtypeStruct((examples // parts, rank * sketch), jnp.float32),
             jax.ShapeDtypeStruct((per, sketch, sketch), jnp.float32),
         ],
-        in_specs=[smem()] + [vmem()] * (parts + len(rows)),
+        in_specs=[smem()] + [vmem()] * 2,
         out_specs=[vmem()] * 2,
         compiler_params=pltpu.CompilerParams(vmem_limit_bytes=8 * 2**20),
         name="factors",
-    )(damping, *in_vmem(*chunks, *rows))
+    )(damping, *in_vmem(held, sent))
 
 
 def solution(mesh):

time: 22.9 us -> 22 us (0.961)
  waiting for transfers between devices: 7.75 us -> 6.56 us
  starting transfers between devices: 8.78 us -> 9.08 us
    ppermute x7 -> x8, waiting for transfers between devices: 7.75 us -> 6.56 us  [exchange(): lax.ppermute(x, ('ex', 'mp'), [(m * parts + b, (m ^ ex_distance) * parts...]
    ppermute x7 -> x8, starting transfers between devices: 8.78 us -> 9.08 us  [exchange(): lax.ppermute(x, ('ex', 'mp'), [(m * parts + b, (m ^ ex_distance) * parts...]
  transfers between devices with their start and end apart: 7 -> 8, of which waited for: 6 -> 6; matrix products, arithmetic and copies ran while one was open for 0% -> 0% of each run, Pallas kernels for 0% -> 0%
where the time goes in v10:
time: 22 us; the launch traced here: 21.9 us
  starting transfers between devices  9.08 us (41%)
  waiting for transfers between devices  6.56 us (30%)
  Pallas kernels  4.91 us (22%)
  between operations  1.3 us (6%)
    ppermute x8, starting transfers between devices, exchange(): lax.ppermute(x, ('ex', 'mp'), [(m * parts + b, (m ^ ex_distance) * parts...  9.08 us
    ppermute x8, waiting for transfers between devices, exchange(): lax.ppermute(x, ('ex', 'mp'), [(m * parts + b, (m ^ ex_distance) * parts...  6.56 us
    pallas_call x1, Pallas kernels, local(): pl.pallas_call(functools.partial(partial_kernel, parts, scaling), out_sha...  2.57 us
    pallas_call x1, Pallas kernels, local(): pl.pallas_call(functools.partial(factor_kernel, parts), out_shape=[jax.Sh...  2.33 us
  transfers between devices with their start and end apart: 8, of which 6 were waited for; matrix products, arithmetic and copies ran while one was open for 0% of the time, Pallas kernels for 0%

profile of v10, /device:TPU:0, one launch (start us, length us, event | category | flops | bytes accessed | tf_op | source)
XLA Modules:
  0.0 21.9 jit_solution(16011762340263349918)
XLA Ops:
  0.6 2.6 %partials.1 = (f32[32,256]{1,0:T(8,128)S(1)}, f32[32,256]{1,0:T(8,128)S(1)}, f32[32,256]{1,0:T(8,128)S(1)}, f32[32,256]{1,0:T(8,128)S(1)}) custom-call(bf16[1,128,4096]{2,1,0:T(8,128)(2,1)} %acts_hbm.1, bf16[1,128,1024]{2,1,0:T(8,128)(2,1)} %grads_hbm.1, bf16[1,16,4096]{2,1,0:T(8,128)(2,1)} %down_hbm.1, bf16[1,16,1024]{2,1,0:T(8,128)(2,1)} %up_hbm.1, ...), custom_call_target="tpu_custom_call" | custom-call | tf_op jit(solution)/shard_map/partials/pallas_call | solution.py:358
  3.2 4.6 %collective-permute-start = (f32[32,256]{1,0:T(8,128)S(1)}, f32[32,256]{1,0:T(8,128)S(1)}, u32[]{:S(2)}, u32[]{:S(2)}) collective-permute-start(f32[32,256]{1,0:T(8,128)S(1)} %get-tuple-element.8), channel_id=1, source_target_pairs={{0,7},{1,6},{2,5},{3,4},{4,3},{5,2},{6,1},{7,0},{8,15},{9,14},{10,... | collective-permute-start | bytes 98312 | tf_op jit(solution)/shard_map/ppermute | solution.py:307
  7.8 0.0 collective-permute-start.1
  7.8 0.9 %collective-permute-start.2 = (f32[32,256]{1,0:T(8,128)S(1)}, f32[32,256]{1,0:T(8,128)S(1)}, u32[]{:S(2)}, u32[]{:S(2)}) collective-permute-start(f32[32,256]{1,0:T(8,128)S(1)} %get-tuple-element.10), channel_id=1, source_target_pairs={{0,5},{1,4},{2,7},{3,6},{4,1},{5,0},{6,3},{7,2},{8,13},{9,12},{10,... | collective-permute-start | bytes 98312 | tf_op jit(solution)/shard_map/ppermute | solution.py:307
  8.7 0.0 collective-permute-start.3
  8.7 0.9 %collective-permute-done.refs_0_ = f32[32,256]{1,0:T(8,128)S(1)} collective-permute-done((f32[32,256]{1,0:T(8,128)S(1)}, f32[32,256]{1,0:T(8,128)S(1)}, u32[]{:S(2)}, u32[]{:S(2)}) %collective-permute-start) | collective-permute-done | bytes 32800 | tf_op jit(solution)/shard_map/ppermute | solution.py:307
  9.5 2.8 %collective-permute-done.1.refs_1_ = f32[32,256]{1,0:T(8,128)S(1)} collective-permute-done((f32[32,256]{1,0:T(8,128)S(1)}, f32[32,256]{1,0:T(8,128)S(1)}, u32[]{:S(2)}, u32[]{:S(2)}) %collective-permute-start.1) | collective-permute-done | bytes 32800 | tf_op jit(solution)/shard_map/ppermute | solution.py:307
  12.3 0.0 collective-permute-done.2.refs_2_
  12.3 0.0 collective-permute-done.3.refs_3_
  12.3 2.5 %collective-permute-start.6 = (f32[16,256]{1,0:T(8,128)S(1)}, f32[16,256]{1,0:T(8,128)S(1)}, u32[]{:S(2)}, u32[]{:S(2)}) collective-permute-start(f32[16,256]{1,0:T(8,128)S(1)} %get-tuple-element.12.refs_0_), channel_id=1, source_target_pairs={{0,28},{1,29},{2,30},{3,31},{4,24},{5,25},{6,26},{7,27},{8,20},{9,... | collective-permute-start | bytes 49160 | tf_op jit(solution)/shard_map/ppermute | solution.py:307
  14.8 0.3 %collective-permute-start.5 = (f32[16,256]{1,0:T(8,128)S(1)}, f32[16,256]{1,0:T(8,128)S(1)}, u32[]{:S(2)}, u32[]{:S(2)}) collective-permute-start(f32[16,256]{1,0:T(8,128)S(1)} %get-tuple-element.12.refs_0_), channel_id=1, source_target_pairs={{0,20},{1,21},{2,22},{3,23},{4,16},{5,17},{6,18},{7,19},{8,28},{9,... | collective-permute-start | bytes 49160 | tf_op jit(solution)/shard_map/ppermute | solution.py:307
  15.1 0.5 %collective-permute-start.4 = (f32[16,256]{1,0:T(8,128)S(1)}, f32[16,256]{1,0:T(8,128)S(1)}, u32[]{:S(2)}, u32[]{:S(2)}) collective-permute-start(f32[16,256]{1,0:T(8,128)S(1)} %get-tuple-element.12.refs_0_), channel_id=1, source_target_pairs={{0,12},{1,13},{2,14},{3,15},{4,8},{5,9},{6,10},{7,11},{8,4},{9,5},... | collective-permute-start | bytes 49160 | tf_op jit(solution)/shard_map/ppermute | solution.py:307
  15.6 0.9 %collective-permute-done.6.refs_3_ = f32[16,256]{1,0:T(8,128)S(1)} collective-permute-done((f32[16,256]{1,0:T(8,128)S(1)}, f32[16,256]{1,0:T(8,128)S(1)}, u32[]{:S(2)}, u32[]{:S(2)}) %collective-permute-start.6) | collective-permute-done | bytes 16416 | tf_op jit(solution)/shard_map/ppermute | solution.py:307
  16.5 1.5 %collective-permute-done.5.refs_2_ = f32[16,256]{1,0:T(8,128)S(1)} collective-permute-done((f32[16,256]{1,0:T(8,128)S(1)}, f32[16,256]{1,0:T(8,128)S(1)}, u32[]{:S(2)}, u32[]{:S(2)}) %collective-permute-start.5) | collective-permute-done | bytes 16416 | tf_op jit(solution)/shard_map/ppermute | solution.py:307
  18.0 0.3 %collective-permute-done.4.refs_1_ = f32[16,256]{1,0:T(8,128)S(1)} collective-permute-done((f32[16,256]{1,0:T(8,128)S(1)}, f32[16,256]{1,0:T(8,128)S(1)}, u32[]{:S(2)}, u32[]{:S(2)}) %collective-permute-start.4) | collective-permute-done | bytes 16416 | tf_op jit(solution)/shard_map/ppermute | solution.py:307
  18.3 0.4 %collective-permute-start.7 = (f32[80,256]{1,0:T(8,128)S(1)}, f32[80,256]{1,0:T(8,128)S(1)}, u32[]{:S(2)}, u32[]{:S(2)}) collective-permute-start(f32[80,256]{1,0:T(8,128)S(1)} %stack.1.held), channel_id=1, source_target_pairs={{0,4},{1,5},{2,6},{3,7},{4,0},{5,1},{6,2},{7,3},{8,12},{9,13},{10,... | collective-permute-start | bytes 245768 | tf_op jit(solution)/shard_map/ppermute | solution.py:307
  19.3 0.3 %collective-permute-done.7.sent = f32[80,256]{1,0:T(8,128)S(1)} collective-permute-done((f32[80,256]{1,0:T(8,128)S(1)}, f32[80,256]{1,0:T(8,128)S(1)}, u32[]{:S(2)}, u32[]{:S(2)}) %collective-permute-start.7) | collective-permute-done | bytes 81952 | tf_op jit(solution)/shard_map/ppermute | solution.py:307
  19.5 2.3 %factors.1 = (f32[4,1024]{1,0:T(4,128)}, f32[4,64,64]{2,1,0:T(8,128)}) custom-call(f32[1]{0:T(128)S(6)} %copy.10.damping, f32[80,256]{1,0:T(8,128)S(1)} %stack.1.held, f32[80,256]{1,0:T(8,128)S(1)} %collective-permute-done.7.sent), custom_call_target="tpu_custom_call" | custom-call | tf_op jit(solution)/shard_map/factors/pallas_call | solution.py:408
  (2 shorter events, 0.0 us)
Async XLA Ops:
  3.2 6.3 %collective-permute-start = (f32[32,256]{1,0:T(8,128)S(1)}, f32[32,256]{1,0:T(8,128)S(1)}, u32[]{:S(2)}, u32[]{:S(2)}) collective-permute-start(f32[32,256]{1,0:T(8,128)S(1)} %get-tuple-element.8), channel_id=1, source_target_pairs={{0,7},{1,6},{2,5},{3,4},{4,3},{5,2},{6,1},{7,0},{8,15},{9,14},{10,... | collective-permute-start | bytes 98312 | tf_op jit(solution)/shard_map/ppermute | solution.py:307
  7.8 4.5 %collective-permute-start.1 = (f32[32,256]{1,0:T(8,128)S(1)}, f32[32,256]{1,0:T(8,128)S(1)}, u32[]{:S(2)}, u32[]{:S(2)}) collective-permute-start(f32[32,256]{1,0:T(8,128)S(1)} %get-tuple-element.9), channel_id=1, source_target_pairs={{0,6},{1,7},{2,4},{3,5},{4,2},{5,3},{6,0},{7,1},{8,14},{9,15},{10,... | collective-permute-start | bytes 98312 | tf_op jit(solution)/shard_map/ppermute | solution.py:307
  7.8 4.5 %collective-permute-start.2 = (f32[32,256]{1,0:T(8,128)S(1)}, f32[32,256]{1,0:T(8,128)S(1)}, u32[]{:S(2)}, u32[]{:S(2)}) collective-permute-start(f32[32,256]{1,0:T(8,128)S(1)} %get-tuple-element.10), channel_id=1, source_target_pairs={{0,5},{1,4},{2,7},{3,6},{4,1},{5,0},{6,3},{7,2},{8,13},{9,12},{10,... | collective-permute-start | bytes 98312 | tf_op jit(solution)/shard_map/ppermute | solution.py:307
  8.7 3.6 %collective-permute-start.3 = (f32[32,256]{1,0:T(8,128)S(1)}, f32[32,256]{1,0:T(8,128)S(1)}, u32[]{:S(2)}, u32[]{:S(2)}) collective-permute-start(f32[32,256]{1,0:T(8,128)S(1)} %get-tuple-element.11), channel_id=1, source_target_pairs={{0,4},{1,5},{2,6},{3,7},{4,0},{5,1},{6,2},{7,3},{8,12},{9,13},{10,... | collective-permute-start | bytes 98312 | tf_op jit(solution)/shard_map/ppermute | solution.py:307
  12.3 4.1 %collective-permute-start.6 = (f32[16,256]{1,0:T(8,128)S(1)}, f32[16,256]{1,0:T(8,128)S(1)}, u32[]{:S(2)}, u32[]{:S(2)}) collective-permute-start(f32[16,256]{1,0:T(8,128)S(1)} %get-tuple-element.12.refs_0_), channel_id=1, source_target_pairs={{0,28},{1,29},{2,30},{3,31},{4,24},{5,25},{6,26},{7,27},{8,20},{9,... | collective-permute-start | bytes 49160 | tf_op jit(solution)/shard_map/ppermute | solution.py:307
  14.8 3.2 %collective-permute-start.5 = (f32[16,256]{1,0:T(8,128)S(1)}, f32[16,256]{1,0:T(8,128)S(1)}, u32[]{:S(2)}, u32[]{:S(2)}) collective-permute-start(f32[16,256]{1,0:T(8,128)S(1)} %get-tuple-element.12.refs_0_), channel_id=1, source_target_pairs={{0,20},{1,21},{2,22},{3,23},{4,16},{5,17},{6,18},{7,19},{8,28},{9,... | collective-permute-start | bytes 49160 | tf_op jit(solution)/shard_map/ppermute | solution.py:307
  15.1 3.2 %collective-permute-start.4 = (f32[16,256]{1,0:T(8,128)S(1)}, f32[16,256]{1,0:T(8,128)S(1)}, u32[]{:S(2)}, u32[]{:S(2)}) collective-permute-start(f32[16,256]{1,0:T(8,128)S(1)} %get-tuple-element.12.refs_0_), channel_id=1, source_target_pairs={{0,12},{1,13},{2,14},{3,15},{4,8},{5,9},{6,10},{7,11},{8,4},{9,5},... | collective-permute-start | bytes 49160 | tf_op jit(solution)/shard_map/ppermute | solution.py:307
  18.3 1.3 %collective-permute-start.7 = (f32[80,256]{1,0:T(8,128)S(1)}, f32[80,256]{1,0:T(8,128)S(1)}, u32[]{:S(2)}, u32[]{:S(2)}) collective-permute-start(f32[80,256]{1,0:T(8,128)S(1)} %stack.1.held), channel_id=1, source_target_pairs={{0,4},{1,5},{2,6},{3,7},{4,0},{5,1},{6,2},{7,3},{8,12},{9,13},{10,... | collective-permute-start | bytes 245768 | tf_op jit(solution)/shard_map/ppermute | solution.py:307

commit v11 on v10

--- a/solution.py
+++ b/solution.py
@@ -22,10 +22,8 @@
     )
 
 
-def dot_tn(a, b):
-    return lax.dot_general(
-        a, b, (((0,), (0,)), ((), ())), preferred_element_type=jnp.float32
-    )
+def dot_nn(a, b):
+    return jnp.dot(a, b, preferred_element_type=jnp.float32)
 
 
 def split(x):
@@ -124,9 +122,9 @@
         axis=0,
     )
     right_high, right_low = split(right)
-    spread = (
-        dot_nt(left_high, right_low) + dot_nt(left_low, right_high)
-    ) + dot_nt(left_high, right_high)
+    both = dot_nt(jnp.concatenate([left_high, left_low], axis=0), right_high)
+    size = left_high.shape[0]
+    spread = (dot_nt(left_high, right_low) + both[size:]) + both[:size]
     column = lax.broadcasted_iota(jnp.int32, (rows, per * sketch), 1)
     channel = (column // SLOT) % per
     total = spread[:rows]
@@ -203,7 +201,11 @@
     per_half = SLOT // PANEL
     stacked = jnp.concatenate([held[:gathered, :], sent[:gathered, :]], axis=0)
     high, rest = split(stacked)
-    gram = (dot_tn(high, rest) + dot_tn(rest, high)) + dot_tn(high, high)
+    turned_high, turned_rest = split(jnp.transpose(stacked))
+    gram = dot_nn(turned_high, rest) + dot_nn(
+        jnp.concatenate([turned_rest, turned_high], axis=1),
+        jnp.concatenate([high, high], axis=0),
+    )
     lane = lax.broadcasted_iota(jnp.int32, (PANEL, LANES), 1)
     sub = lax.broadcasted_iota(jnp.int32, (PANEL, LANES), 0)
     slot = lane // SLOT

time: 22 us -> 22 us (level)
  no operation moved by 1% of the time
where the time goes in v11:
time: 22 us; the launch traced here: 21.9 us
  starting transfers between devices  9.08 us (41%)
  waiting for transfers between devices  6.56 us (30%)
  Pallas kernels  4.91 us (22%)
  between operations  1.3 us (6%)
    ppermute x8, starting transfers between devices, exchange(): lax.ppermute(x, ('ex', 'mp'), [(m * parts + b, (m ^ ex_distance) * parts...  9.08 us
    ppermute x8, waiting for transfers between devices, exchange(): lax.ppermute(x, ('ex', 'mp'), [(m * parts + b, (m ^ ex_distance) * parts...  6.56 us
    pallas_call x1, Pallas kernels, local(): pl.pallas_call(functools.partial(partial_kernel, parts, scaling), out_sha...  2.57 us
    pallas_call x1, Pallas kernels, local(): pl.pallas_call(functools.partial(factor_kernel, parts), out_shape=[jax.Sh...  2.32 us
  transfers between devices with their start and end apart: 8, of which 6 were waited for; matrix products, arithmetic and copies ran while one was open for 0% of the time, Pallas kernels for 0%

profile of v11, /device:TPU:0, one launch (start us, length us, event | category | flops | bytes accessed | tf_op | source)
XLA Modules:
  0.0 21.9 jit_solution(15421510295998071306)
XLA Ops:
  0.6 2.6 %partials.1 = (f32[32,256]{1,0:T(8,128)S(1)}, f32[32,256]{1,0:T(8,128)S(1)}, f32[32,256]{1,0:T(8,128)S(1)}, f32[32,256]{1,0:T(8,128)S(1)}) custom-call(bf16[1,128,4096]{2,1,0:T(8,128)(2,1)} %acts_hbm.1, bf16[1,128,1024]{2,1,0:T(8,128)(2,1)} %grads_hbm.1, bf16[1,16,4096]{2,1,0:T(8,128)(2,1)} %down_hbm.1, bf16[1,16,1024]{2,1,0:T(8,128)(2,1)} %up_hbm.1, ...), custom_call_target="tpu_custom_call" | custom-call | tf_op jit(solution)/shard_map/partials/pallas_call | solution.py:360
  3.2 4.6 %collective-permute-start = (f32[32,256]{1,0:T(8,128)S(1)}, f32[32,256]{1,0:T(8,128)S(1)}, u32[]{:S(2)}, u32[]{:S(2)}) collective-permute-start(f32[32,256]{1,0:T(8,128)S(1)} %get-tuple-element.8), channel_id=1, source_target_pairs={{0,7},{1,6},{2,5},{3,4},{4,3},{5,2},{6,1},{7,0},{8,15},{9,14},{10,... | collective-permute-start | bytes 98312 | tf_op jit(solution)/shard_map/ppermute | solution.py:309
  7.8 0.0 collective-permute-start.1
  7.8 0.9 %collective-permute-start.2 = (f32[32,256]{1,0:T(8,128)S(1)}, f32[32,256]{1,0:T(8,128)S(1)}, u32[]{:S(2)}, u32[]{:S(2)}) collective-permute-start(f32[32,256]{1,0:T(8,128)S(1)} %get-tuple-element.10), channel_id=1, source_target_pairs={{0,5},{1,4},{2,7},{3,6},{4,1},{5,0},{6,3},{7,2},{8,13},{9,12},{10,... | collective-permute-start | bytes 98312 | tf_op jit(solution)/shard_map/ppermute | solution.py:309
  8.7 0.0 collective-permute-start.3
  8.7 0.9 %collective-permute-done.refs_0_ = f32[32,256]{1,0:T(8,128)S(1)} collective-permute-done((f32[32,256]{1,0:T(8,128)S(1)}, f32[32,256]{1,0:T(8,128)S(1)}, u32[]{:S(2)}, u32[]{:S(2)}) %collective-permute-start) | collective-permute-done | bytes 32800 | tf_op jit(solution)/shard_map/ppermute | solution.py:309
  9.5 2.8 %collective-permute-done.1.refs_1_ = f32[32,256]{1,0:T(8,128)S(1)} collective-permute-done((f32[32,256]{1,0:T(8,128)S(1)}, f32[32,256]{1,0:T(8,128)S(1)}, u32[]{:S(2)}, u32[]{:S(2)}) %collective-permute-start.1) | collective-permute-done | bytes 32800 | tf_op jit(solution)/shard_map/ppermute | solution.py:309
  12.3 0.0 collective-permute-done.2.refs_2_
  12.3 0.0 collective-permute-done.3.refs_3_
  12.3 2.5 %collective-permute-start.6 = (f32[16,256]{1,0:T(8,128)S(1)}, f32[16,256]{1,0:T(8,128)S(1)}, u32[]{:S(2)}, u32[]{:S(2)}) collective-permute-start(f32[16,256]{1,0:T(8,128)S(1)} %get-tuple-element.12.refs_0_), channel_id=1, source_target_pairs={{0,28},{1,29},{2,30},{3,31},{4,24},{5,25},{6,26},{7,27},{8,20},{9,... | collective-permute-start | bytes 49160 | tf_op jit(solution)/shard_map/ppermute | solution.py:309
  14.8 0.3 %collective-permute-start.5 = (f32[16,256]{1,0:T(8,128)S(1)}, f32[16,256]{1,0:T(8,128)S(1)}, u32[]{:S(2)}, u32[]{:S(2)}) collective-permute-start(f32[16,256]{1,0:T(8,128)S(1)} %get-tuple-element.12.refs_0_), channel_id=1, source_target_pairs={{0,20},{1,21},{2,22},{3,23},{4,16},{5,17},{6,18},{7,19},{8,28},{9,... | collective-permute-start | bytes 49160 | tf_op jit(solution)/shard_map/ppermute | solution.py:309
  15.1 0.5 %collective-permute-start.4 = (f32[16,256]{1,0:T(8,128)S(1)}, f32[16,256]{1,0:T(8,128)S(1)}, u32[]{:S(2)}, u32[]{:S(2)}) collective-permute-start(f32[16,256]{1,0:T(8,128)S(1)} %get-tuple-element.12.refs_0_), channel_id=1, source_target_pairs={{0,12},{1,13},{2,14},{3,15},{4,8},{5,9},{6,10},{7,11},{8,4},{9,5},... | collective-permute-start | bytes 49160 | tf_op jit(solution)/shard_map/ppermute | solution.py:309
  15.6 0.9 %collective-permute-done.6.refs_3_ = f32[16,256]{1,0:T(8,128)S(1)} collective-permute-done((f32[16,256]{1,0:T(8,128)S(1)}, f32[16,256]{1,0:T(8,128)S(1)}, u32[]{:S(2)}, u32[]{:S(2)}) %collective-permute-start.6) | collective-permute-done | bytes 16416 | tf_op jit(solution)/shard_map/ppermute | solution.py:309
  16.5 1.5 %collective-permute-done.5.refs_2_ = f32[16,256]{1,0:T(8,128)S(1)} collective-permute-done((f32[16,256]{1,0:T(8,128)S(1)}, f32[16,256]{1,0:T(8,128)S(1)}, u32[]{:S(2)}, u32[]{:S(2)}) %collective-permute-start.5) | collective-permute-done | bytes 16416 | tf_op jit(solution)/shard_map/ppermute | solution.py:309
  18.0 0.3 %collective-permute-done.4.refs_1_ = f32[16,256]{1,0:T(8,128)S(1)} collective-permute-done((f32[16,256]{1,0:T(8,128)S(1)}, f32[16,256]{1,0:T(8,128)S(1)}, u32[]{:S(2)}, u32[]{:S(2)}) %collective-permute-start.4) | collective-permute-done | bytes 16416 | tf_op jit(solution)/shard_map/ppermute | solution.py:309
  18.3 0.4 %collective-permute-start.7 = (f32[80,256]{1,0:T(8,128)S(1)}, f32[80,256]{1,0:T(8,128)S(1)}, u32[]{:S(2)}, u32[]{:S(2)}) collective-permute-start(f32[80,256]{1,0:T(8,128)S(1)} %stack.1.held), channel_id=1, source_target_pairs={{0,4},{1,5},{2,6},{3,7},{4,0},{5,1},{6,2},{7,3},{8,12},{9,13},{10,... | collective-permute-start | bytes 245768 | tf_op jit(solution)/shard_map/ppermute | solution.py:309
  19.3 0.3 %collective-permute-done.7.sent = f32[80,256]{1,0:T(8,128)S(1)} collective-permute-done((f32[80,256]{1,0:T(8,128)S(1)}, f32[80,256]{1,0:T(8,128)S(1)}, u32[]{:S(2)}, u32[]{:S(2)}) %collective-permute-start.7) | collective-permute-done | bytes 81952 | tf_op jit(solution)/shard_map/ppermute | solution.py:309
  19.5 2.3 %factors.1 = (f32[4,1024]{1,0:T(4,128)}, f32[4,64,64]{2,1,0:T(8,128)}) custom-call(f32[1]{0:T(128)S(6)} %copy.10.damping, f32[80,256]{1,0:T(8,128)S(1)} %stack.1.held, f32[80,256]{1,0:T(8,128)S(1)} %collective-permute-done.7.sent), custom_call_target="tpu_custom_call" | custom-call | tf_op jit(solution)/shard_map/factors/pallas_call | solution.py:410
  (2 shorter events, 0.0 us)
Async XLA Ops:
  3.2 6.3 %collective-permute-start = (f32[32,256]{1,0:T(8,128)S(1)}, f32[32,256]{1,0:T(8,128)S(1)}, u32[]{:S(2)}, u32[]{:S(2)}) collective-permute-start(f32[32,256]{1,0:T(8,128)S(1)} %get-tuple-element.8), channel_id=1, source_target_pairs={{0,7},{1,6},{2,5},{3,4},{4,3},{5,2},{6,1},{7,0},{8,15},{9,14},{10,... | collective-permute-start | bytes 98312 | tf_op jit(solution)/shard_map/ppermute | solution.py:309
  7.8 4.5 %collective-permute-start.1 = (f32[32,256]{1,0:T(8,128)S(1)}, f32[32,256]{1,0:T(8,128)S(1)}, u32[]{:S(2)}, u32[]{:S(2)}) collective-permute-start(f32[32,256]{1,0:T(8,128)S(1)} %get-tuple-element.9), channel_id=1, source_target_pairs={{0,6},{1,7},{2,4},{3,5},{4,2},{5,3},{6,0},{7,1},{8,14},{9,15},{10,... | collective-permute-start | bytes 98312 | tf_op jit(solution)/shard_map/ppermute | solution.py:309
  7.8 4.5 %collective-permute-start.2 = (f32[32,256]{1,0:T(8,128)S(1)}, f32[32,256]{1,0:T(8,128)S(1)}, u32[]{:S(2)}, u32[]{:S(2)}) collective-permute-start(f32[32,256]{1,0:T(8,128)S(1)} %get-tuple-element.10), channel_id=1, source_target_pairs={{0,5},{1,4},{2,7},{3,6},{4,1},{5,0},{6,3},{7,2},{8,13},{9,12},{10,... | collective-permute-start | bytes 98312 | tf_op jit(solution)/shard_map/ppermute | solution.py:309
  8.7 3.6 %collective-permute-start.3 = (f32[32,256]{1,0:T(8,128)S(1)}, f32[32,256]{1,0:T(8,128)S(1)}, u32[]{:S(2)}, u32[]{:S(2)}) collective-permute-start(f32[32,256]{1,0:T(8,128)S(1)} %get-tuple-element.11), channel_id=1, source_target_pairs={{0,4},{1,5},{2,6},{3,7},{4,0},{5,1},{6,2},{7,3},{8,12},{9,13},{10,... | collective-permute-start | bytes 98312 | tf_op jit(solution)/shard_map/ppermute | solution.py:309
  12.3 4.1 %collective-permute-start.6 = (f32[16,256]{1,0:T(8,128)S(1)}, f32[16,256]{1,0:T(8,128)S(1)}, u32[]{:S(2)}, u32[]{:S(2)}) collective-permute-start(f32[16,256]{1,0:T(8,128)S(1)} %get-tuple-element.12.refs_0_), channel_id=1, source_target_pairs={{0,28},{1,29},{2,30},{3,31},{4,24},{5,25},{6,26},{7,27},{8,20},{9,... | collective-permute-start | bytes 49160 | tf_op jit(solution)/shard_map/ppermute | solution.py:309
  14.8 3.2 %collective-permute-start.5 = (f32[16,256]{1,0:T(8,128)S(1)}, f32[16,256]{1,0:T(8,128)S(1)}, u32[]{:S(2)}, u32[]{:S(2)}) collective-permute-start(f32[16,256]{1,0:T(8,128)S(1)} %get-tuple-element.12.refs_0_), channel_id=1, source_target_pairs={{0,20},{1,21},{2,22},{3,23},{4,16},{5,17},{6,18},{7,19},{8,28},{9,... | collective-permute-start | bytes 49160 | tf_op jit(solution)/shard_map/ppermute | solution.py:309
  15.1 3.2 %collective-permute-start.4 = (f32[16,256]{1,0:T(8,128)S(1)}, f32[16,256]{1,0:T(8,128)S(1)}, u32[]{:S(2)}, u32[]{:S(2)}) collective-permute-start(f32[16,256]{1,0:T(8,128)S(1)} %get-tuple-element.12.refs_0_), channel_id=1, source_target_pairs={{0,12},{1,13},{2,14},{3,15},{4,8},{5,9},{6,10},{7,11},{8,4},{9,5},... | collective-permute-start | bytes 49160 | tf_op jit(solution)/shard_map/ppermute | solution.py:309
  18.3 1.3 %collective-permute-start.7 = (f32[80,256]{1,0:T(8,128)S(1)}, f32[80,256]{1,0:T(8,128)S(1)}, u32[]{:S(2)}, u32[]{:S(2)}) collective-permute-start(f32[80,256]{1,0:T(8,128)S(1)} %stack.1.held), channel_id=1, source_target_pairs={{0,4},{1,5},{2,6},{3,7},{4,0},{5,1},{6,2},{7,3},{8,12},{9,13},{10,... | collective-permute-start | bytes 245768 | tf_op jit(solution)/shard_map/ppermute | solution.py:309

commit v12 on v11

--- a/solution.py
+++ b/solution.py
@@ -13,7 +13,7 @@
 SLOT = 32
 GROUP = LANES // SLOT
 PANEL = 8
-CHUNK = 1024
+CHUNK = 512
 
 
 def dot_nt(a, b):
@@ -229,11 +229,20 @@
 
     zero = jnp.zeros((PANEL, LANES), jnp.float32)
     finished = []
+    ahead = [pick_lanes(tile[0][0], slot * SLOT + r) for r in range(PANEL)]
     for q in range(panels):
         hq, at = divmod(q, per_half)
+        if q + 1 < panels:
+            hn, an = divmod(q + 1, per_half)
+            behind = [
+                pick_lanes(tile[q + 1][hn], slot * SLOT + an * PANEL + r)
+                for r in range(PANEL)
+            ]
         column = [
             {
-                j: pick_lanes(tile[j][hq], slot * SLOT + at * PANEL + r)
+                j: ahead[r]
+                if j == q
+                else pick_lanes(tile[j][hq], slot * SLOT + at * PANEL + r)
                 for j in range(q, panels)
             }
             for r in range(PANEL)
@@ -290,6 +299,14 @@
         finished.append(result)
         for j in range(q + 1, panels):
             weights = [column[r][j] * inverse[r] for r in range(PANEL)]
+            if j == q + 1:
+                ahead = behind
+                for r in range(PANEL):
+                    for s in range(PANEL):
+                        factor = jnp.broadcast_to(
+                            column[r][j][s : s + 1, :], (PANEL, LANES)
+                        )
+                        ahead[s] = ahead[s] - weights[r] * factor
             for h in range((q + 1) // per_half, halves):
                 value = tile[j][h]
                 for r in range(PANEL):

time: 22 us -> 22.1 us (level)
    pallas_call x1, Pallas kernels: 2.57 us -> 2.92 us  [local(): pl.pallas_call(functools.partial(partial_kernel, parts, scaling), out_sha...]
    pallas_call x1, Pallas kernels: 2.32 us -> 2.07 us  [local(): pl.pallas_call(functools.partial(factor_kernel, parts), out_shape=[jax.Sh...]
where the time goes in v12:
time: 22.1 us; the launch traced here: 22 us
  starting transfers between devices  9.09 us (41%)
  waiting for transfers between devices  6.56 us (30%)
  Pallas kernels  5.01 us (23%)
  between operations  1.3 us (6%)
    ppermute x8, starting transfers between devices, exchange(): lax.ppermute(x, ('ex', 'mp'), [(m * parts + b, (m ^ ex_distance) * parts...  9.09 us
    ppermute x8, waiting for transfers between devices, exchange(): lax.ppermute(x, ('ex', 'mp'), [(m * parts + b, (m ^ ex_distance) * parts...  6.56 us
    pallas_call x1, Pallas kernels, local(): pl.pallas_call(functools.partial(partial_kernel, parts, scaling), out_sha...  2.92 us
    pallas_call x1, Pallas kernels, local(): pl.pallas_call(functools.partial(factor_kernel, parts), out_shape=[jax.Sh...  2.07 us
  transfers between devices with their start and end apart: 8, of which 6 were waited for; matrix products, arithmetic and copies ran while one was open for 0% of the time, Pallas kernels for 0%

profile of v12, /device:TPU:0, one launch (start us, length us, event | category | flops | bytes accessed | tf_op | source)
XLA Modules:
  0.0 22.0 jit_solution(9325953047650235168)
XLA Ops:
  0.6 2.9 %partials.1 = (f32[32,256]{1,0:T(8,128)S(1)}, f32[32,256]{1,0:T(8,128)S(1)}, f32[32,256]{1,0:T(8,128)S(1)}, f32[32,256]{1,0:T(8,128)S(1)}) custom-call(bf16[1,128,4096]{2,1,0:T(8,128)(2,1)} %acts_hbm.1, bf16[1,128,1024]{2,1,0:T(8,128)(2,1)} %grads_hbm.1, bf16[1,16,4096]{2,1,0:T(8,128)(2,1)} %down_hbm.1, bf16[1,16,1024]{2,1,0:T(8,128)(2,1)} %up_hbm.1, ...), custom_call_target="tpu_custom_call" | custom-call | tf_op jit(solution)/shard_map/partials/pallas_call | solution.py:377
  3.6 4.6 %collective-permute-start = (f32[32,256]{1,0:T(8,128)S(1)}, f32[32,256]{1,0:T(8,128)S(1)}, u32[]{:S(2)}, u32[]{:S(2)}) collective-permute-start(f32[32,256]{1,0:T(8,128)S(1)} %get-tuple-element.8), channel_id=1, source_target_pairs={{0,7},{1,6},{2,5},{3,4},{4,3},{5,2},{6,1},{7,0},{8,15},{9,14},{10,... | collective-permute-start | bytes 98312 | tf_op jit(solution)/shard_map/ppermute | solution.py:326
  8.1 0.0 collective-permute-start.1
  8.1 0.9 %collective-permute-start.2 = (f32[32,256]{1,0:T(8,128)S(1)}, f32[32,256]{1,0:T(8,128)S(1)}, u32[]{:S(2)}, u32[]{:S(2)}) collective-permute-start(f32[32,256]{1,0:T(8,128)S(1)} %get-tuple-element.10), channel_id=1, source_target_pairs={{0,5},{1,4},{2,7},{3,6},{4,1},{5,0},{6,3},{7,2},{8,13},{9,12},{10,... | collective-permute-start | bytes 98312 | tf_op jit(solution)/shard_map/ppermute | solution.py:326
  9.0 0.0 collective-permute-start.3
  9.0 0.8 %collective-permute-done.refs_0_ = f32[32,256]{1,0:T(8,128)S(1)} collective-permute-done((f32[32,256]{1,0:T(8,128)S(1)}, f32[32,256]{1,0:T(8,128)S(1)}, u32[]{:S(2)}, u32[]{:S(2)}) %collective-permute-start) | collective-permute-done | bytes 32800 | tf_op jit(solution)/shard_map/ppermute | solution.py:326
  9.9 2.8 %collective-permute-done.1.refs_1_ = f32[32,256]{1,0:T(8,128)S(1)} collective-permute-done((f32[32,256]{1,0:T(8,128)S(1)}, f32[32,256]{1,0:T(8,128)S(1)}, u32[]{:S(2)}, u32[]{:S(2)}) %collective-permute-start.1) | collective-permute-done | bytes 32800 | tf_op jit(solution)/shard_map/ppermute | solution.py:326
  12.7 0.0 collective-permute-done.2.refs_2_
  12.7 0.0 collective-permute-done.3.refs_3_
  12.7 2.5 %collective-permute-start.6 = (f32[16,256]{1,0:T(8,128)S(1)}, f32[16,256]{1,0:T(8,128)S(1)}, u32[]{:S(2)}, u32[]{:S(2)}) collective-permute-start(f32[16,256]{1,0:T(8,128)S(1)} %get-tuple-element.12.refs_0_), channel_id=1, source_target_pairs={{0,28},{1,29},{2,30},{3,31},{4,24},{5,25},{6,26},{7,27},{8,20},{9,... | collective-permute-start | bytes 49160 | tf_op jit(solution)/shard_map/ppermute | solution.py:326
  15.2 0.3 %collective-permute-start.5 = (f32[16,256]{1,0:T(8,128)S(1)}, f32[16,256]{1,0:T(8,128)S(1)}, u32[]{:S(2)}, u32[]{:S(2)}) collective-permute-start(f32[16,256]{1,0:T(8,128)S(1)} %get-tuple-element.12.refs_0_), channel_id=1, source_target_pairs={{0,20},{1,21},{2,22},{3,23},{4,16},{5,17},{6,18},{7,19},{8,28},{9,... | collective-permute-start | bytes 49160 | tf_op jit(solution)/shard_map/ppermute | solution.py:326
  15.4 0.5 %collective-permute-start.4 = (f32[16,256]{1,0:T(8,128)S(1)}, f32[16,256]{1,0:T(8,128)S(1)}, u32[]{:S(2)}, u32[]{:S(2)}) collective-permute-start(f32[16,256]{1,0:T(8,128)S(1)} %get-tuple-element.12.refs_0_), channel_id=1, source_target_pairs={{0,12},{1,13},{2,14},{3,15},{4,8},{5,9},{6,10},{7,11},{8,4},{9,5},... | collective-permute-start | bytes 49160 | tf_op jit(solution)/shard_map/ppermute | solution.py:326
  15.9 0.9 %collective-permute-done.6.refs_3_ = f32[16,256]{1,0:T(8,128)S(1)} collective-permute-done((f32[16,256]{1,0:T(8,128)S(1)}, f32[16,256]{1,0:T(8,128)S(1)}, u32[]{:S(2)}, u32[]{:S(2)}) %collective-permute-start.6) | collective-permute-done | bytes 16416 | tf_op jit(solution)/shard_map/ppermute | solution.py:326
  16.8 1.5 %collective-permute-done.5.refs_2_ = f32[16,256]{1,0:T(8,128)S(1)} collective-permute-done((f32[16,256]{1,0:T(8,128)S(1)}, f32[16,256]{1,0:T(8,128)S(1)}, u32[]{:S(2)}, u32[]{:S(2)}) %collective-permute-start.5) | collective-permute-done | bytes 16416 | tf_op jit(solution)/shard_map/ppermute | solution.py:326
  18.3 0.3 %collective-permute-done.4.refs_1_ = f32[16,256]{1,0:T(8,128)S(1)} collective-permute-done((f32[16,256]{1,0:T(8,128)S(1)}, f32[16,256]{1,0:T(8,128)S(1)}, u32[]{:S(2)}, u32[]{:S(2)}) %collective-permute-start.4) | collective-permute-done | bytes 16416 | tf_op jit(solution)/shard_map/ppermute | solution.py:326
  18.6 0.4 %collective-permute-start.7 = (f32[80,256]{1,0:T(8,128)S(1)}, f32[80,256]{1,0:T(8,128)S(1)}, u32[]{:S(2)}, u32[]{:S(2)}) collective-permute-start(f32[80,256]{1,0:T(8,128)S(1)} %stack.1.held), channel_id=1, source_target_pairs={{0,4},{1,5},{2,6},{3,7},{4,0},{5,1},{6,2},{7,3},{8,12},{9,13},{10,... | collective-permute-start | bytes 245768 | tf_op jit(solution)/shard_map/ppermute | solution.py:326
  19.6 0.3 %collective-permute-done.7.sent = f32[80,256]{1,0:T(8,128)S(1)} collective-permute-done((f32[80,256]{1,0:T(8,128)S(1)}, f32[80,256]{1,0:T(8,128)S(1)}, u32[]{:S(2)}, u32[]{:S(2)}) %collective-permute-start.7) | collective-permute-done | bytes 81952 | tf_op jit(solution)/shard_map/ppermute | solution.py:326
  19.9 2.1 %factors.1 = (f32[4,1024]{1,0:T(4,128)}, f32[4,64,64]{2,1,0:T(8,128)}) custom-call(f32[1]{0:T(128)S(6)} %copy.10.damping, f32[80,256]{1,0:T(8,128)S(1)} %stack.1.held, f32[80,256]{1,0:T(8,128)S(1)} %collective-permute-done.7.sent), custom_call_target="tpu_custom_call" | custom-call | tf_op jit(solution)/shard_map/factors/pallas_call | solution.py:427
  (2 shorter events, 0.0 us)
Async XLA Ops:
  3.6 6.3 %collective-permute-start = (f32[32,256]{1,0:T(8,128)S(1)}, f32[32,256]{1,0:T(8,128)S(1)}, u32[]{:S(2)}, u32[]{:S(2)}) collective-permute-start(f32[32,256]{1,0:T(8,128)S(1)} %get-tuple-element.8), channel_id=1, source_target_pairs={{0,7},{1,6},{2,5},{3,4},{4,3},{5,2},{6,1},{7,0},{8,15},{9,14},{10,... | collective-permute-start | bytes 98312 | tf_op jit(solution)/shard_map/ppermute | solution.py:326
  8.1 4.5 %collective-permute-start.1 = (f32[32,256]{1,0:T(8,128)S(1)}, f32[32,256]{1,0:T(8,128)S(1)}, u32[]{:S(2)}, u32[]{:S(2)}) collective-permute-start(f32[32,256]{1,0:T(8,128)S(1)} %get-tuple-element.9), channel_id=1, source_target_pairs={{0,6},{1,7},{2,4},{3,5},{4,2},{5,3},{6,0},{7,1},{8,14},{9,15},{10,... | collective-permute-start | bytes 98312 | tf_op jit(solution)/shard_map/ppermute | solution.py:326
  8.1 4.5 %collective-permute-start.2 = (f32[32,256]{1,0:T(8,128)S(1)}, f32[32,256]{1,0:T(8,128)S(1)}, u32[]{:S(2)}, u32[]{:S(2)}) collective-permute-start(f32[32,256]{1,0:T(8,128)S(1)} %get-tuple-element.10), channel_id=1, source_target_pairs={{0,5},{1,4},{2,7},{3,6},{4,1},{5,0},{6,3},{7,2},{8,13},{9,12},{10,... | collective-permute-start | bytes 98312 | tf_op jit(solution)/shard_map/ppermute | solution.py:326
  9.0 3.6 %collective-permute-start.3 = (f32[32,256]{1,0:T(8,128)S(1)}, f32[32,256]{1,0:T(8,128)S(1)}, u32[]{:S(2)}, u32[]{:S(2)}) collective-permute-start(f32[32,256]{1,0:T(8,128)S(1)} %get-tuple-element.11), channel_id=1, source_target_pairs={{0,4},{1,5},{2,6},{3,7},{4,0},{5,1},{6,2},{7,3},{8,12},{9,13},{10,... | collective-permute-start | bytes 98312 | tf_op jit(solution)/shard_map/ppermute | solution.py:326
  12.7 4.1 %collective-permute-start.6 = (f32[16,256]{1,0:T(8,128)S(1)}, f32[16,256]{1,0:T(8,128)S(1)}, u32[]{:S(2)}, u32[]{:S(2)}) collective-permute-start(f32[16,256]{1,0:T(8,128)S(1)} %get-tuple-element.12.refs_0_), channel_id=1, source_target_pairs={{0,28},{1,29},{2,30},{3,31},{4,24},{5,25},{6,26},{7,27},{8,20},{9,... | collective-permute-start | bytes 49160 | tf_op jit(solution)/shard_map/ppermute | solution.py:326
  15.2 3.2 %collective-permute-start.5 = (f32[16,256]{1,0:T(8,128)S(1)}, f32[16,256]{1,0:T(8,128)S(1)}, u32[]{:S(2)}, u32[]{:S(2)}) collective-permute-start(f32[16,256]{1,0:T(8,128)S(1)} %get-tuple-element.12.refs_0_), channel_id=1, source_target_pairs={{0,20},{1,21},{2,22},{3,23},{4,16},{5,17},{6,18},{7,19},{8,28},{9,... | collective-permute-start | bytes 49160 | tf_op jit(solution)/shard_map/ppermute | solution.py:326
  15.4 3.2 %collective-permute-start.4 = (f32[16,256]{1,0:T(8,128)S(1)}, f32[16,256]{1,0:T(8,128)S(1)}, u32[]{:S(2)}, u32[]{:S(2)}) collective-permute-start(f32[16,256]{1,0:T(8,128)S(1)} %get-tuple-element.12.refs_0_), channel_id=1, source_target_pairs={{0,12},{1,13},{2,14},{3,15},{4,8},{5,9},{6,10},{7,11},{8,4},{9,5},... | collective-permute-start | bytes 49160 | tf_op jit(solution)/shard_map/ppermute | solution.py:326
  18.6 1.3 %collective-permute-start.7 = (f32[80,256]{1,0:T(8,128)S(1)}, f32[80,256]{1,0:T(8,128)S(1)}, u32[]{:S(2)}, u32[]{:S(2)}) collective-permute-start(f32[80,256]{1,0:T(8,128)S(1)} %stack.1.held), channel_id=1, source_target_pairs={{0,4},{1,5},{2,6},{3,7},{4,0},{5,1},{6,2},{7,3},{8,12},{9,13},{10,... | collective-permute-start | bytes 245768 | tf_op jit(solution)/shard_map/ppermute | solution.py:326

commit v13 on v12

--- a/solution.py
+++ b/solution.py
@@ -13,7 +13,7 @@
 SLOT = 32
 GROUP = LANES // SLOT
 PANEL = 8
-CHUNK = 512
+CHUNK = 2048
 
 
 def dot_nt(a, b):
@@ -52,32 +52,37 @@
     per = rank // parts
     halves = sketch // SLOT
 
-    def copies(source, target, sem, start, size):
-        return pltpu.make_async_copy(
-            source.at[0, :, pl.ds(start, size)],
-            target.at[:, pl.ds(start, size)],
-            sem,
-        )
-
-    order_copy = pltpu.make_async_copy(order_hbm.at[0], order, order_sem)
-    order_copy.start()
-    sources = [
-        (grads_hbm, grads, proj_out_hbm, up_hbm, weights_out),
-        (acts_hbm, acts, proj_in_hbm, down_hbm, weights_in),
-    ]
+    def copy_in(source, target, sem):
+        copy = pltpu.make_async_copy(source, target, sem)
+        copy.start()
+        return copy
+
+    order_copy = copy_in(order_hbm.at[0], order, order_sem)
     pending = []
-    for data_hbm, data, first_hbm, second_hbm, weights in sources:
+    for n, (data_hbm, data, first_hbm, second_hbm, weights) in enumerate(
+        [
+            (grads_hbm, grads, proj_out_hbm, up_hbm, weights_out),
+            (acts_hbm, acts, proj_in_hbm, down_hbm, weights_in),
+        ]
+    ):
+        first = [
+            copy_in(first_hbm.at[0], weights.at[pl.ds(0, sketch)], sems.at[n, 0]),
+            copy_in(second_hbm.at[0], weights.at[pl.ds(sketch, rank)], sems.at[n, 1]),
+        ]
+        chunks = []
         for start in range(0, data.shape[1], CHUNK):
-            n = len(pending)
-            pending.append(
-                [
-                    copies(first_hbm, weights.at[pl.ds(0, sketch)], sems.at[n, 0], start, CHUNK),
-                    copies(second_hbm, weights.at[pl.ds(sketch, rank)], sems.at[n, 1], start, CHUNK),
-                    copies(data_hbm, data, sems.at[n, 2], start, CHUNK),
-                ]
+            here = pl.ds(start, min(CHUNK, data.shape[1] - start))
+            chunks.append(
+                (
+                    here,
+                    copy_in(
+                        data_hbm.at[0, :, here],
+                        data.at[:, here],
+                        sems.at[n, 2 + len(chunks)],
+                    ),
+                )
             )
-            for copy in pending[-1]:
-                copy.start()
+        pending.append((first, chunks))
 
     order_copy.wait()
     rows = examples * parts
@@ -90,18 +95,19 @@
     place = lax.broadcasted_iota(jnp.int32, (rows, 2 * tokens), 0) // parts
     mask[...] = jnp.where(target == place, scaling, 0.0)
 
-    def product(first, data, weights):
+    def product(n, data, weights):
+        first, chunks = pending[n]
+        for copy in first:
+            copy.wait()
         total = None
-        for n in range(data.shape[1] // CHUNK):
-            for copy in pending[first + n]:
-                copy.wait()
-            here = pl.ds(n * CHUNK, CHUNK)
+        for here, copy in chunks:
+            copy.wait()
             term = dot_nt(weights[:, here], data[:, here])
             total = term if total is None else total + term
         return total
 
     from_grads = product(0, grads, weights_out)
-    from_acts = product(grads.shape[1] // CHUNK, acts, weights_in)
+    from_acts = product(1, acts, weights_in)
     sketches = jnp.concatenate([from_acts[:sketch], from_grads[:sketch]], axis=1)
     low[0] = from_grads[sketch:]
     low[1] = from_acts[sketch:]
@@ -388,7 +394,7 @@
             pltpu.VMEM((2, rank, tokens), jnp.float32),
             pltpu.VMEM((examples * parts, 2 * tokens), jnp.float32),
             pltpu.VMEM((examples * parts, LANES), jnp.float32),
-            pltpu.SemaphoreType.DMA(((width + key_width) // CHUNK, 3)),
+            pltpu.SemaphoreType.DMA((2, 2 + pl.cdiv(max(width, key_width), CHUNK))),
             pltpu.SemaphoreType.DMA,
         ],
         compiler_params=pltpu.CompilerParams(vmem_limit_bytes=8 * 2**20),

time: 22.1 us -> 21.9 us (level)
  Pallas kernels: 5.01 us -> 4.76 us
    pallas_call x1, Pallas kernels: 2.92 us -> 2.67 us  [local(): pl.pallas_call(functools.partial(partial_kernel, parts, scaling), out_sha...]
where the time goes in v13:
time: 21.9 us; the launch traced here: 21.7 us
  starting transfers between devices  9.09 us (42%)
  waiting for transfers between devices  6.56 us (30%)
  Pallas kernels  4.76 us (22%)
  between operations  1.3 us (6%)
    ppermute x8, starting transfers between devices, exchange(): lax.ppermute(x, ('ex', 'mp'), [(m * parts + b, (m ^ ex_distance) * parts...  9.09 us
    ppermute x8, waiting for transfers between devices, exchange(): lax.ppermute(x, ('ex', 'mp'), [(m * parts + b, (m ^ ex_distance) * parts...  6.56 us
    pallas_call x1, Pallas kernels, local(): pl.pallas_call(functools.partial(partial_kernel, parts, scaling), out_sha...  2.67 us
    pallas_call x1, Pallas kernels, local(): pl.pallas_call(functools.partial(factor_kernel, parts), out_shape=[jax.Sh...  2.07 us
  transfers between devices with their start and end apart: 8, of which 6 were waited for; matrix products, arithmetic and copies ran while one was open for 0% of the time, Pallas kernels for 0%

profile of v13, /device:TPU:0, one launch (start us, length us, event | category | flops | bytes accessed | tf_op | source)
XLA Modules:
  0.0 21.7 jit_solution(15166202525831996911)
XLA Ops:
  0.6 2.7 %partials.1 = (f32[32,256]{1,0:T(8,128)S(1)}, f32[32,256]{1,0:T(8,128)S(1)}, f32[32,256]{1,0:T(8,128)S(1)}, f32[32,256]{1,0:T(8,128)S(1)}) custom-call(bf16[1,128,4096]{2,1,0:T(8,128)(2,1)} %acts_hbm.1, bf16[1,128,1024]{2,1,0:T(8,128)(2,1)} %grads_hbm.1, bf16[1,16,4096]{2,1,0:T(8,128)(2,1)} %down_hbm.1, bf16[1,16,1024]{2,1,0:T(8,128)(2,1)} %up_hbm.1, ...), custom_call_target="tpu_custom_call" | custom-call | tf_op jit(solution)/shard_map/partials/pallas_call | solution.py:383
  3.3 4.6 %collective-permute-start = (f32[32,256]{1,0:T(8,128)S(1)}, f32[32,256]{1,0:T(8,128)S(1)}, u32[]{:S(2)}, u32[]{:S(2)}) collective-permute-start(f32[32,256]{1,0:T(8,128)S(1)} %get-tuple-element.8), channel_id=1, source_target_pairs={{0,7},{1,6},{2,5},{3,4},{4,3},{5,2},{6,1},{7,0},{8,15},{9,14},{10,... | collective-permute-start | bytes 98312 | tf_op jit(solution)/shard_map/ppermute | solution.py:332
  7.9 0.0 collective-permute-start.1
  7.9 0.9 %collective-permute-start.2 = (f32[32,256]{1,0:T(8,128)S(1)}, f32[32,256]{1,0:T(8,128)S(1)}, u32[]{:S(2)}, u32[]{:S(2)}) collective-permute-start(f32[32,256]{1,0:T(8,128)S(1)} %get-tuple-element.10), channel_id=1, source_target_pairs={{0,5},{1,4},{2,7},{3,6},{4,1},{5,0},{6,3},{7,2},{8,13},{9,12},{10,... | collective-permute-start | bytes 98312 | tf_op jit(solution)/shard_map/ppermute | solution.py:332
  8.8 0.0 collective-permute-start.3
  8.8 0.9 %collective-permute-done.refs_0_ = f32[32,256]{1,0:T(8,128)S(1)} collective-permute-done((f32[32,256]{1,0:T(8,128)S(1)}, f32[32,256]{1,0:T(8,128)S(1)}, u32[]{:S(2)}, u32[]{:S(2)}) %collective-permute-start) | collective-permute-done | bytes 32800 | tf_op jit(solution)/shard_map/ppermute | solution.py:332
  9.6 2.8 %collective-permute-done.1.refs_1_ = f32[32,256]{1,0:T(8,128)S(1)} collective-permute-done((f32[32,256]{1,0:T(8,128)S(1)}, f32[32,256]{1,0:T(8,128)S(1)}, u32[]{:S(2)}, u32[]{:S(2)}) %collective-permute-start.1) | collective-permute-done | bytes 32800 | tf_op jit(solution)/shard_map/ppermute | solution.py:332
  12.4 0.0 collective-permute-done.2.refs_2_
  12.4 0.0 collective-permute-done.3.refs_3_
  12.4 2.5 %collective-permute-start.6 = (f32[16,256]{1,0:T(8,128)S(1)}, f32[16,256]{1,0:T(8,128)S(1)}, u32[]{:S(2)}, u32[]{:S(2)}) collective-permute-start(f32[16,256]{1,0:T(8,128)S(1)} %get-tuple-element.12.refs_0_), channel_id=1, source_target_pairs={{0,28},{1,29},{2,30},{3,31},{4,24},{5,25},{6,26},{7,27},{8,20},{9,... | collective-permute-start | bytes 49160 | tf_op jit(solution)/shard_map/ppermute | solution.py:332
  14.9 0.3 %collective-permute-start.5 = (f32[16,256]{1,0:T(8,128)S(1)}, f32[16,256]{1,0:T(8,128)S(1)}, u32[]{:S(2)}, u32[]{:S(2)}) collective-permute-start(f32[16,256]{1,0:T(8,128)S(1)} %get-tuple-element.12.refs_0_), channel_id=1, source_target_pairs={{0,20},{1,21},{2,22},{3,23},{4,16},{5,17},{6,18},{7,19},{8,28},{9,... | collective-permute-start | bytes 49160 | tf_op jit(solution)/shard_map/ppermute | solution.py:332
  15.2 0.5 %collective-permute-start.4 = (f32[16,256]{1,0:T(8,128)S(1)}, f32[16,256]{1,0:T(8,128)S(1)}, u32[]{:S(2)}, u32[]{:S(2)}) collective-permute-start(f32[16,256]{1,0:T(8,128)S(1)} %get-tuple-element.12.refs_0_), channel_id=1, source_target_pairs={{0,12},{1,13},{2,14},{3,15},{4,8},{5,9},{6,10},{7,11},{8,4},{9,5},... | collective-permute-start | bytes 49160 | tf_op jit(solution)/shard_map/ppermute | solution.py:332
  15.7 0.9 %collective-permute-done.6.refs_3_ = f32[16,256]{1,0:T(8,128)S(1)} collective-permute-done((f32[16,256]{1,0:T(8,128)S(1)}, f32[16,256]{1,0:T(8,128)S(1)}, u32[]{:S(2)}, u32[]{:S(2)}) %collective-permute-start.6) | collective-permute-done | bytes 16416 | tf_op jit(solution)/shard_map/ppermute | solution.py:332
  16.6 1.5 %collective-permute-done.5.refs_2_ = f32[16,256]{1,0:T(8,128)S(1)} collective-permute-done((f32[16,256]{1,0:T(8,128)S(1)}, f32[16,256]{1,0:T(8,128)S(1)}, u32[]{:S(2)}, u32[]{:S(2)}) %collective-permute-start.5) | collective-permute-done | bytes 16416 | tf_op jit(solution)/shard_map/ppermute | solution.py:332
  18.1 0.3 %collective-permute-done.4.refs_1_ = f32[16,256]{1,0:T(8,128)S(1)} collective-permute-done((f32[16,256]{1,0:T(8,128)S(1)}, f32[16,256]{1,0:T(8,128)S(1)}, u32[]{:S(2)}, u32[]{:S(2)}) %collective-permute-start.4) | collective-permute-done | bytes 16416 | tf_op jit(solution)/shard_map/ppermute | solution.py:332
  18.4 0.4 %collective-permute-start.7 = (f32[80,256]{1,0:T(8,128)S(1)}, f32[80,256]{1,0:T(8,128)S(1)}, u32[]{:S(2)}, u32[]{:S(2)}) collective-permute-start(f32[80,256]{1,0:T(8,128)S(1)} %stack.1.held), channel_id=1, source_target_pairs={{0,4},{1,5},{2,6},{3,7},{4,0},{5,1},{6,2},{7,3},{8,12},{9,13},{10,... | collective-permute-start | bytes 245768 | tf_op jit(solution)/shard_map/ppermute | solution.py:332
  19.4 0.3 %collective-permute-done.7.sent = f32[80,256]{1,0:T(8,128)S(1)} collective-permute-done((f32[80,256]{1,0:T(8,128)S(1)}, f32[80,256]{1,0:T(8,128)S(1)}, u32[]{:S(2)}, u32[]{:S(2)}) %collective-permute-start.7) | collective-permute-done | bytes 81952 | tf_op jit(solution)/shard_map/ppermute | solution.py:332
  19.6 2.1 %factors.1 = (f32[4,1024]{1,0:T(4,128)}, f32[4,64,64]{2,1,0:T(8,128)}) custom-call(f32[1]{0:T(128)S(6)} %copy.10.damping, f32[80,256]{1,0:T(8,128)S(1)} %stack.1.held, f32[80,256]{1,0:T(8,128)S(1)} %collective-permute-done.7.sent), custom_call_target="tpu_custom_call" | custom-call | tf_op jit(solution)/shard_map/factors/pallas_call | solution.py:433
  (2 shorter events, 0.0 us)
Async XLA Ops:
  3.3 6.3 %collective-permute-start = (f32[32,256]{1,0:T(8,128)S(1)}, f32[32,256]{1,0:T(8,128)S(1)}, u32[]{:S(2)}, u32[]{:S(2)}) collective-permute-start(f32[32,256]{1,0:T(8,128)S(1)} %get-tuple-element.8), channel_id=1, source_target_pairs={{0,7},{1,6},{2,5},{3,4},{4,3},{5,2},{6,1},{7,0},{8,15},{9,14},{10,... | collective-permute-start | bytes 98312 | tf_op jit(solution)/shard_map/ppermute | solution.py:332
  7.9 4.5 %collective-permute-start.1 = (f32[32,256]{1,0:T(8,128)S(1)}, f32[32,256]{1,0:T(8,128)S(1)}, u32[]{:S(2)}, u32[]{:S(2)}) collective-permute-start(f32[32,256]{1,0:T(8,128)S(1)} %get-tuple-element.9), channel_id=1, source_target_pairs={{0,6},{1,7},{2,4},{3,5},{4,2},{5,3},{6,0},{7,1},{8,14},{9,15},{10,... | collective-permute-start | bytes 98312 | tf_op jit(solution)/shard_map/ppermute | solution.py:332
  7.9 4.5 %collective-permute-start.2 = (f32[32,256]{1,0:T(8,128)S(1)}, f32[32,256]{1,0:T(8,128)S(1)}, u32[]{:S(2)}, u32[]{:S(2)}) collective-permute-start(f32[32,256]{1,0:T(8,128)S(1)} %get-tuple-element.10), channel_id=1, source_target_pairs={{0,5},{1,4},{2,7},{3,6},{4,1},{5,0},{6,3},{7,2},{8,13},{9,12},{10,... | collective-permute-start | bytes 98312 | tf_op jit(solution)/shard_map/ppermute | solution.py:332
  8.8 3.6 %collective-permute-start.3 = (f32[32,256]{1,0:T(8,128)S(1)}, f32[32,256]{1,0:T(8,128)S(1)}, u32[]{:S(2)}, u32[]{:S(2)}) collective-permute-start(f32[32,256]{1,0:T(8,128)S(1)} %get-tuple-element.11), channel_id=1, source_target_pairs={{0,4},{1,5},{2,6},{3,7},{4,0},{5,1},{6,2},{7,3},{8,12},{9,13},{10,... | collective-permute-start | bytes 98312 | tf_op jit(solution)/shard_map/ppermute | solution.py:332
  12.4 4.1 %collective-permute-start.6 = (f32[16,256]{1,0:T(8,128)S(1)}, f32[16,256]{1,0:T(8,128)S(1)}, u32[]{:S(2)}, u32[]{:S(2)}) collective-permute-start(f32[16,256]{1,0:T(8,128)S(1)} %get-tuple-element.12.refs_0_), channel_id=1, source_target_pairs={{0,28},{1,29},{2,30},{3,31},{4,24},{5,25},{6,26},{7,27},{8,20},{9,... | collective-permute-start | bytes 49160 | tf_op jit(solution)/shard_map/ppermute | solution.py:332
  14.9 3.2 %collective-permute-start.5 = (f32[16,256]{1,0:T(8,128)S(1)}, f32[16,256]{1,0:T(8,128)S(1)}, u32[]{:S(2)}, u32[]{:S(2)}) collective-permute-start(f32[16,256]{1,0:T(8,128)S(1)} %get-tuple-element.12.refs_0_), channel_id=1, source_target_pairs={{0,20},{1,21},{2,22},{3,23},{4,16},{5,17},{6,18},{7,19},{8,28},{9,... | collective-permute-start | bytes 49160 | tf_op jit(solution)/shard_map/ppermute | solution.py:332
  15.2 3.2 %collective-permute-start.4 = (f32[16,256]{1,0:T(8,128)S(1)}, f32[16,256]{1,0:T(8,128)S(1)}, u32[]{:S(2)}, u32[]{:S(2)}) collective-permute-start(f32[16,256]{1,0:T(8,128)S(1)} %get-tuple-element.12.refs_0_), channel_id=1, source_target_pairs={{0,12},{1,13},{2,14},{3,15},{4,8},{5,9},{6,10},{7,11},{8,4},{9,5},... | collective-permute-start | bytes 49160 | tf_op jit(solution)/shard_map/ppermute | solution.py:332
  18.4 1.3 %collective-permute-start.7 = (f32[80,256]{1,0:T(8,128)S(1)}, f32[80,256]{1,0:T(8,128)S(1)}, u32[]{:S(2)}, u32[]{:S(2)}) collective-permute-start(f32[80,256]{1,0:T(8,128)S(1)} %stack.1.held), channel_id=1, source_target_pairs={{0,4},{1,5},{2,6},{3,7},{4,0},{5,1},{6,2},{7,3},{8,12},{9,13},{10,... | collective-permute-start | bytes 245768 | tf_op jit(solution)/shard_map/ppermute | solution.py:332

commit v14 on v13

--- a/solution.py
+++ b/solution.py
@@ -1,4 +1,5 @@
 import functools
+import itertools
 import math
 
 import jax
@@ -13,7 +14,7 @@
 SLOT = 32
 GROUP = LANES // SLOT
 PANEL = 8
-CHUNK = 2048
+CHUNK = 1024
 
 
 def dot_nt(a, b):
@@ -52,9 +53,11 @@
     per = rank // parts
     halves = sketch // SLOT
 
+    queue = itertools.cycle((0, 1))
+
     def copy_in(source, target, sem):
         copy = pltpu.make_async_copy(source, target, sem)
-        copy.start()
+        copy.start(priority=next(queue))
         return copy
 
     order_copy = copy_in(order_hbm.at[0], order, order_sem)

time: 21.9 us -> 22 us (level)
  no operation moved by 1% of the time
where the time goes in v14:
time: 22 us; the launch traced here: 21.9 us
  starting transfers between devices  9.09 us (41%)
  waiting for transfers between devices  6.56 us (30%)
  Pallas kernels  4.93 us (22%)
  between operations  1.3 us (6%)
    ppermute x8, starting transfers between devices, exchange(): lax.ppermute(x, ('ex', 'mp'), [(m * parts + b, (m ^ ex_distance) * parts...  9.09 us
    ppermute x8, waiting for transfers between devices, exchange(): lax.ppermute(x, ('ex', 'mp'), [(m * parts + b, (m ^ ex_distance) * parts...  6.56 us
    pallas_call x1, Pallas kernels, local(): pl.pallas_call(functools.partial(partial_kernel, parts, scaling), out_sha...  2.83 us
    pallas_call x1, Pallas kernels, local(): pl.pallas_call(functools.partial(factor_kernel, parts), out_shape=[jax.Sh...  2.07 us
  transfers between devices with their start and end apart: 8, of which 6 were waited for; matrix products, arithmetic and copies ran while one was open for 0% of the time, Pallas kernels for 0%

profile of v14, /device:TPU:0, one launch (start us, length us, event | category | flops | bytes accessed | tf_op | source)
XLA Modules:
  0.0 21.9 jit_solution(2479782321644826791)
XLA Ops:
  0.6 2.8 %partials.1 = (f32[32,256]{1,0:T(8,128)S(1)}, f32[32,256]{1,0:T(8,128)S(1)}, f32[32,256]{1,0:T(8,128)S(1)}, f32[32,256]{1,0:T(8,128)S(1)}) custom-call(bf16[1,128,4096]{2,1,0:T(8,128)(2,1)} %acts_hbm.1, bf16[1,128,1024]{2,1,0:T(8,128)(2,1)} %grads_hbm.1, bf16[1,16,4096]{2,1,0:T(8,128)(2,1)} %down_hbm.1, bf16[1,16,1024]{2,1,0:T(8,128)(2,1)} %up_hbm.1, ...), custom_call_target="tpu_custom_call" | custom-call | tf_op jit(solution)/shard_map/partials/pallas_call | solution.py:386
  3.5 4.6 %collective-permute-start = (f32[32,256]{1,0:T(8,128)S(1)}, f32[32,256]{1,0:T(8,128)S(1)}, u32[]{:S(2)}, u32[]{:S(2)}) collective-permute-start(f32[32,256]{1,0:T(8,128)S(1)} %get-tuple-element.8), channel_id=1, source_target_pairs={{0,7},{1,6},{2,5},{3,4},{4,3},{5,2},{6,1},{7,0},{8,15},{9,14},{10,... | collective-permute-start | bytes 98312 | tf_op jit(solution)/shard_map/ppermute | solution.py:335
  8.0 0.0 collective-permute-start.1
  8.0 0.9 %collective-permute-start.2 = (f32[32,256]{1,0:T(8,128)S(1)}, f32[32,256]{1,0:T(8,128)S(1)}, u32[]{:S(2)}, u32[]{:S(2)}) collective-permute-start(f32[32,256]{1,0:T(8,128)S(1)} %get-tuple-element.10), channel_id=1, source_target_pairs={{0,5},{1,4},{2,7},{3,6},{4,1},{5,0},{6,3},{7,2},{8,13},{9,12},{10,... | collective-permute-start | bytes 98312 | tf_op jit(solution)/shard_map/ppermute | solution.py:335
  9.0 0.0 collective-permute-start.3
  9.0 0.9 %collective-permute-done.refs_0_ = f32[32,256]{1,0:T(8,128)S(1)} collective-permute-done((f32[32,256]{1,0:T(8,128)S(1)}, f32[32,256]{1,0:T(8,128)S(1)}, u32[]{:S(2)}, u32[]{:S(2)}) %collective-permute-start) | collective-permute-done | bytes 32800 | tf_op jit(solution)/shard_map/ppermute | solution.py:335
  9.8 2.8 %collective-permute-done.1.refs_1_ = f32[32,256]{1,0:T(8,128)S(1)} collective-permute-done((f32[32,256]{1,0:T(8,128)S(1)}, f32[32,256]{1,0:T(8,128)S(1)}, u32[]{:S(2)}, u32[]{:S(2)}) %collective-permute-start.1) | collective-permute-done | bytes 32800 | tf_op jit(solution)/shard_map/ppermute | solution.py:335
  12.6 0.0 collective-permute-done.2.refs_2_
  12.6 0.0 collective-permute-done.3.refs_3_
  12.6 2.5 %collective-permute-start.6 = (f32[16,256]{1,0:T(8,128)S(1)}, f32[16,256]{1,0:T(8,128)S(1)}, u32[]{:S(2)}, u32[]{:S(2)}) collective-permute-start(f32[16,256]{1,0:T(8,128)S(1)} %get-tuple-element.12.refs_0_), channel_id=1, source_target_pairs={{0,28},{1,29},{2,30},{3,31},{4,24},{5,25},{6,26},{7,27},{8,20},{9,... | collective-permute-start | bytes 49160 | tf_op jit(solution)/shard_map/ppermute | solution.py:335
  15.1 0.3 %collective-permute-start.5 = (f32[16,256]{1,0:T(8,128)S(1)}, f32[16,256]{1,0:T(8,128)S(1)}, u32[]{:S(2)}, u32[]{:S(2)}) collective-permute-start(f32[16,256]{1,0:T(8,128)S(1)} %get-tuple-element.12.refs_0_), channel_id=1, source_target_pairs={{0,20},{1,21},{2,22},{3,23},{4,16},{5,17},{6,18},{7,19},{8,28},{9,... | collective-permute-start | bytes 49160 | tf_op jit(solution)/shard_map/ppermute | solution.py:335
  15.3 0.5 %collective-permute-start.4 = (f32[16,256]{1,0:T(8,128)S(1)}, f32[16,256]{1,0:T(8,128)S(1)}, u32[]{:S(2)}, u32[]{:S(2)}) collective-permute-start(f32[16,256]{1,0:T(8,128)S(1)} %get-tuple-element.12.refs_0_), channel_id=1, source_target_pairs={{0,12},{1,13},{2,14},{3,15},{4,8},{5,9},{6,10},{7,11},{8,4},{9,5},... | collective-permute-start | bytes 49160 | tf_op jit(solution)/shard_map/ppermute | solution.py:335
  15.9 0.9 %collective-permute-done.6.refs_3_ = f32[16,256]{1,0:T(8,128)S(1)} collective-permute-done((f32[16,256]{1,0:T(8,128)S(1)}, f32[16,256]{1,0:T(8,128)S(1)}, u32[]{:S(2)}, u32[]{:S(2)}) %collective-permute-start.6) | collective-permute-done | bytes 16416 | tf_op jit(solution)/shard_map/ppermute | solution.py:335
  16.7 1.5 %collective-permute-done.5.refs_2_ = f32[16,256]{1,0:T(8,128)S(1)} collective-permute-done((f32[16,256]{1,0:T(8,128)S(1)}, f32[16,256]{1,0:T(8,128)S(1)}, u32[]{:S(2)}, u32[]{:S(2)}) %collective-permute-start.5) | collective-permute-done | bytes 16416 | tf_op jit(solution)/shard_map/ppermute | solution.py:335
  18.2 0.3 %collective-permute-done.4.refs_1_ = f32[16,256]{1,0:T(8,128)S(1)} collective-permute-done((f32[16,256]{1,0:T(8,128)S(1)}, f32[16,256]{1,0:T(8,128)S(1)}, u32[]{:S(2)}, u32[]{:S(2)}) %collective-permute-start.4) | collective-permute-done | bytes 16416 | tf_op jit(solution)/shard_map/ppermute | solution.py:335
  18.5 0.4 %collective-permute-start.7 = (f32[80,256]{1,0:T(8,128)S(1)}, f32[80,256]{1,0:T(8,128)S(1)}, u32[]{:S(2)}, u32[]{:S(2)}) collective-permute-start(f32[80,256]{1,0:T(8,128)S(1)} %stack.1.held), channel_id=1, source_target_pairs={{0,4},{1,5},{2,6},{3,7},{4,0},{5,1},{6,2},{7,3},{8,12},{9,13},{10,... | collective-permute-start | bytes 245768 | tf_op jit(solution)/shard_map/ppermute | solution.py:335
  19.5 0.3 %collective-permute-done.7.sent = f32[80,256]{1,0:T(8,128)S(1)} collective-permute-done((f32[80,256]{1,0:T(8,128)S(1)}, f32[80,256]{1,0:T(8,128)S(1)}, u32[]{:S(2)}, u32[]{:S(2)}) %collective-permute-start.7) | collective-permute-done | bytes 81952 | tf_op jit(solution)/shard_map/ppermute | solution.py:335
  19.8 2.1 %factors.1 = (f32[4,1024]{1,0:T(4,128)}, f32[4,64,64]{2,1,0:T(8,128)}) custom-call(f32[1]{0:T(128)S(6)} %copy.10.damping, f32[80,256]{1,0:T(8,128)S(1)} %stack.1.held, f32[80,256]{1,0:T(8,128)S(1)} %collective-permute-done.7.sent), custom_call_target="tpu_custom_call" | custom-call | tf_op jit(solution)/shard_map/factors/pallas_call | solution.py:436
  (2 shorter events, 0.0 us)
Async XLA Ops:
  3.5 6.3 %collective-permute-start = (f32[32,256]{1,0:T(8,128)S(1)}, f32[32,256]{1,0:T(8,128)S(1)}, u32[]{:S(2)}, u32[]{:S(2)}) collective-permute-start(f32[32,256]{1,0:T(8,128)S(1)} %get-tuple-element.8), channel_id=1, source_target_pairs={{0,7},{1,6},{2,5},{3,4},{4,3},{5,2},{6,1},{7,0},{8,15},{9,14},{10,... | collective-permute-start | bytes 98312 | tf_op jit(solution)/shard_map/ppermute | solution.py:335
  8.0 4.5 %collective-permute-start.1 = (f32[32,256]{1,0:T(8,128)S(1)}, f32[32,256]{1,0:T(8,128)S(1)}, u32[]{:S(2)}, u32[]{:S(2)}) collective-permute-start(f32[32,256]{1,0:T(8,128)S(1)} %get-tuple-element.9), channel_id=1, source_target_pairs={{0,6},{1,7},{2,4},{3,5},{4,2},{5,3},{6,0},{7,1},{8,14},{9,15},{10,... | collective-permute-start | bytes 98312 | tf_op jit(solution)/shard_map/ppermute | solution.py:335
  8.0 4.5 %collective-permute-start.2 = (f32[32,256]{1,0:T(8,128)S(1)}, f32[32,256]{1,0:T(8,128)S(1)}, u32[]{:S(2)}, u32[]{:S(2)}) collective-permute-start(f32[32,256]{1,0:T(8,128)S(1)} %get-tuple-element.10), channel_id=1, source_target_pairs={{0,5},{1,4},{2,7},{3,6},{4,1},{5,0},{6,3},{7,2},{8,13},{9,12},{10,... | collective-permute-start | bytes 98312 | tf_op jit(solution)/shard_map/ppermute | solution.py:335
  9.0 3.6 %collective-permute-start.3 = (f32[32,256]{1,0:T(8,128)S(1)}, f32[32,256]{1,0:T(8,128)S(1)}, u32[]{:S(2)}, u32[]{:S(2)}) collective-permute-start(f32[32,256]{1,0:T(8,128)S(1)} %get-tuple-element.11), channel_id=1, source_target_pairs={{0,4},{1,5},{2,6},{3,7},{4,0},{5,1},{6,2},{7,3},{8,12},{9,13},{10,... | collective-permute-start | bytes 98312 | tf_op jit(solution)/shard_map/ppermute | solution.py:335
  12.6 4.1 %collective-permute-start.6 = (f32[16,256]{1,0:T(8,128)S(1)}, f32[16,256]{1,0:T(8,128)S(1)}, u32[]{:S(2)}, u32[]{:S(2)}) collective-permute-start(f32[16,256]{1,0:T(8,128)S(1)} %get-tuple-element.12.refs_0_), channel_id=1, source_target_pairs={{0,28},{1,29},{2,30},{3,31},{4,24},{5,25},{6,26},{7,27},{8,20},{9,... | collective-permute-start | bytes 49160 | tf_op jit(solution)/shard_map/ppermute | solution.py:335
  15.1 3.2 %collective-permute-start.5 = (f32[16,256]{1,0:T(8,128)S(1)}, f32[16,256]{1,0:T(8,128)S(1)}, u32[]{:S(2)}, u32[]{:S(2)}) collective-permute-start(f32[16,256]{1,0:T(8,128)S(1)} %get-tuple-element.12.refs_0_), channel_id=1, source_target_pairs={{0,20},{1,21},{2,22},{3,23},{4,16},{5,17},{6,18},{7,19},{8,28},{9,... | collective-permute-start | bytes 49160 | tf_op jit(solution)/shard_map/ppermute | solution.py:335
  15.3 3.2 %collective-permute-start.4 = (f32[16,256]{1,0:T(8,128)S(1)}, f32[16,256]{1,0:T(8,128)S(1)}, u32[]{:S(2)}, u32[]{:S(2)}) collective-permute-start(f32[16,256]{1,0:T(8,128)S(1)} %get-tuple-element.12.refs_0_), channel_id=1, source_target_pairs={{0,12},{1,13},{2,14},{3,15},{4,8},{5,9},{6,10},{7,11},{8,4},{9,5},... | collective-permute-start | bytes 49160 | tf_op jit(solution)/shard_map/ppermute | solution.py:335
  18.5 1.3 %collective-permute-start.7 = (f32[80,256]{1,0:T(8,128)S(1)}, f32[80,256]{1,0:T(8,128)S(1)}, u32[]{:S(2)}, u32[]{:S(2)}) collective-permute-start(f32[80,256]{1,0:T(8,128)S(1)} %stack.1.held), channel_id=1, source_target_pairs={{0,4},{1,5},{2,6},{3,7},{4,0},{5,1},{6,2},{7,3},{8,12},{9,13},{10,... | collective-permute-start | bytes 245768 | tf_op jit(solution)/shard_map/ppermute | solution.py:335

commit v15 on v12

--- a/solution.py
+++ b/solution.py
@@ -13,7 +13,7 @@
 SLOT = 32
 GROUP = LANES // SLOT
 PANEL = 8
-CHUNK = 512
+CHUNK = 1024
 
 
 def dot_nt(a, b):
@@ -96,15 +96,17 @@
             for copy in pending[first + n]:
                 copy.wait()
             here = pl.ds(n * CHUNK, CHUNK)
-            term = dot_nt(weights[:, here], data[:, here])
+            term = dot_nt(data[:, here], weights[:, here])
             total = term if total is None else total + term
         return total
 
     from_grads = product(0, grads, weights_out)
     from_acts = product(grads.shape[1] // CHUNK, acts, weights_in)
-    sketches = jnp.concatenate([from_acts[:sketch], from_grads[:sketch]], axis=1)
-    low[0] = from_grads[sketch:]
-    low[1] = from_acts[sketch:]
+    low[0] = jnp.transpose(from_grads)[sketch:]
+    low[1] = jnp.transpose(from_acts)[sketch:]
+    right_high, right_low = split(
+        jnp.concatenate([from_acts[:, :sketch], from_grads[:, :sketch]], axis=0)
+    )
 
     highs, lows = [], []
     for c in range(per):
@@ -117,19 +119,23 @@
         lows.append(rest)
     left_high = jnp.concatenate(highs, axis=0)
     left_low = jnp.concatenate(lows, axis=0)
-    right = jnp.concatenate(
-        [sketches[h * SLOT : (h + 1) * SLOT] for h in range(halves) for _ in range(per)],
-        axis=0,
-    )
-    right_high, right_low = split(right)
-    both = dot_nt(jnp.concatenate([left_high, left_low], axis=0), right_high)
+    both = jnp.dot(
+        jnp.concatenate([left_high, left_low], axis=0),
+        right_high,
+        preferred_element_type=jnp.float32,
+    )
     size = left_high.shape[0]
-    spread = (dot_nt(left_high, right_low) + both[size:]) + both[:size]
-    column = lax.broadcasted_iota(jnp.int32, (rows, per * sketch), 1)
-    channel = (column // SLOT) % per
-    total = spread[:rows]
-    for c in range(1, per):
-        total = jnp.where(channel == c, spread[c * rows : (c + 1) * rows], total)
+    spread = (
+        jnp.dot(left_high, right_low, preferred_element_type=jnp.float32) + both[size:]
+    ) + both[:size]
+    total = jnp.concatenate(
+        [
+            spread[c * rows : (c + 1) * rows, h * SLOT : (h + 1) * SLOT]
+            for h in range(halves)
+            for c in range(per)
+        ],
+        axis=1,
+    )
     me = lax.axis_index("mp")
     for start in range(0, per * sketch, LANES):
         stop = min(start + LANES, per * sketch)

time: 22.1 us -> 21.9 us (level)
  Pallas kernels: 5.01 us -> 4.75 us
    pallas_call x1, Pallas kernels: 2.92 us -> 2.66 us  [local(): pl.pallas_call(functools.partial(partial_kernel, parts, scaling), out_sha...]
where the time goes in v15:
time: 21.9 us; the launch traced here: 21.7 us
  starting transfers between devices  9.11 us (42%)
  waiting for transfers between devices  6.54 us (30%)
  Pallas kernels  4.75 us (22%)
  between operations  1.3 us (6%)
    ppermute x8, starting transfers between devices, exchange(): lax.ppermute(x, ('ex', 'mp'), [(m * parts + b, (m ^ ex_distance) * parts...  9.11 us
    ppermute x8, waiting for transfers between devices, exchange(): lax.ppermute(x, ('ex', 'mp'), [(m * parts + b, (m ^ ex_distance) * parts...  6.54 us
    pallas_call x1, Pallas kernels, local(): pl.pallas_call(functools.partial(partial_kernel, parts, scaling), out_sha...  2.66 us
    pallas_call x1, Pallas kernels, local(): pl.pallas_call(functools.partial(factor_kernel, parts), out_shape=[jax.Sh...  2.08 us
  transfers between devices with their start and end apart: 8, of which 6 were waited for; matrix products, arithmetic and copies ran while one was open for 0% of the time, Pallas kernels for 0%

profile of v15, /device:TPU:0, one launch (start us, length us, event | category | flops | bytes accessed | tf_op | source)
XLA Modules:
  0.0 21.7 jit_solution(14534140014369213059)
XLA Ops:
  0.6 2.7 %partials.1 = (f32[32,256]{1,0:T(8,128)S(1)}, f32[32,256]{1,0:T(8,128)S(1)}, f32[32,256]{1,0:T(8,128)S(1)}, f32[32,256]{1,0:T(8,128)S(1)}) custom-call(bf16[1,128,4096]{2,1,0:T(8,128)(2,1)} %acts_hbm.1, bf16[1,128,1024]{2,1,0:T(8,128)(2,1)} %grads_hbm.1, bf16[1,16,4096]{2,1,0:T(8,128)(2,1)} %down_hbm.1, bf16[1,16,1024]{2,1,0:T(8,128)(2,1)} %up_hbm.1, ...), custom_call_target="tpu_custom_call" | custom-call | tf_op jit(solution)/shard_map/partials/pallas_call | solution.py:383
  3.3 4.6 %collective-permute-start = (f32[32,256]{1,0:T(8,128)S(1)}, f32[32,256]{1,0:T(8,128)S(1)}, u32[]{:S(2)}, u32[]{:S(2)}) collective-permute-start(f32[32,256]{1,0:T(8,128)S(1)} %get-tuple-element.8), channel_id=1, source_target_pairs={{0,7},{1,6},{2,5},{3,4},{4,3},{5,2},{6,1},{7,0},{8,15},{9,14},{10,... | collective-permute-start | bytes 98312 | tf_op jit(solution)/shard_map/ppermute | solution.py:332
  7.8 0.0 collective-permute-start.1
  7.9 0.9 %collective-permute-start.2 = (f32[32,256]{1,0:T(8,128)S(1)}, f32[32,256]{1,0:T(8,128)S(1)}, u32[]{:S(2)}, u32[]{:S(2)}) collective-permute-start(f32[32,256]{1,0:T(8,128)S(1)} %get-tuple-element.10), channel_id=1, source_target_pairs={{0,5},{1,4},{2,7},{3,6},{4,1},{5,0},{6,3},{7,2},{8,13},{9,12},{10,... | collective-permute-start | bytes 98312 | tf_op jit(solution)/shard_map/ppermute | solution.py:332
  8.8 0.0 collective-permute-start.3
  8.8 0.8 %collective-permute-done.refs_0_ = f32[32,256]{1,0:T(8,128)S(1)} collective-permute-done((f32[32,256]{1,0:T(8,128)S(1)}, f32[32,256]{1,0:T(8,128)S(1)}, u32[]{:S(2)}, u32[]{:S(2)}) %collective-permute-start) | collective-permute-done | bytes 32800 | tf_op jit(solution)/shard_map/ppermute | solution.py:332
  9.6 2.8 %collective-permute-done.1.refs_1_ = f32[32,256]{1,0:T(8,128)S(1)} collective-permute-done((f32[32,256]{1,0:T(8,128)S(1)}, f32[32,256]{1,0:T(8,128)S(1)}, u32[]{:S(2)}, u32[]{:S(2)}) %collective-permute-start.1) | collective-permute-done | bytes 32800 | tf_op jit(solution)/shard_map/ppermute | solution.py:332
  12.4 0.0 collective-permute-done.2.refs_2_
  12.4 0.0 collective-permute-done.3.refs_3_
  12.4 2.5 %collective-permute-start.6 = (f32[16,256]{1,0:T(8,128)S(1)}, f32[16,256]{1,0:T(8,128)S(1)}, u32[]{:S(2)}, u32[]{:S(2)}) collective-permute-start(f32[16,256]{1,0:T(8,128)S(1)} %get-tuple-element.12.refs_0_), channel_id=1, source_target_pairs={{0,28},{1,29},{2,30},{3,31},{4,24},{5,25},{6,26},{7,27},{8,20},{9,... | collective-permute-start | bytes 49160 | tf_op jit(solution)/shard_map/ppermute | solution.py:332
  14.9 0.3 %collective-permute-start.5 = (f32[16,256]{1,0:T(8,128)S(1)}, f32[16,256]{1,0:T(8,128)S(1)}, u32[]{:S(2)}, u32[]{:S(2)}) collective-permute-start(f32[16,256]{1,0:T(8,128)S(1)} %get-tuple-element.12.refs_0_), channel_id=1, source_target_pairs={{0,20},{1,21},{2,22},{3,23},{4,16},{5,17},{6,18},{7,19},{8,28},{9,... | collective-permute-start | bytes 49160 | tf_op jit(solution)/shard_map/ppermute | solution.py:332
  15.2 0.5 %collective-permute-start.4 = (f32[16,256]{1,0:T(8,128)S(1)}, f32[16,256]{1,0:T(8,128)S(1)}, u32[]{:S(2)}, u32[]{:S(2)}) collective-permute-start(f32[16,256]{1,0:T(8,128)S(1)} %get-tuple-element.12.refs_0_), channel_id=1, source_target_pairs={{0,12},{1,13},{2,14},{3,15},{4,8},{5,9},{6,10},{7,11},{8,4},{9,5},... | collective-permute-start | bytes 49160 | tf_op jit(solution)/shard_map/ppermute | solution.py:332
  15.7 0.9 %collective-permute-done.6.refs_3_ = f32[16,256]{1,0:T(8,128)S(1)} collective-permute-done((f32[16,256]{1,0:T(8,128)S(1)}, f32[16,256]{1,0:T(8,128)S(1)}, u32[]{:S(2)}, u32[]{:S(2)}) %collective-permute-start.6) | collective-permute-done | bytes 16416 | tf_op jit(solution)/shard_map/ppermute | solution.py:332
  16.6 1.5 %collective-permute-done.5.refs_2_ = f32[16,256]{1,0:T(8,128)S(1)} collective-permute-done((f32[16,256]{1,0:T(8,128)S(1)}, f32[16,256]{1,0:T(8,128)S(1)}, u32[]{:S(2)}, u32[]{:S(2)}) %collective-permute-start.5) | collective-permute-done | bytes 16416 | tf_op jit(solution)/shard_map/ppermute | solution.py:332
  18.1 0.3 %collective-permute-done.4.refs_1_ = f32[16,256]{1,0:T(8,128)S(1)} collective-permute-done((f32[16,256]{1,0:T(8,128)S(1)}, f32[16,256]{1,0:T(8,128)S(1)}, u32[]{:S(2)}, u32[]{:S(2)}) %collective-permute-start.4) | collective-permute-done | bytes 16416 | tf_op jit(solution)/shard_map/ppermute | solution.py:332
  18.4 0.4 %collective-permute-start.7 = (f32[80,256]{1,0:T(8,128)S(1)}, f32[80,256]{1,0:T(8,128)S(1)}, u32[]{:S(2)}, u32[]{:S(2)}) collective-permute-start(f32[80,256]{1,0:T(8,128)S(1)} %stack.1.held), channel_id=1, source_target_pairs={{0,4},{1,5},{2,6},{3,7},{4,0},{5,1},{6,2},{7,3},{8,12},{9,13},{10,... | collective-permute-start | bytes 245768 | tf_op jit(solution)/shard_map/ppermute | solution.py:332
  19.4 0.3 %collective-permute-done.7.sent = f32[80,256]{1,0:T(8,128)S(1)} collective-permute-done((f32[80,256]{1,0:T(8,128)S(1)}, f32[80,256]{1,0:T(8,128)S(1)}, u32[]{:S(2)}, u32[]{:S(2)}) %collective-permute-start.7) | collective-permute-done | bytes 81952 | tf_op jit(solution)/shard_map/ppermute | solution.py:332
  19.6 2.1 %factors.1 = (f32[4,1024]{1,0:T(4,128)}, f32[4,64,64]{2,1,0:T(8,128)}) custom-call(f32[1]{0:T(128)S(6)} %copy.10.damping, f32[80,256]{1,0:T(8,128)S(1)} %stack.1.held, f32[80,256]{1,0:T(8,128)S(1)} %collective-permute-done.7.sent), custom_call_target="tpu_custom_call" | custom-call | tf_op jit(solution)/shard_map/factors/pallas_call | solution.py:433
  (2 shorter events, 0.0 us)
Async XLA Ops:
  3.3 6.3 %collective-permute-start = (f32[32,256]{1,0:T(8,128)S(1)}, f32[32,256]{1,0:T(8,128)S(1)}, u32[]{:S(2)}, u32[]{:S(2)}) collective-permute-start(f32[32,256]{1,0:T(8,128)S(1)} %get-tuple-element.8), channel_id=1, source_target_pairs={{0,7},{1,6},{2,5},{3,4},{4,3},{5,2},{6,1},{7,0},{8,15},{9,14},{10,... | collective-permute-start | bytes 98312 | tf_op jit(solution)/shard_map/ppermute | solution.py:332
  7.8 4.5 %collective-permute-start.1 = (f32[32,256]{1,0:T(8,128)S(1)}, f32[32,256]{1,0:T(8,128)S(1)}, u32[]{:S(2)}, u32[]{:S(2)}) collective-permute-start(f32[32,256]{1,0:T(8,128)S(1)} %get-tuple-element.9), channel_id=1, source_target_pairs={{0,6},{1,7},{2,4},{3,5},{4,2},{5,3},{6,0},{7,1},{8,14},{9,15},{10,... | collective-permute-start | bytes 98312 | tf_op jit(solution)/shard_map/ppermute | solution.py:332
  7.9 4.5 %collective-permute-start.2 = (f32[32,256]{1,0:T(8,128)S(1)}, f32[32,256]{1,0:T(8,128)S(1)}, u32[]{:S(2)}, u32[]{:S(2)}) collective-permute-start(f32[32,256]{1,0:T(8,128)S(1)} %get-tuple-element.10), channel_id=1, source_target_pairs={{0,5},{1,4},{2,7},{3,6},{4,1},{5,0},{6,3},{7,2},{8,13},{9,12},{10,... | collective-permute-start | bytes 98312 | tf_op jit(solution)/shard_map/ppermute | solution.py:332
  8.8 3.6 %collective-permute-start.3 = (f32[32,256]{1,0:T(8,128)S(1)}, f32[32,256]{1,0:T(8,128)S(1)}, u32[]{:S(2)}, u32[]{:S(2)}) collective-permute-start(f32[32,256]{1,0:T(8,128)S(1)} %get-tuple-element.11), channel_id=1, source_target_pairs={{0,4},{1,5},{2,6},{3,7},{4,0},{5,1},{6,2},{7,3},{8,12},{9,13},{10,... | collective-permute-start | bytes 98312 | tf_op jit(solution)/shard_map/ppermute | solution.py:332
  12.4 4.2 %collective-permute-start.6 = (f32[16,256]{1,0:T(8,128)S(1)}, f32[16,256]{1,0:T(8,128)S(1)}, u32[]{:S(2)}, u32[]{:S(2)}) collective-permute-start(f32[16,256]{1,0:T(8,128)S(1)} %get-tuple-element.12.refs_0_), channel_id=1, source_target_pairs={{0,28},{1,29},{2,30},{3,31},{4,24},{5,25},{6,26},{7,27},{8,20},{9,... | collective-permute-start | bytes 49160 | tf_op jit(solution)/shard_map/ppermute | solution.py:332
  14.9 3.2 %collective-permute-start.5 = (f32[16,256]{1,0:T(8,128)S(1)}, f32[16,256]{1,0:T(8,128)S(1)}, u32[]{:S(2)}, u32[]{:S(2)}) collective-permute-start(f32[16,256]{1,0:T(8,128)S(1)} %get-tuple-element.12.refs_0_), channel_id=1, source_target_pairs={{0,20},{1,21},{2,22},{3,23},{4,16},{5,17},{6,18},{7,19},{8,28},{9,... | collective-permute-start | bytes 49160 | tf_op jit(solution)/shard_map/ppermute | solution.py:332
  15.2 3.2 %collective-permute-start.4 = (f32[16,256]{1,0:T(8,128)S(1)}, f32[16,256]{1,0:T(8,128)S(1)}, u32[]{:S(2)}, u32[]{:S(2)}) collective-permute-start(f32[16,256]{1,0:T(8,128)S(1)} %get-tuple-element.12.refs_0_), channel_id=1, source_target_pairs={{0,12},{1,13},{2,14},{3,15},{4,8},{5,9},{6,10},{7,11},{8,4},{9,5},... | collective-permute-start | bytes 49160 | tf_op jit(solution)/shard_map/ppermute | solution.py:332
  18.4 1.3 %collective-permute-start.7 = (f32[80,256]{1,0:T(8,128)S(1)}, f32[80,256]{1,0:T(8,128)S(1)}, u32[]{:S(2)}, u32[]{:S(2)}) collective-permute-start(f32[80,256]{1,0:T(8,128)S(1)} %stack.1.held), channel_id=1, source_target_pairs={{0,4},{1,5},{2,6},{3,7},{4,0},{5,1},{6,2},{7,3},{8,12},{9,13},{10,... | collective-permute-start | bytes 245768 | tf_op jit(solution)/shard_map/ppermute | solution.py:332

commit v16 on v12

--- a/solution.py
+++ b/solution.py
@@ -13,7 +13,7 @@
 SLOT = 32
 GROUP = LANES // SLOT
 PANEL = 8
-CHUNK = 512
+CHUNK = 1024
 
 
 def dot_nt(a, b):
@@ -81,13 +81,12 @@
 
     order_copy.wait()
     rows = examples * parts
-    lane = lax.broadcasted_iota(jnp.int32, (rows, 2 * tokens), 1)
-    source = (lane % tokens) // EXAMPLE_LENGTH
-    target = jnp.zeros((8, 2 * tokens), jnp.int32)
+    source = lax.broadcasted_iota(jnp.int32, (8, tokens), 1) // EXAMPLE_LENGTH
+    target = jnp.zeros((8, tokens), jnp.int32)
     for s in range(examples):
-        target = jnp.where(source[:8] == s, order[0, s], target)
+        target = jnp.where(source == s, order[0, s], target)
     target = jnp.concatenate([target] * (rows // 8), axis=0)
-    place = lax.broadcasted_iota(jnp.int32, (rows, 2 * tokens), 0) // parts
+    place = lax.broadcasted_iota(jnp.int32, (rows, tokens), 0) // parts
     mask[...] = jnp.where(target == place, scaling, 0.0)
 
     def product(first, data, weights):
@@ -100,28 +99,36 @@
             total = term if total is None else total + term
         return total
 
+    def spread_low(values, n):
+        low[n] = values
+        tiles = []
+        for c in range(per):
+            chosen = low[n, pl.ds(c, parts, stride=per), :]
+            chosen = jnp.concatenate([chosen] * max(1, 8 // parts), axis=0)
+            chosen = jnp.concatenate([chosen] * (rows // chosen.shape[0]), axis=0)
+            tiles.append(split(chosen * mask[...]))
+        return [jnp.concatenate(half, axis=0) for half in zip(*tiles)]
+
+    def spread_sketch(values):
+        return split(
+            jnp.concatenate(
+                [values[h * SLOT : (h + 1) * SLOT] for h in range(halves) for _ in range(per)],
+                axis=0,
+            )
+        )
+
     from_grads = product(0, grads, weights_out)
+    left_grads = spread_low(from_grads[sketch:], 0)
+    right_grads = spread_sketch(from_grads[:sketch])
     from_acts = product(grads.shape[1] // CHUNK, acts, weights_in)
-    sketches = jnp.concatenate([from_acts[:sketch], from_grads[:sketch]], axis=1)
-    low[0] = from_grads[sketch:]
-    low[1] = from_acts[sketch:]
-
-    highs, lows = [], []
-    for c in range(per):
-        chosen = jnp.concatenate(
-            [low[i, pl.ds(c, parts, stride=per), :] for i in range(2)], axis=1
-        )
-        chosen = jnp.concatenate([chosen] * examples, axis=0)
-        high, rest = split(chosen * mask[...])
-        highs.append(high)
-        lows.append(rest)
-    left_high = jnp.concatenate(highs, axis=0)
-    left_low = jnp.concatenate(lows, axis=0)
-    right = jnp.concatenate(
-        [sketches[h * SLOT : (h + 1) * SLOT] for h in range(halves) for _ in range(per)],
-        axis=0,
-    )
-    right_high, right_low = split(right)
+    left_acts = spread_low(from_acts[sketch:], 1)
+    right_acts = spread_sketch(from_acts[:sketch])
+    left_high, left_low = [
+        jnp.concatenate(pair, axis=1) for pair in zip(left_grads, left_acts)
+    ]
+    right_high, right_low = [
+        jnp.concatenate(pair, axis=1) for pair in zip(right_acts, right_grads)
+    ]
     both = dot_nt(jnp.concatenate([left_high, left_low], axis=0), right_high)
     size = left_high.shape[0]
     spread = (dot_nt(left_high, right_low) + both[size:]) + both[:size]
@@ -386,7 +393,7 @@
             pltpu.VMEM((sketch + rank, key_width), grads.dtype),
             pltpu.SMEM(order.shape[1:], order.dtype),
             pltpu.VMEM((2, rank, tokens), jnp.float32),
-            pltpu.VMEM((examples * parts, 2 * tokens), jnp.float32),
+            pltpu.VMEM((examples * parts, tokens), jnp.float32),
             pltpu.VMEM((examples * parts, LANES), jnp.float32),
             pltpu.SemaphoreType.DMA(((width + key_width) // CHUNK, 3)),
             pltpu.SemaphoreType.DMA,

time: 22.1 us -> 21.8 us (0.986)
  Pallas kernels: 5.01 us -> 4.68 us
    pallas_call x1, Pallas kernels: 2.92 us -> 2.59 us  [local(): pl.pallas_call(functools.partial(partial_kernel, parts, scaling), out_sha...]
where the time goes in v16:
time: 21.8 us; the launch traced here: 21.6 us
  starting transfers between devices  9.08 us (42%)
  waiting for transfers between devices  6.56 us (30%)
  Pallas kernels  4.68 us (21%)
  between operations  1.3 us (6%)
    ppermute x8, starting transfers between devices, exchange(): lax.ppermute(x, ('ex', 'mp'), [(m * parts + b, (m ^ ex_distance) * parts...  9.08 us
    ppermute x8, waiting for transfers between devices, exchange(): lax.ppermute(x, ('ex', 'mp'), [(m * parts + b, (m ^ ex_distance) * parts...  6.56 us
    pallas_call x1, Pallas kernels, local(): pl.pallas_call(functools.partial(partial_kernel, parts, scaling), out_sha...  2.59 us
    pallas_call x1, Pallas kernels, local(): pl.pallas_call(functools.partial(factor_kernel, parts), out_shape=[jax.Sh...  2.07 us
  transfers between devices with their start and end apart: 8, of which 6 were waited for; matrix products, arithmetic and copies ran while one was open for 0% of the time, Pallas kernels for 0%

profile of v16, /device:TPU:0, one launch (start us, length us, event | category | flops | bytes accessed | tf_op | source)
XLA Modules:
  0.0 21.6 jit_solution(16471880777455099485)
XLA Ops:
  0.6 2.6 %partials.1 = (f32[32,256]{1,0:T(8,128)S(1)}, f32[32,256]{1,0:T(8,128)S(1)}, f32[32,256]{1,0:T(8,128)S(1)}, f32[32,256]{1,0:T(8,128)S(1)}) custom-call(bf16[1,128,4096]{2,1,0:T(8,128)(2,1)} %acts_hbm.1, bf16[1,128,1024]{2,1,0:T(8,128)(2,1)} %grads_hbm.1, bf16[1,16,4096]{2,1,0:T(8,128)(2,1)} %down_hbm.1, bf16[1,16,1024]{2,1,0:T(8,128)(2,1)} %up_hbm.1, ...), custom_call_target="tpu_custom_call" | custom-call | tf_op jit(solution)/shard_map/partials/pallas_call | solution.py:384
  3.2 4.6 %collective-permute-start = (f32[32,256]{1,0:T(8,128)S(1)}, f32[32,256]{1,0:T(8,128)S(1)}, u32[]{:S(2)}, u32[]{:S(2)}) collective-permute-start(f32[32,256]{1,0:T(8,128)S(1)} %get-tuple-element.8), channel_id=1, source_target_pairs={{0,7},{1,6},{2,5},{3,4},{4,3},{5,2},{6,1},{7,0},{8,15},{9,14},{10,... | collective-permute-start | bytes 98312 | tf_op jit(solution)/shard_map/ppermute | solution.py:333
  7.8 0.0 collective-permute-start.1
  7.8 0.9 %collective-permute-start.2 = (f32[32,256]{1,0:T(8,128)S(1)}, f32[32,256]{1,0:T(8,128)S(1)}, u32[]{:S(2)}, u32[]{:S(2)}) collective-permute-start(f32[32,256]{1,0:T(8,128)S(1)} %get-tuple-element.10), channel_id=1, source_target_pairs={{0,5},{1,4},{2,7},{3,6},{4,1},{5,0},{6,3},{7,2},{8,13},{9,12},{10,... | collective-permute-start | bytes 98312 | tf_op jit(solution)/shard_map/ppermute | solution.py:333
  8.7 0.0 collective-permute-start.3
  8.7 0.9 %collective-permute-done.refs_0_ = f32[32,256]{1,0:T(8,128)S(1)} collective-permute-done((f32[32,256]{1,0:T(8,128)S(1)}, f32[32,256]{1,0:T(8,128)S(1)}, u32[]{:S(2)}, u32[]{:S(2)}) %collective-permute-start) | collective-permute-done | bytes 32800 | tf_op jit(solution)/shard_map/ppermute | solution.py:333
  9.6 2.8 %collective-permute-done.1.refs_1_ = f32[32,256]{1,0:T(8,128)S(1)} collective-permute-done((f32[32,256]{1,0:T(8,128)S(1)}, f32[32,256]{1,0:T(8,128)S(1)}, u32[]{:S(2)}, u32[]{:S(2)}) %collective-permute-start.1) | collective-permute-done | bytes 32800 | tf_op jit(solution)/shard_map/ppermute | solution.py:333
  12.3 0.0 collective-permute-done.2.refs_2_
  12.3 0.0 collective-permute-done.3.refs_3_
  12.3 2.5 %collective-permute-start.6 = (f32[16,256]{1,0:T(8,128)S(1)}, f32[16,256]{1,0:T(8,128)S(1)}, u32[]{:S(2)}, u32[]{:S(2)}) collective-permute-start(f32[16,256]{1,0:T(8,128)S(1)} %get-tuple-element.12.refs_0_), channel_id=1, source_target_pairs={{0,28},{1,29},{2,30},{3,31},{4,24},{5,25},{6,26},{7,27},{8,20},{9,... | collective-permute-start | bytes 49160 | tf_op jit(solution)/shard_map/ppermute | solution.py:333
  14.8 0.3 %collective-permute-start.5 = (f32[16,256]{1,0:T(8,128)S(1)}, f32[16,256]{1,0:T(8,128)S(1)}, u32[]{:S(2)}, u32[]{:S(2)}) collective-permute-start(f32[16,256]{1,0:T(8,128)S(1)} %get-tuple-element.12.refs_0_), channel_id=1, source_target_pairs={{0,20},{1,21},{2,22},{3,23},{4,16},{5,17},{6,18},{7,19},{8,28},{9,... | collective-permute-start | bytes 49160 | tf_op jit(solution)/shard_map/ppermute | solution.py:333
  15.1 0.5 %collective-permute-start.4 = (f32[16,256]{1,0:T(8,128)S(1)}, f32[16,256]{1,0:T(8,128)S(1)}, u32[]{:S(2)}, u32[]{:S(2)}) collective-permute-start(f32[16,256]{1,0:T(8,128)S(1)} %get-tuple-element.12.refs_0_), channel_id=1, source_target_pairs={{0,12},{1,13},{2,14},{3,15},{4,8},{5,9},{6,10},{7,11},{8,4},{9,5},... | collective-permute-start | bytes 49160 | tf_op jit(solution)/shard_map/ppermute | solution.py:333
  15.6 0.9 %collective-permute-done.6.refs_3_ = f32[16,256]{1,0:T(8,128)S(1)} collective-permute-done((f32[16,256]{1,0:T(8,128)S(1)}, f32[16,256]{1,0:T(8,128)S(1)}, u32[]{:S(2)}, u32[]{:S(2)}) %collective-permute-start.6) | collective-permute-done | bytes 16416 | tf_op jit(solution)/shard_map/ppermute | solution.py:333
  16.5 1.5 %collective-permute-done.5.refs_2_ = f32[16,256]{1,0:T(8,128)S(1)} collective-permute-done((f32[16,256]{1,0:T(8,128)S(1)}, f32[16,256]{1,0:T(8,128)S(1)}, u32[]{:S(2)}, u32[]{:S(2)}) %collective-permute-start.5) | collective-permute-done | bytes 16416 | tf_op jit(solution)/shard_map/ppermute | solution.py:333
  18.0 0.3 %collective-permute-done.4.refs_1_ = f32[16,256]{1,0:T(8,128)S(1)} collective-permute-done((f32[16,256]{1,0:T(8,128)S(1)}, f32[16,256]{1,0:T(8,128)S(1)}, u32[]{:S(2)}, u32[]{:S(2)}) %collective-permute-start.4) | collective-permute-done | bytes 16416 | tf_op jit(solution)/shard_map/ppermute | solution.py:333
  18.3 0.4 %collective-permute-start.7 = (f32[80,256]{1,0:T(8,128)S(1)}, f32[80,256]{1,0:T(8,128)S(1)}, u32[]{:S(2)}, u32[]{:S(2)}) collective-permute-start(f32[80,256]{1,0:T(8,128)S(1)} %stack.1.held), channel_id=1, source_target_pairs={{0,4},{1,5},{2,6},{3,7},{4,0},{5,1},{6,2},{7,3},{8,12},{9,13},{10,... | collective-permute-start | bytes 245768 | tf_op jit(solution)/shard_map/ppermute | solution.py:333
  19.3 0.3 %collective-permute-done.7.sent = f32[80,256]{1,0:T(8,128)S(1)} collective-permute-done((f32[80,256]{1,0:T(8,128)S(1)}, f32[80,256]{1,0:T(8,128)S(1)}, u32[]{:S(2)}, u32[]{:S(2)}) %collective-permute-start.7) | collective-permute-done | bytes 81952 | tf_op jit(solution)/shard_map/ppermute | solution.py:333
  19.6 2.1 %factors.1 = (f32[4,1024]{1,0:T(4,128)}, f32[4,64,64]{2,1,0:T(8,128)}) custom-call(f32[1]{0:T(128)S(6)} %copy.10.damping, f32[80,256]{1,0:T(8,128)S(1)} %stack.1.held, f32[80,256]{1,0:T(8,128)S(1)} %collective-permute-done.7.sent), custom_call_target="tpu_custom_call" | custom-call | tf_op jit(solution)/shard_map/factors/pallas_call | solution.py:434
  (2 shorter events, 0.0 us)
Async XLA Ops:
  3.2 6.3 %collective-permute-start = (f32[32,256]{1,0:T(8,128)S(1)}, f32[32,256]{1,0:T(8,128)S(1)}, u32[]{:S(2)}, u32[]{:S(2)}) collective-permute-start(f32[32,256]{1,0:T(8,128)S(1)} %get-tuple-element.8), channel_id=1, source_target_pairs={{0,7},{1,6},{2,5},{3,4},{4,3},{5,2},{6,1},{7,0},{8,15},{9,14},{10,... | collective-permute-start | bytes 98312 | tf_op jit(solution)/shard_map/ppermute | solution.py:333
  7.8 4.5 %collective-permute-start.1 = (f32[32,256]{1,0:T(8,128)S(1)}, f32[32,256]{1,0:T(8,128)S(1)}, u32[]{:S(2)}, u32[]{:S(2)}) collective-permute-start(f32[32,256]{1,0:T(8,128)S(1)} %get-tuple-element.9), channel_id=1, source_target_pairs={{0,6},{1,7},{2,4},{3,5},{4,2},{5,3},{6,0},{7,1},{8,14},{9,15},{10,... | collective-permute-start | bytes 98312 | tf_op jit(solution)/shard_map/ppermute | solution.py:333
  7.8 4.5 %collective-permute-start.2 = (f32[32,256]{1,0:T(8,128)S(1)}, f32[32,256]{1,0:T(8,128)S(1)}, u32[]{:S(2)}, u32[]{:S(2)}) collective-permute-start(f32[32,256]{1,0:T(8,128)S(1)} %get-tuple-element.10), channel_id=1, source_target_pairs={{0,5},{1,4},{2,7},{3,6},{4,1},{5,0},{6,3},{7,2},{8,13},{9,12},{10,... | collective-permute-start | bytes 98312 | tf_op jit(solution)/shard_map/ppermute | solution.py:333
  8.7 3.6 %collective-permute-start.3 = (f32[32,256]{1,0:T(8,128)S(1)}, f32[32,256]{1,0:T(8,128)S(1)}, u32[]{:S(2)}, u32[]{:S(2)}) collective-permute-start(f32[32,256]{1,0:T(8,128)S(1)} %get-tuple-element.11), channel_id=1, source_target_pairs={{0,4},{1,5},{2,6},{3,7},{4,0},{5,1},{6,2},{7,3},{8,12},{9,13},{10,... | collective-permute-start | bytes 98312 | tf_op jit(solution)/shard_map/ppermute | solution.py:333
  12.3 4.1 %collective-permute-start.6 = (f32[16,256]{1,0:T(8,128)S(1)}, f32[16,256]{1,0:T(8,128)S(1)}, u32[]{:S(2)}, u32[]{:S(2)}) collective-permute-start(f32[16,256]{1,0:T(8,128)S(1)} %get-tuple-element.12.refs_0_), channel_id=1, source_target_pairs={{0,28},{1,29},{2,30},{3,31},{4,24},{5,25},{6,26},{7,27},{8,20},{9,... | collective-permute-start | bytes 49160 | tf_op jit(solution)/shard_map/ppermute | solution.py:333
  14.8 3.2 %collective-permute-start.5 = (f32[16,256]{1,0:T(8,128)S(1)}, f32[16,256]{1,0:T(8,128)S(1)}, u32[]{:S(2)}, u32[]{:S(2)}) collective-permute-start(f32[16,256]{1,0:T(8,128)S(1)} %get-tuple-element.12.refs_0_), channel_id=1, source_target_pairs={{0,20},{1,21},{2,22},{3,23},{4,16},{5,17},{6,18},{7,19},{8,28},{9,... | collective-permute-start | bytes 49160 | tf_op jit(solution)/shard_map/ppermute | solution.py:333
  15.1 3.2 %collective-permute-start.4 = (f32[16,256]{1,0:T(8,128)S(1)}, f32[16,256]{1,0:T(8,128)S(1)}, u32[]{:S(2)}, u32[]{:S(2)}) collective-permute-start(f32[16,256]{1,0:T(8,128)S(1)} %get-tuple-element.12.refs_0_), channel_id=1, source_target_pairs={{0,12},{1,13},{2,14},{3,15},{4,8},{5,9},{6,10},{7,11},{8,4},{9,5},... | collective-permute-start | bytes 49160 | tf_op jit(solution)/shard_map/ppermute | solution.py:333
  18.3 1.3 %collective-permute-start.7 = (f32[80,256]{1,0:T(8,128)S(1)}, f32[80,256]{1,0:T(8,128)S(1)}, u32[]{:S(2)}, u32[]{:S(2)}) collective-permute-start(f32[80,256]{1,0:T(8,128)S(1)} %stack.1.held), channel_id=1, source_target_pairs={{0,4},{1,5},{2,6},{3,7},{4,0},{5,1},{6,2},{7,3},{8,12},{9,13},{10,... | collective-permute-start | bytes 245768 | tf_op jit(solution)/shard_map/ppermute | solution.py:333

commit v17 on v13

--- a/solution.py
+++ b/solution.py
@@ -13,7 +13,7 @@
 SLOT = 32
 GROUP = LANES // SLOT
 PANEL = 8
-CHUNK = 2048
+CHUNK = 1024
 
 
 def dot_nt(a, b):
@@ -86,13 +86,12 @@
 
     order_copy.wait()
     rows = examples * parts
-    lane = lax.broadcasted_iota(jnp.int32, (rows, 2 * tokens), 1)
-    source = (lane % tokens) // EXAMPLE_LENGTH
-    target = jnp.zeros((8, 2 * tokens), jnp.int32)
+    source = lax.broadcasted_iota(jnp.int32, (8, tokens), 1) // EXAMPLE_LENGTH
+    target = jnp.zeros((8, tokens), jnp.int32)
     for s in range(examples):
-        target = jnp.where(source[:8] == s, order[0, s], target)
+        target = jnp.where(source == s, order[0, s], target)
     target = jnp.concatenate([target] * (rows // 8), axis=0)
-    place = lax.broadcasted_iota(jnp.int32, (rows, 2 * tokens), 0) // parts
+    place = lax.broadcasted_iota(jnp.int32, (rows, tokens), 0) // parts
     mask[...] = jnp.where(target == place, scaling, 0.0)
 
     def product(n, data, weights):
@@ -106,28 +105,36 @@
             total = term if total is None else total + term
         return total
 
+    def spread_low(values, n):
+        low[n] = values
+        tiles = []
+        for c in range(per):
+            chosen = low[n, pl.ds(c, parts, stride=per), :]
+            chosen = jnp.concatenate([chosen] * max(1, 8 // parts), axis=0)
+            chosen = jnp.concatenate([chosen] * (rows // chosen.shape[0]), axis=0)
+            tiles.append(split(chosen * mask[...]))
+        return [jnp.concatenate(half, axis=0) for half in zip(*tiles)]
+
+    def spread_sketch(values):
+        return split(
+            jnp.concatenate(
+                [values[h * SLOT : (h + 1) * SLOT] for h in range(halves) for _ in range(per)],
+                axis=0,
+            )
+        )
+
     from_grads = product(0, grads, weights_out)
+    left_grads = spread_low(from_grads[sketch:], 0)
+    right_grads = spread_sketch(from_grads[:sketch])
     from_acts = product(1, acts, weights_in)
-    sketches = jnp.concatenate([from_acts[:sketch], from_grads[:sketch]], axis=1)
-    low[0] = from_grads[sketch:]
-    low[1] = from_acts[sketch:]
-
-    highs, lows = [], []
-    for c in range(per):
-        chosen = jnp.concatenate(
-            [low[i, pl.ds(c, parts, stride=per), :] for i in range(2)], axis=1
-        )
-        chosen = jnp.concatenate([chosen] * examples, axis=0)
-        high, rest = split(chosen * mask[...])
-        highs.append(high)
-        lows.append(rest)
-    left_high = jnp.concatenate(highs, axis=0)
-    left_low = jnp.concatenate(lows, axis=0)
-    right = jnp.concatenate(
-        [sketches[h * SLOT : (h + 1) * SLOT] for h in range(halves) for _ in range(per)],
-        axis=0,
-    )
-    right_high, right_low = split(right)
+    left_acts = spread_low(from_acts[sketch:], 1)
+    right_acts = spread_sketch(from_acts[:sketch])
+    left_high, left_low = [
+        jnp.concatenate(pair, axis=1) for pair in zip(left_grads, left_acts)
+    ]
+    right_high, right_low = [
+        jnp.concatenate(pair, axis=1) for pair in zip(right_acts, right_grads)
+    ]
     both = dot_nt(jnp.concatenate([left_high, left_low], axis=0), right_high)
     size = left_high.shape[0]
     spread = (dot_nt(left_high, right_low) + both[size:]) + both[:size]
@@ -191,9 +198,10 @@
     return jnp.take_along_axis(x, index, axis=1)
 
 
-def reciprocal(x):
+def reciprocal(x, scale=None):
     guess = pl.reciprocal(x, approx=True)
-    return guess * (2.0 - x * guess)
+    rest = 2.0 - x * guess
+    return (guess if scale is None else scale * guess) * rest
 
 
 def factor_kernel(parts, damping, held, sent, features, factors):
@@ -273,10 +281,11 @@
         ]
         inverse = []
 
-        def eliminate(r, s, inv):
+        def eliminate(r, s, inv, near=()):
             ratio = block[r][s] * inv
             for t in range(s, PANEL):
-                block[s][t] = block[s][t] - ratio * block[r][t]
+                step = (block[r][s] * block[r][t]) * inv if t in near else ratio * block[r][t]
+                block[s][t] = block[s][t] - step
             for j in range(q + 1, panels):
                 column[s][j] = column[s][j] - ratio * column[r][j]
             for h in range(hq, halves):
@@ -286,11 +295,12 @@
             pivot = block[r][r]
             minor = pivot * block[r + 1][r + 1] - block[r][r + 1] * block[r][r + 1]
             inverse.append(reciprocal(pivot))
-            inverse.append(pivot * reciprocal(minor))
+            inverse.append(reciprocal(minor, pivot))
             eliminate(r, r + 1, inverse[r])
             for s in range(r + 2, PANEL):
-                eliminate(r, s, inverse[r])
-                eliminate(r + 1, s, inverse[r + 1])
+                near = (r + 2, r + 3) if s < r + 4 else ()
+                eliminate(r, s, inverse[r], near)
+                eliminate(r + 1, s, inverse[r + 1], near)
         result = []
         for h in range(halves):
             if h < hq:
@@ -312,7 +322,12 @@
                         factor = jnp.broadcast_to(
                             column[r][j][s : s + 1, :], (PANEL, LANES)
                         )
-                        ahead[s] = ahead[s] - weights[r] * factor
+                        step = (
+                            (column[r][j] * factor) * inverse[r]
+                            if r >= PANEL - 2
+                            else weights[r] * factor
+                        )
+                        ahead[s] = ahead[s] - step
             for h in range((q + 1) // per_half, halves):
                 value = tile[j][h]
                 for r in range(PANEL):
@@ -392,7 +407,7 @@
             pltpu.VMEM((sketch + rank, key_width), grads.dtype),
             pltpu.SMEM(order.shape[1:], order.dtype),
             pltpu.VMEM((2, rank, tokens), jnp.float32),
-            pltpu.VMEM((examples * parts, 2 * tokens), jnp.float32),
+            pltpu.VMEM((examples * parts, tokens), jnp.float32),
             pltpu.VMEM((examples * parts, LANES), jnp.float32),
             pltpu.SemaphoreType.DMA((2, 2 + pl.cdiv(max(width, key_width), CHUNK))),
             pltpu.SemaphoreType.DMA,

time: 21.9 us -> 21.8 us (level)
  no operation moved by 1% of the time
where the time goes in v17:
time: 21.8 us; the launch traced here: 21.7 us
  starting transfers between devices  9.09 us (42%)
  waiting for transfers between devices  6.56 us (30%)
  Pallas kernels  4.69 us (22%)
  between operations  1.3 us (6%)
    ppermute x8, starting transfers between devices, exchange(): lax.ppermute(x, ('ex', 'mp'), [(m * parts + b, (m ^ ex_distance) * parts...  9.09 us
    ppermute x8, waiting for transfers between devices, exchange(): lax.ppermute(x, ('ex', 'mp'), [(m * parts + b, (m ^ ex_distance) * parts...  6.56 us
    pallas_call x1, Pallas kernels, local(): pl.pallas_call(functools.partial(partial_kernel, parts, scaling), out_sha...  2.58 us
    pallas_call x1, Pallas kernels, local(): pl.pallas_call(functools.partial(factor_kernel, parts), out_shape=[jax.Sh...  2.1 us
  transfers between devices with their start and end apart: 8, of which 6 were waited for; matrix products, arithmetic and copies ran while one was open for 0% of the time, Pallas kernels for 0%

profile of v17, /device:TPU:0, one launch (start us, length us, event | category | flops | bytes accessed | tf_op | source)
XLA Modules:
  0.0 21.7 jit_solution(17538344495882016271)
XLA Ops:
  0.6 2.6 %partials.1 = (f32[32,256]{1,0:T(8,128)S(1)}, f32[32,256]{1,0:T(8,128)S(1)}, f32[32,256]{1,0:T(8,128)S(1)}, f32[32,256]{1,0:T(8,128)S(1)}) custom-call(bf16[1,128,4096]{2,1,0:T(8,128)(2,1)} %acts_hbm.1, bf16[1,128,1024]{2,1,0:T(8,128)(2,1)} %grads_hbm.1, bf16[1,16,4096]{2,1,0:T(8,128)(2,1)} %down_hbm.1, bf16[1,16,1024]{2,1,0:T(8,128)(2,1)} %up_hbm.1, ...), custom_call_target="tpu_custom_call" | custom-call | tf_op jit(solution)/shard_map/partials/pallas_call | solution.py:398
  3.2 4.6 %collective-permute-start = (f32[32,256]{1,0:T(8,128)S(1)}, f32[32,256]{1,0:T(8,128)S(1)}, u32[]{:S(2)}, u32[]{:S(2)}) collective-permute-start(f32[32,256]{1,0:T(8,128)S(1)} %get-tuple-element.8), channel_id=1, source_target_pairs={{0,7},{1,6},{2,5},{3,4},{4,3},{5,2},{6,1},{7,0},{8,15},{9,14},{10,... | collective-permute-start | bytes 98312 | tf_op jit(solution)/shard_map/ppermute | solution.py:347
  7.8 0.0 collective-permute-start.1
  7.8 0.9 %collective-permute-start.2 = (f32[32,256]{1,0:T(8,128)S(1)}, f32[32,256]{1,0:T(8,128)S(1)}, u32[]{:S(2)}, u32[]{:S(2)}) collective-permute-start(f32[32,256]{1,0:T(8,128)S(1)} %get-tuple-element.10), channel_id=1, source_target_pairs={{0,5},{1,4},{2,7},{3,6},{4,1},{5,0},{6,3},{7,2},{8,13},{9,12},{10,... | collective-permute-start | bytes 98312 | tf_op jit(solution)/shard_map/ppermute | solution.py:347
  8.7 0.0 collective-permute-start.3
  8.7 0.9 %collective-permute-done.refs_0_ = f32[32,256]{1,0:T(8,128)S(1)} collective-permute-done((f32[32,256]{1,0:T(8,128)S(1)}, f32[32,256]{1,0:T(8,128)S(1)}, u32[]{:S(2)}, u32[]{:S(2)}) %collective-permute-start) | collective-permute-done | bytes 32800 | tf_op jit(solution)/shard_map/ppermute | solution.py:347
  9.6 2.8 %collective-permute-done.1.refs_1_ = f32[32,256]{1,0:T(8,128)S(1)} collective-permute-done((f32[32,256]{1,0:T(8,128)S(1)}, f32[32,256]{1,0:T(8,128)S(1)}, u32[]{:S(2)}, u32[]{:S(2)}) %collective-permute-start.1) | collective-permute-done | bytes 32800 | tf_op jit(solution)/shard_map/ppermute | solution.py:347
  12.3 0.0 collective-permute-done.2.refs_2_
  12.3 0.0 collective-permute-done.3.refs_3_
  12.3 2.5 %collective-permute-start.6 = (f32[16,256]{1,0:T(8,128)S(1)}, f32[16,256]{1,0:T(8,128)S(1)}, u32[]{:S(2)}, u32[]{:S(2)}) collective-permute-start(f32[16,256]{1,0:T(8,128)S(1)} %get-tuple-element.12.refs_0_), channel_id=1, source_target_pairs={{0,28},{1,29},{2,30},{3,31},{4,24},{5,25},{6,26},{7,27},{8,20},{9,... | collective-permute-start | bytes 49160 | tf_op jit(solution)/shard_map/ppermute | solution.py:347
  14.8 0.3 %collective-permute-start.5 = (f32[16,256]{1,0:T(8,128)S(1)}, f32[16,256]{1,0:T(8,128)S(1)}, u32[]{:S(2)}, u32[]{:S(2)}) collective-permute-start(f32[16,256]{1,0:T(8,128)S(1)} %get-tuple-element.12.refs_0_), channel_id=1, source_target_pairs={{0,20},{1,21},{2,22},{3,23},{4,16},{5,17},{6,18},{7,19},{8,28},{9,... | collective-permute-start | bytes 49160 | tf_op jit(solution)/shard_map/ppermute | solution.py:347
  15.1 0.5 %collective-permute-start.4 = (f32[16,256]{1,0:T(8,128)S(1)}, f32[16,256]{1,0:T(8,128)S(1)}, u32[]{:S(2)}, u32[]{:S(2)}) collective-permute-start(f32[16,256]{1,0:T(8,128)S(1)} %get-tuple-element.12.refs_0_), channel_id=1, source_target_pairs={{0,12},{1,13},{2,14},{3,15},{4,8},{5,9},{6,10},{7,11},{8,4},{9,5},... | collective-permute-start | bytes 49160 | tf_op jit(solution)/shard_map/ppermute | solution.py:347
  15.6 0.9 %collective-permute-done.6.refs_3_ = f32[16,256]{1,0:T(8,128)S(1)} collective-permute-done((f32[16,256]{1,0:T(8,128)S(1)}, f32[16,256]{1,0:T(8,128)S(1)}, u32[]{:S(2)}, u32[]{:S(2)}) %collective-permute-start.6) | collective-permute-done | bytes 16416 | tf_op jit(solution)/shard_map/ppermute | solution.py:347
  16.5 1.5 %collective-permute-done.5.refs_2_ = f32[16,256]{1,0:T(8,128)S(1)} collective-permute-done((f32[16,256]{1,0:T(8,128)S(1)}, f32[16,256]{1,0:T(8,128)S(1)}, u32[]{:S(2)}, u32[]{:S(2)}) %collective-permute-start.5) | collective-permute-done | bytes 16416 | tf_op jit(solution)/shard_map/ppermute | solution.py:347
  18.0 0.3 %collective-permute-done.4.refs_1_ = f32[16,256]{1,0:T(8,128)S(1)} collective-permute-done((f32[16,256]{1,0:T(8,128)S(1)}, f32[16,256]{1,0:T(8,128)S(1)}, u32[]{:S(2)}, u32[]{:S(2)}) %collective-permute-start.4) | collective-permute-done | bytes 16416 | tf_op jit(solution)/shard_map/ppermute | solution.py:347
  18.3 0.4 %collective-permute-start.7 = (f32[80,256]{1,0:T(8,128)S(1)}, f32[80,256]{1,0:T(8,128)S(1)}, u32[]{:S(2)}, u32[]{:S(2)}) collective-permute-start(f32[80,256]{1,0:T(8,128)S(1)} %stack.1.held), channel_id=1, source_target_pairs={{0,4},{1,5},{2,6},{3,7},{4,0},{5,1},{6,2},{7,3},{8,12},{9,13},{10,... | collective-permute-start | bytes 245768 | tf_op jit(solution)/shard_map/ppermute | solution.py:347
  19.3 0.3 %collective-permute-done.7.sent = f32[80,256]{1,0:T(8,128)S(1)} collective-permute-done((f32[80,256]{1,0:T(8,128)S(1)}, f32[80,256]{1,0:T(8,128)S(1)}, u32[]{:S(2)}, u32[]{:S(2)}) %collective-permute-start.7) | collective-permute-done | bytes 81952 | tf_op jit(solution)/shard_map/ppermute | solution.py:347
  19.6 2.1 %factors.1 = (f32[4,1024]{1,0:T(4,128)}, f32[4,64,64]{2,1,0:T(8,128)}) custom-call(f32[1]{0:T(128)S(6)} %copy.10.damping, f32[80,256]{1,0:T(8,128)S(1)} %stack.1.held, f32[80,256]{1,0:T(8,128)S(1)} %collective-permute-done.7.sent), custom_call_target="tpu_custom_call" | custom-call | tf_op jit(solution)/shard_map/factors/pallas_call | solution.py:448
  (2 shorter events, 0.0 us)
Async XLA Ops:
  3.2 6.3 %collective-permute-start = (f32[32,256]{1,0:T(8,128)S(1)}, f32[32,256]{1,0:T(8,128)S(1)}, u32[]{:S(2)}, u32[]{:S(2)}) collective-permute-start(f32[32,256]{1,0:T(8,128)S(1)} %get-tuple-element.8), channel_id=1, source_target_pairs={{0,7},{1,6},{2,5},{3,4},{4,3},{5,2},{6,1},{7,0},{8,15},{9,14},{10,... | collective-permute-start | bytes 98312 | tf_op jit(solution)/shard_map/ppermute | solution.py:347
  7.8 4.5 %collective-permute-start.1 = (f32[32,256]{1,0:T(8,128)S(1)}, f32[32,256]{1,0:T(8,128)S(1)}, u32[]{:S(2)}, u32[]{:S(2)}) collective-permute-start(f32[32,256]{1,0:T(8,128)S(1)} %get-tuple-element.9), channel_id=1, source_target_pairs={{0,6},{1,7},{2,4},{3,5},{4,2},{5,3},{6,0},{7,1},{8,14},{9,15},{10,... | collective-permute-start | bytes 98312 | tf_op jit(solution)/shard_map/ppermute | solution.py:347
  7.8 4.5 %collective-permute-start.2 = (f32[32,256]{1,0:T(8,128)S(1)}, f32[32,256]{1,0:T(8,128)S(1)}, u32[]{:S(2)}, u32[]{:S(2)}) collective-permute-start(f32[32,256]{1,0:T(8,128)S(1)} %get-tuple-element.10), channel_id=1, source_target_pairs={{0,5},{1,4},{2,7},{3,6},{4,1},{5,0},{6,3},{7,2},{8,13},{9,12},{10,... | collective-permute-start | bytes 98312 | tf_op jit(solution)/shard_map/ppermute | solution.py:347
  8.7 3.6 %collective-permute-start.3 = (f32[32,256]{1,0:T(8,128)S(1)}, f32[32,256]{1,0:T(8,128)S(1)}, u32[]{:S(2)}, u32[]{:S(2)}) collective-permute-start(f32[32,256]{1,0:T(8,128)S(1)} %get-tuple-element.11), channel_id=1, source_target_pairs={{0,4},{1,5},{2,6},{3,7},{4,0},{5,1},{6,2},{7,3},{8,12},{9,13},{10,... | collective-permute-start | bytes 98312 | tf_op jit(solution)/shard_map/ppermute | solution.py:347
  12.3 4.1 %collective-permute-start.6 = (f32[16,256]{1,0:T(8,128)S(1)}, f32[16,256]{1,0:T(8,128)S(1)}, u32[]{:S(2)}, u32[]{:S(2)}) collective-permute-start(f32[16,256]{1,0:T(8,128)S(1)} %get-tuple-element.12.refs_0_), channel_id=1, source_target_pairs={{0,28},{1,29},{2,30},{3,31},{4,24},{5,25},{6,26},{7,27},{8,20},{9,... | collective-permute-start | bytes 49160 | tf_op jit(solution)/shard_map/ppermute | solution.py:347
  14.8 3.2 %collective-permute-start.5 = (f32[16,256]{1,0:T(8,128)S(1)}, f32[16,256]{1,0:T(8,128)S(1)}, u32[]{:S(2)}, u32[]{:S(2)}) collective-permute-start(f32[16,256]{1,0:T(8,128)S(1)} %get-tuple-element.12.refs_0_), channel_id=1, source_target_pairs={{0,20},{1,21},{2,22},{3,23},{4,16},{5,17},{6,18},{7,19},{8,28},{9,... | collective-permute-start | bytes 49160 | tf_op jit(solution)/shard_map/ppermute | solution.py:347
  15.1 3.2 %collective-permute-start.4 = (f32[16,256]{1,0:T(8,128)S(1)}, f32[16,256]{1,0:T(8,128)S(1)}, u32[]{:S(2)}, u32[]{:S(2)}) collective-permute-start(f32[16,256]{1,0:T(8,128)S(1)} %get-tuple-element.12.refs_0_), channel_id=1, source_target_pairs={{0,12},{1,13},{2,14},{3,15},{4,8},{5,9},{6,10},{7,11},{8,4},{9,5},... | collective-permute-start | bytes 49160 | tf_op jit(solution)/shard_map/ppermute | solution.py:347
  18.3 1.3 %collective-permute-start.7 = (f32[80,256]{1,0:T(8,128)S(1)}, f32[80,256]{1,0:T(8,128)S(1)}, u32[]{:S(2)}, u32[]{:S(2)}) collective-permute-start(f32[80,256]{1,0:T(8,128)S(1)} %stack.1.held), channel_id=1, source_target_pairs={{0,4},{1,5},{2,6},{3,7},{4,0},{5,1},{6,2},{7,3},{8,12},{9,13},{10,... | collective-permute-start | bytes 245768 | tf_op jit(solution)/shard_map/ppermute | solution.py:347

commit v18 on v17

--- a/solution.py
+++ b/solution.py
@@ -44,7 +44,7 @@
     *refs,
 ):
     sends, refs = refs[:parts], refs[parts:]
-    acts, grads, weights_in, weights_out, order, low, mask, out, sems, order_sem = refs
+    acts, grads, weights_in, weights_out, order, sketches, out, line, sems, order_sem = refs
     tokens, width = acts.shape
     rank = down_hbm.shape[1]
     sketch = proj_in_hbm.shape[1]
@@ -61,13 +61,19 @@
     pending = []
     for n, (data_hbm, data, first_hbm, second_hbm, weights) in enumerate(
         [
-            (grads_hbm, grads, proj_out_hbm, up_hbm, weights_out),
+            (grads_hbm, grads, up_hbm, proj_out_hbm, weights_out),
             (acts_hbm, acts, proj_in_hbm, down_hbm, weights_in),
         ]
     ):
         first = [
-            copy_in(first_hbm.at[0], weights.at[pl.ds(0, sketch)], sems.at[n, 0]),
-            copy_in(second_hbm.at[0], weights.at[pl.ds(sketch, rank)], sems.at[n, 1]),
+            copy_in(
+                first_hbm.at[0], weights.at[pl.ds(0, first_hbm.shape[1])], sems.at[n, 0]
+            ),
+            copy_in(
+                second_hbm.at[0],
+                weights.at[pl.ds(sketch, second_hbm.shape[1])],
+                sems.at[n, 1],
+            ),
         ]
         chunks = []
         for start in range(0, data.shape[1], CHUNK):
@@ -83,16 +89,9 @@
                 )
             )
         pending.append((first, chunks))
-
-    order_copy.wait()
-    rows = examples * parts
-    source = lax.broadcasted_iota(jnp.int32, (8, tokens), 1) // EXAMPLE_LENGTH
-    target = jnp.zeros((8, tokens), jnp.int32)
-    for s in range(examples):
-        target = jnp.where(source == s, order[0, s], target)
-    target = jnp.concatenate([target] * (rows // 8), axis=0)
-    place = lax.broadcasted_iota(jnp.int32, (rows, tokens), 0) // parts
-    mask[...] = jnp.where(target == place, scaling, 0.0)
+    for weights, rows in ((weights_in, sketch + rank), (weights_out, rank)):
+        stop = LANES if rows > sketch else sketch
+        weights[rows:stop, :] = jnp.zeros((stop - rows, weights.shape[1]), weights.dtype)
 
     def product(n, data, weights):
         first, chunks = pending[n]
@@ -101,60 +100,56 @@
         total = None
         for here, copy in chunks:
             copy.wait()
-            term = dot_nt(weights[:, here], data[:, here])
+            term = dot_nt(data[:, here], weights[:, here])
             total = term if total is None else total + term
         return total
 
-    def spread_low(values, n):
-        low[n] = values
-        tiles = []
-        for c in range(per):
-            chosen = low[n, pl.ds(c, parts, stride=per), :]
-            chosen = jnp.concatenate([chosen] * max(1, 8 // parts), axis=0)
-            chosen = jnp.concatenate([chosen] * (rows // chosen.shape[0]), axis=0)
-            tiles.append(split(chosen * mask[...]))
-        return [jnp.concatenate(half, axis=0) for half in zip(*tiles)]
-
-    def spread_sketch(values):
-        return split(
-            jnp.concatenate(
-                [values[h * SLOT : (h + 1) * SLOT] for h in range(halves) for _ in range(per)],
-                axis=0,
-            )
-        )
-
     from_grads = product(0, grads, weights_out)
-    left_grads = spread_low(from_grads[sketch:], 0)
-    right_grads = spread_sketch(from_grads[:sketch])
     from_acts = product(1, acts, weights_in)
-    left_acts = spread_low(from_acts[sketch:], 1)
-    right_acts = spread_sketch(from_acts[:sketch])
-    left_high, left_low = [
-        jnp.concatenate(pair, axis=1) for pair in zip(left_grads, left_acts)
+    lane = lax.broadcasted_iota(jnp.int32, (tokens, LANES), 1)
+    sketches[...] = jnp.where(lane < sketch, from_acts, from_grads)
+    lows = jnp.transpose(jnp.where(lane < sketch, from_grads, from_acts)) * scaling
+    low_out, low_in = lows[:rank], lows[sketch : sketch + rank]
+    first = lax.broadcasted_iota(jnp.int32, (rank, LANES), 1) < sketch
+    low = [
+        jnp.where(first, low_out, pltpu.roll(low_in, sketch, 1)),
+        jnp.where(first, pltpu.roll(low_out, sketch, 1), low_in),
     ]
-    right_high, right_low = [
-        jnp.concatenate(pair, axis=1) for pair in zip(right_acts, right_grads)
+    half = lax.broadcasted_iota(jnp.int32, (8, LANES), 1) // sketch * sketch
+    order_copy.wait()
+    for s in range(examples):
+        sums = [None] * (rank // 8)
+        for t in range(s * EXAMPLE_LENGTH, (s + 1) * EXAMPLE_LENGTH):
+            row = jnp.broadcast_to(sketches[t : t + 1, :], (8, LANES))
+            for c in range(rank // 8):
+                part = low[t // sketch][c * 8 : (c + 1) * 8]
+                term = pick_lanes(part, half + t % sketch) * row
+                sums[c] = term if sums[c] is None else sums[c] + term
+        for c, value in enumerate(sums):
+            start = pl.multiple_of(order[0, s] * rank + c * 8, 8)
+            out[pl.ds(start, 8), :] = value + pltpu.roll(value, sketch, 1)
+
+    rows = examples * parts
+    slot = lax.broadcasted_iota(jnp.int32, (rows, LANES), 1) // SLOT
+    me = lax.axis_index("mp")
+    picked = [
+        out[pl.ds(c, rows, stride=per), :] if per > 1 else out[...] for c in range(per)
     ]
-    both = dot_nt(jnp.concatenate([left_high, left_low], axis=0), right_high)
-    size = left_high.shape[0]
-    spread = (dot_nt(left_high, right_low) + both[size:]) + both[:size]
-    column = lax.broadcasted_iota(jnp.int32, (rows, per * sketch), 1)
-    channel = (column // SLOT) % per
-    total = spread[:rows]
-    for c in range(1, per):
-        total = jnp.where(channel == c, spread[c * rows : (c + 1) * rows], total)
-    me = lax.axis_index("mp")
-    for start in range(0, per * sketch, LANES):
-        stop = min(start + LANES, per * sketch)
-        out[:, : stop - start] = total[:, start:stop]
+    for h in range(halves):
+        total = None
+        for c, value in enumerate(picked):
+            if (c - h) * SLOT % sketch:
+                value = pltpu.roll(value, SLOT, 1)
+            total = value if c == 0 else jnp.where(slot == c, value, total)
+        span = per * SLOT
+        here = pl.ds(h * span, span)
+        line[...] = total
         for d in range(parts):
             g = me ^ d
-            sends[d][:examples, start:stop] = out[
-                pl.ds(pl.multiple_of(g * examples, examples), examples), : stop - start
-            ]
-            sends[d][examples:, start:stop] = out[pl.ds(g, examples, stride=parts), :][
-                :, : stop - start
-            ]
+            by_row = line[pl.ds(pl.multiple_of(g * examples, examples), examples), :]
+            by_column = line[pl.ds(g, examples, stride=parts), :]
+            sends[d][:examples, here] = by_row[:, :span]
+            sends[d][examples:, here] = by_column[:, :span]
 
 
 def sum_kernel(*refs):
@@ -403,11 +398,11 @@
         scratch_shapes=[
             pltpu.VMEM((tokens, width), acts.dtype),
             pltpu.VMEM((tokens, key_width), grads.dtype),
-            pltpu.VMEM((sketch + rank, width), acts.dtype),
-            pltpu.VMEM((sketch + rank, key_width), grads.dtype),
+            pltpu.VMEM((LANES, width), acts.dtype),
+            pltpu.VMEM((LANES, key_width), grads.dtype),
             pltpu.SMEM(order.shape[1:], order.dtype),
-            pltpu.VMEM((2, rank, tokens), jnp.float32),
-            pltpu.VMEM((examples * parts, tokens), jnp.float32),
+            pltpu.VMEM((tokens, LANES), jnp.float32),
+            pltpu.VMEM((examples * rank, LANES), jnp.float32),
             pltpu.VMEM((examples * parts, LANES), jnp.float32),
             pltpu.SemaphoreType.DMA((2, 2 + pl.cdiv(max(width, key_width), CHUNK))),
             pltpu.SemaphoreType.DMA,

time: 21.8 us -> 23.3 us (1.069)
  Pallas kernels: 4.69 us -> 6.18 us
    pallas_call x1, Pallas kernels: 2.58 us -> 4.07 us  [local(): pl.pallas_call(functools.partial(partial_kernel, parts, scaling), out_sha...]
where the time goes in v18:
time: 23.3 us; the launch traced here: 23.1 us
  starting transfers between devices  9.08 us (39%)
  waiting for transfers between devices  6.58 us (28%)
  Pallas kernels  6.18 us (27%)
  between operations  1.3 us (6%)
    ppermute x8, starting transfers between devices, exchange(): lax.ppermute(x, ('ex', 'mp'), [(m * parts + b, (m ^ ex_distance) * parts...  9.08 us
    ppermute x8, waiting for transfers between devices, exchange(): lax.ppermute(x, ('ex', 'mp'), [(m * parts + b, (m ^ ex_distance) * parts...  6.58 us
    pallas_call x1, Pallas kernels, local(): pl.pallas_call(functools.partial(partial_kernel, parts, scaling), out_sha...  4.07 us
    pallas_call x1, Pallas kernels, local(): pl.pallas_call(functools.partial(factor_kernel, parts), out_shape=[jax.Sh...  2.1 us
  transfers between devices with their start and end apart: 8, of which 6 were waited for; matrix products, arithmetic and copies ran while one was open for 0% of the time, Pallas kernels for 0%

profile of v18, /device:TPU:0, one launch (start us, length us, event | category | flops | bytes accessed | tf_op | source)
XLA Modules:
  0.0 23.1 jit_solution(11415795573556717717)
XLA Ops:
  0.6 4.1 %partials.1 = (f32[32,256]{1,0:T(8,128)S(1)}, f32[32,256]{1,0:T(8,128)S(1)}, f32[32,256]{1,0:T(8,128)S(1)}, f32[32,256]{1,0:T(8,128)S(1)}) custom-call(bf16[1,128,4096]{2,1,0:T(8,128)(2,1)} %acts_hbm.1, bf16[1,128,1024]{2,1,0:T(8,128)(2,1)} %grads_hbm.1, bf16[1,16,4096]{2,1,0:T(8,128)(2,1)} %down_hbm.1, bf16[1,16,1024]{2,1,0:T(8,128)(2,1)} %up_hbm.1, ...), custom_call_target="tpu_custom_call" | custom-call | tf_op jit(solution)/shard_map/partials/pallas_call | solution.py:393
  4.7 4.6 %collective-permute-start = (f32[32,256]{1,0:T(8,128)S(1)}, f32[32,256]{1,0:T(8,128)S(1)}, u32[]{:S(2)}, u32[]{:S(2)}) collective-permute-start(f32[32,256]{1,0:T(8,128)S(1)} %get-tuple-element.8), channel_id=1, source_target_pairs={{0,7},{1,6},{2,5},{3,4},{4,3},{5,2},{6,1},{7,0},{8,15},{9,14},{10,... | collective-permute-start | bytes 98312 | tf_op jit(solution)/shard_map/ppermute | solution.py:342
  9.3 0.0 collective-permute-start.1
  9.3 0.9 %collective-permute-start.2 = (f32[32,256]{1,0:T(8,128)S(1)}, f32[32,256]{1,0:T(8,128)S(1)}, u32[]{:S(2)}, u32[]{:S(2)}) collective-permute-start(f32[32,256]{1,0:T(8,128)S(1)} %get-tuple-element.10), channel_id=1, source_target_pairs={{0,5},{1,4},{2,7},{3,6},{4,1},{5,0},{6,3},{7,2},{8,13},{9,12},{10,... | collective-permute-start | bytes 98312 | tf_op jit(solution)/shard_map/ppermute | solution.py:342
  10.2 0.0 collective-permute-start.3
  10.2 0.9 %collective-permute-done.refs_0_ = f32[32,256]{1,0:T(8,128)S(1)} collective-permute-done((f32[32,256]{1,0:T(8,128)S(1)}, f32[32,256]{1,0:T(8,128)S(1)}, u32[]{:S(2)}, u32[]{:S(2)}) %collective-permute-start) | collective-permute-done | bytes 32800 | tf_op jit(solution)/shard_map/ppermute | solution.py:342
  11.0 2.8 %collective-permute-done.1.refs_1_ = f32[32,256]{1,0:T(8,128)S(1)} collective-permute-done((f32[32,256]{1,0:T(8,128)S(1)}, f32[32,256]{1,0:T(8,128)S(1)}, u32[]{:S(2)}, u32[]{:S(2)}) %collective-permute-start.1) | collective-permute-done | bytes 32800 | tf_op jit(solution)/shard_map/ppermute | solution.py:342
  13.8 0.0 collective-permute-done.2.refs_2_
  13.8 0.0 collective-permute-done.3.refs_3_
  13.8 2.5 %collective-permute-start.6 = (f32[16,256]{1,0:T(8,128)S(1)}, f32[16,256]{1,0:T(8,128)S(1)}, u32[]{:S(2)}, u32[]{:S(2)}) collective-permute-start(f32[16,256]{1,0:T(8,128)S(1)} %get-tuple-element.12.refs_0_), channel_id=1, source_target_pairs={{0,28},{1,29},{2,30},{3,31},{4,24},{5,25},{6,26},{7,27},{8,20},{9,... | collective-permute-start | bytes 49160 | tf_op jit(solution)/shard_map/ppermute | solution.py:342
  16.3 0.3 %collective-permute-start.5 = (f32[16,256]{1,0:T(8,128)S(1)}, f32[16,256]{1,0:T(8,128)S(1)}, u32[]{:S(2)}, u32[]{:S(2)}) collective-permute-start(f32[16,256]{1,0:T(8,128)S(1)} %get-tuple-element.12.refs_0_), channel_id=1, source_target_pairs={{0,20},{1,21},{2,22},{3,23},{4,16},{5,17},{6,18},{7,19},{8,28},{9,... | collective-permute-start | bytes 49160 | tf_op jit(solution)/shard_map/ppermute | solution.py:342
  16.6 0.5 %collective-permute-start.4 = (f32[16,256]{1,0:T(8,128)S(1)}, f32[16,256]{1,0:T(8,128)S(1)}, u32[]{:S(2)}, u32[]{:S(2)}) collective-permute-start(f32[16,256]{1,0:T(8,128)S(1)} %get-tuple-element.12.refs_0_), channel_id=1, source_target_pairs={{0,12},{1,13},{2,14},{3,15},{4,8},{5,9},{6,10},{7,11},{8,4},{9,5},... | collective-permute-start | bytes 49160 | tf_op jit(solution)/shard_map/ppermute | solution.py:342
  17.1 0.9 %collective-permute-done.6.refs_3_ = f32[16,256]{1,0:T(8,128)S(1)} collective-permute-done((f32[16,256]{1,0:T(8,128)S(1)}, f32[16,256]{1,0:T(8,128)S(1)}, u32[]{:S(2)}, u32[]{:S(2)}) %collective-permute-start.6) | collective-permute-done | bytes 16416 | tf_op jit(solution)/shard_map/ppermute | solution.py:342
  18.0 1.5 %collective-permute-done.5.refs_2_ = f32[16,256]{1,0:T(8,128)S(1)} collective-permute-done((f32[16,256]{1,0:T(8,128)S(1)}, f32[16,256]{1,0:T(8,128)S(1)}, u32[]{:S(2)}, u32[]{:S(2)}) %collective-permute-start.5) | collective-permute-done | bytes 16416 | tf_op jit(solution)/shard_map/ppermute | solution.py:342
  19.5 0.3 %collective-permute-done.4.refs_1_ = f32[16,256]{1,0:T(8,128)S(1)} collective-permute-done((f32[16,256]{1,0:T(8,128)S(1)}, f32[16,256]{1,0:T(8,128)S(1)}, u32[]{:S(2)}, u32[]{:S(2)}) %collective-permute-start.4) | collective-permute-done | bytes 16416 | tf_op jit(solution)/shard_map/ppermute | solution.py:342
  19.8 0.3 %collective-permute-start.7 = (f32[80,256]{1,0:T(8,128)S(1)}, f32[80,256]{1,0:T(8,128)S(1)}, u32[]{:S(2)}, u32[]{:S(2)}) collective-permute-start(f32[80,256]{1,0:T(8,128)S(1)} %stack.1.held), channel_id=1, source_target_pairs={{0,4},{1,5},{2,6},{3,7},{4,0},{5,1},{6,2},{7,3},{8,12},{9,13},{10,... | collective-permute-start | bytes 245768 | tf_op jit(solution)/shard_map/ppermute | solution.py:342
  20.8 0.3 %collective-permute-done.7.sent = f32[80,256]{1,0:T(8,128)S(1)} collective-permute-done((f32[80,256]{1,0:T(8,128)S(1)}, f32[80,256]{1,0:T(8,128)S(1)}, u32[]{:S(2)}, u32[]{:S(2)}) %collective-permute-start.7) | collective-permute-done | bytes 81952 | tf_op jit(solution)/shard_map/ppermute | solution.py:342
  21.0 2.1 %factors.1 = (f32[4,1024]{1,0:T(4,128)}, f32[4,64,64]{2,1,0:T(8,128)}) custom-call(f32[1]{0:T(128)S(6)} %copy.10.damping, f32[80,256]{1,0:T(8,128)S(1)} %stack.1.held, f32[80,256]{1,0:T(8,128)S(1)} %collective-permute-done.7.sent), custom_call_target="tpu_custom_call" | custom-call | tf_op jit(solution)/shard_map/factors/pallas_call | solution.py:443
  (2 shorter events, 0.0 us)
Async XLA Ops:
  4.7 6.3 %collective-permute-start = (f32[32,256]{1,0:T(8,128)S(1)}, f32[32,256]{1,0:T(8,128)S(1)}, u32[]{:S(2)}, u32[]{:S(2)}) collective-permute-start(f32[32,256]{1,0:T(8,128)S(1)} %get-tuple-element.8), channel_id=1, source_target_pairs={{0,7},{1,6},{2,5},{3,4},{4,3},{5,2},{6,1},{7,0},{8,15},{9,14},{10,... | collective-permute-start | bytes 98312 | tf_op jit(solution)/shard_map/ppermute | solution.py:342
  9.3 4.5 %collective-permute-start.1 = (f32[32,256]{1,0:T(8,128)S(1)}, f32[32,256]{1,0:T(8,128)S(1)}, u32[]{:S(2)}, u32[]{:S(2)}) collective-permute-start(f32[32,256]{1,0:T(8,128)S(1)} %get-tuple-element.9), channel_id=1, source_target_pairs={{0,6},{1,7},{2,4},{3,5},{4,2},{5,3},{6,0},{7,1},{8,14},{9,15},{10,... | collective-permute-start | bytes 98312 | tf_op jit(solution)/shard_map/ppermute | solution.py:342
  9.3 4.5 %collective-permute-start.2 = (f32[32,256]{1,0:T(8,128)S(1)}, f32[32,256]{1,0:T(8,128)S(1)}, u32[]{:S(2)}, u32[]{:S(2)}) collective-permute-start(f32[32,256]{1,0:T(8,128)S(1)} %get-tuple-element.10), channel_id=1, source_target_pairs={{0,5},{1,4},{2,7},{3,6},{4,1},{5,0},{6,3},{7,2},{8,13},{9,12},{10,... | collective-permute-start | bytes 98312 | tf_op jit(solution)/shard_map/ppermute | solution.py:342
  10.2 3.6 %collective-permute-start.3 = (f32[32,256]{1,0:T(8,128)S(1)}, f32[32,256]{1,0:T(8,128)S(1)}, u32[]{:S(2)}, u32[]{:S(2)}) collective-permute-start(f32[32,256]{1,0:T(8,128)S(1)} %get-tuple-element.11), channel_id=1, source_target_pairs={{0,4},{1,5},{2,6},{3,7},{4,0},{5,1},{6,2},{7,3},{8,12},{9,13},{10,... | collective-permute-start | bytes 98312 | tf_op jit(solution)/shard_map/ppermute | solution.py:342
  13.8 4.1 %collective-permute-start.6 = (f32[16,256]{1,0:T(8,128)S(1)}, f32[16,256]{1,0:T(8,128)S(1)}, u32[]{:S(2)}, u32[]{:S(2)}) collective-permute-start(f32[16,256]{1,0:T(8,128)S(1)} %get-tuple-element.12.refs_0_), channel_id=1, source_target_pairs={{0,28},{1,29},{2,30},{3,31},{4,24},{5,25},{6,26},{7,27},{8,20},{9,... | collective-permute-start | bytes 49160 | tf_op jit(solution)/shard_map/ppermute | solution.py:342
  16.3 3.2 %collective-permute-start.5 = (f32[16,256]{1,0:T(8,128)S(1)}, f32[16,256]{1,0:T(8,128)S(1)}, u32[]{:S(2)}, u32[]{:S(2)}) collective-permute-start(f32[16,256]{1,0:T(8,128)S(1)} %get-tuple-element.12.refs_0_), channel_id=1, source_target_pairs={{0,20},{1,21},{2,22},{3,23},{4,16},{5,17},{6,18},{7,19},{8,28},{9,... | collective-permute-start | bytes 49160 | tf_op jit(solution)/shard_map/ppermute | solution.py:342
  16.6 3.2 %collective-permute-start.4 = (f32[16,256]{1,0:T(8,128)S(1)}, f32[16,256]{1,0:T(8,128)S(1)}, u32[]{:S(2)}, u32[]{:S(2)}) collective-permute-start(f32[16,256]{1,0:T(8,128)S(1)} %get-tuple-element.12.refs_0_), channel_id=1, source_target_pairs={{0,12},{1,13},{2,14},{3,15},{4,8},{5,9},{6,10},{7,11},{8,4},{9,5},... | collective-permute-start | bytes 49160 | tf_op jit(solution)/shard_map/ppermute | solution.py:342
  19.8 1.3 %collective-permute-start.7 = (f32[80,256]{1,0:T(8,128)S(1)}, f32[80,256]{1,0:T(8,128)S(1)}, u32[]{:S(2)}, u32[]{:S(2)}) collective-permute-start(f32[80,256]{1,0:T(8,128)S(1)} %stack.1.held), channel_id=1, source_target_pairs={{0,4},{1,5},{2,6},{3,7},{4,0},{5,1},{6,2},{7,3},{8,12},{9,13},{10,... | collective-permute-start | bytes 245768 | tf_op jit(solution)/shard_map/ppermute | solution.py:342

commit v19 on v16

--- a/solution.py
+++ b/solution.py
@@ -188,13 +188,16 @@
         )
 
 
-def pick_lanes(x, index):
+def pick_lanes(x, index, offset):
+    if offset:
+        x = pltpu.roll(x, LANES - offset, 1)
     return jnp.take_along_axis(x, index, axis=1)
 
 
-def reciprocal(x):
+def reciprocal(x, scale=None):
     guess = pl.reciprocal(x, approx=True)
-    return guess * (2.0 - x * guess)
+    rest = 2.0 - x * guess
+    return (guess if scale is None else scale * guess) * rest
 
 
 def factor_kernel(parts, damping, held, sent, features, factors):
@@ -236,20 +239,20 @@
 
     zero = jnp.zeros((PANEL, LANES), jnp.float32)
     finished = []
-    ahead = [pick_lanes(tile[0][0], slot * SLOT + r) for r in range(PANEL)]
+    ahead = [pick_lanes(tile[0][0], slot * SLOT, r) for r in range(PANEL)]
     for q in range(panels):
         hq, at = divmod(q, per_half)
         if q + 1 < panels:
             hn, an = divmod(q + 1, per_half)
             behind = [
-                pick_lanes(tile[q + 1][hn], slot * SLOT + an * PANEL + r)
+                pick_lanes(tile[q + 1][hn], slot * SLOT, an * PANEL + r)
                 for r in range(PANEL)
             ]
         column = [
             {
                 j: ahead[r]
                 if j == q
-                else pick_lanes(tile[j][hq], slot * SLOT + at * PANEL + r)
+                else pick_lanes(tile[j][hq], slot * SLOT, at * PANEL + r)
                 for j in range(q, panels)
             }
             for r in range(PANEL)
@@ -274,10 +277,11 @@
         ]
         inverse = []
 
-        def eliminate(r, s, inv):
+        def eliminate(r, s, inv, near=()):
             ratio = block[r][s] * inv
             for t in range(s, PANEL):
-                block[s][t] = block[s][t] - ratio * block[r][t]
+                step = (block[r][s] * block[r][t]) * inv if t in near else ratio * block[r][t]
+                block[s][t] = block[s][t] - step
             for j in range(q + 1, panels):
                 column[s][j] = column[s][j] - ratio * column[r][j]
             for h in range(hq, halves):
@@ -287,11 +291,12 @@
             pivot = block[r][r]
             minor = pivot * block[r + 1][r + 1] - block[r][r + 1] * block[r][r + 1]
             inverse.append(reciprocal(pivot))
-            inverse.append(pivot * reciprocal(minor))
+            inverse.append(reciprocal(minor, pivot))
             eliminate(r, r + 1, inverse[r])
             for s in range(r + 2, PANEL):
-                eliminate(r, s, inverse[r])
-                eliminate(r + 1, s, inverse[r + 1])
+                near = (r + 2, r + 3) if s < r + 4 else ()
+                eliminate(r, s, inverse[r], near)
+                eliminate(r + 1, s, inverse[r + 1], near)
         result = []
         for h in range(halves):
             if h < hq:
@@ -313,7 +318,12 @@
                         factor = jnp.broadcast_to(
                             column[r][j][s : s + 1, :], (PANEL, LANES)
                         )
-                        ahead[s] = ahead[s] - weights[r] * factor
+                        step = (
+                            (column[r][j] * factor) * inverse[r]
+                            if r >= PANEL - 2
+                            else weights[r] * factor
+                        )
+                        ahead[s] = ahead[s] - step
             for h in range((q + 1) // per_half, halves):
                 value = tile[j][h]
                 for r in range(PANEL):

time: 21.8 us -> 22.2 us (1.018)
  Pallas kernels: 4.68 us -> 5.07 us
    pallas_call x1, Pallas kernels: 2.07 us -> 2.47 us  [local(): pl.pallas_call(functools.partial(factor_kernel, parts), out_shape=[jax.Sh...]
where the time goes in v19:
time: 22.2 us; the launch traced here: 22 us
  starting transfers between devices  9.08 us (41%)
  waiting for transfers between devices  6.56 us (30%)
  Pallas kernels  5.07 us (23%)
  between operations  1.3 us (6%)
    ppermute x8, starting transfers between devices, exchange(): lax.ppermute(x, ('ex', 'mp'), [(m * parts + b, (m ^ ex_distance) * parts...  9.08 us
    ppermute x8, waiting for transfers between devices, exchange(): lax.ppermute(x, ('ex', 'mp'), [(m * parts + b, (m ^ ex_distance) * parts...  6.56 us
    pallas_call x1, Pallas kernels, local(): pl.pallas_call(functools.partial(partial_kernel, parts, scaling), out_sha...  2.59 us
    pallas_call x1, Pallas kernels, local(): pl.pallas_call(functools.partial(factor_kernel, parts), out_shape=[jax.Sh...  2.47 us
  transfers between devices with their start and end apart: 8, of which 6 were waited for; matrix products, arithmetic and copies ran while one was open for 0% of the time, Pallas kernels for 0%

profile of v19, /device:TPU:0, one launch (start us, length us, event | category | flops | bytes accessed | tf_op | source)
XLA Modules:
  0.0 22.0 jit_solution(10490678720789081462)
XLA Ops:
  0.6 2.6 %partials.1 = (f32[32,256]{1,0:T(8,128)S(1)}, f32[32,256]{1,0:T(8,128)S(1)}, f32[32,256]{1,0:T(8,128)S(1)}, f32[32,256]{1,0:T(8,128)S(1)}) custom-call(bf16[1,128,4096]{2,1,0:T(8,128)(2,1)} %acts_hbm.1, bf16[1,128,1024]{2,1,0:T(8,128)(2,1)} %grads_hbm.1, bf16[1,16,4096]{2,1,0:T(8,128)(2,1)} %down_hbm.1, bf16[1,16,1024]{2,1,0:T(8,128)(2,1)} %up_hbm.1, ...), custom_call_target="tpu_custom_call" | custom-call | tf_op jit(solution)/shard_map/partials/pallas_call | solution.py:394
  3.2 4.6 %collective-permute-start = (f32[32,256]{1,0:T(8,128)S(1)}, f32[32,256]{1,0:T(8,128)S(1)}, u32[]{:S(2)}, u32[]{:S(2)}) collective-permute-start(f32[32,256]{1,0:T(8,128)S(1)} %get-tuple-element.8), channel_id=1, source_target_pairs={{0,7},{1,6},{2,5},{3,4},{4,3},{5,2},{6,1},{7,0},{8,15},{9,14},{10,... | collective-permute-start | bytes 98312 | tf_op jit(solution)/shard_map/ppermute | solution.py:343
  7.8 0.0 collective-permute-start.1
  7.8 0.9 %collective-permute-start.2 = (f32[32,256]{1,0:T(8,128)S(1)}, f32[32,256]{1,0:T(8,128)S(1)}, u32[]{:S(2)}, u32[]{:S(2)}) collective-permute-start(f32[32,256]{1,0:T(8,128)S(1)} %get-tuple-element.10), channel_id=1, source_target_pairs={{0,5},{1,4},{2,7},{3,6},{4,1},{5,0},{6,3},{7,2},{8,13},{9,12},{10,... | collective-permute-start | bytes 98312 | tf_op jit(solution)/shard_map/ppermute | solution.py:343
  8.7 0.0 collective-permute-start.3
  8.7 0.9 %collective-permute-done.refs_0_ = f32[32,256]{1,0:T(8,128)S(1)} collective-permute-done((f32[32,256]{1,0:T(8,128)S(1)}, f32[32,256]{1,0:T(8,128)S(1)}, u32[]{:S(2)}, u32[]{:S(2)}) %collective-permute-start) | collective-permute-done | bytes 32800 | tf_op jit(solution)/shard_map/ppermute | solution.py:343
  9.6 2.8 %collective-permute-done.1.refs_1_ = f32[32,256]{1,0:T(8,128)S(1)} collective-permute-done((f32[32,256]{1,0:T(8,128)S(1)}, f32[32,256]{1,0:T(8,128)S(1)}, u32[]{:S(2)}, u32[]{:S(2)}) %collective-permute-start.1) | collective-permute-done | bytes 32800 | tf_op jit(solution)/shard_map/ppermute | solution.py:343
  12.3 0.0 collective-permute-done.2.refs_2_
  12.3 0.0 collective-permute-done.3.refs_3_
  12.3 2.5 %collective-permute-start.6 = (f32[16,256]{1,0:T(8,128)S(1)}, f32[16,256]{1,0:T(8,128)S(1)}, u32[]{:S(2)}, u32[]{:S(2)}) collective-permute-start(f32[16,256]{1,0:T(8,128)S(1)} %get-tuple-element.12.refs_0_), channel_id=1, source_target_pairs={{0,28},{1,29},{2,30},{3,31},{4,24},{5,25},{6,26},{7,27},{8,20},{9,... | collective-permute-start | bytes 49160 | tf_op jit(solution)/shard_map/ppermute | solution.py:343
  14.8 0.3 %collective-permute-start.5 = (f32[16,256]{1,0:T(8,128)S(1)}, f32[16,256]{1,0:T(8,128)S(1)}, u32[]{:S(2)}, u32[]{:S(2)}) collective-permute-start(f32[16,256]{1,0:T(8,128)S(1)} %get-tuple-element.12.refs_0_), channel_id=1, source_target_pairs={{0,20},{1,21},{2,22},{3,23},{4,16},{5,17},{6,18},{7,19},{8,28},{9,... | collective-permute-start | bytes 49160 | tf_op jit(solution)/shard_map/ppermute | solution.py:343
  15.1 0.5 %collective-permute-start.4 = (f32[16,256]{1,0:T(8,128)S(1)}, f32[16,256]{1,0:T(8,128)S(1)}, u32[]{:S(2)}, u32[]{:S(2)}) collective-permute-start(f32[16,256]{1,0:T(8,128)S(1)} %get-tuple-element.12.refs_0_), channel_id=1, source_target_pairs={{0,12},{1,13},{2,14},{3,15},{4,8},{5,9},{6,10},{7,11},{8,4},{9,5},... | collective-permute-start | bytes 49160 | tf_op jit(solution)/shard_map/ppermute | solution.py:343
  15.6 0.9 %collective-permute-done.6.refs_3_ = f32[16,256]{1,0:T(8,128)S(1)} collective-permute-done((f32[16,256]{1,0:T(8,128)S(1)}, f32[16,256]{1,0:T(8,128)S(1)}, u32[]{:S(2)}, u32[]{:S(2)}) %collective-permute-start.6) | collective-permute-done | bytes 16416 | tf_op jit(solution)/shard_map/ppermute | solution.py:343
  16.5 1.5 %collective-permute-done.5.refs_2_ = f32[16,256]{1,0:T(8,128)S(1)} collective-permute-done((f32[16,256]{1,0:T(8,128)S(1)}, f32[16,256]{1,0:T(8,128)S(1)}, u32[]{:S(2)}, u32[]{:S(2)}) %collective-permute-start.5) | collective-permute-done | bytes 16416 | tf_op jit(solution)/shard_map/ppermute | solution.py:343
  18.0 0.3 %collective-permute-done.4.refs_1_ = f32[16,256]{1,0:T(8,128)S(1)} collective-permute-done((f32[16,256]{1,0:T(8,128)S(1)}, f32[16,256]{1,0:T(8,128)S(1)}, u32[]{:S(2)}, u32[]{:S(2)}) %collective-permute-start.4) | collective-permute-done | bytes 16416 | tf_op jit(solution)/shard_map/ppermute | solution.py:343
  18.3 0.4 %collective-permute-start.7 = (f32[80,256]{1,0:T(8,128)S(1)}, f32[80,256]{1,0:T(8,128)S(1)}, u32[]{:S(2)}, u32[]{:S(2)}) collective-permute-start(f32[80,256]{1,0:T(8,128)S(1)} %stack.1.held), channel_id=1, source_target_pairs={{0,4},{1,5},{2,6},{3,7},{4,0},{5,1},{6,2},{7,3},{8,12},{9,13},{10,... | collective-permute-start | bytes 245768 | tf_op jit(solution)/shard_map/ppermute | solution.py:343
  19.3 0.3 %collective-permute-done.7.sent = f32[80,256]{1,0:T(8,128)S(1)} collective-permute-done((f32[80,256]{1,0:T(8,128)S(1)}, f32[80,256]{1,0:T(8,128)S(1)}, u32[]{:S(2)}, u32[]{:S(2)}) %collective-permute-start.7) | collective-permute-done | bytes 81952 | tf_op jit(solution)/shard_map/ppermute | solution.py:343
  19.6 2.5 %factors.1 = (f32[4,1024]{1,0:T(4,128)}, f32[4,64,64]{2,1,0:T(8,128)}) custom-call(f32[1]{0:T(128)S(6)} %copy.10.damping, f32[80,256]{1,0:T(8,128)S(1)} %stack.1.held, f32[80,256]{1,0:T(8,128)S(1)} %collective-permute-done.7.sent), custom_call_target="tpu_custom_call" | custom-call | tf_op jit(solution)/shard_map/factors/pallas_call | solution.py:444
  (2 shorter events, 0.0 us)
Async XLA Ops:
  3.2 6.3 %collective-permute-start = (f32[32,256]{1,0:T(8,128)S(1)}, f32[32,256]{1,0:T(8,128)S(1)}, u32[]{:S(2)}, u32[]{:S(2)}) collective-permute-start(f32[32,256]{1,0:T(8,128)S(1)} %get-tuple-element.8), channel_id=1, source_target_pairs={{0,7},{1,6},{2,5},{3,4},{4,3},{5,2},{6,1},{7,0},{8,15},{9,14},{10,... | collective-permute-start | bytes 98312 | tf_op jit(solution)/shard_map/ppermute | solution.py:343
  7.8 4.5 %collective-permute-start.1 = (f32[32,256]{1,0:T(8,128)S(1)}, f32[32,256]{1,0:T(8,128)S(1)}, u32[]{:S(2)}, u32[]{:S(2)}) collective-permute-start(f32[32,256]{1,0:T(8,128)S(1)} %get-tuple-element.9), channel_id=1, source_target_pairs={{0,6},{1,7},{2,4},{3,5},{4,2},{5,3},{6,0},{7,1},{8,14},{9,15},{10,... | collective-permute-start | bytes 98312 | tf_op jit(solution)/shard_map/ppermute | solution.py:343
  7.8 4.5 %collective-permute-start.2 = (f32[32,256]{1,0:T(8,128)S(1)}, f32[32,256]{1,0:T(8,128)S(1)}, u32[]{:S(2)}, u32[]{:S(2)}) collective-permute-start(f32[32,256]{1,0:T(8,128)S(1)} %get-tuple-element.10), channel_id=1, source_target_pairs={{0,5},{1,4},{2,7},{3,6},{4,1},{5,0},{6,3},{7,2},{8,13},{9,12},{10,... | collective-permute-start | bytes 98312 | tf_op jit(solution)/shard_map/ppermute | solution.py:343
  8.7 3.6 %collective-permute-start.3 = (f32[32,256]{1,0:T(8,128)S(1)}, f32[32,256]{1,0:T(8,128)S(1)}, u32[]{:S(2)}, u32[]{:S(2)}) collective-permute-start(f32[32,256]{1,0:T(8,128)S(1)} %get-tuple-element.11), channel_id=1, source_target_pairs={{0,4},{1,5},{2,6},{3,7},{4,0},{5,1},{6,2},{7,3},{8,12},{9,13},{10,... | collective-permute-start | bytes 98312 | tf_op jit(solution)/shard_map/ppermute | solution.py:343
  12.3 4.1 %collective-permute-start.6 = (f32[16,256]{1,0:T(8,128)S(1)}, f32[16,256]{1,0:T(8,128)S(1)}, u32[]{:S(2)}, u32[]{:S(2)}) collective-permute-start(f32[16,256]{1,0:T(8,128)S(1)} %get-tuple-element.12.refs_0_), channel_id=1, source_target_pairs={{0,28},{1,29},{2,30},{3,31},{4,24},{5,25},{6,26},{7,27},{8,20},{9,... | collective-permute-start | bytes 49160 | tf_op jit(solution)/shard_map/ppermute | solution.py:343
  14.8 3.2 %collective-permute-start.5 = (f32[16,256]{1,0:T(8,128)S(1)}, f32[16,256]{1,0:T(8,128)S(1)}, u32[]{:S(2)}, u32[]{:S(2)}) collective-permute-start(f32[16,256]{1,0:T(8,128)S(1)} %get-tuple-element.12.refs_0_), channel_id=1, source_target_pairs={{0,20},{1,21},{2,22},{3,23},{4,16},{5,17},{6,18},{7,19},{8,28},{9,... | collective-permute-start | bytes 49160 | tf_op jit(solution)/shard_map/ppermute | solution.py:343
  15.1 3.2 %collective-permute-start.4 = (f32[16,256]{1,0:T(8,128)S(1)}, f32[16,256]{1,0:T(8,128)S(1)}, u32[]{:S(2)}, u32[]{:S(2)}) collective-permute-start(f32[16,256]{1,0:T(8,128)S(1)} %get-tuple-element.12.refs_0_), channel_id=1, source_target_pairs={{0,12},{1,13},{2,14},{3,15},{4,8},{5,9},{6,10},{7,11},{8,4},{9,5},... | collective-permute-start | bytes 49160 | tf_op jit(solution)/shard_map/ppermute | solution.py:343
  18.3 1.3 %collective-permute-start.7 = (f32[80,256]{1,0:T(8,128)S(1)}, f32[80,256]{1,0:T(8,128)S(1)}, u32[]{:S(2)}, u32[]{:S(2)}) collective-permute-start(f32[80,256]{1,0:T(8,128)S(1)} %stack.1.held), channel_id=1, source_target_pairs={{0,4},{1,5},{2,6},{3,7},{4,0},{5,1},{6,2},{7,3},{8,12},{9,13},{10,... | collective-permute-start | bytes 245768 | tf_op jit(solution)/shard_map/ppermute | solution.py:343

commit v20 on v19

--- a/solution.py
+++ b/solution.py
@@ -1,4 +1,5 @@
 import functools
+import itertools
 import math
 
 import jax
@@ -188,9 +189,7 @@
         )
 
 
-def pick_lanes(x, index, offset):
-    if offset:
-        x = pltpu.roll(x, LANES - offset, 1)
+def pick_lanes(x, index):
     return jnp.take_along_axis(x, index, axis=1)
 
 
@@ -200,7 +199,7 @@
     return (guess if scale is None else scale * guess) * rest
 
 
-def factor_kernel(parts, damping, held, sent, features, factors):
+def factor_kernel(parts, damping, held, sent, features, factors, kept):
     channels, sketch, _ = factors.shape
     examples = features.shape[0] * parts
     gathered = held.shape[0] - examples
@@ -237,44 +236,36 @@
             line.append(value)
         tile.append(line)
 
+    places = itertools.count(0, PANEL)
+
+    def rows_of(x):
+        place = next(places)
+        kept[place : place + PANEL, :] = x
+        return [kept[pl.ds(place + s, PANEL, stride=0), :] for s in range(PANEL)]
+
     zero = jnp.zeros((PANEL, LANES), jnp.float32)
     finished = []
-    ahead = [pick_lanes(tile[0][0], slot * SLOT, r) for r in range(PANEL)]
+    ahead = [pick_lanes(tile[0][0], slot * SLOT + r) for r in range(PANEL)]
     for q in range(panels):
         hq, at = divmod(q, per_half)
         if q + 1 < panels:
             hn, an = divmod(q + 1, per_half)
             behind = [
-                pick_lanes(tile[q + 1][hn], slot * SLOT, an * PANEL + r)
+                pick_lanes(tile[q + 1][hn], slot * SLOT + an * PANEL + r)
                 for r in range(PANEL)
             ]
         column = [
             {
                 j: ahead[r]
                 if j == q
-                else pick_lanes(tile[j][hq], slot * SLOT, at * PANEL + r)
+                else pick_lanes(tile[j][hq], slot * SLOT + at * PANEL + r)
                 for j in range(q, panels)
             }
             for r in range(PANEL)
         ]
-        block = [
-            [
-                jnp.broadcast_to(column[r][q][s : s + 1, :], (PANEL, LANES))
-                if s >= r
-                else None
-                for s in range(PANEL)
-            ]
-            for r in range(PANEL)
-        ]
-        line = [
-            [
-                jnp.broadcast_to(tile[q][h][r : r + 1, :], (PANEL, LANES))
-                if h >= hq
-                else None
-                for h in range(halves)
-            ]
-            for r in range(PANEL)
-        ]
+        block = [rows_of(column[r][q]) for r in range(PANEL)]
+        lines = [rows_of(tile[q][h]) if h >= hq else [None] * PANEL for h in range(halves)]
+        line = [list(group) for group in zip(*lines)]
         inverse = []
 
         def eliminate(r, s, inv, near=()):
@@ -314,10 +305,7 @@
             if j == q + 1:
                 ahead = behind
                 for r in range(PANEL):
-                    for s in range(PANEL):
-                        factor = jnp.broadcast_to(
-                            column[r][j][s : s + 1, :], (PANEL, LANES)
-                        )
+                    for s, factor in enumerate(rows_of(column[r][j])):
                         step = (
                             (column[r][j] * factor) * inverse[r]
                             if r >= PANEL - 2
@@ -449,6 +437,11 @@
         ],
         in_specs=[smem()] + [vmem()] * 2,
         out_specs=[vmem()] * 2,
+        scratch_shapes=[
+            pltpu.VMEM(
+                (sketch * (2 * PANEL + sketch // SLOT) + PANEL, LANES), jnp.float32
+            )
+        ],
         compiler_params=pltpu.CompilerParams(vmem_limit_bytes=8 * 2**20),
         name="factors",
     )(damping, *in_vmem(held, sent))

time: 22.2 us -> 21.8 us (0.982)
  Pallas kernels: 5.07 us -> 4.72 us
    pallas_call x1, Pallas kernels: 2.47 us -> 2.11 us  [local(): pl.pallas_call(functools.partial(factor_kernel, parts), out_shape=[jax.Sh...]
where the time goes in v20:
time: 21.8 us; the launch traced here: 21.7 us
  starting transfers between devices  9.08 us (42%)
  waiting for transfers between devices  6.56 us (30%)
  Pallas kernels  4.72 us (22%)
  between operations  1.3 us (6%)
    ppermute x8, starting transfers between devices, exchange(): lax.ppermute(x, ('ex', 'mp'), [(m * parts + b, (m ^ ex_distance) * parts...  9.08 us
    ppermute x8, waiting for transfers between devices, exchange(): lax.ppermute(x, ('ex', 'mp'), [(m * parts + b, (m ^ ex_distance) * parts...  6.56 us
    pallas_call x1, Pallas kernels, local(): pl.pallas_call(functools.partial(partial_kernel, parts, scaling), out_sha...  2.59 us
    pallas_call x1, Pallas kernels, local(): pl.pallas_call(functools.partial(factor_kernel, parts), out_shape=[jax.Sh...  2.11 us
  transfers between devices with their start and end apart: 8, of which 6 were waited for; matrix products, arithmetic and copies ran while one was open for 0% of the time, Pallas kernels for 0%

profile of v20, /device:TPU:0, one launch (start us, length us, event | category | flops | bytes accessed | tf_op | source)
XLA Modules:
  0.0 21.7 jit_solution(15818079208290538917)
XLA Ops:
  0.6 2.6 %partials.1 = (f32[32,256]{1,0:T(8,128)S(1)}, f32[32,256]{1,0:T(8,128)S(1)}, f32[32,256]{1,0:T(8,128)S(1)}, f32[32,256]{1,0:T(8,128)S(1)}) custom-call(bf16[1,128,4096]{2,1,0:T(8,128)(2,1)} %acts_hbm.1, bf16[1,128,1024]{2,1,0:T(8,128)(2,1)} %grads_hbm.1, bf16[1,16,4096]{2,1,0:T(8,128)(2,1)} %down_hbm.1, bf16[1,16,1024]{2,1,0:T(8,128)(2,1)} %up_hbm.1, ...), custom_call_target="tpu_custom_call" | custom-call | tf_op jit(solution)/shard_map/partials/pallas_call | solution.py:382
  3.2 4.6 %collective-permute-start = (f32[32,256]{1,0:T(8,128)S(1)}, f32[32,256]{1,0:T(8,128)S(1)}, u32[]{:S(2)}, u32[]{:S(2)}) collective-permute-start(f32[32,256]{1,0:T(8,128)S(1)} %get-tuple-element.8), channel_id=1, source_target_pairs={{0,7},{1,6},{2,5},{3,4},{4,3},{5,2},{6,1},{7,0},{8,15},{9,14},{10,... | collective-permute-start | bytes 98312 | tf_op jit(solution)/shard_map/ppermute | solution.py:331
  7.8 0.0 collective-permute-start.1
  7.8 0.9 %collective-permute-start.2 = (f32[32,256]{1,0:T(8,128)S(1)}, f32[32,256]{1,0:T(8,128)S(1)}, u32[]{:S(2)}, u32[]{:S(2)}) collective-permute-start(f32[32,256]{1,0:T(8,128)S(1)} %get-tuple-element.10), channel_id=1, source_target_pairs={{0,5},{1,4},{2,7},{3,6},{4,1},{5,0},{6,3},{7,2},{8,13},{9,12},{10,... | collective-permute-start | bytes 98312 | tf_op jit(solution)/shard_map/ppermute | solution.py:331
  8.7 0.0 collective-permute-start.3
  8.7 0.9 %collective-permute-done.refs_0_ = f32[32,256]{1,0:T(8,128)S(1)} collective-permute-done((f32[32,256]{1,0:T(8,128)S(1)}, f32[32,256]{1,0:T(8,128)S(1)}, u32[]{:S(2)}, u32[]{:S(2)}) %collective-permute-start) | collective-permute-done | bytes 32800 | tf_op jit(solution)/shard_map/ppermute | solution.py:331
  9.6 2.8 %collective-permute-done.1.refs_1_ = f32[32,256]{1,0:T(8,128)S(1)} collective-permute-done((f32[32,256]{1,0:T(8,128)S(1)}, f32[32,256]{1,0:T(8,128)S(1)}, u32[]{:S(2)}, u32[]{:S(2)}) %collective-permute-start.1) | collective-permute-done | bytes 32800 | tf_op jit(solution)/shard_map/ppermute | solution.py:331
  12.3 0.0 collective-permute-done.2.refs_2_
  12.3 0.0 collective-permute-done.3.refs_3_
  12.3 2.5 %collective-permute-start.6 = (f32[16,256]{1,0:T(8,128)S(1)}, f32[16,256]{1,0:T(8,128)S(1)}, u32[]{:S(2)}, u32[]{:S(2)}) collective-permute-start(f32[16,256]{1,0:T(8,128)S(1)} %get-tuple-element.12.refs_0_), channel_id=1, source_target_pairs={{0,28},{1,29},{2,30},{3,31},{4,24},{5,25},{6,26},{7,27},{8,20},{9,... | collective-permute-start | bytes 49160 | tf_op jit(solution)/shard_map/ppermute | solution.py:331
  14.8 0.3 %collective-permute-start.5 = (f32[16,256]{1,0:T(8,128)S(1)}, f32[16,256]{1,0:T(8,128)S(1)}, u32[]{:S(2)}, u32[]{:S(2)}) collective-permute-start(f32[16,256]{1,0:T(8,128)S(1)} %get-tuple-element.12.refs_0_), channel_id=1, source_target_pairs={{0,20},{1,21},{2,22},{3,23},{4,16},{5,17},{6,18},{7,19},{8,28},{9,... | collective-permute-start | bytes 49160 | tf_op jit(solution)/shard_map/ppermute | solution.py:331
  15.1 0.5 %collective-permute-start.4 = (f32[16,256]{1,0:T(8,128)S(1)}, f32[16,256]{1,0:T(8,128)S(1)}, u32[]{:S(2)}, u32[]{:S(2)}) collective-permute-start(f32[16,256]{1,0:T(8,128)S(1)} %get-tuple-element.12.refs_0_), channel_id=1, source_target_pairs={{0,12},{1,13},{2,14},{3,15},{4,8},{5,9},{6,10},{7,11},{8,4},{9,5},... | collective-permute-start | bytes 49160 | tf_op jit(solution)/shard_map/ppermute | solution.py:331
  15.6 0.9 %collective-permute-done.6.refs_3_ = f32[16,256]{1,0:T(8,128)S(1)} collective-permute-done((f32[16,256]{1,0:T(8,128)S(1)}, f32[16,256]{1,0:T(8,128)S(1)}, u32[]{:S(2)}, u32[]{:S(2)}) %collective-permute-start.6) | collective-permute-done | bytes 16416 | tf_op jit(solution)/shard_map/ppermute | solution.py:331
  16.5 1.5 %collective-permute-done.5.refs_2_ = f32[16,256]{1,0:T(8,128)S(1)} collective-permute-done((f32[16,256]{1,0:T(8,128)S(1)}, f32[16,256]{1,0:T(8,128)S(1)}, u32[]{:S(2)}, u32[]{:S(2)}) %collective-permute-start.5) | collective-permute-done | bytes 16416 | tf_op jit(solution)/shard_map/ppermute | solution.py:331
  18.0 0.3 %collective-permute-done.4.refs_1_ = f32[16,256]{1,0:T(8,128)S(1)} collective-permute-done((f32[16,256]{1,0:T(8,128)S(1)}, f32[16,256]{1,0:T(8,128)S(1)}, u32[]{:S(2)}, u32[]{:S(2)}) %collective-permute-start.4) | collective-permute-done | bytes 16416 | tf_op jit(solution)/shard_map/ppermute | solution.py:331
  18.3 0.4 %collective-permute-start.7 = (f32[80,256]{1,0:T(8,128)S(1)}, f32[80,256]{1,0:T(8,128)S(1)}, u32[]{:S(2)}, u32[]{:S(2)}) collective-permute-start(f32[80,256]{1,0:T(8,128)S(1)} %stack.1.held), channel_id=1, source_target_pairs={{0,4},{1,5},{2,6},{3,7},{4,0},{5,1},{6,2},{7,3},{8,12},{9,13},{10,... | collective-permute-start | bytes 245768 | tf_op jit(solution)/shard_map/ppermute | solution.py:331
  19.3 0.3 %collective-permute-done.7.sent = f32[80,256]{1,0:T(8,128)S(1)} collective-permute-done((f32[80,256]{1,0:T(8,128)S(1)}, f32[80,256]{1,0:T(8,128)S(1)}, u32[]{:S(2)}, u32[]{:S(2)}) %collective-permute-start.7) | collective-permute-done | bytes 81952 | tf_op jit(solution)/shard_map/ppermute | solution.py:331
  19.6 2.1 %factors.1 = (f32[4,1024]{1,0:T(4,128)}, f32[4,64,64]{2,1,0:T(8,128)}) custom-call(f32[1]{0:T(128)S(6)} %copy.10.damping, f32[80,256]{1,0:T(8,128)S(1)} %stack.1.held, f32[80,256]{1,0:T(8,128)S(1)} %collective-permute-done.7.sent), custom_call_target="tpu_custom_call" | custom-call | tf_op jit(solution)/shard_map/factors/pallas_call | solution.py:432
  (2 shorter events, 0.0 us)
Async XLA Ops:
  3.2 6.3 %collective-permute-start = (f32[32,256]{1,0:T(8,128)S(1)}, f32[32,256]{1,0:T(8,128)S(1)}, u32[]{:S(2)}, u32[]{:S(2)}) collective-permute-start(f32[32,256]{1,0:T(8,128)S(1)} %get-tuple-element.8), channel_id=1, source_target_pairs={{0,7},{1,6},{2,5},{3,4},{4,3},{5,2},{6,1},{7,0},{8,15},{9,14},{10,... | collective-permute-start | bytes 98312 | tf_op jit(solution)/shard_map/ppermute | solution.py:331
  7.8 4.5 %collective-permute-start.1 = (f32[32,256]{1,0:T(8,128)S(1)}, f32[32,256]{1,0:T(8,128)S(1)}, u32[]{:S(2)}, u32[]{:S(2)}) collective-permute-start(f32[32,256]{1,0:T(8,128)S(1)} %get-tuple-element.9), channel_id=1, source_target_pairs={{0,6},{1,7},{2,4},{3,5},{4,2},{5,3},{6,0},{7,1},{8,14},{9,15},{10,... | collective-permute-start | bytes 98312 | tf_op jit(solution)/shard_map/ppermute | solution.py:331
  7.8 4.5 %collective-permute-start.2 = (f32[32,256]{1,0:T(8,128)S(1)}, f32[32,256]{1,0:T(8,128)S(1)}, u32[]{:S(2)}, u32[]{:S(2)}) collective-permute-start(f32[32,256]{1,0:T(8,128)S(1)} %get-tuple-element.10), channel_id=1, source_target_pairs={{0,5},{1,4},{2,7},{3,6},{4,1},{5,0},{6,3},{7,2},{8,13},{9,12},{10,... | collective-permute-start | bytes 98312 | tf_op jit(solution)/shard_map/ppermute | solution.py:331
  8.7 3.6 %collective-permute-start.3 = (f32[32,256]{1,0:T(8,128)S(1)}, f32[32,256]{1,0:T(8,128)S(1)}, u32[]{:S(2)}, u32[]{:S(2)}) collective-permute-start(f32[32,256]{1,0:T(8,128)S(1)} %get-tuple-element.11), channel_id=1, source_target_pairs={{0,4},{1,5},{2,6},{3,7},{4,0},{5,1},{6,2},{7,3},{8,12},{9,13},{10,... | collective-permute-start | bytes 98312 | tf_op jit(solution)/shard_map/ppermute | solution.py:331
  12.3 4.1 %collective-permute-start.6 = (f32[16,256]{1,0:T(8,128)S(1)}, f32[16,256]{1,0:T(8,128)S(1)}, u32[]{:S(2)}, u32[]{:S(2)}) collective-permute-start(f32[16,256]{1,0:T(8,128)S(1)} %get-tuple-element.12.refs_0_), channel_id=1, source_target_pairs={{0,28},{1,29},{2,30},{3,31},{4,24},{5,25},{6,26},{7,27},{8,20},{9,... | collective-permute-start | bytes 49160 | tf_op jit(solution)/shard_map/ppermute | solution.py:331
  14.8 3.2 %collective-permute-start.5 = (f32[16,256]{1,0:T(8,128)S(1)}, f32[16,256]{1,0:T(8,128)S(1)}, u32[]{:S(2)}, u32[]{:S(2)}) collective-permute-start(f32[16,256]{1,0:T(8,128)S(1)} %get-tuple-element.12.refs_0_), channel_id=1, source_target_pairs={{0,20},{1,21},{2,22},{3,23},{4,16},{5,17},{6,18},{7,19},{8,28},{9,... | collective-permute-start | bytes 49160 | tf_op jit(solution)/shard_map/ppermute | solution.py:331
  15.1 3.2 %collective-permute-start.4 = (f32[16,256]{1,0:T(8,128)S(1)}, f32[16,256]{1,0:T(8,128)S(1)}, u32[]{:S(2)}, u32[]{:S(2)}) collective-permute-start(f32[16,256]{1,0:T(8,128)S(1)} %get-tuple-element.12.refs_0_), channel_id=1, source_target_pairs={{0,12},{1,13},{2,14},{3,15},{4,8},{5,9},{6,10},{7,11},{8,4},{9,5},... | collective-permute-start | bytes 49160 | tf_op jit(solution)/shard_map/ppermute | solution.py:331
  18.3 1.3 %collective-permute-start.7 = (f32[80,256]{1,0:T(8,128)S(1)}, f32[80,256]{1,0:T(8,128)S(1)}, u32[]{:S(2)}, u32[]{:S(2)}) collective-permute-start(f32[80,256]{1,0:T(8,128)S(1)} %stack.1.held), channel_id=1, source_target_pairs={{0,4},{1,5},{2,6},{3,7},{4,0},{5,1},{6,2},{7,3},{8,12},{9,13},{10,... | collective-permute-start | bytes 245768 | tf_op jit(solution)/shard_map/ppermute | solution.py:331

commit v21 on v15

--- a/solution.py
+++ b/solution.py
@@ -1,4 +1,5 @@
 import functools
+import itertools
 import math
 
 import jax
@@ -13,7 +14,7 @@
 SLOT = 32
 GROUP = LANES // SLOT
 PANEL = 8
-CHUNK = 1024
+PIECES = 4
 
 
 def dot_nt(a, b):
@@ -52,33 +53,41 @@
     per = rank // parts
     halves = sketch // SLOT
 
-    def copies(source, target, sem, start, size):
-        return pltpu.make_async_copy(
-            source.at[0, :, pl.ds(start, size)],
-            target.at[:, pl.ds(start, size)],
-            sem,
-        )
-
-    order_copy = pltpu.make_async_copy(order_hbm.at[0], order, order_sem)
-    order_copy.start()
-    sources = [
-        (grads_hbm, grads, proj_out_hbm, up_hbm, weights_out),
-        (acts_hbm, acts, proj_in_hbm, down_hbm, weights_in),
-    ]
+    def copy_in(source, target, sem):
+        copy = pltpu.make_async_copy(source, target, sem)
+        copy.start()
+        return copy
+
+    order_copy = copy_in(order_hbm.at[0], order, order_sem)
     pending = []
-    for data_hbm, data, first_hbm, second_hbm, weights in sources:
-        for start in range(0, data.shape[1], CHUNK):
-            n = len(pending)
-            pending.append(
-                [
-                    copies(first_hbm, weights.at[pl.ds(0, sketch)], sems.at[n, 0], start, CHUNK),
-                    copies(second_hbm, weights.at[pl.ds(sketch, rank)], sems.at[n, 1], start, CHUNK),
-                    copies(data_hbm, data, sems.at[n, 2], start, CHUNK),
-                ]
+    for n, (data_hbm, data, first_hbm, second_hbm, weights, count) in enumerate(
+        [
+            (grads_hbm, grads, proj_out_hbm, up_hbm, weights_out, 1),
+            (acts_hbm, acts, proj_in_hbm, down_hbm, weights_in, PIECES),
+        ]
+    ):
+        first = [
+            copy_in(first_hbm.at[0], weights.at[pl.ds(0, sketch)], sems.at[n, 0]),
+            copy_in(second_hbm.at[0], weights.at[pl.ds(sketch, rank)], sems.at[n, 1]),
+        ]
+        pieces = []
+        for i in range(count):
+            here = pl.ds(i * (tokens // count), tokens // count)
+            pieces.append(
+                (here, copy_in(data_hbm.at[0, here], data.at[here], sems.at[n, 2 + i]))
             )
-            for copy in pending[-1]:
-                copy.start()
-
+        pending.append((first, pieces))
+    def product(n, data, weights):
+        first, pieces = pending[n]
+        for copy in first:
+            copy.wait()
+        terms = []
+        for here, copy in pieces:
+            copy.wait()
+            terms.append(dot_nt(data[here, :], weights[...]))
+        return jnp.concatenate(terms, axis=0)
+
+    from_grads = product(0, grads, weights_out)
     order_copy.wait()
     rows = examples * parts
     lane = lax.broadcasted_iota(jnp.int32, (rows, 2 * tokens), 1)
@@ -90,18 +99,7 @@
     place = lax.broadcasted_iota(jnp.int32, (rows, 2 * tokens), 0) // parts
     mask[...] = jnp.where(target == place, scaling, 0.0)
 
-    def product(first, data, weights):
-        total = None
-        for n in range(data.shape[1] // CHUNK):
-            for copy in pending[first + n]:
-                copy.wait()
-            here = pl.ds(n * CHUNK, CHUNK)
-            term = dot_nt(data[:, here], weights[:, here])
-            total = term if total is None else total + term
-        return total
-
-    from_grads = product(0, grads, weights_out)
-    from_acts = product(grads.shape[1] // CHUNK, acts, weights_in)
+    from_acts = product(1, acts, weights_in)
     low[0] = jnp.transpose(from_grads)[sketch:]
     low[1] = jnp.transpose(from_acts)[sketch:]
     right_high, right_low = split(
@@ -113,7 +111,8 @@
         chosen = jnp.concatenate(
             [low[i, pl.ds(c, parts, stride=per), :] for i in range(2)], axis=1
         )
-        chosen = jnp.concatenate([chosen] * examples, axis=0)
+        chosen = jnp.concatenate([chosen] * max(1, 8 // parts), axis=0)
+        chosen = jnp.concatenate([chosen] * (rows // chosen.shape[0]), axis=0)
         high, rest = split(chosen * mask[...])
         highs.append(high)
         lows.append(rest)
@@ -191,12 +190,13 @@
     return jnp.take_along_axis(x, index, axis=1)
 
 
-def reciprocal(x):
+def reciprocal(x, scale=None):
     guess = pl.reciprocal(x, approx=True)
-    return guess * (2.0 - x * guess)
-
-
-def factor_kernel(parts, damping, held, sent, features, factors):
+    rest = 2.0 - x * guess
+    return (guess if scale is None else scale * guess) * rest
+
+
+def factor_kernel(parts, damping, held, sent, features, factors, kept):
     channels, sketch, _ = factors.shape
     examples = features.shape[0] * parts
     gathered = held.shape[0] - examples
@@ -233,6 +233,13 @@
             line.append(value)
         tile.append(line)
 
+    places = itertools.count(0, PANEL)
+
+    def rows_of(x):
+        place = next(places)
+        kept[place : place + PANEL, :] = x
+        return [kept[pl.ds(place + s, PANEL, stride=0), :] for s in range(PANEL)]
+
     zero = jnp.zeros((PANEL, LANES), jnp.float32)
     finished = []
     ahead = [pick_lanes(tile[0][0], slot * SLOT + r) for r in range(PANEL)]
@@ -253,30 +260,16 @@
             }
             for r in range(PANEL)
         ]
-        block = [
-            [
-                jnp.broadcast_to(column[r][q][s : s + 1, :], (PANEL, LANES))
-                if s >= r
-                else None
-                for s in range(PANEL)
-            ]
-            for r in range(PANEL)
-        ]
-        line = [
-            [
-                jnp.broadcast_to(tile[q][h][r : r + 1, :], (PANEL, LANES))
-                if h >= hq
-                else None
-                for h in range(halves)
-            ]
-            for r in range(PANEL)
-        ]
+        block = [rows_of(column[r][q]) for r in range(PANEL)]
+        lines = [rows_of(tile[q][h]) if h >= hq else [None] * PANEL for h in range(halves)]
+        line = [list(group) for group in zip(*lines)]
         inverse = []
 
-        def eliminate(r, s, inv):
+        def eliminate(r, s, inv, near=()):
             ratio = block[r][s] * inv
             for t in range(s, PANEL):
-                block[s][t] = block[s][t] - ratio * block[r][t]
+                step = (block[r][s] * block[r][t]) * inv if t in near else ratio * block[r][t]
+                block[s][t] = block[s][t] - step
             for j in range(q + 1, panels):
                 column[s][j] = column[s][j] - ratio * column[r][j]
             for h in range(hq, halves):
@@ -286,11 +279,12 @@
             pivot = block[r][r]
             minor = pivot * block[r + 1][r + 1] - block[r][r + 1] * block[r][r + 1]
             inverse.append(reciprocal(pivot))
-            inverse.append(pivot * reciprocal(minor))
+            inverse.append(reciprocal(minor, pivot))
             eliminate(r, r + 1, inverse[r])
             for s in range(r + 2, PANEL):
-                eliminate(r, s, inverse[r])
-                eliminate(r + 1, s, inverse[r + 1])
+                near = (r + 2, r + 3) if s < r + 4 else ()
+                eliminate(r, s, inverse[r], near)
+                eliminate(r + 1, s, inverse[r + 1], near)
         result = []
         for h in range(halves):
             if h < hq:
@@ -308,11 +302,13 @@
             if j == q + 1:
                 ahead = behind
                 for r in range(PANEL):
-                    for s in range(PANEL):
-                        factor = jnp.broadcast_to(
-                            column[r][j][s : s + 1, :], (PANEL, LANES)
+                    for s, factor in enumerate(rows_of(column[r][j])):
+                        step = (
+                            (column[r][j] * factor) * inverse[r]
+                            if r >= PANEL - 2
+                            else weights[r] * factor
                         )
-                        ahead[s] = ahead[s] - weights[r] * factor
+                        ahead[s] = ahead[s] - step
             for h in range((q + 1) // per_half, halves):
                 value = tile[j][h]
                 for r in range(PANEL):
@@ -394,7 +390,7 @@
             pltpu.VMEM((2, rank, tokens), jnp.float32),
             pltpu.VMEM((examples * parts, 2 * tokens), jnp.float32),
             pltpu.VMEM((examples * parts, LANES), jnp.float32),
-            pltpu.SemaphoreType.DMA(((width + key_width) // CHUNK, 3)),
+            pltpu.SemaphoreType.DMA((2, 2 + PIECES)),
             pltpu.SemaphoreType.DMA,
         ],
         compiler_params=pltpu.CompilerParams(vmem_limit_bytes=8 * 2**20),
@@ -438,6 +434,11 @@
         ],
         in_specs=[smem()] + [vmem()] * 2,
         out_specs=[vmem()] * 2,
+        scratch_shapes=[
+            pltpu.VMEM(
+                (sketch * (2 * PANEL + sketch // SLOT) + PANEL, LANES), jnp.float32
+            )
+        ],
         compiler_params=pltpu.CompilerParams(vmem_limit_bytes=8 * 2**20),
         name="factors",
     )(damping, *in_vmem(held, sent))

time: 21.9 us -> 23 us (1.050)
  Pallas kernels: 4.75 us -> 5.87 us
    pallas_call x1, Pallas kernels: 2.66 us -> 3.75 us  [local(): pl.pallas_call(functools.partial(partial_kernel, parts, scaling), out_sha...]
where the time goes in v21:
time: 23 us; the launch traced here: 22.8 us
  starting transfers between devices  9.08 us (39%)
  waiting for transfers between devices  6.57 us (29%)
  Pallas kernels  5.87 us (26%)
  between operations  1.3 us (6%)
    ppermute x8, starting transfers between devices, exchange(): lax.ppermute(x, ('ex', 'mp'), [(m * parts + b, (m ^ ex_distance) * parts...  9.08 us
    ppermute x8, waiting for transfers between devices, exchange(): lax.ppermute(x, ('ex', 'mp'), [(m * parts + b, (m ^ ex_distance) * parts...  6.57 us
    pallas_call x1, Pallas kernels, local(): pl.pallas_call(functools.partial(partial_kernel, parts, scaling), out_sha...  3.75 us
    pallas_call x1, Pallas kernels, local(): pl.pallas_call(functools.partial(factor_kernel, parts), out_shape=[jax.Sh...  2.11 us
  transfers between devices with their start and end apart: 8, of which 6 were waited for; matrix products, arithmetic and copies ran while one was open for 0% of the time, Pallas kernels for 0%

profile of v21, /device:TPU:0, one launch (start us, length us, event | category | flops | bytes accessed | tf_op | source)
XLA Modules:
  0.0 22.8 jit_solution(12413348193597336537)
XLA Ops:
  0.6 3.7 %partials.1 = (f32[32,256]{1,0:T(8,128)S(1)}, f32[32,256]{1,0:T(8,128)S(1)}, f32[32,256]{1,0:T(8,128)S(1)}, f32[32,256]{1,0:T(8,128)S(1)}) custom-call(bf16[1,128,4096]{2,1,0:T(8,128)(2,1)} %acts_hbm.1, bf16[1,128,1024]{2,1,0:T(8,128)(2,1)} %grads_hbm.1, bf16[1,16,4096]{2,1,0:T(8,128)(2,1)} %down_hbm.1, bf16[1,16,1024]{2,1,0:T(8,128)(2,1)} %up_hbm.1, ...), custom_call_target="tpu_custom_call" | custom-call | tf_op jit(solution)/shard_map/partials/pallas_call | solution.py:379
  4.4 4.6 %collective-permute-start = (f32[32,256]{1,0:T(8,128)S(1)}, f32[32,256]{1,0:T(8,128)S(1)}, u32[]{:S(2)}, u32[]{:S(2)}) collective-permute-start(f32[32,256]{1,0:T(8,128)S(1)} %get-tuple-element.8), channel_id=1, source_target_pairs={{0,7},{1,6},{2,5},{3,4},{4,3},{5,2},{6,1},{7,0},{8,15},{9,14},{10,... | collective-permute-start | bytes 98312 | tf_op jit(solution)/shard_map/ppermute | solution.py:328
  8.9 0.0 collective-permute-start.1
  8.9 0.9 %collective-permute-start.2 = (f32[32,256]{1,0:T(8,128)S(1)}, f32[32,256]{1,0:T(8,128)S(1)}, u32[]{:S(2)}, u32[]{:S(2)}) collective-permute-start(f32[32,256]{1,0:T(8,128)S(1)} %get-tuple-element.10), channel_id=1, source_target_pairs={{0,5},{1,4},{2,7},{3,6},{4,1},{5,0},{6,3},{7,2},{8,13},{9,12},{10,... | collective-permute-start | bytes 98312 | tf_op jit(solution)/shard_map/ppermute | solution.py:328
  9.9 0.0 collective-permute-start.3
  9.9 0.9 %collective-permute-done.refs_0_ = f32[32,256]{1,0:T(8,128)S(1)} collective-permute-done((f32[32,256]{1,0:T(8,128)S(1)}, f32[32,256]{1,0:T(8,128)S(1)}, u32[]{:S(2)}, u32[]{:S(2)}) %collective-permute-start) | collective-permute-done | bytes 32800 | tf_op jit(solution)/shard_map/ppermute | solution.py:328
  10.7 2.8 %collective-permute-done.1.refs_1_ = f32[32,256]{1,0:T(8,128)S(1)} collective-permute-done((f32[32,256]{1,0:T(8,128)S(1)}, f32[32,256]{1,0:T(8,128)S(1)}, u32[]{:S(2)}, u32[]{:S(2)}) %collective-permute-start.1) | collective-permute-done | bytes 32800 | tf_op jit(solution)/shard_map/ppermute | solution.py:328
  13.5 0.0 collective-permute-done.2.refs_2_
  13.5 0.0 collective-permute-done.3.refs_3_
  13.5 2.5 %collective-permute-start.6 = (f32[16,256]{1,0:T(8,128)S(1)}, f32[16,256]{1,0:T(8,128)S(1)}, u32[]{:S(2)}, u32[]{:S(2)}) collective-permute-start(f32[16,256]{1,0:T(8,128)S(1)} %get-tuple-element.12.refs_0_), channel_id=1, source_target_pairs={{0,28},{1,29},{2,30},{3,31},{4,24},{5,25},{6,26},{7,27},{8,20},{9,... | collective-permute-start | bytes 49160 | tf_op jit(solution)/shard_map/ppermute | solution.py:328
  16.0 0.3 %collective-permute-start.5 = (f32[16,256]{1,0:T(8,128)S(1)}, f32[16,256]{1,0:T(8,128)S(1)}, u32[]{:S(2)}, u32[]{:S(2)}) collective-permute-start(f32[16,256]{1,0:T(8,128)S(1)} %get-tuple-element.12.refs_0_), channel_id=1, source_target_pairs={{0,20},{1,21},{2,22},{3,23},{4,16},{5,17},{6,18},{7,19},{8,28},{9,... | collective-permute-start | bytes 49160 | tf_op jit(solution)/shard_map/ppermute | solution.py:328
  16.3 0.5 %collective-permute-start.4 = (f32[16,256]{1,0:T(8,128)S(1)}, f32[16,256]{1,0:T(8,128)S(1)}, u32[]{:S(2)}, u32[]{:S(2)}) collective-permute-start(f32[16,256]{1,0:T(8,128)S(1)} %get-tuple-element.12.refs_0_), channel_id=1, source_target_pairs={{0,12},{1,13},{2,14},{3,15},{4,8},{5,9},{6,10},{7,11},{8,4},{9,5},... | collective-permute-start | bytes 49160 | tf_op jit(solution)/shard_map/ppermute | solution.py:328
  16.8 0.9 %collective-permute-done.6.refs_3_ = f32[16,256]{1,0:T(8,128)S(1)} collective-permute-done((f32[16,256]{1,0:T(8,128)S(1)}, f32[16,256]{1,0:T(8,128)S(1)}, u32[]{:S(2)}, u32[]{:S(2)}) %collective-permute-start.6) | collective-permute-done | bytes 16416 | tf_op jit(solution)/shard_map/ppermute | solution.py:328
  17.6 1.5 %collective-permute-done.5.refs_2_ = f32[16,256]{1,0:T(8,128)S(1)} collective-permute-done((f32[16,256]{1,0:T(8,128)S(1)}, f32[16,256]{1,0:T(8,128)S(1)}, u32[]{:S(2)}, u32[]{:S(2)}) %collective-permute-start.5) | collective-permute-done | bytes 16416 | tf_op jit(solution)/shard_map/ppermute | solution.py:328
  19.2 0.3 %collective-permute-done.4.refs_1_ = f32[16,256]{1,0:T(8,128)S(1)} collective-permute-done((f32[16,256]{1,0:T(8,128)S(1)}, f32[16,256]{1,0:T(8,128)S(1)}, u32[]{:S(2)}, u32[]{:S(2)}) %collective-permute-start.4) | collective-permute-done | bytes 16416 | tf_op jit(solution)/shard_map/ppermute | solution.py:328
  19.4 0.4 %collective-permute-start.7 = (f32[80,256]{1,0:T(8,128)S(1)}, f32[80,256]{1,0:T(8,128)S(1)}, u32[]{:S(2)}, u32[]{:S(2)}) collective-permute-start(f32[80,256]{1,0:T(8,128)S(1)} %stack.1.held), channel_id=1, source_target_pairs={{0,4},{1,5},{2,6},{3,7},{4,0},{5,1},{6,2},{7,3},{8,12},{9,13},{10,... | collective-permute-start | bytes 245768 | tf_op jit(solution)/shard_map/ppermute | solution.py:328
  20.4 0.3 %collective-permute-done.7.sent = f32[80,256]{1,0:T(8,128)S(1)} collective-permute-done((f32[80,256]{1,0:T(8,128)S(1)}, f32[80,256]{1,0:T(8,128)S(1)}, u32[]{:S(2)}, u32[]{:S(2)}) %collective-permute-start.7) | collective-permute-done | bytes 81952 | tf_op jit(solution)/shard_map/ppermute | solution.py:328
  20.7 2.1 %factors.1 = (f32[4,1024]{1,0:T(4,128)}, f32[4,64,64]{2,1,0:T(8,128)}) custom-call(f32[1]{0:T(128)S(6)} %copy.10.damping, f32[80,256]{1,0:T(8,128)S(1)} %stack.1.held, f32[80,256]{1,0:T(8,128)S(1)} %collective-permute-done.7.sent), custom_call_target="tpu_custom_call" | custom-call | tf_op jit(solution)/shard_map/factors/pallas_call | solution.py:429
  (2 shorter events, 0.0 us)
Async XLA Ops:
  4.4 6.3 %collective-permute-start = (f32[32,256]{1,0:T(8,128)S(1)}, f32[32,256]{1,0:T(8,128)S(1)}, u32[]{:S(2)}, u32[]{:S(2)}) collective-permute-start(f32[32,256]{1,0:T(8,128)S(1)} %get-tuple-element.8), channel_id=1, source_target_pairs={{0,7},{1,6},{2,5},{3,4},{4,3},{5,2},{6,1},{7,0},{8,15},{9,14},{10,... | collective-permute-start | bytes 98312 | tf_op jit(solution)/shard_map/ppermute | solution.py:328
  8.9 4.5 %collective-permute-start.1 = (f32[32,256]{1,0:T(8,128)S(1)}, f32[32,256]{1,0:T(8,128)S(1)}, u32[]{:S(2)}, u32[]{:S(2)}) collective-permute-start(f32[32,256]{1,0:T(8,128)S(1)} %get-tuple-element.9), channel_id=1, source_target_pairs={{0,6},{1,7},{2,4},{3,5},{4,2},{5,3},{6,0},{7,1},{8,14},{9,15},{10,... | collective-permute-start | bytes 98312 | tf_op jit(solution)/shard_map/ppermute | solution.py:328
  8.9 4.5 %collective-permute-start.2 = (f32[32,256]{1,0:T(8,128)S(1)}, f32[32,256]{1,0:T(8,128)S(1)}, u32[]{:S(2)}, u32[]{:S(2)}) collective-permute-start(f32[32,256]{1,0:T(8,128)S(1)} %get-tuple-element.10), channel_id=1, source_target_pairs={{0,5},{1,4},{2,7},{3,6},{4,1},{5,0},{6,3},{7,2},{8,13},{9,12},{10,... | collective-permute-start | bytes 98312 | tf_op jit(solution)/shard_map/ppermute | solution.py:328
  9.9 3.6 %collective-permute-start.3 = (f32[32,256]{1,0:T(8,128)S(1)}, f32[32,256]{1,0:T(8,128)S(1)}, u32[]{:S(2)}, u32[]{:S(2)}) collective-permute-start(f32[32,256]{1,0:T(8,128)S(1)} %get-tuple-element.11), channel_id=1, source_target_pairs={{0,4},{1,5},{2,6},{3,7},{4,0},{5,1},{6,2},{7,3},{8,12},{9,13},{10,... | collective-permute-start | bytes 98312 | tf_op jit(solution)/shard_map/ppermute | solution.py:328
  13.5 4.1 %collective-permute-start.6 = (f32[16,256]{1,0:T(8,128)S(1)}, f32[16,256]{1,0:T(8,128)S(1)}, u32[]{:S(2)}, u32[]{:S(2)}) collective-permute-start(f32[16,256]{1,0:T(8,128)S(1)} %get-tuple-element.12.refs_0_), channel_id=1, source_target_pairs={{0,28},{1,29},{2,30},{3,31},{4,24},{5,25},{6,26},{7,27},{8,20},{9,... | collective-permute-start | bytes 49160 | tf_op jit(solution)/shard_map/ppermute | solution.py:328
  16.0 3.2 %collective-permute-start.5 = (f32[16,256]{1,0:T(8,128)S(1)}, f32[16,256]{1,0:T(8,128)S(1)}, u32[]{:S(2)}, u32[]{:S(2)}) collective-permute-start(f32[16,256]{1,0:T(8,128)S(1)} %get-tuple-element.12.refs_0_), channel_id=1, source_target_pairs={{0,20},{1,21},{2,22},{3,23},{4,16},{5,17},{6,18},{7,19},{8,28},{9,... | collective-permute-start | bytes 49160 | tf_op jit(solution)/shard_map/ppermute | solution.py:328
  16.3 3.2 %collective-permute-start.4 = (f32[16,256]{1,0:T(8,128)S(1)}, f32[16,256]{1,0:T(8,128)S(1)}, u32[]{:S(2)}, u32[]{:S(2)}) collective-permute-start(f32[16,256]{1,0:T(8,128)S(1)} %get-tuple-element.12.refs_0_), channel_id=1, source_target_pairs={{0,12},{1,13},{2,14},{3,15},{4,8},{5,9},{6,10},{7,11},{8,4},{9,5},... | collective-permute-start | bytes 49160 | tf_op jit(solution)/shard_map/ppermute | solution.py:328
  19.4 1.3 %collective-permute-start.7 = (f32[80,256]{1,0:T(8,128)S(1)}, f32[80,256]{1,0:T(8,128)S(1)}, u32[]{:S(2)}, u32[]{:S(2)}) collective-permute-start(f32[80,256]{1,0:T(8,128)S(1)} %stack.1.held), channel_id=1, source_target_pairs={{0,4},{1,5},{2,6},{3,7},{4,0},{5,1},{6,2},{7,3},{8,12},{9,13},{10,... | collective-permute-start | bytes 245768 | tf_op jit(solution)/shard_map/ppermute | solution.py:328

commit v22 on v21

--- a/solution.py
+++ b/solution.py
@@ -14,7 +14,7 @@
 SLOT = 32
 GROUP = LANES // SLOT
 PANEL = 8
-PIECES = 4
+CHUNK = 1024
 
 
 def dot_nt(a, b):
@@ -45,7 +45,7 @@
     *refs,
 ):
     sends, refs = refs[:parts], refs[parts:]
-    acts, grads, weights_in, weights_out, order, low, mask, out, sems, order_sem = refs
+    acts, grads, weights_in, weights_out, turned_in, turned_out, order, low, mask, out, sems = refs
     tokens, width = acts.shape
     rank = down_hbm.shape[1]
     sketch = proj_in_hbm.shape[1]
@@ -53,71 +53,68 @@
     per = rank // parts
     halves = sketch // SLOT
 
-    def copy_in(source, target, sem):
-        copy = pltpu.make_async_copy(source, target, sem)
+    number = itertools.count()
+
+    def copy_in(source, target):
+        copy = pltpu.make_async_copy(source, target, sems.at[next(number)])
         copy.start()
         return copy
 
-    order_copy = copy_in(order_hbm.at[0], order, order_sem)
-    pending = []
-    for n, (data_hbm, data, first_hbm, second_hbm, weights, count) in enumerate(
-        [
-            (grads_hbm, grads, proj_out_hbm, up_hbm, weights_out, 1),
-            (acts_hbm, acts, proj_in_hbm, down_hbm, weights_in, PIECES),
+    def weight_copies(first_hbm, second_hbm, weights):
+        return [
+            copy_in(first_hbm.at[0], weights.at[pl.ds(0, sketch)]),
+            copy_in(second_hbm.at[0], weights.at[pl.ds(sketch, rank)]),
         ]
-    ):
-        first = [
-            copy_in(first_hbm.at[0], weights.at[pl.ds(0, sketch)], sems.at[n, 0]),
-            copy_in(second_hbm.at[0], weights.at[pl.ds(sketch, rank)], sems.at[n, 1]),
-        ]
-        pieces = []
-        for i in range(count):
-            here = pl.ds(i * (tokens // count), tokens // count)
-            pieces.append(
-                (here, copy_in(data_hbm.at[0, here], data.at[here], sems.at[n, 2 + i]))
-            )
-        pending.append((first, pieces))
-    def product(n, data, weights):
-        first, pieces = pending[n]
-        for copy in first:
-            copy.wait()
-        terms = []
-        for here, copy in pieces:
-            copy.wait()
-            terms.append(dot_nt(data[here, :], weights[...]))
-        return jnp.concatenate(terms, axis=0)
-
-    from_grads = product(0, grads, weights_out)
+
+    order_copy = copy_in(order_hbm.at[0], order)
+    out_copies = weight_copies(proj_out_hbm, up_hbm, weights_out)
+    grads_copy = copy_in(grads_hbm.at[0], grads)
+    in_copies = weight_copies(proj_in_hbm, down_hbm, weights_in)
+    strips = [pl.ds(start, CHUNK) for start in range(0, width, CHUNK)]
+    acts_copies = [copy_in(acts_hbm.at[0, :, here], acts.at[:, here]) for here in strips]
+
+    rows = examples * parts
     order_copy.wait()
-    rows = examples * parts
-    lane = lax.broadcasted_iota(jnp.int32, (rows, 2 * tokens), 1)
-    source = (lane % tokens) // EXAMPLE_LENGTH
-    target = jnp.zeros((8, 2 * tokens), jnp.int32)
+    source = lax.broadcasted_iota(jnp.int32, (8, tokens), 1) // EXAMPLE_LENGTH
+    target = jnp.zeros((8, tokens), jnp.int32)
     for s in range(examples):
-        target = jnp.where(source[:8] == s, order[0, s], target)
+        target = jnp.where(source == s, order[0, s], target)
     target = jnp.concatenate([target] * (rows // 8), axis=0)
-    place = lax.broadcasted_iota(jnp.int32, (rows, 2 * tokens), 0) // parts
+    place = lax.broadcasted_iota(jnp.int32, (rows, tokens), 0) // parts
     mask[...] = jnp.where(target == place, scaling, 0.0)
 
-    from_acts = product(1, acts, weights_in)
-    low[0] = jnp.transpose(from_grads)[sketch:]
-    low[1] = jnp.transpose(from_acts)[sketch:]
+    def spread_low(values, n):
+        low[n] = jnp.transpose(values)[sketch:]
+        tiles = []
+        for c in range(per):
+            chosen = low[n, pl.ds(c, parts, stride=per), :]
+            chosen = jnp.concatenate([chosen] * max(1, 8 // parts), axis=0)
+            chosen = jnp.concatenate([chosen] * (rows // chosen.shape[0]), axis=0)
+            tiles.append(split(chosen * mask[...]))
+        return [jnp.concatenate(half, axis=0) for half in zip(*tiles)]
+
+    for copy in out_copies:
+        copy.wait()
+    turned_out[...] = jnp.transpose(weights_out[...])
+    grads_copy.wait()
+    from_grads = dot_nn(grads[...], turned_out[...])
+    left_grads = spread_low(from_grads, 0)
+    for copy in in_copies:
+        copy.wait()
+    for here in strips:
+        turned_in[here, :] = jnp.transpose(weights_in[:, here])
+    from_acts = None
+    for here, copy in zip(strips, acts_copies):
+        copy.wait()
+        term = dot_nn(acts[:, here], turned_in[here, :])
+        from_acts = term if from_acts is None else from_acts + term
+    left_acts = spread_low(from_acts, 1)
+    left_high, left_low = [
+        jnp.concatenate(pair, axis=1) for pair in zip(left_grads, left_acts)
+    ]
     right_high, right_low = split(
         jnp.concatenate([from_acts[:, :sketch], from_grads[:, :sketch]], axis=0)
     )
-
-    highs, lows = [], []
-    for c in range(per):
-        chosen = jnp.concatenate(
-            [low[i, pl.ds(c, parts, stride=per), :] for i in range(2)], axis=1
-        )
-        chosen = jnp.concatenate([chosen] * max(1, 8 // parts), axis=0)
-        chosen = jnp.concatenate([chosen] * (rows // chosen.shape[0]), axis=0)
-        high, rest = split(chosen * mask[...])
-        highs.append(high)
-        lows.append(rest)
-    left_high = jnp.concatenate(highs, axis=0)
-    left_low = jnp.concatenate(lows, axis=0)
     both = jnp.dot(
         jnp.concatenate([left_high, left_low], axis=0),
         right_high,
@@ -386,12 +383,13 @@
             pltpu.VMEM((tokens, key_width), grads.dtype),
             pltpu.VMEM((sketch + rank, width), acts.dtype),
             pltpu.VMEM((sketch + rank, key_width), grads.dtype),
+            pltpu.VMEM((width, sketch + rank), acts.dtype),
+            pltpu.VMEM((key_width, sketch + rank), grads.dtype),
             pltpu.SMEM(order.shape[1:], order.dtype),
             pltpu.VMEM((2, rank, tokens), jnp.float32),
-            pltpu.VMEM((examples * parts, 2 * tokens), jnp.float32),
+            pltpu.VMEM((examples * parts, tokens), jnp.float32),
             pltpu.VMEM((examples * parts, LANES), jnp.float32),
-            pltpu.SemaphoreType.DMA((2, 2 + PIECES)),
-            pltpu.SemaphoreType.DMA,
+            pltpu.SemaphoreType.DMA((6 + width // CHUNK,)),
         ],
         compiler_params=pltpu.CompilerParams(vmem_limit_bytes=8 * 2**20),
         name="partials",

time: 23 us -> 22.3 us (0.970)
  Pallas kernels: 5.87 us -> 5.15 us
    pallas_call x1, Pallas kernels: 3.75 us -> 3.03 us  [local(): pl.pallas_call(functools.partial(partial_kernel, parts, scaling), out_sha...]
where the time goes in v22:
time: 22.3 us; the launch traced here: 22.1 us
  starting transfers between devices  9.08 us (41%)
  waiting for transfers between devices  6.58 us (30%)
  Pallas kernels  5.15 us (23%)
  between operations  1.3 us (6%)
    ppermute x8, starting transfers between devices, exchange(): lax.ppermute(x, ('ex', 'mp'), [(m * parts + b, (m ^ ex_distance) * parts...  9.08 us
    ppermute x8, waiting for transfers between devices, exchange(): lax.ppermute(x, ('ex', 'mp'), [(m * parts + b, (m ^ ex_distance) * parts...  6.58 us
    pallas_call x1, Pallas kernels, local(): pl.pallas_call(functools.partial(partial_kernel, parts, scaling), out_sha...  3.03 us
    pallas_call x1, Pallas kernels, local(): pl.pallas_call(functools.partial(factor_kernel, parts), out_shape=[jax.Sh...  2.11 us
  transfers between devices with their start and end apart: 8, of which 6 were waited for; matrix products, arithmetic and copies ran while one was open for 0% of the time, Pallas kernels for 0%

profile of v22, /device:TPU:0, one launch (start us, length us, event | category | flops | bytes accessed | tf_op | source)
XLA Modules:
  0.0 22.1 jit_solution(7933114413009889888)
XLA Ops:
  0.6 3.0 %partials.1 = (f32[32,256]{1,0:T(8,128)S(1)}, f32[32,256]{1,0:T(8,128)S(1)}, f32[32,256]{1,0:T(8,128)S(1)}, f32[32,256]{1,0:T(8,128)S(1)}) custom-call(bf16[1,128,4096]{2,1,0:T(8,128)(2,1)} %acts_hbm.1, bf16[1,128,1024]{2,1,0:T(8,128)(2,1)} %grads_hbm.1, bf16[1,16,4096]{2,1,0:T(8,128)(2,1)} %down_hbm.1, bf16[1,16,1024]{2,1,0:T(8,128)(2,1)} %up_hbm.1, ...), custom_call_target="tpu_custom_call" | custom-call | tf_op jit(solution)/shard_map/partials/pallas_call | solution.py:376
  3.7 4.6 %collective-permute-start = (f32[32,256]{1,0:T(8,128)S(1)}, f32[32,256]{1,0:T(8,128)S(1)}, u32[]{:S(2)}, u32[]{:S(2)}) collective-permute-start(f32[32,256]{1,0:T(8,128)S(1)} %get-tuple-element.8), channel_id=1, source_target_pairs={{0,7},{1,6},{2,5},{3,4},{4,3},{5,2},{6,1},{7,0},{8,15},{9,14},{10,... | collective-permute-start | bytes 98312 | tf_op jit(solution)/shard_map/ppermute | solution.py:325
  8.2 0.0 collective-permute-start.1
  8.2 0.9 %collective-permute-start.2 = (f32[32,256]{1,0:T(8,128)S(1)}, f32[32,256]{1,0:T(8,128)S(1)}, u32[]{:S(2)}, u32[]{:S(2)}) collective-permute-start(f32[32,256]{1,0:T(8,128)S(1)} %get-tuple-element.10), channel_id=1, source_target_pairs={{0,5},{1,4},{2,7},{3,6},{4,1},{5,0},{6,3},{7,2},{8,13},{9,12},{10,... | collective-permute-start | bytes 98312 | tf_op jit(solution)/shard_map/ppermute | solution.py:325
  9.1 0.0 collective-permute-start.3
  9.1 0.9 %collective-permute-done.refs_0_ = f32[32,256]{1,0:T(8,128)S(1)} collective-permute-done((f32[32,256]{1,0:T(8,128)S(1)}, f32[32,256]{1,0:T(8,128)S(1)}, u32[]{:S(2)}, u32[]{:S(2)}) %collective-permute-start) | collective-permute-done | bytes 32800 | tf_op jit(solution)/shard_map/ppermute | solution.py:325
  10.0 2.8 %collective-permute-done.1.refs_1_ = f32[32,256]{1,0:T(8,128)S(1)} collective-permute-done((f32[32,256]{1,0:T(8,128)S(1)}, f32[32,256]{1,0:T(8,128)S(1)}, u32[]{:S(2)}, u32[]{:S(2)}) %collective-permute-start.1) | collective-permute-done | bytes 32800 | tf_op jit(solution)/shard_map/ppermute | solution.py:325
  12.8 0.0 collective-permute-done.2.refs_2_
  12.8 0.0 collective-permute-done.3.refs_3_
  12.8 2.5 %collective-permute-start.6 = (f32[16,256]{1,0:T(8,128)S(1)}, f32[16,256]{1,0:T(8,128)S(1)}, u32[]{:S(2)}, u32[]{:S(2)}) collective-permute-start(f32[16,256]{1,0:T(8,128)S(1)} %get-tuple-element.12.refs_0_), channel_id=1, source_target_pairs={{0,28},{1,29},{2,30},{3,31},{4,24},{5,25},{6,26},{7,27},{8,20},{9,... | collective-permute-start | bytes 49160 | tf_op jit(solution)/shard_map/ppermute | solution.py:325
  15.3 0.3 %collective-permute-start.5 = (f32[16,256]{1,0:T(8,128)S(1)}, f32[16,256]{1,0:T(8,128)S(1)}, u32[]{:S(2)}, u32[]{:S(2)}) collective-permute-start(f32[16,256]{1,0:T(8,128)S(1)} %get-tuple-element.12.refs_0_), channel_id=1, source_target_pairs={{0,20},{1,21},{2,22},{3,23},{4,16},{5,17},{6,18},{7,19},{8,28},{9,... | collective-permute-start | bytes 49160 | tf_op jit(solution)/shard_map/ppermute | solution.py:325
  15.5 0.5 %collective-permute-start.4 = (f32[16,256]{1,0:T(8,128)S(1)}, f32[16,256]{1,0:T(8,128)S(1)}, u32[]{:S(2)}, u32[]{:S(2)}) collective-permute-start(f32[16,256]{1,0:T(8,128)S(1)} %get-tuple-element.12.refs_0_), channel_id=1, source_target_pairs={{0,12},{1,13},{2,14},{3,15},{4,8},{5,9},{6,10},{7,11},{8,4},{9,5},... | collective-permute-start | bytes 49160 | tf_op jit(solution)/shard_map/ppermute | solution.py:325
  16.0 0.9 %collective-permute-done.6.refs_3_ = f32[16,256]{1,0:T(8,128)S(1)} collective-permute-done((f32[16,256]{1,0:T(8,128)S(1)}, f32[16,256]{1,0:T(8,128)S(1)}, u32[]{:S(2)}, u32[]{:S(2)}) %collective-permute-start.6) | collective-permute-done | bytes 16416 | tf_op jit(solution)/shard_map/ppermute | solution.py:325
  16.9 1.5 %collective-permute-done.5.refs_2_ = f32[16,256]{1,0:T(8,128)S(1)} collective-permute-done((f32[16,256]{1,0:T(8,128)S(1)}, f32[16,256]{1,0:T(8,128)S(1)}, u32[]{:S(2)}, u32[]{:S(2)}) %collective-permute-start.5) | collective-permute-done | bytes 16416 | tf_op jit(solution)/shard_map/ppermute | solution.py:325
  18.4 0.3 %collective-permute-done.4.refs_1_ = f32[16,256]{1,0:T(8,128)S(1)} collective-permute-done((f32[16,256]{1,0:T(8,128)S(1)}, f32[16,256]{1,0:T(8,128)S(1)}, u32[]{:S(2)}, u32[]{:S(2)}) %collective-permute-start.4) | collective-permute-done | bytes 16416 | tf_op jit(solution)/shard_map/ppermute | solution.py:325
  18.7 0.3 %collective-permute-start.7 = (f32[80,256]{1,0:T(8,128)S(1)}, f32[80,256]{1,0:T(8,128)S(1)}, u32[]{:S(2)}, u32[]{:S(2)}) collective-permute-start(f32[80,256]{1,0:T(8,128)S(1)} %stack.1.held), channel_id=1, source_target_pairs={{0,4},{1,5},{2,6},{3,7},{4,0},{5,1},{6,2},{7,3},{8,12},{9,13},{10,... | collective-permute-start | bytes 245768 | tf_op jit(solution)/shard_map/ppermute | solution.py:325
  19.7 0.3 %collective-permute-done.7.sent = f32[80,256]{1,0:T(8,128)S(1)} collective-permute-done((f32[80,256]{1,0:T(8,128)S(1)}, f32[80,256]{1,0:T(8,128)S(1)}, u32[]{:S(2)}, u32[]{:S(2)}) %collective-permute-start.7) | collective-permute-done | bytes 81952 | tf_op jit(solution)/shard_map/ppermute | solution.py:325
  20.0 2.1 %factors.1 = (f32[4,1024]{1,0:T(4,128)}, f32[4,64,64]{2,1,0:T(8,128)}) custom-call(f32[1]{0:T(128)S(6)} %copy.10.damping, f32[80,256]{1,0:T(8,128)S(1)} %stack.1.held, f32[80,256]{1,0:T(8,128)S(1)} %collective-permute-done.7.sent), custom_call_target="tpu_custom_call" | custom-call | tf_op jit(solution)/shard_map/factors/pallas_call | solution.py:427
  (2 shorter events, 0.0 us)
Async XLA Ops:
  3.7 6.3 %collective-permute-start = (f32[32,256]{1,0:T(8,128)S(1)}, f32[32,256]{1,0:T(8,128)S(1)}, u32[]{:S(2)}, u32[]{:S(2)}) collective-permute-start(f32[32,256]{1,0:T(8,128)S(1)} %get-tuple-element.8), channel_id=1, source_target_pairs={{0,7},{1,6},{2,5},{3,4},{4,3},{5,2},{6,1},{7,0},{8,15},{9,14},{10,... | collective-permute-start | bytes 98312 | tf_op jit(solution)/shard_map/ppermute | solution.py:325
  8.2 4.5 %collective-permute-start.1 = (f32[32,256]{1,0:T(8,128)S(1)}, f32[32,256]{1,0:T(8,128)S(1)}, u32[]{:S(2)}, u32[]{:S(2)}) collective-permute-start(f32[32,256]{1,0:T(8,128)S(1)} %get-tuple-element.9), channel_id=1, source_target_pairs={{0,6},{1,7},{2,4},{3,5},{4,2},{5,3},{6,0},{7,1},{8,14},{9,15},{10,... | collective-permute-start | bytes 98312 | tf_op jit(solution)/shard_map/ppermute | solution.py:325
  8.2 4.5 %collective-permute-start.2 = (f32[32,256]{1,0:T(8,128)S(1)}, f32[32,256]{1,0:T(8,128)S(1)}, u32[]{:S(2)}, u32[]{:S(2)}) collective-permute-start(f32[32,256]{1,0:T(8,128)S(1)} %get-tuple-element.10), channel_id=1, source_target_pairs={{0,5},{1,4},{2,7},{3,6},{4,1},{5,0},{6,3},{7,2},{8,13},{9,12},{10,... | collective-permute-start | bytes 98312 | tf_op jit(solution)/shard_map/ppermute | solution.py:325
  9.1 3.6 %collective-permute-start.3 = (f32[32,256]{1,0:T(8,128)S(1)}, f32[32,256]{1,0:T(8,128)S(1)}, u32[]{:S(2)}, u32[]{:S(2)}) collective-permute-start(f32[32,256]{1,0:T(8,128)S(1)} %get-tuple-element.11), channel_id=1, source_target_pairs={{0,4},{1,5},{2,6},{3,7},{4,0},{5,1},{6,2},{7,3},{8,12},{9,13},{10,... | collective-permute-start | bytes 98312 | tf_op jit(solution)/shard_map/ppermute | solution.py:325
  12.8 4.1 %collective-permute-start.6 = (f32[16,256]{1,0:T(8,128)S(1)}, f32[16,256]{1,0:T(8,128)S(1)}, u32[]{:S(2)}, u32[]{:S(2)}) collective-permute-start(f32[16,256]{1,0:T(8,128)S(1)} %get-tuple-element.12.refs_0_), channel_id=1, source_target_pairs={{0,28},{1,29},{2,30},{3,31},{4,24},{5,25},{6,26},{7,27},{8,20},{9,... | collective-permute-start | bytes 49160 | tf_op jit(solution)/shard_map/ppermute | solution.py:325
  15.3 3.2 %collective-permute-start.5 = (f32[16,256]{1,0:T(8,128)S(1)}, f32[16,256]{1,0:T(8,128)S(1)}, u32[]{:S(2)}, u32[]{:S(2)}) collective-permute-start(f32[16,256]{1,0:T(8,128)S(1)} %get-tuple-element.12.refs_0_), channel_id=1, source_target_pairs={{0,20},{1,21},{2,22},{3,23},{4,16},{5,17},{6,18},{7,19},{8,28},{9,... | collective-permute-start | bytes 49160 | tf_op jit(solution)/shard_map/ppermute | solution.py:325
  15.5 3.2 %collective-permute-start.4 = (f32[16,256]{1,0:T(8,128)S(1)}, f32[16,256]{1,0:T(8,128)S(1)}, u32[]{:S(2)}, u32[]{:S(2)}) collective-permute-start(f32[16,256]{1,0:T(8,128)S(1)} %get-tuple-element.12.refs_0_), channel_id=1, source_target_pairs={{0,12},{1,13},{2,14},{3,15},{4,8},{5,9},{6,10},{7,11},{8,4},{9,5},... | collective-permute-start | bytes 49160 | tf_op jit(solution)/shard_map/ppermute | solution.py:325
  18.7 1.3 %collective-permute-start.7 = (f32[80,256]{1,0:T(8,128)S(1)}, f32[80,256]{1,0:T(8,128)S(1)}, u32[]{:S(2)}, u32[]{:S(2)}) collective-permute-start(f32[80,256]{1,0:T(8,128)S(1)} %stack.1.held), channel_id=1, source_target_pairs={{0,4},{1,5},{2,6},{3,7},{4,0},{5,1},{6,2},{7,3},{8,12},{9,13},{10,... | collective-permute-start | bytes 245768 | tf_op jit(solution)/shard_map/ppermute | solution.py:325

commit v23 on v16

--- a/solution.py
+++ b/solution.py
@@ -197,29 +197,18 @@
     return guess * (2.0 - x * guess)
 
 
-def factor_kernel(parts, damping, held, sent, features, factors):
-    channels, sketch, _ = factors.shape
-    examples = features.shape[0] * parts
-    gathered = held.shape[0] - examples
-    span = features.shape[1] // parts
-    write_features(sent[gathered:, :span], parts, channels, features)
-    halves = sketch // SLOT
-    panels = sketch // PANEL
+def gram_tiles(rows):
+    halves = rows.shape[1] // LANES
     per_half = SLOT // PANEL
-    stacked = jnp.concatenate([held[:gathered, :], sent[:gathered, :]], axis=0)
-    high, rest = split(stacked)
-    turned_high, turned_rest = split(jnp.transpose(stacked))
+    high, rest = split(rows)
+    turned_high, turned_rest = split(jnp.transpose(rows))
     gram = dot_nn(turned_high, rest) + dot_nn(
         jnp.concatenate([turned_rest, turned_high], axis=1),
         jnp.concatenate([high, high], axis=0),
     )
-    lane = lax.broadcasted_iota(jnp.int32, (PANEL, LANES), 1)
-    sub = lax.broadcasted_iota(jnp.int32, (PANEL, LANES), 0)
-    slot = lane // SLOT
-    within = lane % SLOT
-    ridge = damping[0]
-    tile = []
-    for q in range(panels):
+    slot = lax.broadcasted_iota(jnp.int32, (PANEL, LANES), 1) // SLOT
+    tiles = []
+    for q in range(halves * per_half):
         hr, at = divmod(q, per_half)
         line = []
         for h in range(halves):
@@ -228,11 +217,38 @@
                 start = hr * LANES + c * SLOT + at * PANEL
                 block = gram[start : start + PANEL, h * LANES : (h + 1) * LANES]
                 value = block if c == 0 else jnp.where(slot == c, block, value)
-            value = value * (1.0 / stacked.shape[0])
+            line.append(value)
+        tiles.append(line)
+    return tiles
+
+
+def gram_kernel(gathered, held, own_tiles):
+    for q, line in enumerate(gram_tiles(held[:gathered, :])):
+        for h, value in enumerate(line):
+            own_tiles[q * PANEL : (q + 1) * PANEL, h * LANES : (h + 1) * LANES] = value
+
+
+def factor_kernel(parts, gathered, damping, own_tiles, sent, features, factors):
+    channels, sketch, _ = factors.shape
+    halves = sketch // SLOT
+    panels = sketch // PANEL
+    per_half = SLOT // PANEL
+    span = features.shape[1] // parts
+    write_features(sent[gathered:, :span], parts, channels, features)
+    lane = lax.broadcasted_iota(jnp.int32, (PANEL, LANES), 1)
+    sub = lax.broadcasted_iota(jnp.int32, (PANEL, LANES), 0)
+    slot = lane // SLOT
+    within = lane % SLOT
+    ridge = damping[0]
+    tile = gram_tiles(sent[:gathered, :])
+    for q in range(panels):
+        hr, at = divmod(q, per_half)
+        for h in range(halves):
+            own = own_tiles[q * PANEL : (q + 1) * PANEL, h * LANES : (h + 1) * LANES]
+            value = (tile[q][h] + own) * (1.0 / (2 * gathered))
             if h == hr:
                 value = value + jnp.where(within == at * PANEL + sub, ridge, 0.0)
-            line.append(value)
-        tile.append(line)
+            tile[q][h] = value
 
     zero = jnp.zeros((PANEL, LANES), jnp.float32)
     finished = []
@@ -431,8 +447,20 @@
         name="stack",
     )(*in_vmem(*near))
     sent = exchange(held, 1)
+    gathered = held.shape[0] - examples
+    own_tiles = pl.pallas_call(
+        functools.partial(gram_kernel, gathered),
+        out_shape=pltpu.VMEM((sketch, padded), jnp.float32),
+        in_specs=[vmem()],
+        out_specs=vmem(),
+        compiler_params=pltpu.CompilerParams(vmem_limit_bytes=8 * 2**20),
+        cost_estimate=pl.CostEstimate(
+            flops=6 * gathered * padded * padded, bytes_accessed=0, transcendentals=0
+        ),
+        name="gram",
+    )(*in_vmem(held))
     return pl.pallas_call(
-        functools.partial(factor_kernel, parts),
+        functools.partial(factor_kernel, parts, gathered),
         out_shape=[
             jax.ShapeDtypeStruct((examples // parts, rank * sketch), jnp.float32),
             jax.ShapeDtypeStruct((per, sketch, sketch), jnp.float32),
@@ -441,7 +469,7 @@
         out_specs=[vmem()] * 2,
         compiler_params=pltpu.CompilerParams(vmem_limit_bytes=8 * 2**20),
         name="factors",
-    )(damping, *in_vmem(held, sent))
+    )(damping, *in_vmem(own_tiles, sent))
 
 
 def solution(mesh):

time: 21.8 us -> 22 us (level)
  Pallas kernels: 4.68 us -> 5.14 us
  waiting for transfers between devices: 6.56 us -> 6.29 us
    pallas_call x1 -> x2, Pallas kernels: 2.07 us -> 2.54 us  [the longest x1 2.14 us: local(): pl.pallas_call(functools.partial(factor_kernel, parts, gathered), out_sha...]
    ppermute x8, waiting for transfers between devices: 6.56 us -> 6.29 us  [exchange(): lax.ppermute(x, ('ex', 'mp'), [(m * parts + b, (m ^ ex_distance) * parts...]
  transfers between devices with their start and end apart: 8 -> 8, of which waited for: 6 -> 5; matrix products, arithmetic and copies ran while one was open for 0% -> 0% of each run, Pallas kernels for 0% -> 2%
where the time goes in v23:
time: 22 us; the launch traced here: 21.8 us
  starting transfers between devices  9.08 us (41%)
  waiting for transfers between devices  6.29 us (29%)
  Pallas kernels  5.14 us (23%)
  between operations  1.32 us (6%)
    ppermute x8, starting transfers between devices, exchange(): lax.ppermute(x, ('ex', 'mp'), [(m * parts + b, (m ^ ex_distance) * parts...  9.08 us
    ppermute x8, waiting for transfers between devices, exchange(): lax.ppermute(x, ('ex', 'mp'), [(m * parts + b, (m ^ ex_distance) * parts...  6.29 us
    pallas_call x1, Pallas kernels, local(): pl.pallas_call(functools.partial(partial_kernel, parts, scaling), out_sha...  2.59 us
    pallas_call x1, Pallas kernels, local(): pl.pallas_call(functools.partial(factor_kernel, parts, gathered), out_sha...  2.14 us
  transfers between devices with their start and end apart: 8, of which 5 were waited for; matrix products, arithmetic and copies ran while one was open for 0% of the time, Pallas kernels for 2%

profile of v23, /device:TPU:0, one launch (start us, length us, event | category | flops | bytes accessed | tf_op | source)
XLA Modules:
  0.0 21.8 jit_solution(7193563978334067958)
XLA Ops:
  0.6 2.6 %partials.1 = (f32[32,256]{1,0:T(8,128)S(1)}, f32[32,256]{1,0:T(8,128)S(1)}, f32[32,256]{1,0:T(8,128)S(1)}, f32[32,256]{1,0:T(8,128)S(1)}) custom-call(bf16[1,128,4096]{2,1,0:T(8,128)(2,1)} %acts_hbm.1, bf16[1,128,1024]{2,1,0:T(8,128)(2,1)} %grads_hbm.1, bf16[1,16,4096]{2,1,0:T(8,128)(2,1)} %down_hbm.1, bf16[1,16,1024]{2,1,0:T(8,128)(2,1)} %up_hbm.1, ...), custom_call_target="tpu_custom_call" | custom-call | tf_op jit(solution)/shard_map/partials/pallas_call | solution.py:400
  3.2 4.6 %collective-permute-start = (f32[32,256]{1,0:T(8,128)S(1)}, f32[32,256]{1,0:T(8,128)S(1)}, u32[]{:S(2)}, u32[]{:S(2)}) collective-permute-start(f32[32,256]{1,0:T(8,128)S(1)} %get-tuple-element.8), channel_id=1, source_target_pairs={{0,7},{1,6},{2,5},{3,4},{4,3},{5,2},{6,1},{7,0},{8,15},{9,14},{10,... | collective-permute-start | bytes 98312 | tf_op jit(solution)/shard_map/ppermute | solution.py:349
  7.8 0.0 collective-permute-start.1
  7.8 0.9 %collective-permute-start.2 = (f32[32,256]{1,0:T(8,128)S(1)}, f32[32,256]{1,0:T(8,128)S(1)}, u32[]{:S(2)}, u32[]{:S(2)}) collective-permute-start(f32[32,256]{1,0:T(8,128)S(1)} %get-tuple-element.10), channel_id=1, source_target_pairs={{0,5},{1,4},{2,7},{3,6},{4,1},{5,0},{6,3},{7,2},{8,13},{9,12},{10,... | collective-permute-start | bytes 98312 | tf_op jit(solution)/shard_map/ppermute | solution.py:349
  8.7 0.0 collective-permute-start.3
  8.7 0.9 %collective-permute-done.refs_0_ = f32[32,256]{1,0:T(8,128)S(1)} collective-permute-done((f32[32,256]{1,0:T(8,128)S(1)}, f32[32,256]{1,0:T(8,128)S(1)}, u32[]{:S(2)}, u32[]{:S(2)}) %collective-permute-start) | collective-permute-done | bytes 32800 | tf_op jit(solution)/shard_map/ppermute | solution.py:349
  9.6 2.8 %collective-permute-done.1.refs_1_ = f32[32,256]{1,0:T(8,128)S(1)} collective-permute-done((f32[32,256]{1,0:T(8,128)S(1)}, f32[32,256]{1,0:T(8,128)S(1)}, u32[]{:S(2)}, u32[]{:S(2)}) %collective-permute-start.1) | collective-permute-done | bytes 32800 | tf_op jit(solution)/shard_map/ppermute | solution.py:349
  12.3 0.0 collective-permute-done.2.refs_2_
  12.3 0.0 collective-permute-done.3.refs_3_
  12.3 2.5 %collective-permute-start.6 = (f32[16,256]{1,0:T(8,128)S(1)}, f32[16,256]{1,0:T(8,128)S(1)}, u32[]{:S(2)}, u32[]{:S(2)}) collective-permute-start(f32[16,256]{1,0:T(8,128)S(1)} %get-tuple-element.12.refs_0_), channel_id=1, source_target_pairs={{0,28},{1,29},{2,30},{3,31},{4,24},{5,25},{6,26},{7,27},{8,20},{9,... | collective-permute-start | bytes 49160 | tf_op jit(solution)/shard_map/ppermute | solution.py:349
  14.8 0.3 %collective-permute-start.5 = (f32[16,256]{1,0:T(8,128)S(1)}, f32[16,256]{1,0:T(8,128)S(1)}, u32[]{:S(2)}, u32[]{:S(2)}) collective-permute-start(f32[16,256]{1,0:T(8,128)S(1)} %get-tuple-element.12.refs_0_), channel_id=1, source_target_pairs={{0,20},{1,21},{2,22},{3,23},{4,16},{5,17},{6,18},{7,19},{8,28},{9,... | collective-permute-start | bytes 49160 | tf_op jit(solution)/shard_map/ppermute | solution.py:349
  15.1 0.5 %collective-permute-start.4 = (f32[16,256]{1,0:T(8,128)S(1)}, f32[16,256]{1,0:T(8,128)S(1)}, u32[]{:S(2)}, u32[]{:S(2)}) collective-permute-start(f32[16,256]{1,0:T(8,128)S(1)} %get-tuple-element.12.refs_0_), channel_id=1, source_target_pairs={{0,12},{1,13},{2,14},{3,15},{4,8},{5,9},{6,10},{7,11},{8,4},{9,5},... | collective-permute-start | bytes 49160 | tf_op jit(solution)/shard_map/ppermute | solution.py:349
  15.6 0.9 %collective-permute-done.6.refs_3_ = f32[16,256]{1,0:T(8,128)S(1)} collective-permute-done((f32[16,256]{1,0:T(8,128)S(1)}, f32[16,256]{1,0:T(8,128)S(1)}, u32[]{:S(2)}, u32[]{:S(2)}) %collective-permute-start.6) | collective-permute-done | bytes 16416 | tf_op jit(solution)/shard_map/ppermute | solution.py:349
  16.5 1.5 %collective-permute-done.5.refs_2_ = f32[16,256]{1,0:T(8,128)S(1)} collective-permute-done((f32[16,256]{1,0:T(8,128)S(1)}, f32[16,256]{1,0:T(8,128)S(1)}, u32[]{:S(2)}, u32[]{:S(2)}) %collective-permute-start.5) | collective-permute-done | bytes 16416 | tf_op jit(solution)/shard_map/ppermute | solution.py:349
  18.0 0.3 %collective-permute-done.4.refs_1_ = f32[16,256]{1,0:T(8,128)S(1)} collective-permute-done((f32[16,256]{1,0:T(8,128)S(1)}, f32[16,256]{1,0:T(8,128)S(1)}, u32[]{:S(2)}, u32[]{:S(2)}) %collective-permute-start.4) | collective-permute-done | bytes 16416 | tf_op jit(solution)/shard_map/ppermute | solution.py:349
  18.3 0.4 %collective-permute-start.7 = (f32[80,256]{1,0:T(8,128)S(1)}, f32[80,256]{1,0:T(8,128)S(1)}, u32[]{:S(2)}, u32[]{:S(2)}) collective-permute-start(f32[80,256]{1,0:T(8,128)S(1)} %stack.1.held), channel_id=1, source_target_pairs={{0,4},{1,5},{2,6},{3,7},{4,0},{5,1},{6,2},{7,3},{8,12},{9,13},{10,... | collective-permute-start | bytes 245768 | tf_op jit(solution)/shard_map/ppermute | solution.py:349
  19.3 0.4 %gram.1.own_tiles = f32[64,256]{1,0:T(8,128)S(1)} custom-call(f32[80,256]{1,0:T(8,128)S(1)} %stack.1.held), custom_call_target="tpu_custom_call" | custom-call | flops 25165824 | tf_op jit(solution)/shard_map/gram/pallas_call | solution.py:451
  19.7 0.0 collective-permute-done.7.sent
  19.7 2.1 %factors.1 = (f32[4,1024]{1,0:T(4,128)}, f32[4,64,64]{2,1,0:T(8,128)}) custom-call(f32[1]{0:T(128)S(6)} %copy.10.damping, f32[64,256]{1,0:T(8,128)S(1)} %gram.1.own_tiles, f32[80,256]{1,0:T(8,128)S(1)} %collective-permute-done.7.sent), custom_call_target="tpu_custom_call" | custom-call | tf_op jit(solution)/shard_map/factors/pallas_call | solution.py:462
  (2 shorter events, 0.0 us)
Async XLA Ops:
  3.2 6.3 %collective-permute-start = (f32[32,256]{1,0:T(8,128)S(1)}, f32[32,256]{1,0:T(8,128)S(1)}, u32[]{:S(2)}, u32[]{:S(2)}) collective-permute-start(f32[32,256]{1,0:T(8,128)S(1)} %get-tuple-element.8), channel_id=1, source_target_pairs={{0,7},{1,6},{2,5},{3,4},{4,3},{5,2},{6,1},{7,0},{8,15},{9,14},{10,... | collective-permute-start | bytes 98312 | tf_op jit(solution)/shard_map/ppermute | solution.py:349
  7.8 4.5 %collective-permute-start.1 = (f32[32,256]{1,0:T(8,128)S(1)}, f32[32,256]{1,0:T(8,128)S(1)}, u32[]{:S(2)}, u32[]{:S(2)}) collective-permute-start(f32[32,256]{1,0:T(8,128)S(1)} %get-tuple-element.9), channel_id=1, source_target_pairs={{0,6},{1,7},{2,4},{3,5},{4,2},{5,3},{6,0},{7,1},{8,14},{9,15},{10,... | collective-permute-start | bytes 98312 | tf_op jit(solution)/shard_map/ppermute | solution.py:349
  7.8 4.5 %collective-permute-start.2 = (f32[32,256]{1,0:T(8,128)S(1)}, f32[32,256]{1,0:T(8,128)S(1)}, u32[]{:S(2)}, u32[]{:S(2)}) collective-permute-start(f32[32,256]{1,0:T(8,128)S(1)} %get-tuple-element.10), channel_id=1, source_target_pairs={{0,5},{1,4},{2,7},{3,6},{4,1},{5,0},{6,3},{7,2},{8,13},{9,12},{10,... | collective-permute-start | bytes 98312 | tf_op jit(solution)/shard_map/ppermute | solution.py:349
  8.7 3.6 %collective-permute-start.3 = (f32[32,256]{1,0:T(8,128)S(1)}, f32[32,256]{1,0:T(8,128)S(1)}, u32[]{:S(2)}, u32[]{:S(2)}) collective-permute-start(f32[32,256]{1,0:T(8,128)S(1)} %get-tuple-element.11), channel_id=1, source_target_pairs={{0,4},{1,5},{2,6},{3,7},{4,0},{5,1},{6,2},{7,3},{8,12},{9,13},{10,... | collective-permute-start | bytes 98312 | tf_op jit(solution)/shard_map/ppermute | solution.py:349
  12.3 4.1 %collective-permute-start.6 = (f32[16,256]{1,0:T(8,128)S(1)}, f32[16,256]{1,0:T(8,128)S(1)}, u32[]{:S(2)}, u32[]{:S(2)}) collective-permute-start(f32[16,256]{1,0:T(8,128)S(1)} %get-tuple-element.12.refs_0_), channel_id=1, source_target_pairs={{0,28},{1,29},{2,30},{3,31},{4,24},{5,25},{6,26},{7,27},{8,20},{9,... | collective-permute-start | bytes 49160 | tf_op jit(solution)/shard_map/ppermute | solution.py:349
  14.8 3.2 %collective-permute-start.5 = (f32[16,256]{1,0:T(8,128)S(1)}, f32[16,256]{1,0:T(8,128)S(1)}, u32[]{:S(2)}, u32[]{:S(2)}) collective-permute-start(f32[16,256]{1,0:T(8,128)S(1)} %get-tuple-element.12.refs_0_), channel_id=1, source_target_pairs={{0,20},{1,21},{2,22},{3,23},{4,16},{5,17},{6,18},{7,19},{8,28},{9,... | collective-permute-start | bytes 49160 | tf_op jit(solution)/shard_map/ppermute | solution.py:349
  15.1 3.2 %collective-permute-start.4 = (f32[16,256]{1,0:T(8,128)S(1)}, f32[16,256]{1,0:T(8,128)S(1)}, u32[]{:S(2)}, u32[]{:S(2)}) collective-permute-start(f32[16,256]{1,0:T(8,128)S(1)} %get-tuple-element.12.refs_0_), channel_id=1, source_target_pairs={{0,12},{1,13},{2,14},{3,15},{4,8},{5,9},{6,10},{7,11},{8,4},{9,5},... | collective-permute-start | bytes 49160 | tf_op jit(solution)/shard_map/ppermute | solution.py:349
  18.3 1.4 %collective-permute-start.7 = (f32[80,256]{1,0:T(8,128)S(1)}, f32[80,256]{1,0:T(8,128)S(1)}, u32[]{:S(2)}, u32[]{:S(2)}) collective-permute-start(f32[80,256]{1,0:T(8,128)S(1)} %stack.1.held), channel_id=1, source_target_pairs={{0,4},{1,5},{2,6},{3,7},{4,0},{5,1},{6,2},{7,3},{8,12},{9,13},{10,... | collective-permute-start | bytes 245768 | tf_op jit(solution)/shard_map/ppermute | solution.py:349

commit v24 on v16

--- a/solution.py
+++ b/solution.py
@@ -250,7 +250,7 @@
                 j: ahead[r]
                 if j == q
                 else pick_lanes(tile[j][hq], slot * SLOT + at * PANEL + r)
-                for j in range(q, panels)
+                for j in range(q, min(q + 3, panels))
             }
             for r in range(PANEL)
         ]
@@ -273,12 +273,13 @@
             for r in range(PANEL)
         ]
         inverse = []
+        ratios = {}
 
         def eliminate(r, s, inv):
-            ratio = block[r][s] * inv
+            ratio = ratios[r, s] = block[r][s] * inv
             for t in range(s, PANEL):
                 block[s][t] = block[s][t] - ratio * block[r][t]
-            for j in range(q + 1, panels):
+            for j in range(q + 1, min(q + 3, panels)):
                 column[s][j] = column[s][j] - ratio * column[r][j]
             for h in range(hq, halves):
                 line[s][h] = line[s][h] - ratio * line[r][h]
@@ -304,7 +305,36 @@
                 value = jnp.where(within >= at * PANEL + sub, value, 0.0)
             result.append(value)
         finished.append(result)
-        for j in range(q + 1, panels):
+        far = range(q + 3, panels)
+        if far:
+            raw = [tile[j][hq] for j in far] + [zero] * (len(far) % 2)
+            raw_high, raw_low = split(jnp.concatenate(raw, axis=0))
+            raw_both = jnp.concatenate([raw_high, raw_low], axis=0)
+            for h in range((q + 1) // per_half, halves):
+                solved = [None] * PANEL
+                packed = zero
+                for r in reversed(range(PANEL)):
+                    value = line[r][h] * inverse[r]
+                    for s in range(r + 1, PANEL):
+                        value = value - ratios[r, s] * solved[s]
+                    solved[r] = value
+                    packed = jnp.where(sub == r, value, packed)
+                right_high, right_low = split(
+                    jnp.concatenate(
+                        [
+                            jnp.where(slot == c, packed, 0.0) if a == at else zero
+                            for c in range(GROUP)
+                            for a in range(per_half)
+                        ],
+                        axis=0,
+                    )
+                )
+                both = dot_nn(raw_both, right_high)
+                size = raw_high.shape[0]
+                change = (dot_nn(raw_high, right_low) + both[size:]) + both[:size]
+                for n, j in enumerate(far):
+                    tile[j][h] = tile[j][h] - change[n * PANEL : (n + 1) * PANEL]
+        for j in range(q + 1, min(q + 3, panels)):
             weights = [column[r][j] * inverse[r] for r in range(PANEL)]
             if j == q + 1:
                 ahead = behind

time: 21.8 us -> 22 us (level)
  Pallas kernels: 4.68 us -> 4.94 us
    pallas_call x1, Pallas kernels: 2.07 us -> 2.33 us  [local(): pl.pallas_call(functools.partial(factor_kernel, parts), out_shape=[jax.Sh...]
where the time goes in v24:
time: 22 us; the launch traced here: 21.9 us
  starting transfers between devices  9.08 us (41%)
  waiting for transfers between devices  6.56 us (30%)
  Pallas kernels  4.94 us (22%)
  between operations  1.3 us (6%)
    ppermute x8, starting transfers between devices, exchange(): lax.ppermute(x, ('ex', 'mp'), [(m * parts + b, (m ^ ex_distance) * parts...  9.08 us
    ppermute x8, waiting for transfers between devices, exchange(): lax.ppermute(x, ('ex', 'mp'), [(m * parts + b, (m ^ ex_distance) * parts...  6.56 us
    pallas_call x1, Pallas kernels, local(): pl.pallas_call(functools.partial(partial_kernel, parts, scaling), out_sha...  2.59 us
    pallas_call x1, Pallas kernels, local(): pl.pallas_call(functools.partial(factor_kernel, parts), out_shape=[jax.Sh...  2.33 us
  transfers between devices with their start and end apart: 8, of which 6 were waited for; matrix products, arithmetic and copies ran while one was open for 0% of the time, Pallas kernels for 0%

profile of v24, /device:TPU:0, one launch (start us, length us, event | category | flops | bytes accessed | tf_op | source)
XLA Modules:
  0.0 21.9 jit_solution(11123519714897120620)
XLA Ops:
  0.6 2.6 %partials.1 = (f32[32,256]{1,0:T(8,128)S(1)}, f32[32,256]{1,0:T(8,128)S(1)}, f32[32,256]{1,0:T(8,128)S(1)}, f32[32,256]{1,0:T(8,128)S(1)}) custom-call(bf16[1,128,4096]{2,1,0:T(8,128)(2,1)} %acts_hbm.1, bf16[1,128,1024]{2,1,0:T(8,128)(2,1)} %grads_hbm.1, bf16[1,16,4096]{2,1,0:T(8,128)(2,1)} %down_hbm.1, bf16[1,16,1024]{2,1,0:T(8,128)(2,1)} %up_hbm.1, ...), custom_call_target="tpu_custom_call" | custom-call | tf_op jit(solution)/shard_map/partials/pallas_call | solution.py:414
  3.2 4.6 %collective-permute-start = (f32[32,256]{1,0:T(8,128)S(1)}, f32[32,256]{1,0:T(8,128)S(1)}, u32[]{:S(2)}, u32[]{:S(2)}) collective-permute-start(f32[32,256]{1,0:T(8,128)S(1)} %get-tuple-element.8), channel_id=1, source_target_pairs={{0,7},{1,6},{2,5},{3,4},{4,3},{5,2},{6,1},{7,0},{8,15},{9,14},{10,... | collective-permute-start | bytes 98312 | tf_op jit(solution)/shard_map/ppermute | solution.py:363
  7.8 0.0 collective-permute-start.1
  7.8 0.9 %collective-permute-start.2 = (f32[32,256]{1,0:T(8,128)S(1)}, f32[32,256]{1,0:T(8,128)S(1)}, u32[]{:S(2)}, u32[]{:S(2)}) collective-permute-start(f32[32,256]{1,0:T(8,128)S(1)} %get-tuple-element.10), channel_id=1, source_target_pairs={{0,5},{1,4},{2,7},{3,6},{4,1},{5,0},{6,3},{7,2},{8,13},{9,12},{10,... | collective-permute-start | bytes 98312 | tf_op jit(solution)/shard_map/ppermute | solution.py:363
  8.7 0.0 collective-permute-start.3
  8.7 0.9 %collective-permute-done.refs_0_ = f32[32,256]{1,0:T(8,128)S(1)} collective-permute-done((f32[32,256]{1,0:T(8,128)S(1)}, f32[32,256]{1,0:T(8,128)S(1)}, u32[]{:S(2)}, u32[]{:S(2)}) %collective-permute-start) | collective-permute-done | bytes 32800 | tf_op jit(solution)/shard_map/ppermute | solution.py:363
  9.6 2.8 %collective-permute-done.1.refs_1_ = f32[32,256]{1,0:T(8,128)S(1)} collective-permute-done((f32[32,256]{1,0:T(8,128)S(1)}, f32[32,256]{1,0:T(8,128)S(1)}, u32[]{:S(2)}, u32[]{:S(2)}) %collective-permute-start.1) | collective-permute-done | bytes 32800 | tf_op jit(solution)/shard_map/ppermute | solution.py:363
  12.3 0.0 collective-permute-done.2.refs_2_
  12.3 0.0 collective-permute-done.3.refs_3_
  12.3 2.5 %collective-permute-start.6 = (f32[16,256]{1,0:T(8,128)S(1)}, f32[16,256]{1,0:T(8,128)S(1)}, u32[]{:S(2)}, u32[]{:S(2)}) collective-permute-start(f32[16,256]{1,0:T(8,128)S(1)} %get-tuple-element.12.refs_0_), channel_id=1, source_target_pairs={{0,28},{1,29},{2,30},{3,31},{4,24},{5,25},{6,26},{7,27},{8,20},{9,... | collective-permute-start | bytes 49160 | tf_op jit(solution)/shard_map/ppermute | solution.py:363
  14.8 0.3 %collective-permute-start.5 = (f32[16,256]{1,0:T(8,128)S(1)}, f32[16,256]{1,0:T(8,128)S(1)}, u32[]{:S(2)}, u32[]{:S(2)}) collective-permute-start(f32[16,256]{1,0:T(8,128)S(1)} %get-tuple-element.12.refs_0_), channel_id=1, source_target_pairs={{0,20},{1,21},{2,22},{3,23},{4,16},{5,17},{6,18},{7,19},{8,28},{9,... | collective-permute-start | bytes 49160 | tf_op jit(solution)/shard_map/ppermute | solution.py:363
  15.1 0.5 %collective-permute-start.4 = (f32[16,256]{1,0:T(8,128)S(1)}, f32[16,256]{1,0:T(8,128)S(1)}, u32[]{:S(2)}, u32[]{:S(2)}) collective-permute-start(f32[16,256]{1,0:T(8,128)S(1)} %get-tuple-element.12.refs_0_), channel_id=1, source_target_pairs={{0,12},{1,13},{2,14},{3,15},{4,8},{5,9},{6,10},{7,11},{8,4},{9,5},... | collective-permute-start | bytes 49160 | tf_op jit(solution)/shard_map/ppermute | solution.py:363
  15.6 0.9 %collective-permute-done.6.refs_3_ = f32[16,256]{1,0:T(8,128)S(1)} collective-permute-done((f32[16,256]{1,0:T(8,128)S(1)}, f32[16,256]{1,0:T(8,128)S(1)}, u32[]{:S(2)}, u32[]{:S(2)}) %collective-permute-start.6) | collective-permute-done | bytes 16416 | tf_op jit(solution)/shard_map/ppermute | solution.py:363
  16.5 1.5 %collective-permute-done.5.refs_2_ = f32[16,256]{1,0:T(8,128)S(1)} collective-permute-done((f32[16,256]{1,0:T(8,128)S(1)}, f32[16,256]{1,0:T(8,128)S(1)}, u32[]{:S(2)}, u32[]{:S(2)}) %collective-permute-start.5) | collective-permute-done | bytes 16416 | tf_op jit(solution)/shard_map/ppermute | solution.py:363
  18.0 0.3 %collective-permute-done.4.refs_1_ = f32[16,256]{1,0:T(8,128)S(1)} collective-permute-done((f32[16,256]{1,0:T(8,128)S(1)}, f32[16,256]{1,0:T(8,128)S(1)}, u32[]{:S(2)}, u32[]{:S(2)}) %collective-permute-start.4) | collective-permute-done | bytes 16416 | tf_op jit(solution)/shard_map/ppermute | solution.py:363
  18.3 0.4 %collective-permute-start.7 = (f32[80,256]{1,0:T(8,128)S(1)}, f32[80,256]{1,0:T(8,128)S(1)}, u32[]{:S(2)}, u32[]{:S(2)}) collective-permute-start(f32[80,256]{1,0:T(8,128)S(1)} %stack.1.held), channel_id=1, source_target_pairs={{0,4},{1,5},{2,6},{3,7},{4,0},{5,1},{6,2},{7,3},{8,12},{9,13},{10,... | collective-permute-start | bytes 245768 | tf_op jit(solution)/shard_map/ppermute | solution.py:363
  19.3 0.3 %collective-permute-done.7.sent = f32[80,256]{1,0:T(8,128)S(1)} collective-permute-done((f32[80,256]{1,0:T(8,128)S(1)}, f32[80,256]{1,0:T(8,128)S(1)}, u32[]{:S(2)}, u32[]{:S(2)}) %collective-permute-start.7) | collective-permute-done | bytes 81952 | tf_op jit(solution)/shard_map/ppermute | solution.py:363
  19.6 2.3 %factors.1 = (f32[4,1024]{1,0:T(4,128)}, f32[4,64,64]{2,1,0:T(8,128)}) custom-call(f32[1]{0:T(128)S(6)} %copy.10.damping, f32[80,256]{1,0:T(8,128)S(1)} %stack.1.held, f32[80,256]{1,0:T(8,128)S(1)} %collective-permute-done.7.sent), custom_call_target="tpu_custom_call" | custom-call | tf_op jit(solution)/shard_map/factors/pallas_call | solution.py:464
  (2 shorter events, 0.0 us)
Async XLA Ops:
  3.2 6.3 %collective-permute-start = (f32[32,256]{1,0:T(8,128)S(1)}, f32[32,256]{1,0:T(8,128)S(1)}, u32[]{:S(2)}, u32[]{:S(2)}) collective-permute-start(f32[32,256]{1,0:T(8,128)S(1)} %get-tuple-element.8), channel_id=1, source_target_pairs={{0,7},{1,6},{2,5},{3,4},{4,3},{5,2},{6,1},{7,0},{8,15},{9,14},{10,... | collective-permute-start | bytes 98312 | tf_op jit(solution)/shard_map/ppermute | solution.py:363
  7.8 4.5 %collective-permute-start.1 = (f32[32,256]{1,0:T(8,128)S(1)}, f32[32,256]{1,0:T(8,128)S(1)}, u32[]{:S(2)}, u32[]{:S(2)}) collective-permute-start(f32[32,256]{1,0:T(8,128)S(1)} %get-tuple-element.9), channel_id=1, source_target_pairs={{0,6},{1,7},{2,4},{3,5},{4,2},{5,3},{6,0},{7,1},{8,14},{9,15},{10,... | collective-permute-start | bytes 98312 | tf_op jit(solution)/shard_map/ppermute | solution.py:363
  7.8 4.5 %collective-permute-start.2 = (f32[32,256]{1,0:T(8,128)S(1)}, f32[32,256]{1,0:T(8,128)S(1)}, u32[]{:S(2)}, u32[]{:S(2)}) collective-permute-start(f32[32,256]{1,0:T(8,128)S(1)} %get-tuple-element.10), channel_id=1, source_target_pairs={{0,5},{1,4},{2,7},{3,6},{4,1},{5,0},{6,3},{7,2},{8,13},{9,12},{10,... | collective-permute-start | bytes 98312 | tf_op jit(solution)/shard_map/ppermute | solution.py:363
  8.7 3.6 %collective-permute-start.3 = (f32[32,256]{1,0:T(8,128)S(1)}, f32[32,256]{1,0:T(8,128)S(1)}, u32[]{:S(2)}, u32[]{:S(2)}) collective-permute-start(f32[32,256]{1,0:T(8,128)S(1)} %get-tuple-element.11), channel_id=1, source_target_pairs={{0,4},{1,5},{2,6},{3,7},{4,0},{5,1},{6,2},{7,3},{8,12},{9,13},{10,... | collective-permute-start | bytes 98312 | tf_op jit(solution)/shard_map/ppermute | solution.py:363
  12.3 4.1 %collective-permute-start.6 = (f32[16,256]{1,0:T(8,128)S(1)}, f32[16,256]{1,0:T(8,128)S(1)}, u32[]{:S(2)}, u32[]{:S(2)}) collective-permute-start(f32[16,256]{1,0:T(8,128)S(1)} %get-tuple-element.12.refs_0_), channel_id=1, source_target_pairs={{0,28},{1,29},{2,30},{3,31},{4,24},{5,25},{6,26},{7,27},{8,20},{9,... | collective-permute-start | bytes 49160 | tf_op jit(solution)/shard_map/ppermute | solution.py:363
  14.8 3.2 %collective-permute-start.5 = (f32[16,256]{1,0:T(8,128)S(1)}, f32[16,256]{1,0:T(8,128)S(1)}, u32[]{:S(2)}, u32[]{:S(2)}) collective-permute-start(f32[16,256]{1,0:T(8,128)S(1)} %get-tuple-element.12.refs_0_), channel_id=1, source_target_pairs={{0,20},{1,21},{2,22},{3,23},{4,16},{5,17},{6,18},{7,19},{8,28},{9,... | collective-permute-start | bytes 49160 | tf_op jit(solution)/shard_map/ppermute | solution.py:363
  15.1 3.2 %collective-permute-start.4 = (f32[16,256]{1,0:T(8,128)S(1)}, f32[16,256]{1,0:T(8,128)S(1)}, u32[]{:S(2)}, u32[]{:S(2)}) collective-permute-start(f32[16,256]{1,0:T(8,128)S(1)} %get-tuple-element.12.refs_0_), channel_id=1, source_target_pairs={{0,12},{1,13},{2,14},{3,15},{4,8},{5,9},{6,10},{7,11},{8,4},{9,5},... | collective-permute-start | bytes 49160 | tf_op jit(solution)/shard_map/ppermute | solution.py:363
  18.3 1.3 %collective-permute-start.7 = (f32[80,256]{1,0:T(8,128)S(1)}, f32[80,256]{1,0:T(8,128)S(1)}, u32[]{:S(2)}, u32[]{:S(2)}) collective-permute-start(f32[80,256]{1,0:T(8,128)S(1)} %stack.1.held), channel_id=1, source_target_pairs={{0,4},{1,5},{2,6},{3,7},{4,0},{5,1},{6,2},{7,3},{8,12},{9,13},{10,... | collective-permute-start | bytes 245768 | tf_op jit(solution)/shard_map/ppermute | solution.py:363

commit v25 on v16

--- a/solution.py
+++ b/solution.py
@@ -328,17 +328,23 @@
             )
 
 
+def permute(x, source):
+    shards, parts = lax.axis_size("ex"), lax.axis_size("mp")
+    pairs = []
+    for m in range(shards):
+        for b in range(parts):
+            sm, sb = source(m, b)
+            pairs.append((sm * parts + sb, m * parts + b))
+    return lax.ppermute(x, ("ex", "mp"), sorted(pairs))
+
+
 def exchange(x, ex_distance, mp_distance=0):
-    shards, parts = lax.axis_size("ex"), lax.axis_size("mp")
-    return lax.ppermute(
-        x,
-        ("ex", "mp"),
-        [
-            (m * parts + b, (m ^ ex_distance) * parts + (b ^ mp_distance))
-            for m in range(shards)
-            for b in range(parts)
-        ],
-    )
+    return permute(x, lambda m, b: (m ^ ex_distance, b ^ mp_distance))
+
+
+def shift_chips(x, distance):
+    shards = lax.axis_size("ex")
+    return permute(x, lambda m, b: ((m - 2 * distance) % shards ^ 1, b))
 
 
 def vmem():
@@ -421,7 +427,8 @@
         compiler_params=pltpu.CompilerParams(vmem_limit_bytes=2 * 2**20),
         name="sums",
     )(*in_vmem(*chunks))
-    near = [columns] + [exchange(columns, d) for d in range(3, shards, 2)] + [feature_rows]
+    shifts = sorted(range(1, shards // 2), key=lambda d: (-min(d, shards // 2 - d), -d))
+    near = [columns] + [shift_chips(columns, d) for d in shifts] + [feature_rows]
     held = pl.pallas_call(
         stack_kernel,
         out_shape=pltpu.VMEM((len(near) * examples, padded), jnp.float32),

time: 21.8 us -> 21.7 us (level)
  waiting for transfers between devices: 6.56 us -> 5.59 us
  starting transfers between devices: 9.08 us -> 10 us
    ppermute x8, waiting for transfers between devices: 6.56 us -> 5.59 us  [permute(): return lax.ppermute(x, ('ex', 'mp'), sorted(pairs))]
    ppermute x8, starting transfers between devices: 9.08 us -> 10 us  [permute(): return lax.ppermute(x, ('ex', 'mp'), sorted(pairs))]
  transfers between devices with their start and end apart: 8 -> 8, of which waited for: 6 -> 5; matrix products, arithmetic and copies ran while one was open for 0% -> 0% of each run, Pallas kernels for 0% -> 0%
where the time goes in v25:
time: 21.7 us; the launch traced here: 21.6 us
  starting transfers between devices  10 us (46%)
  waiting for transfers between devices  5.59 us (26%)
  Pallas kernels  4.68 us (22%)
  between operations  1.3 us (6%)
    ppermute x8, starting transfers between devices, permute(): return lax.ppermute(x, ('ex', 'mp'), sorted(pairs))  10 us
    ppermute x8, waiting for transfers between devices, permute(): return lax.ppermute(x, ('ex', 'mp'), sorted(pairs))  5.59 us
    pallas_call x1, Pallas kernels, local(): pl.pallas_call(functools.partial(partial_kernel, parts, scaling), out_sha...  2.59 us
    pallas_call x1, Pallas kernels, local(): pl.pallas_call(functools.partial(factor_kernel, parts), out_shape=[jax.Sh...  2.07 us
  transfers between devices with their start and end apart: 8, of which 5 were waited for; matrix products, arithmetic and copies ran while one was open for 0% of the time, Pallas kernels for 0%

profile of v25, /device:TPU:0, one launch (start us, length us, event | category | flops | bytes accessed | tf_op | source)
XLA Modules:
  0.0 21.6 jit_solution(10203249795717605202)
XLA Ops:
  0.6 2.6 %partials.1 = (f32[32,256]{1,0:T(8,128)S(1)}, f32[32,256]{1,0:T(8,128)S(1)}, f32[32,256]{1,0:T(8,128)S(1)}, f32[32,256]{1,0:T(8,128)S(1)}) custom-call(bf16[1,128,4096]{2,1,0:T(8,128)(2,1)} %acts_hbm.1, bf16[1,128,1024]{2,1,0:T(8,128)(2,1)} %grads_hbm.1, bf16[1,16,4096]{2,1,0:T(8,128)(2,1)} %down_hbm.1, bf16[1,16,1024]{2,1,0:T(8,128)(2,1)} %up_hbm.1, ...), custom_call_target="tpu_custom_call" | custom-call | tf_op jit(solution)/shard_map/partials/pallas_call | solution.py:390
  3.2 4.6 %collective-permute-start = (f32[32,256]{1,0:T(8,128)S(1)}, f32[32,256]{1,0:T(8,128)S(1)}, u32[]{:S(2)}, u32[]{:S(2)}) collective-permute-start(f32[32,256]{1,0:T(8,128)S(1)} %get-tuple-element.8), channel_id=1, source_target_pairs={{0,7},{1,6},{2,5},{3,4},{4,3},{5,2},{6,1},{7,0},{8,15},{9,14},{10,... | collective-permute-start | bytes 98312 | tf_op jit(solution)/shard_map/ppermute | solution.py:338
  7.8 0.0 collective-permute-start.1
  7.8 0.9 %collective-permute-start.2 = (f32[32,256]{1,0:T(8,128)S(1)}, f32[32,256]{1,0:T(8,128)S(1)}, u32[]{:S(2)}, u32[]{:S(2)}) collective-permute-start(f32[32,256]{1,0:T(8,128)S(1)} %get-tuple-element.10), channel_id=1, source_target_pairs={{0,5},{1,4},{2,7},{3,6},{4,1},{5,0},{6,3},{7,2},{8,13},{9,12},{10,... | collective-permute-start | bytes 98312 | tf_op jit(solution)/shard_map/ppermute | solution.py:338
  8.7 0.0 collective-permute-start.3
  8.7 0.9 %collective-permute-done.refs_0_ = f32[32,256]{1,0:T(8,128)S(1)} collective-permute-done((f32[32,256]{1,0:T(8,128)S(1)}, f32[32,256]{1,0:T(8,128)S(1)}, u32[]{:S(2)}, u32[]{:S(2)}) %collective-permute-start) | collective-permute-done | bytes 32800 | tf_op jit(solution)/shard_map/ppermute | solution.py:338
  9.6 2.8 %collective-permute-done.1.refs_1_ = f32[32,256]{1,0:T(8,128)S(1)} collective-permute-done((f32[32,256]{1,0:T(8,128)S(1)}, f32[32,256]{1,0:T(8,128)S(1)}, u32[]{:S(2)}, u32[]{:S(2)}) %collective-permute-start.1) | collective-permute-done | bytes 32800 | tf_op jit(solution)/shard_map/ppermute | solution.py:338
  12.3 0.0 collective-permute-done.2.refs_2_
  12.3 0.0 collective-permute-done.3.refs_3_
  12.3 1.5 %collective-permute-start.6 = (f32[16,256]{1,0:T(8,128)S(1)}, f32[16,256]{1,0:T(8,128)S(1)}, u32[]{:S(2)}, u32[]{:S(2)}) collective-permute-start(f32[16,256]{1,0:T(8,128)S(1)} %get-tuple-element.12.refs_0_), channel_id=1, source_target_pairs={{0,12},{1,13},{2,14},{3,15},{4,8},{5,9},{6,10},{7,11},{8,20},{9,21... | collective-permute-start | bytes 49160 | tf_op jit(solution)/shard_map/ppermute | solution.py:338
  13.9 1.2 %collective-permute-start.5 = (f32[16,256]{1,0:T(8,128)S(1)}, f32[16,256]{1,0:T(8,128)S(1)}, u32[]{:S(2)}, u32[]{:S(2)}) collective-permute-start(f32[16,256]{1,0:T(8,128)S(1)} %get-tuple-element.12.refs_0_), channel_id=1, source_target_pairs={{0,28},{1,29},{2,30},{3,31},{4,24},{5,25},{6,26},{7,27},{8,4},{9,5... | collective-permute-start | bytes 49160 | tf_op jit(solution)/shard_map/ppermute | solution.py:338
  15.1 1.5 %collective-permute-start.4 = (f32[16,256]{1,0:T(8,128)S(1)}, f32[16,256]{1,0:T(8,128)S(1)}, u32[]{:S(2)}, u32[]{:S(2)}) collective-permute-start(f32[16,256]{1,0:T(8,128)S(1)} %get-tuple-element.12.refs_0_), channel_id=1, source_target_pairs={{0,20},{1,21},{2,22},{3,23},{4,16},{5,17},{6,18},{7,19},{8,28},{9,... | collective-permute-start | bytes 49160 | tf_op jit(solution)/shard_map/ppermute | solution.py:338
  16.5 0.0 collective-permute-done.6.refs_3_
  16.5 0.6 %collective-permute-done.5.refs_2_ = f32[16,256]{1,0:T(8,128)S(1)} collective-permute-done((f32[16,256]{1,0:T(8,128)S(1)}, f32[16,256]{1,0:T(8,128)S(1)}, u32[]{:S(2)}, u32[]{:S(2)}) %collective-permute-start.5) | collective-permute-done | bytes 16416 | tf_op jit(solution)/shard_map/ppermute | solution.py:338
  17.2 1.1 %collective-permute-done.4.refs_1_ = f32[16,256]{1,0:T(8,128)S(1)} collective-permute-done((f32[16,256]{1,0:T(8,128)S(1)}, f32[16,256]{1,0:T(8,128)S(1)}, u32[]{:S(2)}, u32[]{:S(2)}) %collective-permute-start.4) | collective-permute-done | bytes 16416 | tf_op jit(solution)/shard_map/ppermute | solution.py:338
  18.2 0.3 %collective-permute-start.7 = (f32[80,256]{1,0:T(8,128)S(1)}, f32[80,256]{1,0:T(8,128)S(1)}, u32[]{:S(2)}, u32[]{:S(2)}) collective-permute-start(f32[80,256]{1,0:T(8,128)S(1)} %stack.1.held), channel_id=1, source_target_pairs={{0,4},{1,5},{2,6},{3,7},{4,0},{5,1},{6,2},{7,3},{8,12},{9,13},{10,... | collective-permute-start | bytes 245768 | tf_op jit(solution)/shard_map/ppermute | solution.py:338
  19.2 0.3 %collective-permute-done.7.sent = f32[80,256]{1,0:T(8,128)S(1)} collective-permute-done((f32[80,256]{1,0:T(8,128)S(1)}, f32[80,256]{1,0:T(8,128)S(1)}, u32[]{:S(2)}, u32[]{:S(2)}) %collective-permute-start.7) | collective-permute-done | bytes 81952 | tf_op jit(solution)/shard_map/ppermute | solution.py:338
  19.5 2.1 %factors.1 = (f32[4,1024]{1,0:T(4,128)}, f32[4,64,64]{2,1,0:T(8,128)}) custom-call(f32[1]{0:T(128)S(6)} %copy.10.damping, f32[80,256]{1,0:T(8,128)S(1)} %stack.1.held, f32[80,256]{1,0:T(8,128)S(1)} %collective-permute-done.7.sent), custom_call_target="tpu_custom_call" | custom-call | tf_op jit(solution)/shard_map/factors/pallas_call | solution.py:441
  (2 shorter events, 0.0 us)
Async XLA Ops:
  3.2 6.3 %collective-permute-start = (f32[32,256]{1,0:T(8,128)S(1)}, f32[32,256]{1,0:T(8,128)S(1)}, u32[]{:S(2)}, u32[]{:S(2)}) collective-permute-start(f32[32,256]{1,0:T(8,128)S(1)} %get-tuple-element.8), channel_id=1, source_target_pairs={{0,7},{1,6},{2,5},{3,4},{4,3},{5,2},{6,1},{7,0},{8,15},{9,14},{10,... | collective-permute-start | bytes 98312 | tf_op jit(solution)/shard_map/ppermute | solution.py:338
  7.8 4.5 %collective-permute-start.1 = (f32[32,256]{1,0:T(8,128)S(1)}, f32[32,256]{1,0:T(8,128)S(1)}, u32[]{:S(2)}, u32[]{:S(2)}) collective-permute-start(f32[32,256]{1,0:T(8,128)S(1)} %get-tuple-element.9), channel_id=1, source_target_pairs={{0,6},{1,7},{2,4},{3,5},{4,2},{5,3},{6,0},{7,1},{8,14},{9,15},{10,... | collective-permute-start | bytes 98312 | tf_op jit(solution)/shard_map/ppermute | solution.py:338
  7.8 4.5 %collective-permute-start.2 = (f32[32,256]{1,0:T(8,128)S(1)}, f32[32,256]{1,0:T(8,128)S(1)}, u32[]{:S(2)}, u32[]{:S(2)}) collective-permute-start(f32[32,256]{1,0:T(8,128)S(1)} %get-tuple-element.10), channel_id=1, source_target_pairs={{0,5},{1,4},{2,7},{3,6},{4,1},{5,0},{6,3},{7,2},{8,13},{9,12},{10,... | collective-permute-start | bytes 98312 | tf_op jit(solution)/shard_map/ppermute | solution.py:338
  8.7 3.6 %collective-permute-start.3 = (f32[32,256]{1,0:T(8,128)S(1)}, f32[32,256]{1,0:T(8,128)S(1)}, u32[]{:S(2)}, u32[]{:S(2)}) collective-permute-start(f32[32,256]{1,0:T(8,128)S(1)} %get-tuple-element.11), channel_id=1, source_target_pairs={{0,4},{1,5},{2,6},{3,7},{4,0},{5,1},{6,2},{7,3},{8,12},{9,13},{10,... | collective-permute-start | bytes 98312 | tf_op jit(solution)/shard_map/ppermute | solution.py:338
  12.3 4.2 %collective-permute-start.6 = (f32[16,256]{1,0:T(8,128)S(1)}, f32[16,256]{1,0:T(8,128)S(1)}, u32[]{:S(2)}, u32[]{:S(2)}) collective-permute-start(f32[16,256]{1,0:T(8,128)S(1)} %get-tuple-element.12.refs_0_), channel_id=1, source_target_pairs={{0,12},{1,13},{2,14},{3,15},{4,8},{5,9},{6,10},{7,11},{8,20},{9,21... | collective-permute-start | bytes 49160 | tf_op jit(solution)/shard_map/ppermute | solution.py:338
  13.9 3.3 %collective-permute-start.5 = (f32[16,256]{1,0:T(8,128)S(1)}, f32[16,256]{1,0:T(8,128)S(1)}, u32[]{:S(2)}, u32[]{:S(2)}) collective-permute-start(f32[16,256]{1,0:T(8,128)S(1)} %get-tuple-element.12.refs_0_), channel_id=1, source_target_pairs={{0,28},{1,29},{2,30},{3,31},{4,24},{5,25},{6,26},{7,27},{8,4},{9,5... | collective-permute-start | bytes 49160 | tf_op jit(solution)/shard_map/ppermute | solution.py:338
  15.1 3.2 %collective-permute-start.4 = (f32[16,256]{1,0:T(8,128)S(1)}, f32[16,256]{1,0:T(8,128)S(1)}, u32[]{:S(2)}, u32[]{:S(2)}) collective-permute-start(f32[16,256]{1,0:T(8,128)S(1)} %get-tuple-element.12.refs_0_), channel_id=1, source_target_pairs={{0,20},{1,21},{2,22},{3,23},{4,16},{5,17},{6,18},{7,19},{8,28},{9,... | collective-permute-start | bytes 49160 | tf_op jit(solution)/shard_map/ppermute | solution.py:338
  18.2 1.3 %collective-permute-start.7 = (f32[80,256]{1,0:T(8,128)S(1)}, f32[80,256]{1,0:T(8,128)S(1)}, u32[]{:S(2)}, u32[]{:S(2)}) collective-permute-start(f32[80,256]{1,0:T(8,128)S(1)} %stack.1.held), channel_id=1, source_target_pairs={{0,4},{1,5},{2,6},{3,7},{4,0},{5,1},{6,2},{7,3},{8,12},{9,13},{10,... | collective-permute-start | bytes 245768 | tf_op jit(solution)/shard_map/ppermute | solution.py:338

commit v26 on v25

--- a/solution.py
+++ b/solution.py
@@ -343,8 +343,14 @@
 
 
 def shift_chips(x, distance):
-    shards = lax.axis_size("ex")
-    return permute(x, lambda m, b: ((m - 2 * distance) % shards ^ 1, b))
+    chips = lax.axis_size("ex") // 2
+    ring = [i ^ i >> 1 for i in range(chips)]
+    place = {chip: i for i, chip in enumerate(ring)}
+
+    def source(m, b):
+        return 2 * ring[(place[m // 2] - distance) % chips] + (1 - m % 2), b
+
+    return permute(x, source)
 
 
 def vmem():
@@ -417,7 +423,8 @@
             order,
         )
     )
-    chunks = [exchange(sends[d], 1, d) for d in range(parts - 1, -1, -1)]
+    distances = sorted(range(1, parts), key=lambda d: (d < parts // 2, d))
+    chunks = [exchange(sends[d], 1, d) for d in [*distances, 0]]
     padded = max(span, GROUP * sketch)
     columns, feature_rows = pl.pallas_call(
         sum_kernel,

time: 21.7 us -> 21.9 us (level)
  starting transfers between devices: 10 us -> 10.5 us
  waiting for transfers between devices: 5.59 us -> 5.25 us
    ppermute x8, starting transfers between devices: 10 us -> 10.5 us  [permute(): return lax.ppermute(x, ('ex', 'mp'), sorted(pairs))]
    ppermute x8, waiting for transfers between devices: 5.59 us -> 5.25 us  [permute(): return lax.ppermute(x, ('ex', 'mp'), sorted(pairs))]
where the time goes in v26:
time: 21.9 us; the launch traced here: 21.7 us
  starting transfers between devices  10.5 us (48%)
  waiting for transfers between devices  5.25 us (24%)
  Pallas kernels  4.68 us (21%)
  between operations  1.3 us (6%)
    ppermute x8, starting transfers between devices, permute(): return lax.ppermute(x, ('ex', 'mp'), sorted(pairs))  10.5 us
    ppermute x8, waiting for transfers between devices, permute(): return lax.ppermute(x, ('ex', 'mp'), sorted(pairs))  5.25 us
    pallas_call x1, Pallas kernels, local(): pl.pallas_call(functools.partial(partial_kernel, parts, scaling), out_sha...  2.59 us
    pallas_call x1, Pallas kernels, local(): pl.pallas_call(functools.partial(factor_kernel, parts), out_shape=[jax.Sh...  2.07 us
  transfers between devices with their start and end apart: 8, of which 5 were waited for; matrix products, arithmetic and copies ran while one was open for 0% of the time, Pallas kernels for 0%

profile of v26, /device:TPU:0, one launch (start us, length us, event | category | flops | bytes accessed | tf_op | source)
XLA Modules:
  0.0 21.7 jit_solution(9993225207027331594)
XLA Ops:
  0.6 2.6 %partials.1 = (f32[32,256]{1,0:T(8,128)S(1)}, f32[32,256]{1,0:T(8,128)S(1)}, f32[32,256]{1,0:T(8,128)S(1)}, f32[32,256]{1,0:T(8,128)S(1)}) custom-call(bf16[1,128,4096]{2,1,0:T(8,128)(2,1)} %acts_hbm.1, bf16[1,128,1024]{2,1,0:T(8,128)(2,1)} %grads_hbm.1, bf16[1,16,4096]{2,1,0:T(8,128)(2,1)} %down_hbm.1, bf16[1,16,1024]{2,1,0:T(8,128)(2,1)} %up_hbm.1, ...), custom_call_target="tpu_custom_call" | custom-call | tf_op jit(solution)/shard_map/partials/pallas_call | solution.py:396
  3.2 3.5 %collective-permute-start = (f32[32,256]{1,0:T(8,128)S(1)}, f32[32,256]{1,0:T(8,128)S(1)}, u32[]{:S(2)}, u32[]{:S(2)}) collective-permute-start(f32[32,256]{1,0:T(8,128)S(1)} %get-tuple-element.8), channel_id=1, source_target_pairs={{0,6},{1,7},{2,4},{3,5},{4,2},{5,3},{6,0},{7,1},{8,14},{9,15},{10,... | collective-permute-start | bytes 98312 | tf_op jit(solution)/shard_map/ppermute | solution.py:338
  6.8 1.6 %collective-permute-start.1 = (f32[32,256]{1,0:T(8,128)S(1)}, f32[32,256]{1,0:T(8,128)S(1)}, u32[]{:S(2)}, u32[]{:S(2)}) collective-permute-start(f32[32,256]{1,0:T(8,128)S(1)} %get-tuple-element.9), channel_id=1, source_target_pairs={{0,7},{1,6},{2,5},{3,4},{4,3},{5,2},{6,1},{7,0},{8,15},{9,14},{10,... | collective-permute-start | bytes 98312 | tf_op jit(solution)/shard_map/ppermute | solution.py:338
  8.4 0.2 %collective-permute-start.2 = (f32[32,256]{1,0:T(8,128)S(1)}, f32[32,256]{1,0:T(8,128)S(1)}, u32[]{:S(2)}, u32[]{:S(2)}) collective-permute-start(f32[32,256]{1,0:T(8,128)S(1)} %get-tuple-element.10), channel_id=1, source_target_pairs={{0,5},{1,4},{2,7},{3,6},{4,1},{5,0},{6,3},{7,2},{8,13},{9,12},{10,... | collective-permute-start | bytes 98312 | tf_op jit(solution)/shard_map/ppermute | solution.py:338
  8.6 0.0 collective-permute-start.3
  8.6 0.0 collective-permute-done.refs_0_
  8.6 3.4 %collective-permute-done.1.refs_1_ = f32[32,256]{1,0:T(8,128)S(1)} collective-permute-done((f32[32,256]{1,0:T(8,128)S(1)}, f32[32,256]{1,0:T(8,128)S(1)}, u32[]{:S(2)}, u32[]{:S(2)}) %collective-permute-start.1) | collective-permute-done | bytes 32800 | tf_op jit(solution)/shard_map/ppermute | solution.py:338
  12.0 0.1 collective-permute-done.2.refs_2_
  12.2 0.0 collective-permute-done.3.refs_3_
  12.2 1.8 %collective-permute-start.6 = (f32[16,256]{1,0:T(8,128)S(1)}, f32[16,256]{1,0:T(8,128)S(1)}, u32[]{:S(2)}, u32[]{:S(2)}) collective-permute-start(f32[16,256]{1,0:T(8,128)S(1)} %get-tuple-element.12.refs_0_), channel_id=1, source_target_pairs={{0,12},{1,13},{2,14},{3,15},{4,8},{5,9},{6,10},{7,11},{8,28},{9,29... | collective-permute-start | bytes 49160 | tf_op jit(solution)/shard_map/ppermute | solution.py:338
  14.0 0.1 collective-permute-start.5
  14.1 2.6 %collective-permute-start.4 = (f32[16,256]{1,0:T(8,128)S(1)}, f32[16,256]{1,0:T(8,128)S(1)}, u32[]{:S(2)}, u32[]{:S(2)}) collective-permute-start(f32[16,256]{1,0:T(8,128)S(1)} %get-tuple-element.12.refs_0_), channel_id=1, source_target_pairs={{0,28},{1,29},{2,30},{3,31},{4,24},{5,25},{6,26},{7,27},{8,20},{9,... | collective-permute-start | bytes 49160 | tf_op jit(solution)/shard_map/ppermute | solution.py:338
  16.7 0.0 collective-permute-done.6.refs_3_
  16.7 0.5 %collective-permute-done.5.refs_2_ = f32[16,256]{1,0:T(8,128)S(1)} collective-permute-done((f32[16,256]{1,0:T(8,128)S(1)}, f32[16,256]{1,0:T(8,128)S(1)}, u32[]{:S(2)}, u32[]{:S(2)}) %collective-permute-start.5) | collective-permute-done | bytes 16416 | tf_op jit(solution)/shard_map/ppermute | solution.py:338
  17.2 0.9 %collective-permute-done.4.refs_1_ = f32[16,256]{1,0:T(8,128)S(1)} collective-permute-done((f32[16,256]{1,0:T(8,128)S(1)}, f32[16,256]{1,0:T(8,128)S(1)}, u32[]{:S(2)}, u32[]{:S(2)}) %collective-permute-start.4) | collective-permute-done | bytes 16416 | tf_op jit(solution)/shard_map/ppermute | solution.py:338
  18.2 0.6 %collective-permute-start.7 = (f32[80,256]{1,0:T(8,128)S(1)}, f32[80,256]{1,0:T(8,128)S(1)}, u32[]{:S(2)}, u32[]{:S(2)}) collective-permute-start(f32[80,256]{1,0:T(8,128)S(1)} %stack.1.held), channel_id=1, source_target_pairs={{0,4},{1,5},{2,6},{3,7},{4,0},{5,1},{6,2},{7,3},{8,12},{9,13},{10,... | collective-permute-start | bytes 245768 | tf_op jit(solution)/shard_map/ppermute | solution.py:338
  19.4 0.3 %collective-permute-done.7.sent = f32[80,256]{1,0:T(8,128)S(1)} collective-permute-done((f32[80,256]{1,0:T(8,128)S(1)}, f32[80,256]{1,0:T(8,128)S(1)}, u32[]{:S(2)}, u32[]{:S(2)}) %collective-permute-start.7) | collective-permute-done | bytes 81952 | tf_op jit(solution)/shard_map/ppermute | solution.py:338
  19.6 2.1 %factors.1 = (f32[4,1024]{1,0:T(4,128)}, f32[4,64,64]{2,1,0:T(8,128)}) custom-call(f32[1]{0:T(128)S(6)} %copy.10.damping, f32[80,256]{1,0:T(8,128)S(1)} %stack.1.held, f32[80,256]{1,0:T(8,128)S(1)} %collective-permute-done.7.sent), custom_call_target="tpu_custom_call" | custom-call | tf_op jit(solution)/shard_map/factors/pallas_call | solution.py:448
  (2 shorter events, 0.0 us)
Async XLA Ops:
  3.2 5.4 %collective-permute-start = (f32[32,256]{1,0:T(8,128)S(1)}, f32[32,256]{1,0:T(8,128)S(1)}, u32[]{:S(2)}, u32[]{:S(2)}) collective-permute-start(f32[32,256]{1,0:T(8,128)S(1)} %get-tuple-element.8), channel_id=1, source_target_pairs={{0,6},{1,7},{2,4},{3,5},{4,2},{5,3},{6,0},{7,1},{8,14},{9,15},{10,... | collective-permute-start | bytes 98312 | tf_op jit(solution)/shard_map/ppermute | solution.py:338
  6.8 5.2 %collective-permute-start.1 = (f32[32,256]{1,0:T(8,128)S(1)}, f32[32,256]{1,0:T(8,128)S(1)}, u32[]{:S(2)}, u32[]{:S(2)}) collective-permute-start(f32[32,256]{1,0:T(8,128)S(1)} %get-tuple-element.9), channel_id=1, source_target_pairs={{0,7},{1,6},{2,5},{3,4},{4,3},{5,2},{6,1},{7,0},{8,15},{9,14},{10,... | collective-permute-start | bytes 98312 | tf_op jit(solution)/shard_map/ppermute | solution.py:338
  8.4 3.8 %collective-permute-start.2 = (f32[32,256]{1,0:T(8,128)S(1)}, f32[32,256]{1,0:T(8,128)S(1)}, u32[]{:S(2)}, u32[]{:S(2)}) collective-permute-start(f32[32,256]{1,0:T(8,128)S(1)} %get-tuple-element.10), channel_id=1, source_target_pairs={{0,5},{1,4},{2,7},{3,6},{4,1},{5,0},{6,3},{7,2},{8,13},{9,12},{10,... | collective-permute-start | bytes 98312 | tf_op jit(solution)/shard_map/ppermute | solution.py:338
  8.6 3.5 %collective-permute-start.3 = (f32[32,256]{1,0:T(8,128)S(1)}, f32[32,256]{1,0:T(8,128)S(1)}, u32[]{:S(2)}, u32[]{:S(2)}) collective-permute-start(f32[32,256]{1,0:T(8,128)S(1)} %get-tuple-element.11), channel_id=1, source_target_pairs={{0,4},{1,5},{2,6},{3,7},{4,0},{5,1},{6,2},{7,3},{8,12},{9,13},{10,... | collective-permute-start | bytes 98312 | tf_op jit(solution)/shard_map/ppermute | solution.py:338
  12.2 4.5 %collective-permute-start.6 = (f32[16,256]{1,0:T(8,128)S(1)}, f32[16,256]{1,0:T(8,128)S(1)}, u32[]{:S(2)}, u32[]{:S(2)}) collective-permute-start(f32[16,256]{1,0:T(8,128)S(1)} %get-tuple-element.12.refs_0_), channel_id=1, source_target_pairs={{0,12},{1,13},{2,14},{3,15},{4,8},{5,9},{6,10},{7,11},{8,28},{9,29... | collective-permute-start | bytes 49160 | tf_op jit(solution)/shard_map/ppermute | solution.py:338
  14.0 3.2 %collective-permute-start.5 = (f32[16,256]{1,0:T(8,128)S(1)}, f32[16,256]{1,0:T(8,128)S(1)}, u32[]{:S(2)}, u32[]{:S(2)}) collective-permute-start(f32[16,256]{1,0:T(8,128)S(1)} %get-tuple-element.12.refs_0_), channel_id=1, source_target_pairs={{0,20},{1,21},{2,22},{3,23},{4,16},{5,17},{6,18},{7,19},{8,4},{9,5... | collective-permute-start | bytes 49160 | tf_op jit(solution)/shard_map/ppermute | solution.py:338
  14.1 4.1 %collective-permute-start.4 = (f32[16,256]{1,0:T(8,128)S(1)}, f32[16,256]{1,0:T(8,128)S(1)}, u32[]{:S(2)}, u32[]{:S(2)}) collective-permute-start(f32[16,256]{1,0:T(8,128)S(1)} %get-tuple-element.12.refs_0_), channel_id=1, source_target_pairs={{0,28},{1,29},{2,30},{3,31},{4,24},{5,25},{6,26},{7,27},{8,20},{9,... | collective-permute-start | bytes 49160 | tf_op jit(solution)/shard_map/ppermute | solution.py:338
  18.2 1.5 %collective-permute-start.7 = (f32[80,256]{1,0:T(8,128)S(1)}, f32[80,256]{1,0:T(8,128)S(1)}, u32[]{:S(2)}, u32[]{:S(2)}) collective-permute-start(f32[80,256]{1,0:T(8,128)S(1)} %stack.1.held), channel_id=1, source_target_pairs={{0,4},{1,5},{2,6},{3,7},{4,0},{5,1},{6,2},{7,3},{8,12},{9,13},{10,... | collective-permute-start | bytes 245768 | tf_op jit(solution)/shard_map/ppermute | solution.py:338

commit v27 on v25

--- a/solution.py
+++ b/solution.py
@@ -79,22 +79,13 @@
             for copy in pending[-1]:
                 copy.start()
 
-    order_copy.wait()
     rows = examples * parts
-    source = lax.broadcasted_iota(jnp.int32, (8, tokens), 1) // EXAMPLE_LENGTH
-    target = jnp.zeros((8, tokens), jnp.int32)
-    for s in range(examples):
-        target = jnp.where(source == s, order[0, s], target)
-    target = jnp.concatenate([target] * (rows // 8), axis=0)
-    place = lax.broadcasted_iota(jnp.int32, (rows, tokens), 0) // parts
-    mask[...] = jnp.where(target == place, scaling, 0.0)
-
-    def product(first, data, weights):
-        total = None
-        for n in range(data.shape[1] // CHUNK):
-            for copy in pending[first + n]:
+
+    def product(total, n, data, weights, stages):
+        for stage in stages:
+            for copy in pending[n + stage]:
                 copy.wait()
-            here = pl.ds(n * CHUNK, CHUNK)
+            here = pl.ds(stage * CHUNK, CHUNK)
             term = dot_nt(weights[:, here], data[:, here])
             total = term if total is None else total + term
         return total
@@ -110,17 +101,32 @@
         return [jnp.concatenate(half, axis=0) for half in zip(*tiles)]
 
     def spread_sketch(values):
-        return split(
+        return [
             jnp.concatenate(
-                [values[h * SLOT : (h + 1) * SLOT] for h in range(halves) for _ in range(per)],
+                [part[h * SLOT : (h + 1) * SLOT] for h in range(halves) for _ in range(per)],
                 axis=0,
             )
-        )
-
-    from_grads = product(0, grads, weights_out)
+            for part in split(values)
+        ]
+
+    out_stages, in_stages = grads.shape[1] // CHUNK, width // CHUNK
+    from_grads = product(None, 0, grads, weights_out, range(out_stages))
+    from_acts = product(None, out_stages, acts, weights_in, range(in_stages // 2))
+
+    order_copy.wait()
+    source = lax.broadcasted_iota(jnp.int32, (8, tokens), 1) // EXAMPLE_LENGTH
+    target = jnp.zeros((8, tokens), jnp.int32)
+    for s in range(examples):
+        target = jnp.where(source == s, order[0, s], target)
+    target = jnp.concatenate([target] * (rows // 8), axis=0)
+    place = lax.broadcasted_iota(jnp.int32, (rows, tokens), 0) // parts
+    mask[...] = jnp.where(target == place, scaling, 0.0)
     left_grads = spread_low(from_grads[sketch:], 0)
     right_grads = spread_sketch(from_grads[:sketch])
-    from_acts = product(grads.shape[1] // CHUNK, acts, weights_in)
+
+    from_acts = product(
+        from_acts, out_stages, acts, weights_in, range(in_stages // 2, in_stages)
+    )
     left_acts = spread_low(from_acts[sketch:], 1)
     right_acts = spread_sketch(from_acts[:sketch])
     left_high, left_low = [

time: 21.7 us -> 21.8 us (level)
  no operation moved by 1% of the time
where the time goes in v27:
time: 21.8 us; the launch traced here: 21.6 us
  starting transfers between devices  10 us (46%)
  waiting for transfers between devices  5.59 us (26%)
  Pallas kernels  4.71 us (22%)
  between operations  1.3 us (6%)
    ppermute x8, starting transfers between devices, permute(): return lax.ppermute(x, ('ex', 'mp'), sorted(pairs))  10 us
    ppermute x8, waiting for transfers between devices, permute(): return lax.ppermute(x, ('ex', 'mp'), sorted(pairs))  5.59 us
    pallas_call x1, Pallas kernels, local(): pl.pallas_call(functools.partial(partial_kernel, parts, scaling), out_sha...  2.62 us
    pallas_call x1, Pallas kernels, local(): pl.pallas_call(functools.partial(factor_kernel, parts), out_shape=[jax.Sh...  2.07 us
  transfers between devices with their start and end apart: 8, of which 5 were waited for; matrix products, arithmetic and copies ran while one was open for 0% of the time, Pallas kernels for 0%

profile of v27, /device:TPU:0, one launch (start us, length us, event | category | flops | bytes accessed | tf_op | source)
XLA Modules:
  0.0 21.6 jit_solution(4001131462667059434)
XLA Ops:
  0.6 2.6 %partials.1 = (f32[32,256]{1,0:T(8,128)S(1)}, f32[32,256]{1,0:T(8,128)S(1)}, f32[32,256]{1,0:T(8,128)S(1)}, f32[32,256]{1,0:T(8,128)S(1)}) custom-call(bf16[1,128,4096]{2,1,0:T(8,128)(2,1)} %acts_hbm.1, bf16[1,128,1024]{2,1,0:T(8,128)(2,1)} %grads_hbm.1, bf16[1,16,4096]{2,1,0:T(8,128)(2,1)} %down_hbm.1, bf16[1,16,1024]{2,1,0:T(8,128)(2,1)} %up_hbm.1, ...), custom_call_target="tpu_custom_call" | custom-call | tf_op jit(solution)/shard_map/partials/pallas_call | solution.py:396
  3.3 4.6 %collective-permute-start = (f32[32,256]{1,0:T(8,128)S(1)}, f32[32,256]{1,0:T(8,128)S(1)}, u32[]{:S(2)}, u32[]{:S(2)}) collective-permute-start(f32[32,256]{1,0:T(8,128)S(1)} %get-tuple-element.8), channel_id=1, source_target_pairs={{0,7},{1,6},{2,5},{3,4},{4,3},{5,2},{6,1},{7,0},{8,15},{9,14},{10,... | collective-permute-start | bytes 98312 | tf_op jit(solution)/shard_map/ppermute | solution.py:344
  7.8 0.0 collective-permute-start.1
  7.8 0.9 %collective-permute-start.2 = (f32[32,256]{1,0:T(8,128)S(1)}, f32[32,256]{1,0:T(8,128)S(1)}, u32[]{:S(2)}, u32[]{:S(2)}) collective-permute-start(f32[32,256]{1,0:T(8,128)S(1)} %get-tuple-element.10), channel_id=1, source_target_pairs={{0,5},{1,4},{2,7},{3,6},{4,1},{5,0},{6,3},{7,2},{8,13},{9,12},{10,... | collective-permute-start | bytes 98312 | tf_op jit(solution)/shard_map/ppermute | solution.py:344
  8.7 0.0 collective-permute-start.3
  8.7 0.9 %collective-permute-done.refs_0_ = f32[32,256]{1,0:T(8,128)S(1)} collective-permute-done((f32[32,256]{1,0:T(8,128)S(1)}, f32[32,256]{1,0:T(8,128)S(1)}, u32[]{:S(2)}, u32[]{:S(2)}) %collective-permute-start) | collective-permute-done | bytes 32800 | tf_op jit(solution)/shard_map/ppermute | solution.py:344
  9.6 2.8 %collective-permute-done.1.refs_1_ = f32[32,256]{1,0:T(8,128)S(1)} collective-permute-done((f32[32,256]{1,0:T(8,128)S(1)}, f32[32,256]{1,0:T(8,128)S(1)}, u32[]{:S(2)}, u32[]{:S(2)}) %collective-permute-start.1) | collective-permute-done | bytes 32800 | tf_op jit(solution)/shard_map/ppermute | solution.py:344
  12.3 0.0 collective-permute-done.2.refs_2_
  12.3 0.0 collective-permute-done.3.refs_3_
  12.4 1.5 %collective-permute-start.6 = (f32[16,256]{1,0:T(8,128)S(1)}, f32[16,256]{1,0:T(8,128)S(1)}, u32[]{:S(2)}, u32[]{:S(2)}) collective-permute-start(f32[16,256]{1,0:T(8,128)S(1)} %get-tuple-element.12.refs_0_), channel_id=1, source_target_pairs={{0,12},{1,13},{2,14},{3,15},{4,8},{5,9},{6,10},{7,11},{8,20},{9,21... | collective-permute-start | bytes 49160 | tf_op jit(solution)/shard_map/ppermute | solution.py:344
  13.9 1.2 %collective-permute-start.5 = (f32[16,256]{1,0:T(8,128)S(1)}, f32[16,256]{1,0:T(8,128)S(1)}, u32[]{:S(2)}, u32[]{:S(2)}) collective-permute-start(f32[16,256]{1,0:T(8,128)S(1)} %get-tuple-element.12.refs_0_), channel_id=1, source_target_pairs={{0,28},{1,29},{2,30},{3,31},{4,24},{5,25},{6,26},{7,27},{8,4},{9,5... | collective-permute-start | bytes 49160 | tf_op jit(solution)/shard_map/ppermute | solution.py:344
  15.1 1.5 %collective-permute-start.4 = (f32[16,256]{1,0:T(8,128)S(1)}, f32[16,256]{1,0:T(8,128)S(1)}, u32[]{:S(2)}, u32[]{:S(2)}) collective-permute-start(f32[16,256]{1,0:T(8,128)S(1)} %get-tuple-element.12.refs_0_), channel_id=1, source_target_pairs={{0,20},{1,21},{2,22},{3,23},{4,16},{5,17},{6,18},{7,19},{8,28},{9,... | collective-permute-start | bytes 49160 | tf_op jit(solution)/shard_map/ppermute | solution.py:344
  16.6 0.0 collective-permute-done.6.refs_3_
  16.6 0.6 %collective-permute-done.5.refs_2_ = f32[16,256]{1,0:T(8,128)S(1)} collective-permute-done((f32[16,256]{1,0:T(8,128)S(1)}, f32[16,256]{1,0:T(8,128)S(1)}, u32[]{:S(2)}, u32[]{:S(2)}) %collective-permute-start.5) | collective-permute-done | bytes 16416 | tf_op jit(solution)/shard_map/ppermute | solution.py:344
  17.2 1.1 %collective-permute-done.4.refs_1_ = f32[16,256]{1,0:T(8,128)S(1)} collective-permute-done((f32[16,256]{1,0:T(8,128)S(1)}, f32[16,256]{1,0:T(8,128)S(1)}, u32[]{:S(2)}, u32[]{:S(2)}) %collective-permute-start.4) | collective-permute-done | bytes 16416 | tf_op jit(solution)/shard_map/ppermute | solution.py:344
  18.3 0.3 %collective-permute-start.7 = (f32[80,256]{1,0:T(8,128)S(1)}, f32[80,256]{1,0:T(8,128)S(1)}, u32[]{:S(2)}, u32[]{:S(2)}) collective-permute-start(f32[80,256]{1,0:T(8,128)S(1)} %stack.1.held), channel_id=1, source_target_pairs={{0,4},{1,5},{2,6},{3,7},{4,0},{5,1},{6,2},{7,3},{8,12},{9,13},{10,... | collective-permute-start | bytes 245768 | tf_op jit(solution)/shard_map/ppermute | solution.py:344
  19.3 0.3 %collective-permute-done.7.sent = f32[80,256]{1,0:T(8,128)S(1)} collective-permute-done((f32[80,256]{1,0:T(8,128)S(1)}, f32[80,256]{1,0:T(8,128)S(1)}, u32[]{:S(2)}, u32[]{:S(2)}) %collective-permute-start.7) | collective-permute-done | bytes 81952 | tf_op jit(solution)/shard_map/ppermute | solution.py:344
  19.5 2.1 %factors.1 = (f32[4,1024]{1,0:T(4,128)}, f32[4,64,64]{2,1,0:T(8,128)}) custom-call(f32[1]{0:T(128)S(6)} %copy.10.damping, f32[80,256]{1,0:T(8,128)S(1)} %stack.1.held, f32[80,256]{1,0:T(8,128)S(1)} %collective-permute-done.7.sent), custom_call_target="tpu_custom_call" | custom-call | tf_op jit(solution)/shard_map/factors/pallas_call | solution.py:447
  (2 shorter events, 0.0 us)
Async XLA Ops:
  3.3 6.3 %collective-permute-start = (f32[32,256]{1,0:T(8,128)S(1)}, f32[32,256]{1,0:T(8,128)S(1)}, u32[]{:S(2)}, u32[]{:S(2)}) collective-permute-start(f32[32,256]{1,0:T(8,128)S(1)} %get-tuple-element.8), channel_id=1, source_target_pairs={{0,7},{1,6},{2,5},{3,4},{4,3},{5,2},{6,1},{7,0},{8,15},{9,14},{10,... | collective-permute-start | bytes 98312 | tf_op jit(solution)/shard_map/ppermute | solution.py:344
  7.8 4.5 %collective-permute-start.1 = (f32[32,256]{1,0:T(8,128)S(1)}, f32[32,256]{1,0:T(8,128)S(1)}, u32[]{:S(2)}, u32[]{:S(2)}) collective-permute-start(f32[32,256]{1,0:T(8,128)S(1)} %get-tuple-element.9), channel_id=1, source_target_pairs={{0,6},{1,7},{2,4},{3,5},{4,2},{5,3},{6,0},{7,1},{8,14},{9,15},{10,... | collective-permute-start | bytes 98312 | tf_op jit(solution)/shard_map/ppermute | solution.py:344
  7.8 4.5 %collective-permute-start.2 = (f32[32,256]{1,0:T(8,128)S(1)}, f32[32,256]{1,0:T(8,128)S(1)}, u32[]{:S(2)}, u32[]{:S(2)}) collective-permute-start(f32[32,256]{1,0:T(8,128)S(1)} %get-tuple-element.10), channel_id=1, source_target_pairs={{0,5},{1,4},{2,7},{3,6},{4,1},{5,0},{6,3},{7,2},{8,13},{9,12},{10,... | collective-permute-start | bytes 98312 | tf_op jit(solution)/shard_map/ppermute | solution.py:344
  8.7 3.6 %collective-permute-start.3 = (f32[32,256]{1,0:T(8,128)S(1)}, f32[32,256]{1,0:T(8,128)S(1)}, u32[]{:S(2)}, u32[]{:S(2)}) collective-permute-start(f32[32,256]{1,0:T(8,128)S(1)} %get-tuple-element.11), channel_id=1, source_target_pairs={{0,4},{1,5},{2,6},{3,7},{4,0},{5,1},{6,2},{7,3},{8,12},{9,13},{10,... | collective-permute-start | bytes 98312 | tf_op jit(solution)/shard_map/ppermute | solution.py:344
  12.4 4.2 %collective-permute-start.6 = (f32[16,256]{1,0:T(8,128)S(1)}, f32[16,256]{1,0:T(8,128)S(1)}, u32[]{:S(2)}, u32[]{:S(2)}) collective-permute-start(f32[16,256]{1,0:T(8,128)S(1)} %get-tuple-element.12.refs_0_), channel_id=1, source_target_pairs={{0,12},{1,13},{2,14},{3,15},{4,8},{5,9},{6,10},{7,11},{8,20},{9,21... | collective-permute-start | bytes 49160 | tf_op jit(solution)/shard_map/ppermute | solution.py:344
  13.9 3.3 %collective-permute-start.5 = (f32[16,256]{1,0:T(8,128)S(1)}, f32[16,256]{1,0:T(8,128)S(1)}, u32[]{:S(2)}, u32[]{:S(2)}) collective-permute-start(f32[16,256]{1,0:T(8,128)S(1)} %get-tuple-element.12.refs_0_), channel_id=1, source_target_pairs={{0,28},{1,29},{2,30},{3,31},{4,24},{5,25},{6,26},{7,27},{8,4},{9,5... | collective-permute-start | bytes 49160 | tf_op jit(solution)/shard_map/ppermute | solution.py:344
  15.1 3.2 %collective-permute-start.4 = (f32[16,256]{1,0:T(8,128)S(1)}, f32[16,256]{1,0:T(8,128)S(1)}, u32[]{:S(2)}, u32[]{:S(2)}) collective-permute-start(f32[16,256]{1,0:T(8,128)S(1)} %get-tuple-element.12.refs_0_), channel_id=1, source_target_pairs={{0,20},{1,21},{2,22},{3,23},{4,16},{5,17},{6,18},{7,19},{8,28},{9,... | collective-permute-start | bytes 49160 | tf_op jit(solution)/shard_map/ppermute | solution.py:344
  18.3 1.3 %collective-permute-start.7 = (f32[80,256]{1,0:T(8,128)S(1)}, f32[80,256]{1,0:T(8,128)S(1)}, u32[]{:S(2)}, u32[]{:S(2)}) collective-permute-start(f32[80,256]{1,0:T(8,128)S(1)} %stack.1.held), channel_id=1, source_target_pairs={{0,4},{1,5},{2,6},{3,7},{4,0},{5,1},{6,2},{7,3},{8,12},{9,13},{10,... | collective-permute-start | bytes 245768 | tf_op jit(solution)/shard_map/ppermute | solution.py:344

commit v28 on v25

--- a/solution.py
+++ b/solution.py
@@ -151,8 +151,9 @@
             ]
 
 
-def sum_kernel(*refs):
-    chunks, (columns, feature_rows) = refs[:-2], refs[-2:]
+def sum_kernel(damping, *refs):
+    chunks, (columns, feature_rows, ridge) = refs[:-3], refs[-3:]
+    ridge[...] = jnp.full(ridge.shape, damping[0], jnp.float32)
     examples, padded = columns.shape
     total = chunks[0][...]
     for chunk in chunks[1:]:
@@ -197,7 +198,7 @@
     return guess * (2.0 - x * guess)
 
 
-def factor_kernel(parts, damping, held, sent, features, factors):
+def factor_kernel(parts, ridge, held, sent, features, factors):
     channels, sketch, _ = factors.shape
     examples = features.shape[0] * parts
     gathered = held.shape[0] - examples
@@ -217,7 +218,6 @@
     sub = lax.broadcasted_iota(jnp.int32, (PANEL, LANES), 0)
     slot = lane // SLOT
     within = lane % SLOT
-    ridge = damping[0]
     tile = []
     for q in range(panels):
         hr, at = divmod(q, per_half)
@@ -230,7 +230,7 @@
                 value = block if c == 0 else jnp.where(slot == c, block, value)
             value = value * (1.0 / stacked.shape[0])
             if h == hr:
-                value = value + jnp.where(within == at * PANEL + sub, ridge, 0.0)
+                value = value + jnp.where(within == at * PANEL + sub, ridge[...], 0.0)
             line.append(value)
         tile.append(line)
 
@@ -419,14 +419,15 @@
     )
     chunks = [exchange(sends[d], 1, d) for d in range(parts - 1, -1, -1)]
     padded = max(span, GROUP * sketch)
-    columns, feature_rows = pl.pallas_call(
+    columns, feature_rows, ridge = pl.pallas_call(
         sum_kernel,
-        out_shape=[pltpu.VMEM((examples, padded), jnp.float32)] * 2,
-        in_specs=[vmem()] * parts,
-        out_specs=[vmem()] * 2,
+        out_shape=[pltpu.VMEM((examples, padded), jnp.float32)] * 2
+        + [pltpu.VMEM((PANEL, LANES), jnp.float32)],
+        in_specs=[smem()] + [vmem()] * parts,
+        out_specs=[vmem()] * 3,
         compiler_params=pltpu.CompilerParams(vmem_limit_bytes=2 * 2**20),
         name="sums",
-    )(*in_vmem(*chunks))
+    )(damping, *in_vmem(*chunks))
     shifts = sorted(range(1, shards // 2), key=lambda d: (-min(d, shards // 2 - d), -d))
     near = [columns] + [shift_chips(columns, d) for d in shifts] + [feature_rows]
     held = pl.pallas_call(
@@ -444,11 +445,11 @@
             jax.ShapeDtypeStruct((examples // parts, rank * sketch), jnp.float32),
             jax.ShapeDtypeStruct((per, sketch, sketch), jnp.float32),
         ],
-        in_specs=[smem()] + [vmem()] * 2,
+        in_specs=[vmem()] * 3,
         out_specs=[vmem()] * 2,
         compiler_params=pltpu.CompilerParams(vmem_limit_bytes=8 * 2**20),
         name="factors",
-    )(damping, *in_vmem(held, sent))
+    )(*in_vmem(ridge, held, sent))
 
 
 def solution(mesh):

time: 21.7 us -> 21.7 us (level)
  no operation moved by 1% of the time
where the time goes in v28:
time: 21.7 us; the launch traced here: 21.6 us
  starting transfers between devices  10 us (46%)
  waiting for transfers between devices  5.59 us (26%)
  Pallas kernels  4.68 us (22%)
  between operations  1.31 us (6%)
    ppermute x8, starting transfers between devices, permute(): return lax.ppermute(x, ('ex', 'mp'), sorted(pairs))  10 us
    ppermute x8, waiting for transfers between devices, permute(): return lax.ppermute(x, ('ex', 'mp'), sorted(pairs))  5.59 us
    pallas_call x1, Pallas kernels, local(): pl.pallas_call(functools.partial(partial_kernel, parts, scaling), out_sha...  2.59 us
    pallas_call x1, Pallas kernels, local(): pl.pallas_call(functools.partial(factor_kernel, parts), out_shape=[jax.Sh...  2.07 us
  transfers between devices with their start and end apart: 8, of which 5 were waited for; matrix products, arithmetic and copies ran while one was open for 0% of the time, Pallas kernels for 0%

profile of v28, /device:TPU:0, one launch (start us, length us, event | category | flops | bytes accessed | tf_op | source)
XLA Modules:
  0.0 21.6 jit_solution(32921226985314582)
XLA Ops:
  0.6 2.6 %partials.1 = (f32[32,256]{1,0:T(8,128)S(1)}, f32[32,256]{1,0:T(8,128)S(1)}, f32[32,256]{1,0:T(8,128)S(1)}, f32[32,256]{1,0:T(8,128)S(1)}) custom-call(bf16[1,128,4096]{2,1,0:T(8,128)(2,1)} %acts_hbm.1, bf16[1,128,1024]{2,1,0:T(8,128)(2,1)} %grads_hbm.1, bf16[1,16,4096]{2,1,0:T(8,128)(2,1)} %down_hbm.1, bf16[1,16,1024]{2,1,0:T(8,128)(2,1)} %up_hbm.1, ...), custom_call_target="tpu_custom_call" | custom-call | tf_op jit(solution)/shard_map/partials/pallas_call | solution.py:390
  3.2 4.6 %collective-permute-start = (f32[32,256]{1,0:T(8,128)S(1)}, f32[32,256]{1,0:T(8,128)S(1)}, u32[]{:S(2)}, u32[]{:S(2)}) collective-permute-start(f32[32,256]{1,0:T(8,128)S(1)} %get-tuple-element.9), channel_id=1, source_target_pairs={{0,7},{1,6},{2,5},{3,4},{4,3},{5,2},{6,1},{7,0},{8,15},{9,14},{10,... | collective-permute-start | bytes 98312 | tf_op jit(solution)/shard_map/ppermute | solution.py:338
  7.8 0.0 collective-permute-start.1
  7.8 0.9 %collective-permute-start.2 = (f32[32,256]{1,0:T(8,128)S(1)}, f32[32,256]{1,0:T(8,128)S(1)}, u32[]{:S(2)}, u32[]{:S(2)}) collective-permute-start(f32[32,256]{1,0:T(8,128)S(1)} %get-tuple-element.11), channel_id=1, source_target_pairs={{0,5},{1,4},{2,7},{3,6},{4,1},{5,0},{6,3},{7,2},{8,13},{9,12},{10,... | collective-permute-start | bytes 98312 | tf_op jit(solution)/shard_map/ppermute | solution.py:338
  8.7 0.0 collective-permute-start.3
  9.4 0.2 collective-permute-done.refs_0_
  9.6 2.8 %collective-permute-done.1.refs_1_ = f32[32,256]{1,0:T(8,128)S(1)} collective-permute-done((f32[32,256]{1,0:T(8,128)S(1)}, f32[32,256]{1,0:T(8,128)S(1)}, u32[]{:S(2)}, u32[]{:S(2)}) %collective-permute-start.1) | collective-permute-done | bytes 32800 | tf_op jit(solution)/shard_map/ppermute | solution.py:338
  12.3 0.0 collective-permute-done.2.refs_2_
  12.3 0.0 collective-permute-done.3.refs_3_
  12.3 1.5 %collective-permute-start.6 = (f32[16,256]{1,0:T(8,128)S(1)}, f32[16,256]{1,0:T(8,128)S(1)}, u32[]{:S(2)}, u32[]{:S(2)}) collective-permute-start(f32[16,256]{1,0:T(8,128)S(1)} %get-tuple-element.14.refs_0_), channel_id=1, source_target_pairs={{0,12},{1,13},{2,14},{3,15},{4,8},{5,9},{6,10},{7,11},{8,20},{9,21... | collective-permute-start | bytes 49160 | tf_op jit(solution)/shard_map/ppermute | solution.py:338
  13.9 1.2 %collective-permute-start.5 = (f32[16,256]{1,0:T(8,128)S(1)}, f32[16,256]{1,0:T(8,128)S(1)}, u32[]{:S(2)}, u32[]{:S(2)}) collective-permute-start(f32[16,256]{1,0:T(8,128)S(1)} %get-tuple-element.14.refs_0_), channel_id=1, source_target_pairs={{0,28},{1,29},{2,30},{3,31},{4,24},{5,25},{6,26},{7,27},{8,4},{9,5... | collective-permute-start | bytes 49160 | tf_op jit(solution)/shard_map/ppermute | solution.py:338
  15.1 1.5 %collective-permute-start.4 = (f32[16,256]{1,0:T(8,128)S(1)}, f32[16,256]{1,0:T(8,128)S(1)}, u32[]{:S(2)}, u32[]{:S(2)}) collective-permute-start(f32[16,256]{1,0:T(8,128)S(1)} %get-tuple-element.14.refs_0_), channel_id=1, source_target_pairs={{0,20},{1,21},{2,22},{3,23},{4,16},{5,17},{6,18},{7,19},{8,28},{9,... | collective-permute-start | bytes 49160 | tf_op jit(solution)/shard_map/ppermute | solution.py:338
  16.5 0.0 collective-permute-done.6.refs_3_
  16.5 0.6 %collective-permute-done.5.refs_2_ = f32[16,256]{1,0:T(8,128)S(1)} collective-permute-done((f32[16,256]{1,0:T(8,128)S(1)}, f32[16,256]{1,0:T(8,128)S(1)}, u32[]{:S(2)}, u32[]{:S(2)}) %collective-permute-start.5) | collective-permute-done | bytes 16416 | tf_op jit(solution)/shard_map/ppermute | solution.py:338
  17.2 1.1 %collective-permute-done.4.refs_1_ = f32[16,256]{1,0:T(8,128)S(1)} collective-permute-done((f32[16,256]{1,0:T(8,128)S(1)}, f32[16,256]{1,0:T(8,128)S(1)}, u32[]{:S(2)}, u32[]{:S(2)}) %collective-permute-start.4) | collective-permute-done | bytes 16416 | tf_op jit(solution)/shard_map/ppermute | solution.py:338
  18.2 0.3 %collective-permute-start.7 = (f32[80,256]{1,0:T(8,128)S(1)}, f32[80,256]{1,0:T(8,128)S(1)}, u32[]{:S(2)}, u32[]{:S(2)}) collective-permute-start(f32[80,256]{1,0:T(8,128)S(1)} %stack.1.held), channel_id=1, source_target_pairs={{0,4},{1,5},{2,6},{3,7},{4,0},{5,1},{6,2},{7,3},{8,12},{9,13},{10,... | collective-permute-start | bytes 245768 | tf_op jit(solution)/shard_map/ppermute | solution.py:338
  18.6 0.9 %collective-permute-done.7.sent = f32[80,256]{1,0:T(8,128)S(1)} collective-permute-done((f32[80,256]{1,0:T(8,128)S(1)}, f32[80,256]{1,0:T(8,128)S(1)}, u32[]{:S(2)}, u32[]{:S(2)}) %collective-permute-start.7) | collective-permute-done | bytes 81952 | tf_op jit(solution)/shard_map/ppermute | solution.py:338
  19.5 2.1 %factors.1 = (f32[4,1024]{1,0:T(4,128)}, f32[4,64,64]{2,1,0:T(8,128)}) custom-call(f32[8,128]{1,0:T(8,128)S(1)} %get-tuple-element.13.ridge, f32[80,256]{1,0:T(8,128)S(1)} %stack.1.held, f32[80,256]{1,0:T(8,128)S(1)} %collective-permute-done.7.sent), custom_call_target="tpu_custom_call" | custom-call | tf_op jit(solution)/shard_map/factors/pallas_call | solution.py:442
  (2 shorter events, 0.0 us)
Async XLA Ops:
  3.2 6.3 %collective-permute-start = (f32[32,256]{1,0:T(8,128)S(1)}, f32[32,256]{1,0:T(8,128)S(1)}, u32[]{:S(2)}, u32[]{:S(2)}) collective-permute-start(f32[32,256]{1,0:T(8,128)S(1)} %get-tuple-element.9), channel_id=1, source_target_pairs={{0,7},{1,6},{2,5},{3,4},{4,3},{5,2},{6,1},{7,0},{8,15},{9,14},{10,... | collective-permute-start | bytes 98312 | tf_op jit(solution)/shard_map/ppermute | solution.py:338
  7.8 4.5 %collective-permute-start.1 = (f32[32,256]{1,0:T(8,128)S(1)}, f32[32,256]{1,0:T(8,128)S(1)}, u32[]{:S(2)}, u32[]{:S(2)}) collective-permute-start(f32[32,256]{1,0:T(8,128)S(1)} %get-tuple-element.10), channel_id=1, source_target_pairs={{0,6},{1,7},{2,4},{3,5},{4,2},{5,3},{6,0},{7,1},{8,14},{9,15},{10,... | collective-permute-start | bytes 98312 | tf_op jit(solution)/shard_map/ppermute | solution.py:338
  7.8 4.5 %collective-permute-start.2 = (f32[32,256]{1,0:T(8,128)S(1)}, f32[32,256]{1,0:T(8,128)S(1)}, u32[]{:S(2)}, u32[]{:S(2)}) collective-permute-start(f32[32,256]{1,0:T(8,128)S(1)} %get-tuple-element.11), channel_id=1, source_target_pairs={{0,5},{1,4},{2,7},{3,6},{4,1},{5,0},{6,3},{7,2},{8,13},{9,12},{10,... | collective-permute-start | bytes 98312 | tf_op jit(solution)/shard_map/ppermute | solution.py:338
  8.7 3.6 %collective-permute-start.3 = (f32[32,256]{1,0:T(8,128)S(1)}, f32[32,256]{1,0:T(8,128)S(1)}, u32[]{:S(2)}, u32[]{:S(2)}) collective-permute-start(f32[32,256]{1,0:T(8,128)S(1)} %get-tuple-element.12), channel_id=1, source_target_pairs={{0,4},{1,5},{2,6},{3,7},{4,0},{5,1},{6,2},{7,3},{8,12},{9,13},{10,... | collective-permute-start | bytes 98312 | tf_op jit(solution)/shard_map/ppermute | solution.py:338
  12.3 4.2 %collective-permute-start.6 = (f32[16,256]{1,0:T(8,128)S(1)}, f32[16,256]{1,0:T(8,128)S(1)}, u32[]{:S(2)}, u32[]{:S(2)}) collective-permute-start(f32[16,256]{1,0:T(8,128)S(1)} %get-tuple-element.14.refs_0_), channel_id=1, source_target_pairs={{0,12},{1,13},{2,14},{3,15},{4,8},{5,9},{6,10},{7,11},{8,20},{9,21... | collective-permute-start | bytes 49160 | tf_op jit(solution)/shard_map/ppermute | solution.py:338
  13.9 3.3 %collective-permute-start.5 = (f32[16,256]{1,0:T(8,128)S(1)}, f32[16,256]{1,0:T(8,128)S(1)}, u32[]{:S(2)}, u32[]{:S(2)}) collective-permute-start(f32[16,256]{1,0:T(8,128)S(1)} %get-tuple-element.14.refs_0_), channel_id=1, source_target_pairs={{0,28},{1,29},{2,30},{3,31},{4,24},{5,25},{6,26},{7,27},{8,4},{9,5... | collective-permute-start | bytes 49160 | tf_op jit(solution)/shard_map/ppermute | solution.py:338
  15.1 3.2 %collective-permute-start.4 = (f32[16,256]{1,0:T(8,128)S(1)}, f32[16,256]{1,0:T(8,128)S(1)}, u32[]{:S(2)}, u32[]{:S(2)}) collective-permute-start(f32[16,256]{1,0:T(8,128)S(1)} %get-tuple-element.14.refs_0_), channel_id=1, source_target_pairs={{0,20},{1,21},{2,22},{3,23},{4,16},{5,17},{6,18},{7,19},{8,28},{9,... | collective-permute-start | bytes 49160 | tf_op jit(solution)/shard_map/ppermute | solution.py:338
  18.2 1.3 %collective-permute-start.7 = (f32[80,256]{1,0:T(8,128)S(1)}, f32[80,256]{1,0:T(8,128)S(1)}, u32[]{:S(2)}, u32[]{:S(2)}) collective-permute-start(f32[80,256]{1,0:T(8,128)S(1)} %stack.1.held), channel_id=1, source_target_pairs={{0,4},{1,5},{2,6},{3,7},{4,0},{5,1},{6,2},{7,3},{8,12},{9,13},{10,... | collective-permute-start | bytes 245768 | tf_op jit(solution)/shard_map/ppermute | solution.py:338

commit v29 on v28

--- a/solution.py
+++ b/solution.py
@@ -13,7 +13,7 @@
 SLOT = 32
 GROUP = LANES // SLOT
 PANEL = 8
-CHUNK = 1024
+BOUNDS = ((0, 8), (0, 3, 5, 7, 8))
 
 
 def dot_nt(a, b):
@@ -52,12 +52,8 @@
     per = rank // parts
     halves = sketch // SLOT
 
-    def copies(source, target, sem, start, size):
-        return pltpu.make_async_copy(
-            source.at[0, :, pl.ds(start, size)],
-            target.at[:, pl.ds(start, size)],
-            sem,
-        )
+    def copies(source, target, sem, here):
+        return pltpu.make_async_copy(source.at[0, :, here], target.at[:, here], sem)
 
     order_copy = pltpu.make_async_copy(order_hbm.at[0], order, order_sem)
     order_copy.start()
@@ -66,18 +62,21 @@
         (acts_hbm, acts, proj_in_hbm, down_hbm, weights_in),
     ]
     pending = []
-    for data_hbm, data, first_hbm, second_hbm, weights in sources:
-        for start in range(0, data.shape[1], CHUNK):
-            n = len(pending)
-            pending.append(
-                [
-                    copies(first_hbm, weights.at[pl.ds(0, sketch)], sems.at[n, 0], start, CHUNK),
-                    copies(second_hbm, weights.at[pl.ds(sketch, rank)], sems.at[n, 1], start, CHUNK),
-                    copies(data_hbm, data, sems.at[n, 2], start, CHUNK),
-                ]
-            )
-            for copy in pending[-1]:
+    for (data_hbm, data, first_hbm, second_hbm, weights), bounds in zip(sources, BOUNDS):
+        stages = []
+        edges = [data.shape[1] * edge // 8 for edge in bounds]
+        for start, stop in zip(edges, edges[1:]):
+            here = pl.ds(start, stop - start)
+            sem = sems.at[len(pending), len(stages)]
+            stage = [
+                copies(first_hbm, weights.at[pl.ds(0, sketch)], sem.at[0], here),
+                copies(second_hbm, weights.at[pl.ds(sketch, rank)], sem.at[1], here),
+                copies(data_hbm, data, sem.at[2], here),
+            ]
+            for copy in stage:
                 copy.start()
+            stages.append((here, stage))
+        pending.append(stages)
 
     order_copy.wait()
     rows = examples * parts
@@ -89,12 +88,11 @@
     place = lax.broadcasted_iota(jnp.int32, (rows, tokens), 0) // parts
     mask[...] = jnp.where(target == place, scaling, 0.0)
 
-    def product(first, data, weights):
+    def product(n, data, weights):
         total = None
-        for n in range(data.shape[1] // CHUNK):
-            for copy in pending[first + n]:
+        for here, stage in pending[n]:
+            for copy in stage:
                 copy.wait()
-            here = pl.ds(n * CHUNK, CHUNK)
             term = dot_nt(weights[:, here], data[:, here])
             total = term if total is None else total + term
         return total
@@ -120,7 +118,7 @@
     from_grads = product(0, grads, weights_out)
     left_grads = spread_low(from_grads[sketch:], 0)
     right_grads = spread_sketch(from_grads[:sketch])
-    from_acts = product(grads.shape[1] // CHUNK, acts, weights_in)
+    from_acts = product(1, acts, weights_in)
     left_acts = spread_low(from_acts[sketch:], 1)
     right_acts = spread_sketch(from_acts[:sketch])
     left_high, left_low = [
@@ -401,7 +399,7 @@
             pltpu.VMEM((2, rank, tokens), jnp.float32),
             pltpu.VMEM((examples * parts, tokens), jnp.float32),
             pltpu.VMEM((examples * parts, LANES), jnp.float32),
-            pltpu.SemaphoreType.DMA(((width + key_width) // CHUNK, 3)),
+            pltpu.SemaphoreType.DMA((2, len(BOUNDS[1]) - 1, 3)),
             pltpu.SemaphoreType.DMA,
         ],
         compiler_params=pltpu.CompilerParams(vmem_limit_bytes=8 * 2**20),

time: 21.7 us -> 21.9 us (level)
  no operation moved by 1% of the time
where the time goes in v29:
time: 21.9 us; the launch traced here: 21.7 us
  starting transfers between devices  10 us (46%)
  waiting for transfers between devices  5.59 us (26%)
  Pallas kernels  4.79 us (22%)
  between operations  1.31 us (6%)
    ppermute x8, starting transfers between devices, permute(): return lax.ppermute(x, ('ex', 'mp'), sorted(pairs))  10 us
    ppermute x8, waiting for transfers between devices, permute(): return lax.ppermute(x, ('ex', 'mp'), sorted(pairs))  5.59 us
    pallas_call x1, Pallas kernels, local(): pl.pallas_call(functools.partial(partial_kernel, parts, scaling), out_sha...  2.7 us
    pallas_call x1, Pallas kernels, local(): pl.pallas_call(functools.partial(factor_kernel, parts), out_shape=[jax.Sh...  2.08 us
  transfers between devices with their start and end apart: 8, of which 5 were waited for; matrix products, arithmetic and copies ran while one was open for 0% of the time, Pallas kernels for 0%

profile of v29, /device:TPU:0, one launch (start us, length us, event | category | flops | bytes accessed | tf_op | source)
XLA Modules:
  0.0 21.7 jit_solution(17889364786932292210)
XLA Ops:
  0.6 2.7 %partials.1 = (f32[32,256]{1,0:T(8,128)S(1)}, f32[32,256]{1,0:T(8,128)S(1)}, f32[32,256]{1,0:T(8,128)S(1)}, f32[32,256]{1,0:T(8,128)S(1)}) custom-call(bf16[1,128,4096]{2,1,0:T(8,128)(2,1)} %acts_hbm.1, bf16[1,128,1024]{2,1,0:T(8,128)(2,1)} %grads_hbm.1, bf16[1,16,4096]{2,1,0:T(8,128)(2,1)} %down_hbm.1, bf16[1,16,1024]{2,1,0:T(8,128)(2,1)} %up_hbm.1, ...), custom_call_target="tpu_custom_call" | custom-call | tf_op jit(solution)/shard_map/partials/pallas_call | solution.py:388
  3.3 4.6 %collective-permute-start = (f32[32,256]{1,0:T(8,128)S(1)}, f32[32,256]{1,0:T(8,128)S(1)}, u32[]{:S(2)}, u32[]{:S(2)}) collective-permute-start(f32[32,256]{1,0:T(8,128)S(1)} %get-tuple-element.9), channel_id=1, source_target_pairs={{0,7},{1,6},{2,5},{3,4},{4,3},{5,2},{6,1},{7,0},{8,15},{9,14},{10,... | collective-permute-start | bytes 98312 | tf_op jit(solution)/shard_map/ppermute | solution.py:336
  7.9 0.0 collective-permute-start.1
  7.9 0.9 %collective-permute-start.2 = (f32[32,256]{1,0:T(8,128)S(1)}, f32[32,256]{1,0:T(8,128)S(1)}, u32[]{:S(2)}, u32[]{:S(2)}) collective-permute-start(f32[32,256]{1,0:T(8,128)S(1)} %get-tuple-element.11), channel_id=1, source_target_pairs={{0,5},{1,4},{2,7},{3,6},{4,1},{5,0},{6,3},{7,2},{8,13},{9,12},{10,... | collective-permute-start | bytes 98312 | tf_op jit(solution)/shard_map/ppermute | solution.py:336
  8.8 0.0 collective-permute-start.3
  9.5 0.2 collective-permute-done.refs_0_
  9.7 2.8 %collective-permute-done.1.refs_1_ = f32[32,256]{1,0:T(8,128)S(1)} collective-permute-done((f32[32,256]{1,0:T(8,128)S(1)}, f32[32,256]{1,0:T(8,128)S(1)}, u32[]{:S(2)}, u32[]{:S(2)}) %collective-permute-start.1) | collective-permute-done | bytes 32800 | tf_op jit(solution)/shard_map/ppermute | solution.py:336
  12.4 0.0 collective-permute-done.2.refs_2_
  12.4 0.0 collective-permute-done.3.refs_3_
  12.4 1.5 %collective-permute-start.6 = (f32[16,256]{1,0:T(8,128)S(1)}, f32[16,256]{1,0:T(8,128)S(1)}, u32[]{:S(2)}, u32[]{:S(2)}) collective-permute-start(f32[16,256]{1,0:T(8,128)S(1)} %get-tuple-element.14.refs_0_), channel_id=1, source_target_pairs={{0,12},{1,13},{2,14},{3,15},{4,8},{5,9},{6,10},{7,11},{8,20},{9,21... | collective-permute-start | bytes 49160 | tf_op jit(solution)/shard_map/ppermute | solution.py:336
  14.0 1.2 %collective-permute-start.5 = (f32[16,256]{1,0:T(8,128)S(1)}, f32[16,256]{1,0:T(8,128)S(1)}, u32[]{:S(2)}, u32[]{:S(2)}) collective-permute-start(f32[16,256]{1,0:T(8,128)S(1)} %get-tuple-element.14.refs_0_), channel_id=1, source_target_pairs={{0,28},{1,29},{2,30},{3,31},{4,24},{5,25},{6,26},{7,27},{8,4},{9,5... | collective-permute-start | bytes 49160 | tf_op jit(solution)/shard_map/ppermute | solution.py:336
  15.2 1.5 %collective-permute-start.4 = (f32[16,256]{1,0:T(8,128)S(1)}, f32[16,256]{1,0:T(8,128)S(1)}, u32[]{:S(2)}, u32[]{:S(2)}) collective-permute-start(f32[16,256]{1,0:T(8,128)S(1)} %get-tuple-element.14.refs_0_), channel_id=1, source_target_pairs={{0,20},{1,21},{2,22},{3,23},{4,16},{5,17},{6,18},{7,19},{8,28},{9,... | collective-permute-start | bytes 49160 | tf_op jit(solution)/shard_map/ppermute | solution.py:336
  16.6 0.0 collective-permute-done.6.refs_3_
  16.6 0.6 %collective-permute-done.5.refs_2_ = f32[16,256]{1,0:T(8,128)S(1)} collective-permute-done((f32[16,256]{1,0:T(8,128)S(1)}, f32[16,256]{1,0:T(8,128)S(1)}, u32[]{:S(2)}, u32[]{:S(2)}) %collective-permute-start.5) | collective-permute-done | bytes 16416 | tf_op jit(solution)/shard_map/ppermute | solution.py:336
  17.3 1.1 %collective-permute-done.4.refs_1_ = f32[16,256]{1,0:T(8,128)S(1)} collective-permute-done((f32[16,256]{1,0:T(8,128)S(1)}, f32[16,256]{1,0:T(8,128)S(1)}, u32[]{:S(2)}, u32[]{:S(2)}) %collective-permute-start.4) | collective-permute-done | bytes 16416 | tf_op jit(solution)/shard_map/ppermute | solution.py:336
  18.3 0.3 %collective-permute-start.7 = (f32[80,256]{1,0:T(8,128)S(1)}, f32[80,256]{1,0:T(8,128)S(1)}, u32[]{:S(2)}, u32[]{:S(2)}) collective-permute-start(f32[80,256]{1,0:T(8,128)S(1)} %stack.1.held), channel_id=1, source_target_pairs={{0,4},{1,5},{2,6},{3,7},{4,0},{5,1},{6,2},{7,3},{8,12},{9,13},{10,... | collective-permute-start | bytes 245768 | tf_op jit(solution)/shard_map/ppermute | solution.py:336
  18.7 0.9 %collective-permute-done.7.sent = f32[80,256]{1,0:T(8,128)S(1)} collective-permute-done((f32[80,256]{1,0:T(8,128)S(1)}, f32[80,256]{1,0:T(8,128)S(1)}, u32[]{:S(2)}, u32[]{:S(2)}) %collective-permute-start.7) | collective-permute-done | bytes 81952 | tf_op jit(solution)/shard_map/ppermute | solution.py:336
  19.6 2.1 %factors.1 = (f32[4,1024]{1,0:T(4,128)}, f32[4,64,64]{2,1,0:T(8,128)}) custom-call(f32[8,128]{1,0:T(8,128)S(1)} %get-tuple-element.13.ridge, f32[80,256]{1,0:T(8,128)S(1)} %stack.1.held, f32[80,256]{1,0:T(8,128)S(1)} %collective-permute-done.7.sent), custom_call_target="tpu_custom_call" | custom-call | tf_op jit(solution)/shard_map/factors/pallas_call | solution.py:440
  (2 shorter events, 0.0 us)
Async XLA Ops:
  3.3 6.3 %collective-permute-start = (f32[32,256]{1,0:T(8,128)S(1)}, f32[32,256]{1,0:T(8,128)S(1)}, u32[]{:S(2)}, u32[]{:S(2)}) collective-permute-start(f32[32,256]{1,0:T(8,128)S(1)} %get-tuple-element.9), channel_id=1, source_target_pairs={{0,7},{1,6},{2,5},{3,4},{4,3},{5,2},{6,1},{7,0},{8,15},{9,14},{10,... | collective-permute-start | bytes 98312 | tf_op jit(solution)/shard_map/ppermute | solution.py:336
  7.9 4.5 %collective-permute-start.1 = (f32[32,256]{1,0:T(8,128)S(1)}, f32[32,256]{1,0:T(8,128)S(1)}, u32[]{:S(2)}, u32[]{:S(2)}) collective-permute-start(f32[32,256]{1,0:T(8,128)S(1)} %get-tuple-element.10), channel_id=1, source_target_pairs={{0,6},{1,7},{2,4},{3,5},{4,2},{5,3},{6,0},{7,1},{8,14},{9,15},{10,... | collective-permute-start | bytes 98312 | tf_op jit(solution)/shard_map/ppermute | solution.py:336
  7.9 4.5 %collective-permute-start.2 = (f32[32,256]{1,0:T(8,128)S(1)}, f32[32,256]{1,0:T(8,128)S(1)}, u32[]{:S(2)}, u32[]{:S(2)}) collective-permute-start(f32[32,256]{1,0:T(8,128)S(1)} %get-tuple-element.11), channel_id=1, source_target_pairs={{0,5},{1,4},{2,7},{3,6},{4,1},{5,0},{6,3},{7,2},{8,13},{9,12},{10,... | collective-permute-start | bytes 98312 | tf_op jit(solution)/shard_map/ppermute | solution.py:336
  8.8 3.6 %collective-permute-start.3 = (f32[32,256]{1,0:T(8,128)S(1)}, f32[32,256]{1,0:T(8,128)S(1)}, u32[]{:S(2)}, u32[]{:S(2)}) collective-permute-start(f32[32,256]{1,0:T(8,128)S(1)} %get-tuple-element.12), channel_id=1, source_target_pairs={{0,4},{1,5},{2,6},{3,7},{4,0},{5,1},{6,2},{7,3},{8,12},{9,13},{10,... | collective-permute-start | bytes 98312 | tf_op jit(solution)/shard_map/ppermute | solution.py:336
  12.4 4.2 %collective-permute-start.6 = (f32[16,256]{1,0:T(8,128)S(1)}, f32[16,256]{1,0:T(8,128)S(1)}, u32[]{:S(2)}, u32[]{:S(2)}) collective-permute-start(f32[16,256]{1,0:T(8,128)S(1)} %get-tuple-element.14.refs_0_), channel_id=1, source_target_pairs={{0,12},{1,13},{2,14},{3,15},{4,8},{5,9},{6,10},{7,11},{8,20},{9,21... | collective-permute-start | bytes 49160 | tf_op jit(solution)/shard_map/ppermute | solution.py:336
  14.0 3.3 %collective-permute-start.5 = (f32[16,256]{1,0:T(8,128)S(1)}, f32[16,256]{1,0:T(8,128)S(1)}, u32[]{:S(2)}, u32[]{:S(2)}) collective-permute-start(f32[16,256]{1,0:T(8,128)S(1)} %get-tuple-element.14.refs_0_), channel_id=1, source_target_pairs={{0,28},{1,29},{2,30},{3,31},{4,24},{5,25},{6,26},{7,27},{8,4},{9,5... | collective-permute-start | bytes 49160 | tf_op jit(solution)/shard_map/ppermute | solution.py:336
  15.2 3.2 %collective-permute-start.4 = (f32[16,256]{1,0:T(8,128)S(1)}, f32[16,256]{1,0:T(8,128)S(1)}, u32[]{:S(2)}, u32[]{:S(2)}) collective-permute-start(f32[16,256]{1,0:T(8,128)S(1)} %get-tuple-element.14.refs_0_), channel_id=1, source_target_pairs={{0,20},{1,21},{2,22},{3,23},{4,16},{5,17},{6,18},{7,19},{8,28},{9,... | collective-permute-start | bytes 49160 | tf_op jit(solution)/shard_map/ppermute | solution.py:336
  18.3 1.3 %collective-permute-start.7 = (f32[80,256]{1,0:T(8,128)S(1)}, f32[80,256]{1,0:T(8,128)S(1)}, u32[]{:S(2)}, u32[]{:S(2)}) collective-permute-start(f32[80,256]{1,0:T(8,128)S(1)} %stack.1.held), channel_id=1, source_target_pairs={{0,4},{1,5},{2,6},{3,7},{4,0},{5,1},{6,2},{7,3},{8,12},{9,13},{10,... | collective-permute-start | bytes 245768 | tf_op jit(solution)/shard_map/ppermute | solution.py:336

commit v30 on v29

--- a/solution.py
+++ b/solution.py
@@ -13,7 +13,7 @@
 SLOT = 32
 GROUP = LANES // SLOT
 PANEL = 8
-BOUNDS = ((0, 8), (0, 3, 5, 7, 8))
+BOUNDS = ((0, 8), (0, 1, 3, 5, 8))
 
 
 def dot_nt(a, b):

time: 21.9 us -> 21.9 us (level)
  no operation moved by 1% of the time
where the time goes in v30:
time: 21.9 us; the launch traced here: 21.7 us
  starting transfers between devices  10 us (46%)
  waiting for transfers between devices  5.59 us (26%)
  Pallas kernels  4.79 us (22%)
  between operations  1.31 us (6%)
    ppermute x8, starting transfers between devices, permute(): return lax.ppermute(x, ('ex', 'mp'), sorted(pairs))  10 us
    ppermute x8, waiting for transfers between devices, permute(): return lax.ppermute(x, ('ex', 'mp'), sorted(pairs))  5.59 us
    pallas_call x1, Pallas kernels, local(): pl.pallas_call(functools.partial(partial_kernel, parts, scaling), out_sha...  2.7 us
    pallas_call x1, Pallas kernels, local(): pl.pallas_call(functools.partial(factor_kernel, parts), out_shape=[jax.Sh...  2.08 us
  transfers between devices with their start and end apart: 8, of which 5 were waited for; matrix products, arithmetic and copies ran while one was open for 0% of the time, Pallas kernels for 0%

profile of v30, /device:TPU:0, one launch (start us, length us, event | category | flops | bytes accessed | tf_op | source)
XLA Modules:
  0.0 21.7 jit_solution(11199551835021849259)
XLA Ops:
  0.6 2.7 %partials.1 = (f32[32,256]{1,0:T(8,128)S(1)}, f32[32,256]{1,0:T(8,128)S(1)}, f32[32,256]{1,0:T(8,128)S(1)}, f32[32,256]{1,0:T(8,128)S(1)}) custom-call(bf16[1,128,4096]{2,1,0:T(8,128)(2,1)} %acts_hbm.1, bf16[1,128,1024]{2,1,0:T(8,128)(2,1)} %grads_hbm.1, bf16[1,16,4096]{2,1,0:T(8,128)(2,1)} %down_hbm.1, bf16[1,16,1024]{2,1,0:T(8,128)(2,1)} %up_hbm.1, ...), custom_call_target="tpu_custom_call" | custom-call | tf_op jit(solution)/shard_map/partials/pallas_call | solution.py:388
  3.3 4.6 %collective-permute-start = (f32[32,256]{1,0:T(8,128)S(1)}, f32[32,256]{1,0:T(8,128)S(1)}, u32[]{:S(2)}, u32[]{:S(2)}) collective-permute-start(f32[32,256]{1,0:T(8,128)S(1)} %get-tuple-element.9), channel_id=1, source_target_pairs={{0,7},{1,6},{2,5},{3,4},{4,3},{5,2},{6,1},{7,0},{8,15},{9,14},{10,... | collective-permute-start | bytes 98312 | tf_op jit(solution)/shard_map/ppermute | solution.py:336
  7.9 0.0 collective-permute-start.1
  7.9 0.9 %collective-permute-start.2 = (f32[32,256]{1,0:T(8,128)S(1)}, f32[32,256]{1,0:T(8,128)S(1)}, u32[]{:S(2)}, u32[]{:S(2)}) collective-permute-start(f32[32,256]{1,0:T(8,128)S(1)} %get-tuple-element.11), channel_id=1, source_target_pairs={{0,5},{1,4},{2,7},{3,6},{4,1},{5,0},{6,3},{7,2},{8,13},{9,12},{10,... | collective-permute-start | bytes 98312 | tf_op jit(solution)/shard_map/ppermute | solution.py:336
  8.8 0.0 collective-permute-start.3
  9.5 0.2 collective-permute-done.refs_0_
  9.7 2.8 %collective-permute-done.1.refs_1_ = f32[32,256]{1,0:T(8,128)S(1)} collective-permute-done((f32[32,256]{1,0:T(8,128)S(1)}, f32[32,256]{1,0:T(8,128)S(1)}, u32[]{:S(2)}, u32[]{:S(2)}) %collective-permute-start.1) | collective-permute-done | bytes 32800 | tf_op jit(solution)/shard_map/ppermute | solution.py:336
  12.4 0.0 collective-permute-done.2.refs_2_
  12.4 0.0 collective-permute-done.3.refs_3_
  12.4 1.5 %collective-permute-start.6 = (f32[16,256]{1,0:T(8,128)S(1)}, f32[16,256]{1,0:T(8,128)S(1)}, u32[]{:S(2)}, u32[]{:S(2)}) collective-permute-start(f32[16,256]{1,0:T(8,128)S(1)} %get-tuple-element.14.refs_0_), channel_id=1, source_target_pairs={{0,12},{1,13},{2,14},{3,15},{4,8},{5,9},{6,10},{7,11},{8,20},{9,21... | collective-permute-start | bytes 49160 | tf_op jit(solution)/shard_map/ppermute | solution.py:336
  14.0 1.2 %collective-permute-start.5 = (f32[16,256]{1,0:T(8,128)S(1)}, f32[16,256]{1,0:T(8,128)S(1)}, u32[]{:S(2)}, u32[]{:S(2)}) collective-permute-start(f32[16,256]{1,0:T(8,128)S(1)} %get-tuple-element.14.refs_0_), channel_id=1, source_target_pairs={{0,28},{1,29},{2,30},{3,31},{4,24},{5,25},{6,26},{7,27},{8,4},{9,5... | collective-permute-start | bytes 49160 | tf_op jit(solution)/shard_map/ppermute | solution.py:336
  15.2 1.5 %collective-permute-start.4 = (f32[16,256]{1,0:T(8,128)S(1)}, f32[16,256]{1,0:T(8,128)S(1)}, u32[]{:S(2)}, u32[]{:S(2)}) collective-permute-start(f32[16,256]{1,0:T(8,128)S(1)} %get-tuple-element.14.refs_0_), channel_id=1, source_target_pairs={{0,20},{1,21},{2,22},{3,23},{4,16},{5,17},{6,18},{7,19},{8,28},{9,... | collective-permute-start | bytes 49160 | tf_op jit(solution)/shard_map/ppermute | solution.py:336
  16.6 0.0 collective-permute-done.6.refs_3_
  16.6 0.6 %collective-permute-done.5.refs_2_ = f32[16,256]{1,0:T(8,128)S(1)} collective-permute-done((f32[16,256]{1,0:T(8,128)S(1)}, f32[16,256]{1,0:T(8,128)S(1)}, u32[]{:S(2)}, u32[]{:S(2)}) %collective-permute-start.5) | collective-permute-done | bytes 16416 | tf_op jit(solution)/shard_map/ppermute | solution.py:336
  17.3 1.1 %collective-permute-done.4.refs_1_ = f32[16,256]{1,0:T(8,128)S(1)} collective-permute-done((f32[16,256]{1,0:T(8,128)S(1)}, f32[16,256]{1,0:T(8,128)S(1)}, u32[]{:S(2)}, u32[]{:S(2)}) %collective-permute-start.4) | collective-permute-done | bytes 16416 | tf_op jit(solution)/shard_map/ppermute | solution.py:336
  18.3 0.3 %collective-permute-start.7 = (f32[80,256]{1,0:T(8,128)S(1)}, f32[80,256]{1,0:T(8,128)S(1)}, u32[]{:S(2)}, u32[]{:S(2)}) collective-permute-start(f32[80,256]{1,0:T(8,128)S(1)} %stack.1.held), channel_id=1, source_target_pairs={{0,4},{1,5},{2,6},{3,7},{4,0},{5,1},{6,2},{7,3},{8,12},{9,13},{10,... | collective-permute-start | bytes 245768 | tf_op jit(solution)/shard_map/ppermute | solution.py:336
  18.7 0.9 %collective-permute-done.7.sent = f32[80,256]{1,0:T(8,128)S(1)} collective-permute-done((f32[80,256]{1,0:T(8,128)S(1)}, f32[80,256]{1,0:T(8,128)S(1)}, u32[]{:S(2)}, u32[]{:S(2)}) %collective-permute-start.7) | collective-permute-done | bytes 81952 | tf_op jit(solution)/shard_map/ppermute | solution.py:336
  19.6 2.1 %factors.1 = (f32[4,1024]{1,0:T(4,128)}, f32[4,64,64]{2,1,0:T(8,128)}) custom-call(f32[8,128]{1,0:T(8,128)S(1)} %get-tuple-element.13.ridge, f32[80,256]{1,0:T(8,128)S(1)} %stack.1.held, f32[80,256]{1,0:T(8,128)S(1)} %collective-permute-done.7.sent), custom_call_target="tpu_custom_call" | custom-call | tf_op jit(solution)/shard_map/factors/pallas_call | solution.py:440
  (2 shorter events, 0.0 us)
Async XLA Ops:
  3.3 6.3 %collective-permute-start = (f32[32,256]{1,0:T(8,128)S(1)}, f32[32,256]{1,0:T(8,128)S(1)}, u32[]{:S(2)}, u32[]{:S(2)}) collective-permute-start(f32[32,256]{1,0:T(8,128)S(1)} %get-tuple-element.9), channel_id=1, source_target_pairs={{0,7},{1,6},{2,5},{3,4},{4,3},{5,2},{6,1},{7,0},{8,15},{9,14},{10,... | collective-permute-start | bytes 98312 | tf_op jit(solution)/shard_map/ppermute | solution.py:336
  7.9 4.5 %collective-permute-start.1 = (f32[32,256]{1,0:T(8,128)S(1)}, f32[32,256]{1,0:T(8,128)S(1)}, u32[]{:S(2)}, u32[]{:S(2)}) collective-permute-start(f32[32,256]{1,0:T(8,128)S(1)} %get-tuple-element.10), channel_id=1, source_target_pairs={{0,6},{1,7},{2,4},{3,5},{4,2},{5,3},{6,0},{7,1},{8,14},{9,15},{10,... | collective-permute-start | bytes 98312 | tf_op jit(solution)/shard_map/ppermute | solution.py:336
  7.9 4.5 %collective-permute-start.2 = (f32[32,256]{1,0:T(8,128)S(1)}, f32[32,256]{1,0:T(8,128)S(1)}, u32[]{:S(2)}, u32[]{:S(2)}) collective-permute-start(f32[32,256]{1,0:T(8,128)S(1)} %get-tuple-element.11), channel_id=1, source_target_pairs={{0,5},{1,4},{2,7},{3,6},{4,1},{5,0},{6,3},{7,2},{8,13},{9,12},{10,... | collective-permute-start | bytes 98312 | tf_op jit(solution)/shard_map/ppermute | solution.py:336
  8.8 3.6 %collective-permute-start.3 = (f32[32,256]{1,0:T(8,128)S(1)}, f32[32,256]{1,0:T(8,128)S(1)}, u32[]{:S(2)}, u32[]{:S(2)}) collective-permute-start(f32[32,256]{1,0:T(8,128)S(1)} %get-tuple-element.12), channel_id=1, source_target_pairs={{0,4},{1,5},{2,6},{3,7},{4,0},{5,1},{6,2},{7,3},{8,12},{9,13},{10,... | collective-permute-start | bytes 98312 | tf_op jit(solution)/shard_map/ppermute | solution.py:336
  12.4 4.2 %collective-permute-start.6 = (f32[16,256]{1,0:T(8,128)S(1)}, f32[16,256]{1,0:T(8,128)S(1)}, u32[]{:S(2)}, u32[]{:S(2)}) collective-permute-start(f32[16,256]{1,0:T(8,128)S(1)} %get-tuple-element.14.refs_0_), channel_id=1, source_target_pairs={{0,12},{1,13},{2,14},{3,15},{4,8},{5,9},{6,10},{7,11},{8,20},{9,21... | collective-permute-start | bytes 49160 | tf_op jit(solution)/shard_map/ppermute | solution.py:336
  14.0 3.3 %collective-permute-start.5 = (f32[16,256]{1,0:T(8,128)S(1)}, f32[16,256]{1,0:T(8,128)S(1)}, u32[]{:S(2)}, u32[]{:S(2)}) collective-permute-start(f32[16,256]{1,0:T(8,128)S(1)} %get-tuple-element.14.refs_0_), channel_id=1, source_target_pairs={{0,28},{1,29},{2,30},{3,31},{4,24},{5,25},{6,26},{7,27},{8,4},{9,5... | collective-permute-start | bytes 49160 | tf_op jit(solution)/shard_map/ppermute | solution.py:336
  15.2 3.2 %collective-permute-start.4 = (f32[16,256]{1,0:T(8,128)S(1)}, f32[16,256]{1,0:T(8,128)S(1)}, u32[]{:S(2)}, u32[]{:S(2)}) collective-permute-start(f32[16,256]{1,0:T(8,128)S(1)} %get-tuple-element.14.refs_0_), channel_id=1, source_target_pairs={{0,20},{1,21},{2,22},{3,23},{4,16},{5,17},{6,18},{7,19},{8,28},{9,... | collective-permute-start | bytes 49160 | tf_op jit(solution)/shard_map/ppermute | solution.py:336
  18.3 1.3 %collective-permute-start.7 = (f32[80,256]{1,0:T(8,128)S(1)}, f32[80,256]{1,0:T(8,128)S(1)}, u32[]{:S(2)}, u32[]{:S(2)}) collective-permute-start(f32[80,256]{1,0:T(8,128)S(1)} %stack.1.held), channel_id=1, source_target_pairs={{0,4},{1,5},{2,6},{3,7},{4,0},{5,1},{6,2},{7,3},{8,12},{9,13},{10,... | collective-permute-start | bytes 245768 | tf_op jit(solution)/shard_map/ppermute | solution.py:336

commit v31 on v28

--- a/solution.py
+++ b/solution.py
@@ -428,7 +428,7 @@
         compiler_params=pltpu.CompilerParams(vmem_limit_bytes=2 * 2**20),
         name="sums",
     )(damping, *in_vmem(*chunks))
-    shifts = sorted(range(1, shards // 2), key=lambda d: (-min(d, shards // 2 - d), -d))
+    shifts = sorted(range(1, shards // 2), key=lambda d: (-min(d, shards // 2 - d), d))
     near = [columns] + [shift_chips(columns, d) for d in shifts] + [feature_rows]
     held = pl.pallas_call(
         stack_kernel,

time: 21.7 us -> 22.5 us (1.037)
  waiting for transfers between devices: 5.59 us -> 7.33 us
  starting transfers between devices: 10 us -> 8.99 us
    ppermute x8, waiting for transfers between devices: 5.59 us -> 7.33 us  [permute(): return lax.ppermute(x, ('ex', 'mp'), sorted(pairs))]
    ppermute x8, starting transfers between devices: 10 us -> 8.99 us  [permute(): return lax.ppermute(x, ('ex', 'mp'), sorted(pairs))]
where the time goes in v31:
time: 22.5 us; the launch traced here: 22.3 us
  starting transfers between devices  8.99 us (40%)
  waiting for transfers between devices  7.33 us (33%)
  Pallas kernels  4.68 us (21%)
  between operations  1.31 us (6%)
    ppermute x8, starting transfers between devices, permute(): return lax.ppermute(x, ('ex', 'mp'), sorted(pairs))  8.99 us
    ppermute x8, waiting for transfers between devices, permute(): return lax.ppermute(x, ('ex', 'mp'), sorted(pairs))  7.33 us
    pallas_call x1, Pallas kernels, local(): pl.pallas_call(functools.partial(partial_kernel, parts, scaling), out_sha...  2.59 us
    pallas_call x1, Pallas kernels, local(): pl.pallas_call(functools.partial(factor_kernel, parts), out_shape=[jax.Sh...  2.07 us
  transfers between devices with their start and end apart: 8, of which 5 were waited for; matrix products, arithmetic and copies ran while one was open for 0% of the time, Pallas kernels for 0%

profile of v31, /device:TPU:0, one launch (start us, length us, event | category | flops | bytes accessed | tf_op | source)
XLA Modules:
  0.0 22.3 jit_solution(547214936811666533)
XLA Ops:
  0.6 2.6 %partials.1 = (f32[32,256]{1,0:T(8,128)S(1)}, f32[32,256]{1,0:T(8,128)S(1)}, f32[32,256]{1,0:T(8,128)S(1)}, f32[32,256]{1,0:T(8,128)S(1)}) custom-call(bf16[1,128,4096]{2,1,0:T(8,128)(2,1)} %acts_hbm.1, bf16[1,128,1024]{2,1,0:T(8,128)(2,1)} %grads_hbm.1, bf16[1,16,4096]{2,1,0:T(8,128)(2,1)} %down_hbm.1, bf16[1,16,1024]{2,1,0:T(8,128)(2,1)} %up_hbm.1, ...), custom_call_target="tpu_custom_call" | custom-call | tf_op jit(solution)/shard_map/partials/pallas_call | solution.py:390
  3.2 4.6 %collective-permute-start = (f32[32,256]{1,0:T(8,128)S(1)}, f32[32,256]{1,0:T(8,128)S(1)}, u32[]{:S(2)}, u32[]{:S(2)}) collective-permute-start(f32[32,256]{1,0:T(8,128)S(1)} %get-tuple-element.9), channel_id=1, source_target_pairs={{0,7},{1,6},{2,5},{3,4},{4,3},{5,2},{6,1},{7,0},{8,15},{9,14},{10,... | collective-permute-start | bytes 98312 | tf_op jit(solution)/shard_map/ppermute | solution.py:338
  7.8 0.0 collective-permute-start.1
  7.8 0.9 %collective-permute-start.2 = (f32[32,256]{1,0:T(8,128)S(1)}, f32[32,256]{1,0:T(8,128)S(1)}, u32[]{:S(2)}, u32[]{:S(2)}) collective-permute-start(f32[32,256]{1,0:T(8,128)S(1)} %get-tuple-element.11), channel_id=1, source_target_pairs={{0,5},{1,4},{2,7},{3,6},{4,1},{5,0},{6,3},{7,2},{8,13},{9,12},{10,... | collective-permute-start | bytes 98312 | tf_op jit(solution)/shard_map/ppermute | solution.py:338
  8.7 0.0 collective-permute-start.3
  9.4 0.2 collective-permute-done.refs_0_
  9.6 2.8 %collective-permute-done.1.refs_1_ = f32[32,256]{1,0:T(8,128)S(1)} collective-permute-done((f32[32,256]{1,0:T(8,128)S(1)}, f32[32,256]{1,0:T(8,128)S(1)}, u32[]{:S(2)}, u32[]{:S(2)}) %collective-permute-start.1) | collective-permute-done | bytes 32800 | tf_op jit(solution)/shard_map/ppermute | solution.py:338
  12.3 0.0 collective-permute-done.2.refs_2_
  12.3 0.0 collective-permute-done.3.refs_3_
  12.3 2.5 %collective-permute-start.6 = (f32[16,256]{1,0:T(8,128)S(1)}, f32[16,256]{1,0:T(8,128)S(1)}, u32[]{:S(2)}, u32[]{:S(2)}) collective-permute-start(f32[16,256]{1,0:T(8,128)S(1)} %get-tuple-element.14.refs_0_), channel_id=1, source_target_pairs={{0,28},{1,29},{2,30},{3,31},{4,24},{5,25},{6,26},{7,27},{8,4},{9,5... | collective-permute-start | bytes 49160 | tf_op jit(solution)/shard_map/ppermute | solution.py:338
  14.8 0.0 collective-permute-start.5
  14.8 0.8 %collective-permute-start.4 = (f32[16,256]{1,0:T(8,128)S(1)}, f32[16,256]{1,0:T(8,128)S(1)}, u32[]{:S(2)}, u32[]{:S(2)}) collective-permute-start(f32[16,256]{1,0:T(8,128)S(1)} %get-tuple-element.14.refs_0_), channel_id=1, source_target_pairs={{0,20},{1,21},{2,22},{3,23},{4,16},{5,17},{6,18},{7,19},{8,28},{9,... | collective-permute-start | bytes 49160 | tf_op jit(solution)/shard_map/ppermute | solution.py:338
  15.6 0.6 %collective-permute-done.6.refs_3_ = f32[16,256]{1,0:T(8,128)S(1)} collective-permute-done((f32[16,256]{1,0:T(8,128)S(1)}, f32[16,256]{1,0:T(8,128)S(1)}, u32[]{:S(2)}, u32[]{:S(2)}) %collective-permute-start.6) | collective-permute-done | bytes 16416 | tf_op jit(solution)/shard_map/ppermute | solution.py:338
  16.3 2.6 %collective-permute-done.5.refs_2_ = f32[16,256]{1,0:T(8,128)S(1)} collective-permute-done((f32[16,256]{1,0:T(8,128)S(1)}, f32[16,256]{1,0:T(8,128)S(1)}, u32[]{:S(2)}, u32[]{:S(2)}) %collective-permute-start.5) | collective-permute-done | bytes 16416 | tf_op jit(solution)/shard_map/ppermute | solution.py:338
  18.9 0.0 collective-permute-done.4.refs_1_
  18.9 0.2 collective-permute-start.7
  19.1 1.1 %collective-permute-done.7.sent = f32[80,256]{1,0:T(8,128)S(1)} collective-permute-done((f32[80,256]{1,0:T(8,128)S(1)}, f32[80,256]{1,0:T(8,128)S(1)}, u32[]{:S(2)}, u32[]{:S(2)}) %collective-permute-start.7) | collective-permute-done | bytes 81952 | tf_op jit(solution)/shard_map/ppermute | solution.py:338
  20.2 2.1 %factors.1 = (f32[4,1024]{1,0:T(4,128)}, f32[4,64,64]{2,1,0:T(8,128)}) custom-call(f32[8,128]{1,0:T(8,128)S(1)} %get-tuple-element.13.ridge, f32[80,256]{1,0:T(8,128)S(1)} %stack.1.held, f32[80,256]{1,0:T(8,128)S(1)} %collective-permute-done.7.sent), custom_call_target="tpu_custom_call" | custom-call | tf_op jit(solution)/shard_map/factors/pallas_call | solution.py:442
  (2 shorter events, 0.0 us)
Async XLA Ops:
  3.2 6.3 %collective-permute-start = (f32[32,256]{1,0:T(8,128)S(1)}, f32[32,256]{1,0:T(8,128)S(1)}, u32[]{:S(2)}, u32[]{:S(2)}) collective-permute-start(f32[32,256]{1,0:T(8,128)S(1)} %get-tuple-element.9), channel_id=1, source_target_pairs={{0,7},{1,6},{2,5},{3,4},{4,3},{5,2},{6,1},{7,0},{8,15},{9,14},{10,... | collective-permute-start | bytes 98312 | tf_op jit(solution)/shard_map/ppermute | solution.py:338
  7.8 4.5 %collective-permute-start.1 = (f32[32,256]{1,0:T(8,128)S(1)}, f32[32,256]{1,0:T(8,128)S(1)}, u32[]{:S(2)}, u32[]{:S(2)}) collective-permute-start(f32[32,256]{1,0:T(8,128)S(1)} %get-tuple-element.10), channel_id=1, source_target_pairs={{0,6},{1,7},{2,4},{3,5},{4,2},{5,3},{6,0},{7,1},{8,14},{9,15},{10,... | collective-permute-start | bytes 98312 | tf_op jit(solution)/shard_map/ppermute | solution.py:338
  7.8 4.5 %collective-permute-start.2 = (f32[32,256]{1,0:T(8,128)S(1)}, f32[32,256]{1,0:T(8,128)S(1)}, u32[]{:S(2)}, u32[]{:S(2)}) collective-permute-start(f32[32,256]{1,0:T(8,128)S(1)} %get-tuple-element.11), channel_id=1, source_target_pairs={{0,5},{1,4},{2,7},{3,6},{4,1},{5,0},{6,3},{7,2},{8,13},{9,12},{10,... | collective-permute-start | bytes 98312 | tf_op jit(solution)/shard_map/ppermute | solution.py:338
  8.7 3.6 %collective-permute-start.3 = (f32[32,256]{1,0:T(8,128)S(1)}, f32[32,256]{1,0:T(8,128)S(1)}, u32[]{:S(2)}, u32[]{:S(2)}) collective-permute-start(f32[32,256]{1,0:T(8,128)S(1)} %get-tuple-element.12), channel_id=1, source_target_pairs={{0,4},{1,5},{2,6},{3,7},{4,0},{5,1},{6,2},{7,3},{8,12},{9,13},{10,... | collective-permute-start | bytes 98312 | tf_op jit(solution)/shard_map/ppermute | solution.py:338
  12.3 3.9 %collective-permute-start.6 = (f32[16,256]{1,0:T(8,128)S(1)}, f32[16,256]{1,0:T(8,128)S(1)}, u32[]{:S(2)}, u32[]{:S(2)}) collective-permute-start(f32[16,256]{1,0:T(8,128)S(1)} %get-tuple-element.14.refs_0_), channel_id=1, source_target_pairs={{0,28},{1,29},{2,30},{3,31},{4,24},{5,25},{6,26},{7,27},{8,4},{9,5... | collective-permute-start | bytes 49160 | tf_op jit(solution)/shard_map/ppermute | solution.py:338
  14.8 4.1 %collective-permute-start.5 = (f32[16,256]{1,0:T(8,128)S(1)}, f32[16,256]{1,0:T(8,128)S(1)}, u32[]{:S(2)}, u32[]{:S(2)}) collective-permute-start(f32[16,256]{1,0:T(8,128)S(1)} %get-tuple-element.14.refs_0_), channel_id=1, source_target_pairs={{0,12},{1,13},{2,14},{3,15},{4,8},{5,9},{6,10},{7,11},{8,20},{9,21... | collective-permute-start | bytes 49160 | tf_op jit(solution)/shard_map/ppermute | solution.py:338
  14.8 4.1 %collective-permute-start.4 = (f32[16,256]{1,0:T(8,128)S(1)}, f32[16,256]{1,0:T(8,128)S(1)}, u32[]{:S(2)}, u32[]{:S(2)}) collective-permute-start(f32[16,256]{1,0:T(8,128)S(1)} %get-tuple-element.14.refs_0_), channel_id=1, source_target_pairs={{0,20},{1,21},{2,22},{3,23},{4,16},{5,17},{6,18},{7,19},{8,28},{9,... | collective-permute-start | bytes 49160 | tf_op jit(solution)/shard_map/ppermute | solution.py:338
  18.9 1.3 %collective-permute-start.7 = (f32[80,256]{1,0:T(8,128)S(1)}, f32[80,256]{1,0:T(8,128)S(1)}, u32[]{:S(2)}, u32[]{:S(2)}) collective-permute-start(f32[80,256]{1,0:T(8,128)S(1)} %stack.1.held), channel_id=1, source_target_pairs={{0,4},{1,5},{2,6},{3,7},{4,0},{5,1},{6,2},{7,3},{8,12},{9,13},{10,... | collective-permute-start | bytes 245768 | tf_op jit(solution)/shard_map/ppermute | solution.py:338
